TPU v7x, 256 devices: a whole 4x4x8 slice. The times are simulated.
256 devices in a mesh: dp: 8 (over z), seq: 32 (over y, x, core).
Axes of the slice: x: 4, y: 4, z: 8, core: 2. Of those that a mesh axis runs over, the one named last changes fastest.
Arguments:
- inputs: bfloat16 [16, 2048, 1024], P('dp', 'seq'), may hold values from -32 to 32
- grad_out: bfloat16 [16, 2048, 1024], P('dp', 'seq'), may hold values from -6 to 6
- w_qkv: bfloat16 [1024, 3072], replicated, may hold values from -0.1875 to 0.1875
Outputs:
- grad_inputs: bfloat16 [16, 2048, 1024], P('dp', 'seq')
- grad_weights: float32 [1024, 3072], P(('dp', 'seq'))
All inputs are finite; a program needn't handle non-finite values.
Results may differ from a plain program's by a relative error of at most 0.0075.
Values sent between devices are 32-bit elements; how exact they have to be, the bound alone decides.
No kernel may reach another device: no remote copies, remote signals or barrier semaphores. Data moves between devices by JAX's collectives and lax.ppermute only.
A program may use at most 192 MiB of HBM per device.

v0:
```python
import math

import jax
import jax.numpy as jnp
from jax import lax
from jax.sharding import PartitionSpec as P

H = 8
DH = 128
D = 1024


def prefix(part, axis, combine, identity, reverse):
    count = lax.axis_size(axis)
    place = lax.axis_index(axis)
    ahead = count - 1 - place if reverse else place
    gathered = lax.all_gather(part, axis)
    state = jnp.zeros_like(part) + jnp.asarray(identity, part.dtype)

    def one(hop, state):
        source = count - 1 - hop if reverse else hop
        return combine(state, lax.dynamic_index_in_dim(gathered, source, 0, False))

    return lax.fori_loop(0, ahead, one, state)


def add_states(earlier, later_one):
    return earlier + later_one


def body(inputs, grad_out, w_qkv):
    user_count, row_count, feature_count = inputs.shape
    seqlen_total = row_count * lax.axis_size("seq")
    scaling = 1.0 / math.sqrt(DH * seqlen_total)
    flat_inputs = inputs.reshape(user_count * row_count, feature_count)
    projected = jnp.dot(flat_inputs, w_qkv, preferred_element_type=jnp.float32).astype(jnp.bfloat16)
    queries = projected[:, :feature_count].reshape(user_count, row_count, H, DH)
    key_rows = projected[:, feature_count : 2 * feature_count].reshape(user_count, row_count, H, DH)
    values = projected[:, 2 * feature_count :].reshape(user_count, row_count, H, DH)
    cotangent = grad_out.reshape(user_count, row_count, H, DH)
    key_state = jnp.einsum("bshd,bshe->bhde", key_rows, values, preferred_element_type=jnp.float32)
    query_state = jnp.einsum(
        "bthd,bthe->bhde", queries, cotangent, preferred_element_type=jnp.float32
    )
    empty_state = jnp.zeros_like(key_state)
    prior_state = prefix(key_state, "seq", add_states, empty_state, False)
    later_state = prefix(query_state, "seq", add_states, empty_state, True)
    prior_half = prior_state.astype(jnp.bfloat16)
    later_half = later_state.astype(jnp.bfloat16)
    causal = jnp.arange(row_count)[:, None] >= jnp.arange(row_count)[None, :]
    out_value = jnp.einsum("bthe,bshe->bhts", cotangent, values, preferred_element_type=jnp.float32)
    out_value = jnp.where(causal, out_value, 0.0).astype(jnp.bfloat16)
    query_key = jnp.einsum("bthd,bshd->bhts", queries, key_rows, preferred_element_type=jnp.float32)
    query_key = jnp.where(causal, query_key, 0.0).astype(jnp.bfloat16)
    grad_query = scaling * (
        jnp.einsum("bhts,bshd->bthd", out_value, key_rows, preferred_element_type=jnp.float32)
        + jnp.einsum("bthe,bhde->bthd", cotangent, prior_half, preferred_element_type=jnp.float32)
    )
    grad_key = scaling * (
        jnp.einsum("bhts,bthd->bshd", out_value, queries, preferred_element_type=jnp.float32)
        + jnp.einsum("bshe,bhde->bshd", values, later_half, preferred_element_type=jnp.float32)
    )
    grad_value = scaling * (
        jnp.einsum("bhts,bthe->bshe", query_key, cotangent, preferred_element_type=jnp.float32)
        + jnp.einsum("bshd,bhde->bshe", key_rows, later_half, preferred_element_type=jnp.float32)
    )
    total_rows = user_count * row_count
    grad_proj = jnp.concatenate(
        [
            grad_query.reshape(total_rows, feature_count).astype(jnp.bfloat16),
            grad_key.reshape(total_rows, feature_count).astype(jnp.bfloat16),
            grad_value.reshape(total_rows, feature_count).astype(jnp.bfloat16),
        ],
        axis=1,
    )
    grad_rows = lax.dot_general(
        grad_proj, w_qkv, (((1,), (1,)), ((), ())), preferred_element_type=jnp.float32
    ).astype(jnp.bfloat16)
    grad_inputs = grad_rows.reshape(user_count, row_count, feature_count)
    local_grad = lax.psum_scatter(
        lax.dot_general(
            flat_inputs, grad_proj, (((0,), (0,)), ((), ())), preferred_element_type=jnp.float32
        ),
        ("dp", "seq"),
        scatter_dimension=0,
        tiled=True,
    )
    total_sq = lax.psum(jnp.sum(local_grad * local_grad), ("dp", "seq"))
    factor = jnp.minimum(1.0, D / jnp.sqrt(total_sq + 1e-06))
    return (grad_inputs, local_grad * factor)


def solution(mesh):
    in_specs = (P("dp", "seq", None), P("dp", "seq", None), P())
    out_specs = (P("dp", "seq", None), P(("dp", "seq"), None))
    return jax.shard_map(body, mesh=mesh, in_specs=in_specs, out_specs=out_specs, check_vma=False)
```

profile of v0, /device:TPU:1, one launch (start us, length us, event | category | flops | bytes accessed | tf_op | source)
XLA Modules:
  0.0 694.1 jit_solution(4949628631327203472)
XLA Ops:
  7.2 0.0 all-gather.7.cloned.1.call-start
  7.2 0.9 copy-done
  8.1 3.8 convolution_convert_fusion
  11.9 0.1 slice_bitcast_fusion
  12.1 1.4 fusion.15
  13.4 0.0 all-gather.7.cloned.1.call-update
  13.4 0.0 all-gather.5.cloned.1.call-start
  13.6 1.3 fusion.29
  14.9 0.0 all-gather.5.cloned.1.call-update
  15.0 0.0 all-reduce.3.cloned.1.call-start
  15.0 0.3 fusion.8
  15.3 121.4 %all-gather.7.cloned.1.call-done = f32[64,8,128,128]{3,2,1,0:T(8,128)} async-done(((f32[2,8,128,128]{3,2,1,0:T(8,128)}), f32[64,8,128,128]{3,2,1,0:T(8,128)}) %all-gather.7.cloned.1.call-update) | async-done | bytes 33554448 | tf_op jit(solution)/shard_map/all_gather | solution.py:17
  136.7 0.1 broadcast_in_dim.19.clone.1
  136.8 46.0 %while.23 = (s32[]{:T(128)}, f32[2,8,128,128]{3,2,1,0:T(8,128)S(1)}, s32[]{:T(128)}, f32[32,2,8,128,128]{4,3,2,1,0:T(8,128)}, s32[]{:T(128)}, /*index=5*/s32[]{:T(128)}, s32[]{:T(128)}, s32[]{:T(128)}) while((s32[]{:T(128)}, f32[2,8,128,128]{3,2,1,0:T(8,128)S(1)}, s32[]{:T(128)}, f32[32,2,8,128,128]{4,3,2,1,0:T(8,128)}, s32[]{:T(128)}, ...), condition=%wide.region_3.4_spmd, body=%wide.region_2.3_spmd.sunk | while | flops 262150 | bytes 3145863 | solution.py:24
  136.8 1.5 bitcast_add_fusion.5
  138.3 1.5 bitcast_add_fusion.5
  139.8 1.5 bitcast_add_fusion.5
  141.3 1.5 bitcast_add_fusion.5
  142.9 1.5 bitcast_add_fusion.5
  144.4 1.5 bitcast_add_fusion.5
  145.9 1.5 bitcast_add_fusion.5
  147.4 1.5 bitcast_add_fusion.5
  148.9 1.5 bitcast_add_fusion.5
  150.5 1.6 bitcast_add_fusion.5
  152.1 1.6 bitcast_add_fusion.5
  153.8 1.5 bitcast_add_fusion.5
  155.3 1.5 bitcast_add_fusion.5
  156.8 1.5 bitcast_add_fusion.5
  158.3 1.5 bitcast_add_fusion.5
  159.9 1.5 bitcast_add_fusion.5
  161.4 1.5 bitcast_add_fusion.5
  163.0 1.5 bitcast_add_fusion.5
  164.5 1.5 bitcast_add_fusion.5
  166.0 1.5 bitcast_add_fusion.5
  167.6 1.5 bitcast_add_fusion.5
  169.1 1.5 bitcast_add_fusion.5
  170.6 1.5 bitcast_add_fusion.5
  172.1 1.5 bitcast_add_fusion.5
  173.7 1.5 bitcast_add_fusion.5
  175.2 1.5 bitcast_add_fusion.5
  176.7 1.5 bitcast_add_fusion.5
  178.2 1.5 bitcast_add_fusion.5
  179.7 1.5 bitcast_add_fusion.5
  181.2 1.5 bitcast_add_fusion.5
  182.7 0.5 fusion.20
  183.2 1.1 convolution_bitcast_fusion.1
  184.3 73.2 %all-gather.5.cloned.1.call-done = f32[64,8,128,128]{3,2,1,0:T(8,128)} async-done(((f32[2,8,128,128]{3,2,1,0:T(8,128)}), f32[64,8,128,128]{3,2,1,0:T(8,128)}) %all-gather.5.cloned.1.call-update) | async-done | bytes 33554448 | tf_op jit(solution)/shard_map/all_gather | solution.py:17
  257.5 0.1 broadcast_in_dim.19.clone
  257.6 1.5 while.22
  257.6 1.5 bitcast_add_fusion.4
  259.1 0.5 fusion.12
  259.5 0.3 fusion.11
  259.8 0.2 copy.43
  260.0 0.2 fusion.10
  260.3 0.2 copy.48
  260.5 1.4 fusion.7
  261.9 0.2 copy.54
  262.1 6.3 convolution_bitcast_fusion
  268.5 329.7 %all-reduce.3.cloned.1.call-done = f32[1024,3072]{0,1:T(8,128)} async-done(((f32[1024,3072]{0,1:T(8,128)}), f32[1024,3072]{0,1:T(8,128)}) %all-reduce.3.cloned.1.call-update) | async-done | bytes 12582928
  598.2 2.5 multiply_reduce_fusion
  600.6 5.7 convolution_convert_fusion.1
  606.3 77.6 %psum.7 = f32[]{:T(128)} all-reduce(f32[]{:T(128)} %multiply_reduce_fusion), channel_id=1, replica_groups=mesh['dp'=8,'seq'=32] {'dp','seq'}, use_global_device_ids=true, to_apply=%region_6.7 | all-reduce | flops 1 | bytes 8 | tf_op jit(solution)/shard_map/psum | solution.py:88
  684.6 1.9 dynamic-slice_multiply_fusion
  686.5 1.1 copy.55
  (11 shorter events, 0.3 us)
Async XLA Ops:
  7.2 1.0 copy-start
  7.2 129.5 %all-gather.7.cloned.1.call-start = ((), (), s32[]{:S(2)}) async-start(), calls=%async_computation.1 | async-start | bytes 34603008 | tf_op jit(solution)/shard_map/all_gather | solution.py:17
  8.1 3.9 copy-start.1
  13.4 244.0 %all-gather.5.cloned.1.call-start = ((), (), s32[]{:S(2)}) async-start(), calls=%async_computation | async-start | bytes 34603008 | tf_op jit(solution)/shard_map/all_gather | solution.py:17
  15.0 583.2 %all-reduce.3.cloned.1.call-start = ((), (), s32[]{:S(2)}) async-start(), calls=%async_computation.2 | async-start | bytes 25165824
Sparse Core Ops, SparseCore 0:
  13.6 123.0 all-gather.6
  139.2 118.1 all-gather.4
  268.6 329.5 all-reduce.2
where the time goes:
time: 696 us; the launch traced here: 694 us
  waiting for transfers between devices  524 us (75%)
  blocking collectives  77.6 us (11%)
  other arithmetic  51 us (7%)
  matrix products  22.7 us (3%)
  between operations  14.6 us (2%)
    unnamed x4, waiting for transfers between devices  330 us
    all_gather x2, waiting for transfers between devices, prefix(): gathered = lax.all_gather(part, axis)  195 us
    psum x1, blocking collectives, body(): total_sq = lax.psum(jnp.sum(local_grad * local_grad), ('dp', 'seq'))  77.6 us
    add x31, other arithmetic, add_states(): return earlier + later_one  46.6 us
  transfers between devices with their start and end apart: 3, of which 3 were waited for; matrix products, arithmetic and copies ran while one was open for 7% of the time, Pallas kernels for 0%

commit v1 on v0

v1 whole, which is shorter than its diff:
```python
import functools
import math

import jax
import jax.numpy as jnp
from jax import lax
from jax.experimental import pallas as pl
from jax.experimental.pallas import tpu as pltpu
from jax.sharding import PartitionSpec as P

H = 8
DH = 128
D = 1024
NY = 4
NX = 4
GROUP = 2 * NX
BF16 = jnp.bfloat16
F32 = jnp.float32
VMEM = pl.BlockSpec(memory_space=pltpu.VMEM)
SMEM = pl.BlockSpec(memory_space=pltpu.SMEM)
MIB = 1 << 20


def seq_perm(dy, dx, dc):
    moves = []
    for y in range(NY):
        for x in range(NX):
            for c in range(2):
                source = (y * NX + x) * 2 + c
                target = (((y + dy) % NY) * NX + (x + dx) % NX) * 2 + (c ^ dc)
                moves.append((source, target))
    return moves


def send(value, dy=0, dx=0, dc=0):
    return lax.ppermute(value, "seq", seq_perm(dy, dx, dc))


def head_columns(array, head):
    return lax.dynamic_slice_in_dim(array, head * DH, DH, 1)


def struct(shape, dtype):
    return jax.ShapeDtypeStruct(shape, dtype)


def dot(a, b, over_a, over_b):
    return lax.dot_general(a, b, (((over_a,), (over_b,)), ((), ())), preferred_element_type=F32)


def block_kernel(users, *refs):
    first, second, w, cot, rows_t, proj, cot_half, key_state, query_state, intra = refs
    total = first.shape[0]
    size = total // users
    causal = lax.broadcasted_iota(jnp.int32, (size, size), 0) >= lax.broadcasted_iota(
        jnp.int32, (size, size), 1
    )
    cot_half[...] = cot[...].astype(BF16)
    for i, ref in enumerate((first, second)):
        x = ref[...].astype(BF16)
        rows_t[:, i * total : (i + 1) * total] = x.T
        proj[i * total : (i + 1) * total, :] = dot(x, w[...], 1, 0).astype(BF16)
        for u in range(users):
            here = slice(i * total + u * size, i * total + (u + 1) * size)
            q, k, v = (proj[here, part * DH : (part + 1) * DH] for part in range(3))
            g = cot_half[here, :]
            key_state[i, u] = dot(k, v, 0, 0)
            query_state[i, u] = dot(q, g, 0, 0)
            out_value = jnp.where(causal, dot(g, v, 1, 1), 0.0).astype(BF16)
            query_key = jnp.where(causal, dot(q, k, 1, 1), 0.0).astype(BF16)
            intra[here, :DH] = dot(out_value, k, 1, 0)
            intra[here, DH : 2 * DH] = dot(out_value, q, 0, 0)
            intra[here, 2 * DH :] = dot(query_key, g, 0, 0)


def blocks(first, second, w_head, cot, users):
    total, features = first.shape
    return pl.pallas_call(
        functools.partial(block_kernel, users),
        out_shape=(
            struct((features, 2 * total), BF16),
            struct((2 * total, 3 * DH), BF16),
            struct((2 * total, DH), BF16),
            struct((2, users, DH, DH), F32),
            struct((2, users, DH, DH), F32),
            struct((2 * total, 3 * DH), F32),
        ),
        in_specs=[VMEM] * 4,
        out_specs=(VMEM,) * 6,
        compiler_params=pltpu.CompilerParams(vmem_limit_bytes=24 * MIB),
        cost_estimate=pl.CostEstimate(
            flops=2 * 2 * total * features * 3 * DH, bytes_accessed=4 * MIB, transcendentals=0
        ),
        name="blocks",
    )(first, second, w_head, cot)


def total_kernel(place, *refs):
    keys, queries, outs = refs[:NX], refs[NX : 2 * NX], refs[2 * NX :]
    key_total = sum(ref[i] for ref in keys for i in range(2))
    query_total = sum(ref[i] for ref in queries for i in range(2))
    for dy in range(1, NY):
        outs[dy - 1][...] = jnp.where(place[0] + dy < NY, key_total, query_total)


def totals(place, key_states, query_states):
    shape = key_states[0].shape[1:]
    return pl.pallas_call(
        total_kernel,
        out_shape=(struct(shape, F32),) * (NY - 1),
        in_specs=[SMEM] + [VMEM] * (2 * NX),
        out_specs=(VMEM,) * (NY - 1),
        compiler_params=pltpu.CompilerParams(vmem_limit_bytes=16 * MIB),
        cost_estimate=pl.CostEstimate(flops=MIB, bytes_accessed=3 * MIB, transcendentals=0),
        name="totals",
    )(place, *key_states, *query_states)


def grad_kernel(scaling, users, dp_count, place, *refs):
    y, x, c = place[0], place[1], place[2]
    arrived, refs = refs[: NY - 1], refs[NY - 1 :]
    keys, refs = refs[:NX], refs[NX:]
    queries, refs = refs[:NX], refs[NX:]
    rows_t, refs = refs[:NX], refs[NX:]
    proj, refs = refs[:NX], refs[NX:]
    cots, refs = refs[:NX], refs[NX:]
    intra, refs = refs[:NX], refs[NX:]
    grad_proj, pieces, refs = refs[0], refs[1 : 1 + NY], refs[1 + NY :]
    key_all, query_all, prior_all, later_all, product = refs
    for dx in range(NX):
        key_all[2 * dx : 2 * dx + 2] = keys[dx][...]
        query_all[2 * dx : 2 * dx + 2] = queries[dx][...]
    prior = jnp.zeros(arrived[0].shape, F32)
    later = jnp.zeros(arrived[0].shape, F32)
    for dy in range(1, NY):
        value = arrived[dy - 1][...]
        prior = prior + jnp.where(y >= dy, value, 0.0)
        later = later + jnp.where(y >= dy, 0.0, value)

    def slot(position):
        return ((x + NX - position // 2) % NX) * 2 + (c ^ (position % 2))

    for position in range(GROUP):
        here = slot(position)
        prior_all[here] = prior.astype(BF16)
        prior = prior + key_all[here]
    for position in reversed(range(GROUP)):
        here = slot(position)
        later_all[here] = later.astype(BF16)
        later = later + query_all[here]
    total = proj[0].shape[0] // 2
    size = total // users
    for dx in range(NX):
        for i in range(2):
            for u in range(users):
                here = slice(i * total + u * size, i * total + (u + 1) * size)
                there = slice(dx * 2 * total + here.start, dx * 2 * total + here.stop)
                k, v = proj[dx][here, DH : 2 * DH], proj[dx][here, 2 * DH :]
                prior_state = prior_all[2 * dx + i, u]
                later_state = later_all[2 * dx + i, u]
                parts = (
                    dot(cots[dx][here, :], prior_state, 1, 1),
                    dot(v, later_state, 1, 1),
                    dot(k, later_state, 1, 0),
                )
                for part in range(3):
                    columns = slice(part * DH, (part + 1) * DH)
                    grad_proj[there, columns] = (
                        scaling * (intra[dx][here, columns] + parts[part])
                    ).astype(BF16)
    span = 2 * total
    product[...] = sum(
        dot(rows_t[dx][...], grad_proj[dx * span : (dx + 1) * span, :], 1, 0)
        for dx in range(NX)
    )
    row_block = product.shape[0] // (dp_count * NY)
    for dy in range(NY):
        target = (y + dy) % NY
        for z in range(dp_count):
            start = pl.multiple_of((z * NY + target) * row_block, row_block)
            pieces[dy][z] = product[pl.ds(start, row_block), :]


def gradients(place, arrived, parts, scaling, users, dp_count):
    rows_t, proj, cots, keys, queries, intra = zip(*parts)
    features, span = rows_t[0].shape
    row_block = features // (dp_count * NY)
    return pl.pallas_call(
        functools.partial(grad_kernel, scaling, users, dp_count),
        out_shape=(struct((NX * span, 3 * DH), BF16),)
        + (struct((dp_count, row_block, 3 * DH), F32),) * NY,
        in_specs=[SMEM] + [VMEM] * (NY - 1 + 6 * NX),
        out_specs=(VMEM,) * (1 + NY),
        scratch_shapes=[
            pltpu.VMEM((GROUP, users, DH, DH), F32),
            pltpu.VMEM((GROUP, users, DH, DH), F32),
            pltpu.VMEM((GROUP, users, DH, DH), BF16),
            pltpu.VMEM((GROUP, users, DH, DH), BF16),
            pltpu.VMEM((features, 3 * DH), F32),
        ],
        compiler_params=pltpu.CompilerParams(vmem_limit_bytes=32 * MIB),
        cost_estimate=pl.CostEstimate(
            flops=2 * NX * span * features * 3 * DH, bytes_accessed=10 * MIB, transcendentals=0
        ),
        name="gradients",
    )(place, *arrived, *keys, *queries, *rows_t, *proj, *cots, *intra)


def input_kernel(place, *refs):
    x, c = place[1], place[2]
    keep, swap, w, out, full = refs[:NX], refs[NX], refs[NX + 1], refs[NX + 2], refs[NX + 3]
    total = out.shape[0]
    for dx in range(NX):
        for dc in range(2):
            head = ((x + dx) % NX) * 2 + (c ^ dc)
            for part in range(3):
                columns = slice(part * DH, (part + 1) * DH)
                value = keep[dx][:total, columns] if dc == 0 else swap[dx, :, columns]
                start = pl.multiple_of((part * H + head) * DH, DH)
                full[:, pl.ds(start, DH)] = value.astype(BF16)
    out[...] = dot(full[...], w[...], 1, 1).astype(BF16)


def input_gradient(place, keep, swap, w_qkv):
    total = swap.shape[1]
    features, width = w_qkv.shape
    return pl.pallas_call(
        input_kernel,
        out_shape=struct((total, features), BF16),
        in_specs=[SMEM] + [VMEM] * (NX + 2),
        out_specs=VMEM,
        scratch_shapes=[pltpu.VMEM((total, width), BF16)],
        compiler_params=pltpu.CompilerParams(vmem_limit_bytes=24 * MIB),
        cost_estimate=pl.CostEstimate(
            flops=2 * total * features * width, bytes_accessed=10 * MIB, transcendentals=0
        ),
        name="input_gradient",
    )(place, *keep, swap, w_qkv)


def body(inputs, grad_out, w_qkv):
    user_count, row_count, feature_count = inputs.shape
    seqlen_total = row_count * lax.axis_size("seq")
    dp_count = lax.axis_size("dp")
    scaling = 1.0 / math.sqrt(DH * seqlen_total)
    index = lax.axis_index("seq")
    y, x, c = index // GROUP, (index // 2) % NX, index % 2
    place = jnp.stack([y, x, c])
    head = x * 2 + c
    total_rows = user_count * row_count

    own = inputs.reshape(total_rows, feature_count).astype(F32)
    half = total_rows // 2
    from_left = send(own, dx=1)
    from_right = send(own, dx=-1)
    other = send(own, dc=1)
    far_low = send(from_left[:half], dx=1)
    far_high = send(from_right[half:], dx=-1)
    left_other = send(from_left, dc=1)
    right_other = send(from_right, dc=1)
    far = jnp.concatenate([far_low, far_high], axis=0)
    far_other = send(far, dc=1)

    cot = grad_out.reshape(total_rows, feature_count).astype(F32)
    by_head = cot.reshape(total_rows, NX, 2, DH)
    mine = lax.dynamic_index_in_dim(by_head, c, 2, False)
    theirs = lax.dynamic_index_in_dim(by_head, 1 - c, 2, False)
    swapped = send(theirs.reshape(total_rows, NX * DH), dc=1)
    pair = jnp.concatenate([mine.reshape(total_rows, NX * DH), swapped], axis=0)
    cot_pieces = [head_columns(pair, x)]
    for dx in range(1, NX):
        piece = send(head_columns(pair, (x + dx) % NX), dx=dx)
        cot_pieces.append(piece)

    w_head = jnp.concatenate(
        [head_columns(w_qkv, part * H + head) for part in range(3)], axis=1
    )
    pairs = [(own, other), (from_left, left_other), (far, far_other), (from_right, right_other)]
    parts = [
        blocks(first, second, w_head, cot_piece, user_count)
        for (first, second), cot_piece in zip(pairs, cot_pieces)
    ]
    sent = totals(place, [part[3] for part in parts], [part[4] for part in parts])
    arrived = [send(sent[dy - 1], dy=dy) for dy in range(1, NY)]
    grad_proj, *pieces = gradients(place, arrived, parts, scaling, user_count, dp_count)

    summed = pieces[0]
    for dy in range(1, NY):
        summed = summed + send(pieces[dy], dy=dy)
    tile = jnp.sum(lax.all_to_all(summed, "dp", 0, 0), axis=0)

    span = 2 * total_rows
    back = [grad_proj[:span].astype(F32)]
    for dx in range(1, NX):
        back.append(send(grad_proj[dx * span : (dx + 1) * span].astype(F32), dx=-dx))
    swap = send(jnp.stack([piece[total_rows:] for piece in back]), dc=1)
    grad_rows = input_gradient(place, back, swap, w_qkv)
    grad_inputs = grad_rows.reshape(user_count, row_count, feature_count)

    square = jnp.sum(tile * tile)
    row_block = tile.shape[0]
    out_rows = row_block // H
    by_owner = tile.reshape(H, out_rows * 3, DH)
    got = jnp.zeros((H, out_rows * 3, DH), F32)
    for dx in range(NX):
        for dc in range(2):
            target = ((x + dx) % NX) * 2 + (c ^ dc)
            piece = lax.dynamic_index_in_dim(by_owner, target, 0, False)
            if dx or dc:
                piece = send(piece, dx=dx, dc=dc)
            source = ((x - dx) % NX) * 2 + (c ^ dc)
            got = lax.dynamic_update_index_in_dim(got, piece, source, 0)
    device_count = dp_count * lax.axis_size("seq")
    squares = lax.all_to_all(
        jnp.full((device_count, DH), square), ("dp", "seq"), 0, 0, tiled=True
    )
    total_sq = jnp.sum(squares[:, 0])
    factor = jnp.minimum(1.0, D / jnp.sqrt(total_sq + 1e-06))
    weights = jnp.transpose(got.reshape(H, out_rows, 3, DH), (1, 2, 0, 3))
    return (grad_inputs, weights.reshape(out_rows, 3 * feature_count) * factor)


def solution(mesh):
    in_specs = (P("dp", "seq", None), P("dp", "seq", None), P())
    out_specs = (P("dp", "seq", None), P(("dp", "seq"), None))
    return jax.shard_map(body, mesh=mesh, in_specs=in_specs, out_specs=out_specs, check_vma=False)
```

time: 696 us -> 140 us (0.20)
  waiting for transfers between devices: 524 us -> 35.9 us
  blocking collectives: 77.6 us -> 0 us
  starting transfers between devices: 0.12 us -> 68.8 us
  other arithmetic: 51 us -> 4.86 us
  matrix products: 22.7 us -> 0 us
  Pallas kernels: 0 us -> 13.9 us
  between operations: 14.6 us -> 1.92 us
  local copies, waits for them, and re-layouts: 2.99 us -> 14.3 us
    unnamed x4 -> x0, waiting for transfers between devices: 330 us -> none
    all_gather x2 -> x0, waiting for transfers between devices: 195 us -> none  [prefix(): gathered = lax.all_gather(part, axis)]
    psum x1 -> x0, blocking collectives: 77.6 us -> none  [body(): total_sq = lax.psum(jnp.sum(local_grad * local_grad), ('dp', 'seq'))]
    ppermute x0 -> x29, starting transfers between devices: none -> 48.6 us  [send(): return lax.ppermute(value, 'seq', seq_perm(dy, dx, dc))]
    add x31 -> x1, other arithmetic: 46.6 us -> 0.84 us  [body(): summed = summed + send(pieces[dy], dy=dy)]
    ppermute x0 -> x29, waiting for transfers between devices: none -> 26.2 us  [send(): return lax.ppermute(value, 'seq', seq_perm(dy, dx, dc))]
    dot_general x12 -> x0, matrix products: 22.7 us -> none  [the longest x1 6.31 us: body(): lax.dot_general(flat_inputs, grad_proj, (((0,), (0,)), ((), ())), preferr...]
    all_to_all x0 -> x2, starting transfers between devices: none -> 20.2 us  [the longest x1 11.8 us: body(): lax.all_to_all(jnp.full((device_count, DH), square), ('dp', 'seq'), 0, 0,...]
  transfers between devices with their start and end apart: 3 -> 31, of which waited for: 3 -> 12; matrix products, arithmetic and copies ran while one was open for 7% -> 10% of each run, Pallas kernels for 0% -> 6%
where the time goes in v1:
time: 140 us
  starting transfers between devices  68.8 us (49%)
  waiting for transfers between devices  35.9 us (26%)
  local copies, waits for them, and re-layouts  14.3 us (10%)
  Pallas kernels  13.9 us (10%)
  other arithmetic  4.86 us (3%)
  between operations  1.92 us (1%)
    ppermute x29, starting transfers between devices, send(): return lax.ppermute(value, 'seq', seq_perm(dy, dx, dc))  48.6 us
    ppermute x29, waiting for transfers between devices, send(): return lax.ppermute(value, 'seq', seq_perm(dy, dx, dc))  26.2 us
    all_to_all x1, starting transfers between devices, body(): lax.all_to_all(jnp.full((device_count, DH), square), ('dp', 'seq'), 0, 0,...  11.8 us
    all_to_all x1, waiting for transfers between devices, body(): tile = jnp.sum(lax.all_to_all(summed, 'dp', 0, 0), axis=0)  9.76 us
    all_to_all x1, starting transfers between devices, body(): tile = jnp.sum(lax.all_to_all(summed, 'dp', 0, 0), axis=0)  8.37 us
    pallas_call x4, Pallas kernels, blocks(): pl.pallas_call(functools.partial(block_kernel, users), out_shape=(struct(...  6.73 us
    unnamed x6, local copies, waits for them, and re-layouts  5.12 us
    pallas_call x1, Pallas kernels, input_gradient(): pl.pallas_call(input_kernel, out_shape=struct((total, features), BF16), i...  3.55 us
  transfers between devices with their start and end apart: 31, of which 12 were waited for; matrix products, arithmetic and copies ran while one was open for 10% of the time, Pallas kernels for 6%

profile of v1, /device:TPU:1, one launch (start us, length us, event | category | flops | bytes accessed | tf_op | source)
XLA Modules:
  0.0 139.6 jit_solution(8249350149563333019)
XLA Ops:
  0.6 1.0 bitcast_convert_fusion.refs_0_
  1.6 2.1 %collective-permute-start.2 = (f32[128,1024]{1,0:T(8,128)S(1)}, f32[128,1024]{1,0:T(8,128)S(1)}, u32[]{:S(2)}, u32[]{:S(2)}) collective-permute-start(f32[128,1024]{1,0:T(8,128)S(1)} %bitcast_convert_fusion.refs_0_), channel_id=1, source_target_pairs={{0,2},{1,3},{2,4},{3,5},{4,6},{5,7},{6,0},{7,1},{8,10},{9,11},{10,... | collective-permute-start | bytes 1572872 | tf_op jit(solution)/shard_map/ppermute | solution.py:36
  3.7 1.4 collective-permute-start.6
  5.1 3.1 %collective-permute-start = (f32[128,1024]{1,0:T(8,128)S(1)}, f32[128,1024]{1,0:T(8,128)S(1)}, u32[]{:S(2)}, u32[]{:S(2)}) collective-permute-start(f32[128,1024]{1,0:T(8,128)S(1)} %bitcast_convert_fusion.refs_0_), channel_id=1, source_target_pairs={{0,1},{1,0},{2,3},{3,2},{4,5},{5,4},{6,7},{7,6},{8,9},{9,8},{10,11... | collective-permute-start | bytes 1572872 | tf_op jit(solution)/shard_map/ppermute | solution.py:36
  8.2 1.5 %reshape.39 = f32[128,4,2,128]{3,2,1,0:T(2,128)S(1)} reshape(bf16[2,64,1024]{2,1,0:T(8,128)(2,1)} %param.4) | data formatting | bytes 786432 | tf_op jit(solution)/shard_map/convert_element_type | solution.py:264
  9.7 0.5 constant_dynamic-slice_fusion.5
  10.1 0.7 copy.28
  10.9 3.5 %collective-permute-done.2.refs_0_ = f32[128,1024]{1,0:T(8,128)S(1)} collective-permute-done((f32[128,1024]{1,0:T(8,128)S(1)}, f32[128,1024]{1,0:T(8,128)S(1)}, u32[]{:S(2)}, u32[]{:S(2)}) %collective-permute-start.2) | collective-permute-done | bytes 524320 | tf_op jit(solution)/shard_map/ppermute | solution.py:36
  14.4 0.7 slice.44
  15.1 1.9 %collective-permute-start.5 = (f32[64,1024]{1,0:T(8,128)}, f32[64,1024]{1,0:T(8,128)}, u32[]{:S(2)}, u32[]{:S(2)}) collective-permute-start(f32[64,1024]{1,0:T(8,128)} %slice.44), channel_id=1, source_target_pairs={{0,2},{1,3},{2,4},{3,5},{4,6},{5,7},{6,0},{7,1},{8,10},{9,11},{10,... | collective-permute-start | bytes 786440 | tf_op jit(solution)/shard_map/ppermute | solution.py:36
  17.0 0.7 slice.45
  17.7 1.6 %collective-permute-start.7 = (f32[64,1024]{1,0:T(8,128)}, f32[64,1024]{1,0:T(8,128)}, u32[]{:S(2)}, u32[]{:S(2)}) collective-permute-start(f32[64,1024]{1,0:T(8,128)} %slice.45), channel_id=1, source_target_pairs={{0,6},{1,7},{2,0},{3,1},{4,2},{5,3},{6,4},{7,5},{8,14},{9,15},{10,... | collective-permute-start | bytes 786440 | tf_op jit(solution)/shard_map/ppermute | solution.py:36
  19.3 1.2 constant_dynamic-slice_fusion.9
  20.6 3.4 %collective-permute-start.10 = (f32[128,1024]{1,0:T(8,128)S(1)}, f32[128,1024]{1,0:T(8,128)S(1)}, u32[]{:S(2)}, u32[]{:S(2)}) collective-permute-start(f32[128,1024]{1,0:T(8,128)S(1)} %collective-permute-done.6.refs_0_), channel_id=1, source_target_pairs={{0,1},{1,0},{2,3},{3,2},{4,5},{5,4},{6,7},{7,6},{8,9},{9,8},{10,11... | collective-permute-start | bytes 1572872 | tf_op jit(solution)/shard_map/ppermute | solution.py:36
  24.0 2.5 %collective-permute-start.3 = (f32[128,1024]{1,0:T(8,128)S(1)}, f32[128,1024]{1,0:T(8,128)S(1)}, u32[]{:S(2)}, u32[]{:S(2)}) collective-permute-start(f32[128,1024]{1,0:T(8,128)S(1)} %collective-permute-done.2.refs_0_), channel_id=1, source_target_pairs={{0,1},{1,0},{2,3},{3,2},{4,5},{5,4},{6,7},{7,6},{8,9},{9,8},{10,11... | collective-permute-start | bytes 1572872 | tf_op jit(solution)/shard_map/ppermute | solution.py:36
  26.5 1.0 constant_dynamic-update-slice_fusion.2
  27.5 1.0 constant_dynamic-update-slice_fusion.1.refs_0_
  28.6 1.0 constant_dynamic-update-slice_fusion
  29.6 2.8 %collective-permute-start.11 = (f32[256,128]{1,0:T(8,128)S(1)}, f32[256,128]{1,0:T(8,128)S(1)}, u32[]{:S(2)}, u32[]{:S(2)}) collective-permute-start(f32[256,128]{1,0:T(8,128)S(1)} %get-tuple-element.73), channel_id=1, source_target_pairs={{0,6},{1,7},{2,0},{3,1},{4,2},{5,3},{6,4},{7,5},{8,14},{9,15},{10,... | collective-permute-start | bytes 393224 | tf_op jit(solution)/shard_map/ppermute | solution.py:36
  32.5 2.8 %collective-permute-done.11.refs_3_ = f32[256,128]{1,0:T(8,128)S(1)} collective-permute-done((f32[256,128]{1,0:T(8,128)S(1)}, f32[256,128]{1,0:T(8,128)S(1)}, u32[]{:S(2)}, u32[]{:S(2)}) %collective-permute-start.11) | collective-permute-done | bytes 131104 | tf_op jit(solution)/shard_map/ppermute | solution.py:36
  35.3 2.1 %collective-permute-start.9 = (f32[256,128]{1,0:T(8,128)S(1)}, f32[256,128]{1,0:T(8,128)S(1)}, u32[]{:S(2)}, u32[]{:S(2)}) collective-permute-start(f32[256,128]{1,0:T(8,128)S(1)} %get-tuple-element.74), channel_id=1, source_target_pairs={{0,4},{1,5},{2,6},{3,7},{4,0},{5,1},{6,2},{7,3},{8,12},{9,13},{10,... | collective-permute-start | bytes 393224 | tf_op jit(solution)/shard_map/ppermute | solution.py:36
  37.5 1.9 %collective-permute-start.4 = (f32[256,128]{1,0:T(8,128)S(1)}, f32[256,128]{1,0:T(8,128)S(1)}, u32[]{:S(2)}, u32[]{:S(2)}) collective-permute-start(f32[256,128]{1,0:T(8,128)S(1)} %get-tuple-element.75), channel_id=1, source_target_pairs={{0,2},{1,3},{2,4},{3,5},{4,6},{5,7},{6,0},{7,1},{8,10},{9,11},{10,... | collective-permute-start | bytes 393224 | tf_op jit(solution)/shard_map/ppermute | solution.py:36
  39.4 1.7 %blocks.4 = (bf16[1024,256]{1,0:T(8,128)(2,1)S(1)}, bf16[256,384]{1,0:T(8,128)(2,1)S(1)}, bf16[256,128]{1,0:T(8,128)(2,1)S(1)}, f32[2,2,128,128]{3,2,1,0:T(8,128...) custom-call(f32[128,1024]{1,0:T(8,128)S(1)} %bitcast_convert_fusion.refs_0_, ...), custom_call_target="tpu_custom_call" | custom-call | flops 201326592 | bytes 4194304 | tf_op jit(solution)/shard_map/blocks/pallas_call | solution.py:78
  41.1 1.7 %blocks.7 = (bf16[1024,256]{1,0:T(8,128)(2,1)S(1)}, bf16[256,384]{1,0:T(8,128)(2,1)S(1)}, bf16[256,128]{1,0:T(8,128)(2,1)S(1)}, f32[2,2,128,128]{3,2,1,0:T(8,128...) custom-call(f32[128,1024]{1,0:T(8,128)S(1)} %collective-permute-done.6.refs_0_, ...), custom_call_target="tpu_custom_call" | custom-call | flops 201326592 | bytes 4194304 | tf_op jit(solution)/shard_map/blocks/pallas_call | solution.py:78
  42.8 1.8 %collective-permute-done.4.refs_3_ = f32[256,128]{1,0:T(8,128)S(1)} collective-permute-done((f32[256,128]{1,0:T(8,128)S(1)}, f32[256,128]{1,0:T(8,128)S(1)}, u32[]{:S(2)}, u32[]{:S(2)}) %collective-permute-start.4) | collective-permute-done | bytes 131104 | tf_op jit(solution)/shard_map/ppermute | solution.py:36
  44.5 1.7 %blocks.5 = (bf16[1024,256]{1,0:T(8,128)(2,1)S(1)}, bf16[256,384]{1,0:T(8,128)(2,1)S(1)}, bf16[256,128]{1,0:T(8,128)(2,1)S(1)}, f32[2,2,128,128]{3,2,1,0:T(8,128...) custom-call(f32[128,1024]{1,0:T(8,128)S(1)} %collective-permute-done.2.refs_0_, ...), custom_call_target="tpu_custom_call" | custom-call | flops 201326592 | bytes 4194304 | tf_op jit(solution)/shard_map/blocks/pallas_call | solution.py:78
  46.3 1.7 %blocks.6 = (bf16[1024,256]{1,0:T(8,128)(2,1)S(1)}, bf16[256,384]{1,0:T(8,128)(2,1)S(1)}, bf16[256,128]{1,0:T(8,128)(2,1)S(1)}, f32[2,2,128,128]{3,2,1,0:T(8,128...) custom-call(f32[128,1024]{1,0:T(8,128)S(1)} %constant_dynamic-update-slice_fusion.1.refs_0_, ...), custom_call_target="tpu_custom_call" | custom-call | flops 201326592 | bytes 4194304 | tf_op jit(solution)/shard_map/blocks/pallas_call | solution.py:78
  47.9 0.6 totals.1
  48.6 2.1 %collective-permute-start.12 = (f32[2,128,128]{2,1,0:T(8,128)S(1)}, f32[2,128,128]{2,1,0:T(8,128)S(1)}, u32[]{:S(2)}, u32[]{:S(2)}) collective-permute-start(f32[2,128,128]{2,1,0:T(8,128)S(1)} %get-tuple-element.42), channel_id=1, source_target_pairs={{0,8},{1,9},{2,10},{3,11},{4,12},{5,13},{6,14},{7,15},{8,16},{9,17... | collective-permute-start | bytes 393224 | tf_op jit(solution)/shard_map/ppermute | solution.py:36
  50.7 2.6 %collective-permute-start.13 = (f32[2,128,128]{2,1,0:T(8,128)S(1)}, f32[2,128,128]{2,1,0:T(8,128)S(1)}, u32[]{:S(2)}, u32[]{:S(2)}) collective-permute-start(f32[2,128,128]{2,1,0:T(8,128)S(1)} %get-tuple-element.43), channel_id=1, source_target_pairs={{0,16},{1,17},{2,18},{3,19},{4,20},{5,21},{6,22},{7,23},{8,24},{9,... | collective-permute-start | bytes 393224 | tf_op jit(solution)/shard_map/ppermute | solution.py:36
  53.3 1.1 collective-permute-start.14
  54.4 0.5 collective-permute-done.12.refs_0_
  54.9 3.4 %collective-permute-done.13.refs_1_ = f32[2,128,128]{2,1,0:T(8,128)S(1)} collective-permute-done((f32[2,128,128]{2,1,0:T(8,128)S(1)}, f32[2,128,128]{2,1,0:T(8,128)S(1)}, u32[]{:S(2)}, u32[]{:S(2)}) %collective-permute-start.13) | collective-permute-done | bytes 131104 | tf_op jit(solution)/shard_map/ppermute | solution.py:36
  58.2 0.4 collective-permute-done.14.refs_2_
  58.6 2.9 %gradients.1 = (bf16[1024,384]{1,0:T(8,128)(2,1)S(1)}, f32[8,32,384]{2,1,0:T(8,128)S(1)}, f32[8,32,384]{2,1,0:T(8,128)S(1)}, f32[8,32,384]{2,1,0:T(8,128)S(1)}, f32[8,32,384]{2,1,0:T(8,128)S(1)}) custom-call(s32[3]{0:T(128)S(1)} %pad_add_fusion.place, f32[2,128,128]{2,1,0:T(8,128)S(1)} %collective-permute-done.12.refs_0_, ...), custom_call_target="tpu_custom_call" | custom-call | flops 805306368 | bytes 10485760 | tf_op jit(solution)/shard_map/gradients/pallas_call | solution.py:188
  61.6 1.1 collective-permute-start.19
  62.7 2.6 %collective-permute-start.20 = (f32[8,32,384]{2,1,0:T(8,128)S(1)}, f32[8,32,384]{2,1,0:T(8,128)S(1)}, u32[]{:S(2)}, u32[]{:S(2)}) collective-permute-start(f32[8,32,384]{2,1,0:T(8,128)S(1)} %get-tuple-element.64), channel_id=1, source_target_pairs={{0,16},{1,17},{2,18},{3,19},{4,20},{5,21},{6,22},{7,23},{8,24},{9,... | collective-permute-start | bytes 1179656 | tf_op jit(solution)/shard_map/ppermute | solution.py:36
  65.3 0.4 collective-permute-start.21
  65.8 0.1 collective-permute-start.17
  65.9 3.3 %collective-permute-start.16 = (f32[256,384]{1,0:T(8,128)S(1)}, f32[256,384]{1,0:T(8,128)S(1)}, u32[]{:S(2)}, u32[]{:S(2)}) collective-permute-start(f32[256,384]{1,0:T(8,128)S(1)} %get-tuple-element.70), channel_id=1, source_target_pairs={{0,4},{1,5},{2,6},{3,7},{4,0},{5,1},{6,2},{7,3},{8,12},{9,13},{10,... | collective-permute-start | bytes 1179656 | tf_op jit(solution)/shard_map/ppermute | solution.py:36
  69.3 2.2 %collective-permute-done.19 = f32[8,32,384]{2,1,0:T(8,128)S(1)} collective-permute-done((f32[8,32,384]{2,1,0:T(8,128)S(1)}, f32[8,32,384]{2,1,0:T(8,128)S(1)}, u32[]{:S(2)}, u32[]{:S(2)}) %collective-permute-start.19) | collective-permute-done | bytes 393248 | tf_op jit(solution)/shard_map/ppermute | solution.py:36
  71.6 9.8 %collective-permute-done.20 = f32[8,32,384]{2,1,0:T(8,128)S(1)} collective-permute-done((f32[8,32,384]{2,1,0:T(8,128)S(1)}, f32[8,32,384]{2,1,0:T(8,128)S(1)}, u32[]{:S(2)}, u32[]{:S(2)}) %collective-permute-start.20) | collective-permute-done | bytes 393248 | tf_op jit(solution)/shard_map/ppermute | solution.py:36
  81.4 0.5 collective-permute-done.21
  81.9 0.8 add_add_fusion
  82.7 8.4 %all-to-all-start = ((f32[8,32,384]{2,1,0:T(8,128)}), f32[8,32,384]{2,1,0:T(8,128)S(1)}, u32[]{:S(2)}, u32[]{:S(2)}) async-start(f32[8,32,384]{2,1,0:T(8,128)} %add_add_fusion), calls=%async_computation | async-start | bytes 786432 | tf_op jit(solution)/shard_map/all_to_all | solution.py:290
  91.3 2.3 %collective-permute-start.18 = (f32[4,128,384]{2,1,0:T(8,128)S(1)}, f32[4,128,384]{2,1,0:T(8,128)S(1)}, u32[]{:S(2)}, u32[]{:S(2)}) collective-permute-start(f32[4,128,384]{2,1,0:T(8,128)S(1)} %pad_maximum_fusion.1), channel_id=1, source_target_pairs={{0,1},{1,0},{2,3},{3,2},{4,5},{5,4},{6,7},{7,6},{8,9},{9,8},{10,11... | collective-permute-start | bytes 2359304 | tf_op jit(solution)/shard_map/ppermute | solution.py:36
  93.5 9.8 %all-to-all-done = f32[8,32,384]{2,1,0:T(8,128)S(1)} async-done(((f32[8,32,384]{2,1,0:T(8,128)}), f32[8,32,384]{2,1,0:T(8,128)S(1)}, u32[]{:S(2)}, u32[]{:S(2)}) %all-to-all-start) | async-done | bytes 393248 | tf_op jit(solution)/shard_map/all_to_all | solution.py:290
  103.3 0.6 reduce_sum.27
  103.9 1.4 %multiply_reduce_fusion = f32[]{:T(128)} fusion(f32[32,384]{1,0:T(8,128)} %reduce_sum.27), kind=kLoop, calls=%fused_computation.16 | loop fusion | flops 24575 | bytes 49156 | tf_op jit(solution)/shard_map/reduce_sum | solution.py:300
  105.3 1.4 broadcast_in_dim.37
  106.7 11.8 %all-to-all-start.1 = ((f32[256,1,128]{2,1,0:T(1,128)}), f32[256,1,128]{2,1,0:T(1,128)S(1)}, u32[]{:S(2)}, u32[]{:S(2)}) async-start(f32[256,1,128]{2,1,0:T(1,128)} %broadcast_in_dim.37), calls=%async_computation.1 | async-start | bytes 262144 | tf_op jit(solution)/shard_map/all_to_all | solution.py:314
  118.6 0.8 reshape.37
  119.4 2.2 %collective-permute-start.22 = (f32[12,128]{1,0:T(8,128)S(1)}, f32[12,128]{1,0:T(8,128)S(1)}, u32[]{:S(2)}, u32[]{:S(2)}) collective-permute-start(f32[12,128]{1,0:T(8,128)S(1)} %get-tuple-element.85), channel_id=1, source_target_pairs={{0,1},{1,0},{2,3},{3,2},{4,5},{5,4},{6,7},{7,6},{8,9},{9,8},{10,11... | collective-permute-start | bytes 18440 | tf_op jit(solution)/shard_map/ppermute | solution.py:36
  121.7 1.1 collective-permute-start.24
  122.8 3.0 %collective-permute-start.25 = (f32[12,128]{1,0:T(8,128)S(1)}, f32[12,128]{1,0:T(8,128)S(1)}, u32[]{:S(2)}, u32[]{:S(2)}) collective-permute-start(f32[12,128]{1,0:T(8,128)S(1)} %get-tuple-element.82), channel_id=1, source_target_pairs={{0,4},{1,5},{2,6},{3,7},{4,0},{5,1},{6,2},{7,3},{8,12},{9,13},{10,... | collective-permute-start | bytes 18440 | tf_op jit(solution)/shard_map/ppermute | solution.py:36
  125.8 0.2 collective-permute-start.26
  126.0 1.9 %collective-permute-start.27 = (f32[12,128]{1,0:T(8,128)S(1)}, f32[12,128]{1,0:T(8,128)S(1)}, u32[]{:S(2)}, u32[]{:S(2)}) collective-permute-start(f32[12,128]{1,0:T(8,128)S(1)} %get-tuple-element.80), channel_id=1, source_target_pairs={{0,6},{1,7},{2,0},{3,1},{4,2},{5,3},{6,4},{7,5},{8,14},{9,15},{10,... | collective-permute-start | bytes 18440 | tf_op jit(solution)/shard_map/ppermute | solution.py:36
  127.9 1.7 %collective-permute-start.28 = (f32[12,128]{1,0:T(8,128)S(1)}, f32[12,128]{1,0:T(8,128)S(1)}, u32[]{:S(2)}, u32[]{:S(2)}) collective-permute-start(f32[12,128]{1,0:T(8,128)S(1)} %get-tuple-element.79), channel_id=1, source_target_pairs={{0,7},{1,6},{2,1},{3,0},{4,3},{5,2},{6,5},{7,4},{8,15},{9,14},{10,... | collective-permute-start | bytes 18440 | tf_op jit(solution)/shard_map/ppermute | solution.py:36
  129.9 0.7 collective-permute-done.26
  130.8 0.5 collective-permute-done.28
  131.3 2.8 %copy-done = bf16[1024,3072]{1,0:T(8,128)(2,1)S(1)} copy-done((bf16[1024,3072]{1,0:T(8,128)(2,1)S(1)}, bf16[1024,3072]{1,0:T(8,128)(2,1)}, u32[]{:S(2)}) %copy-start) | copy-done | bytes 6291480
  134.1 3.5 %input_gradient.1 = bf16[128,1024]{1,0:T(8,128)(2,1)} custom-call(s32[3]{0:T(128)S(1)} %pad_add_fusion.place, f32[256,384]{1,0:T(8,128)S(1)} %get-tuple-element.72.refs_0_, f32[256,384]{1,0:T(8,128)S(1)} %collective-permute-done.15.refs_1_, f32[256,384]{1,0:T(8,128)S(1)} %collective-permute-done.16.refs_2_, f32[256,384]{1,0:T(8,128)S(1)} %collective-permute-done.17.refs_3_, ...), custom_call_target="tpu_custom_call" | custom-call | flops 805306368 | bytes 10485760 | tf_op jit(solution)/shard_map/input_gradient/pallas_call | solution.py:227
  137.7 0.6 slice_reduce_fusion
  139.0 0.6 copy.29
  (53 shorter events, 1.1 us)
Async XLA Ops:
  1.6 12.7 %collective-permute-start.2 = (f32[128,1024]{1,0:T(8,128)S(1)}, f32[128,1024]{1,0:T(8,128)S(1)}, u32[]{:S(2)}, u32[]{:S(2)}) collective-permute-start(f32[128,1024]{1,0:T(8,128)S(1)} %bitcast_convert_fusion.refs_0_), channel_id=1, source_target_pairs={{0,2},{1,3},{2,4},{3,5},{4,6},{5,7},{6,0},{7,1},{8,10},{9,11},{10,... | collective-permute-start | bytes 1572872 | tf_op jit(solution)/shard_map/ppermute | solution.py:36
  3.7 13.2 %collective-permute-start.6 = (f32[128,1024]{1,0:T(8,128)S(1)}, f32[128,1024]{1,0:T(8,128)S(1)}, u32[]{:S(2)}, u32[]{:S(2)}) collective-permute-start(f32[128,1024]{1,0:T(8,128)S(1)} %bitcast_convert_fusion.refs_0_), channel_id=1, source_target_pairs={{0,6},{1,7},{2,0},{3,1},{4,2},{5,3},{6,4},{7,5},{8,14},{9,15},{10,... | collective-permute-start | bytes 1572872 | tf_op jit(solution)/shard_map/ppermute | solution.py:36
  5.1 32.3 %collective-permute-start = (f32[128,1024]{1,0:T(8,128)S(1)}, f32[128,1024]{1,0:T(8,128)S(1)}, u32[]{:S(2)}, u32[]{:S(2)}) collective-permute-start(f32[128,1024]{1,0:T(8,128)S(1)} %bitcast_convert_fusion.refs_0_), channel_id=1, source_target_pairs={{0,1},{1,0},{2,3},{3,2},{4,5},{5,4},{6,7},{7,6},{8,9},{9,8},{10,11... | collective-permute-start | bytes 1572872 | tf_op jit(solution)/shard_map/ppermute | solution.py:36
  10.9 17.7 %collective-permute-start.1 = (f32[128,512]{1,0:T(8,128)}, f32[128,512]{1,0:T(8,128)}, u32[]{:S(2)}, u32[]{:S(2)}) collective-permute-start(f32[128,512]{1,0:T(8,128)} %bitcast.49), channel_id=1, source_target_pairs={{0,1},{1,0},{2,3},{3,2},{4,5},{5,4},{6,7},{7,6},{8,9},{9,8},{10,11... | collective-permute-start | bytes 786440 | tf_op jit(solution)/shard_map/ppermute | solution.py:36
  15.1 8.9 %collective-permute-start.5 = (f32[64,1024]{1,0:T(8,128)}, f32[64,1024]{1,0:T(8,128)}, u32[]{:S(2)}, u32[]{:S(2)}) collective-permute-start(f32[64,1024]{1,0:T(8,128)} %slice.44), channel_id=1, source_target_pairs={{0,2},{1,3},{2,4},{3,5},{4,6},{5,7},{6,0},{7,1},{8,10},{9,11},{10,... | collective-permute-start | bytes 786440 | tf_op jit(solution)/shard_map/ppermute | solution.py:36
  17.7 9.8 %collective-permute-start.7 = (f32[64,1024]{1,0:T(8,128)}, f32[64,1024]{1,0:T(8,128)}, u32[]{:S(2)}, u32[]{:S(2)}) collective-permute-start(f32[64,1024]{1,0:T(8,128)} %slice.45), channel_id=1, source_target_pairs={{0,6},{1,7},{2,0},{3,1},{4,2},{5,3},{6,4},{7,5},{8,14},{9,15},{10,... | collective-permute-start | bytes 786440 | tf_op jit(solution)/shard_map/ppermute | solution.py:36
  20.6 20.5 %collective-permute-start.10 = (f32[128,1024]{1,0:T(8,128)S(1)}, f32[128,1024]{1,0:T(8,128)S(1)}, u32[]{:S(2)}, u32[]{:S(2)}) collective-permute-start(f32[128,1024]{1,0:T(8,128)S(1)} %collective-permute-done.6.refs_0_), channel_id=1, source_target_pairs={{0,1},{1,0},{2,3},{3,2},{4,5},{5,4},{6,7},{7,6},{8,9},{9,8},{10,11... | collective-permute-start | bytes 1572872 | tf_op jit(solution)/shard_map/ppermute | solution.py:36
  24.0 20.5 %collective-permute-start.3 = (f32[128,1024]{1,0:T(8,128)S(1)}, f32[128,1024]{1,0:T(8,128)S(1)}, u32[]{:S(2)}, u32[]{:S(2)}) collective-permute-start(f32[128,1024]{1,0:T(8,128)S(1)} %collective-permute-done.2.refs_0_), channel_id=1, source_target_pairs={{0,1},{1,0},{2,3},{3,2},{4,5},{5,4},{6,7},{7,6},{8,9},{9,8},{10,11... | collective-permute-start | bytes 1572872 | tf_op jit(solution)/shard_map/ppermute | solution.py:36
  28.5 17.8 %collective-permute-start.8 = (f32[128,1024]{1,0:T(8,128)S(1)}, f32[128,1024]{1,0:T(8,128)S(1)}, u32[]{:S(2)}, u32[]{:S(2)}) collective-permute-start(f32[128,1024]{1,0:T(8,128)S(1)} %constant_dynamic-update-slice_fusion.1.refs_0_), channel_id=1, source_target_pairs={{0,1},{1,0},{2,3},{3,2},{4,5},{5,4},{6,7},{7,6},{8,9},{9,8},{10,11... | collective-permute-start | bytes 1572872 | tf_op jit(solution)/shard_map/ppermute | solution.py:36
  29.6 5.7 %collective-permute-start.11 = (f32[256,128]{1,0:T(8,128)S(1)}, f32[256,128]{1,0:T(8,128)S(1)}, u32[]{:S(2)}, u32[]{:S(2)}) collective-permute-start(f32[256,128]{1,0:T(8,128)S(1)} %get-tuple-element.73), channel_id=1, source_target_pairs={{0,6},{1,7},{2,0},{3,1},{4,2},{5,3},{6,4},{7,5},{8,14},{9,15},{10,... | collective-permute-start | bytes 393224 | tf_op jit(solution)/shard_map/ppermute | solution.py:36
  35.3 10.9 %collective-permute-start.9 = (f32[256,128]{1,0:T(8,128)S(1)}, f32[256,128]{1,0:T(8,128)S(1)}, u32[]{:S(2)}, u32[]{:S(2)}) collective-permute-start(f32[256,128]{1,0:T(8,128)S(1)} %get-tuple-element.74), channel_id=1, source_target_pairs={{0,4},{1,5},{2,6},{3,7},{4,0},{5,1},{6,2},{7,3},{8,12},{9,13},{10,... | collective-permute-start | bytes 393224 | tf_op jit(solution)/shard_map/ppermute | solution.py:36
  37.5 7.1 %collective-permute-start.4 = (f32[256,128]{1,0:T(8,128)S(1)}, f32[256,128]{1,0:T(8,128)S(1)}, u32[]{:S(2)}, u32[]{:S(2)}) collective-permute-start(f32[256,128]{1,0:T(8,128)S(1)} %get-tuple-element.75), channel_id=1, source_target_pairs={{0,2},{1,3},{2,4},{3,5},{4,6},{5,7},{6,0},{7,1},{8,10},{9,11},{10,... | collective-permute-start | bytes 393224 | tf_op jit(solution)/shard_map/ppermute | solution.py:36
  48.6 6.3 %collective-permute-start.12 = (f32[2,128,128]{2,1,0:T(8,128)S(1)}, f32[2,128,128]{2,1,0:T(8,128)S(1)}, u32[]{:S(2)}, u32[]{:S(2)}) collective-permute-start(f32[2,128,128]{2,1,0:T(8,128)S(1)} %get-tuple-element.42), channel_id=1, source_target_pairs={{0,8},{1,9},{2,10},{3,11},{4,12},{5,13},{6,14},{7,15},{8,16},{9,17... | collective-permute-start | bytes 393224 | tf_op jit(solution)/shard_map/ppermute | solution.py:36
  50.7 7.6 %collective-permute-start.13 = (f32[2,128,128]{2,1,0:T(8,128)S(1)}, f32[2,128,128]{2,1,0:T(8,128)S(1)}, u32[]{:S(2)}, u32[]{:S(2)}) collective-permute-start(f32[2,128,128]{2,1,0:T(8,128)S(1)} %get-tuple-element.43), channel_id=1, source_target_pairs={{0,16},{1,17},{2,18},{3,19},{4,20},{5,21},{6,22},{7,23},{8,24},{9,... | collective-permute-start | bytes 393224 | tf_op jit(solution)/shard_map/ppermute | solution.py:36
  53.3 5.3 %collective-permute-start.14 = (f32[2,128,128]{2,1,0:T(8,128)S(1)}, f32[2,128,128]{2,1,0:T(8,128)S(1)}, u32[]{:S(2)}, u32[]{:S(2)}) collective-permute-start(f32[2,128,128]{2,1,0:T(8,128)S(1)} %get-tuple-element.44), channel_id=1, source_target_pairs={{0,24},{1,25},{2,26},{3,27},{4,28},{5,29},{6,30},{7,31},{8,0},{9,1... | collective-permute-start | bytes 393224 | tf_op jit(solution)/shard_map/ppermute | solution.py:36
  61.6 10.0 %collective-permute-start.19 = (f32[8,32,384]{2,1,0:T(8,128)S(1)}, f32[8,32,384]{2,1,0:T(8,128)S(1)}, u32[]{:S(2)}, u32[]{:S(2)}) collective-permute-start(f32[8,32,384]{2,1,0:T(8,128)S(1)} %get-tuple-element.63), channel_id=1, source_target_pairs={{0,8},{1,9},{2,10},{3,11},{4,12},{5,13},{6,14},{7,15},{8,16},{9,17... | collective-permute-start | bytes 1179656 | tf_op jit(solution)/shard_map/ppermute | solution.py:36
  62.7 18.7 %collective-permute-start.20 = (f32[8,32,384]{2,1,0:T(8,128)S(1)}, f32[8,32,384]{2,1,0:T(8,128)S(1)}, u32[]{:S(2)}, u32[]{:S(2)}) collective-permute-start(f32[8,32,384]{2,1,0:T(8,128)S(1)} %get-tuple-element.64), channel_id=1, source_target_pairs={{0,16},{1,17},{2,18},{3,19},{4,20},{5,21},{6,22},{7,23},{8,24},{9,... | collective-permute-start | bytes 1179656 | tf_op jit(solution)/shard_map/ppermute | solution.py:36
  65.3 16.6 %collective-permute-start.21 = (f32[8,32,384]{2,1,0:T(8,128)S(1)}, f32[8,32,384]{2,1,0:T(8,128)S(1)}, u32[]{:S(2)}, u32[]{:S(2)}) collective-permute-start(f32[8,32,384]{2,1,0:T(8,128)S(1)} %get-tuple-element.65), channel_id=1, source_target_pairs={{0,24},{1,25},{2,26},{3,27},{4,28},{5,29},{6,30},{7,31},{8,0},{9,1... | collective-permute-start | bytes 1179656 | tf_op jit(solution)/shard_map/ppermute | solution.py:36
  65.8 25.3 %collective-permute-start.17 = (f32[256,384]{1,0:T(8,128)S(1)}, f32[256,384]{1,0:T(8,128)S(1)}, u32[]{:S(2)}, u32[]{:S(2)}) collective-permute-start(f32[256,384]{1,0:T(8,128)S(1)} %get-tuple-element.69), channel_id=1, source_target_pairs={{0,2},{1,3},{2,4},{3,5},{4,6},{5,7},{6,0},{7,1},{8,10},{9,11},{10,... | collective-permute-start | bytes 1179656 | tf_op jit(solution)/shard_map/ppermute | solution.py:36
  65.9 25.2 %collective-permute-start.16 = (f32[256,384]{1,0:T(8,128)S(1)}, f32[256,384]{1,0:T(8,128)S(1)}, u32[]{:S(2)}, u32[]{:S(2)}) collective-permute-start(f32[256,384]{1,0:T(8,128)S(1)} %get-tuple-element.70), channel_id=1, source_target_pairs={{0,4},{1,5},{2,6},{3,7},{4,0},{5,1},{6,2},{7,3},{8,12},{9,13},{10,... | collective-permute-start | bytes 1179656 | tf_op jit(solution)/shard_map/ppermute | solution.py:36
  71.5 19.6 %collective-permute-start.15 = (f32[256,384]{1,0:T(8,128)S(1)}, f32[256,384]{1,0:T(8,128)S(1)}, u32[]{:S(2)}, u32[]{:S(2)}) collective-permute-start(f32[256,384]{1,0:T(8,128)S(1)} %get-tuple-element.71), channel_id=1, source_target_pairs={{0,6},{1,7},{2,0},{3,1},{4,2},{5,3},{6,4},{7,5},{8,14},{9,15},{10,... | collective-permute-start | bytes 1179656 | tf_op jit(solution)/shard_map/ppermute | solution.py:36
  82.7 20.5 %all-to-all-start = ((f32[8,32,384]{2,1,0:T(8,128)}), f32[8,32,384]{2,1,0:T(8,128)S(1)}, u32[]{:S(2)}, u32[]{:S(2)}) async-start(f32[8,32,384]{2,1,0:T(8,128)} %add_add_fusion), calls=%async_computation | async-start | bytes 786432 | tf_op jit(solution)/shard_map/all_to_all | solution.py:290
  91.3 40.1 %collective-permute-start.18 = (f32[4,128,384]{2,1,0:T(8,128)S(1)}, f32[4,128,384]{2,1,0:T(8,128)S(1)}, u32[]{:S(2)}, u32[]{:S(2)}) collective-permute-start(f32[4,128,384]{2,1,0:T(8,128)S(1)} %pad_maximum_fusion.1), channel_id=1, source_target_pairs={{0,1},{1,0},{2,3},{3,2},{4,5},{5,4},{6,7},{7,6},{8,9},{9,8},{10,11... | collective-permute-start | bytes 2359304 | tf_op jit(solution)/shard_map/ppermute | solution.py:36
  106.7 31.0 %all-to-all-start.1 = ((f32[256,1,128]{2,1,0:T(1,128)}), f32[256,1,128]{2,1,0:T(1,128)S(1)}, u32[]{:S(2)}, u32[]{:S(2)}) async-start(f32[256,1,128]{2,1,0:T(1,128)} %broadcast_in_dim.37), calls=%async_computation.1 | async-start | bytes 262144 | tf_op jit(solution)/shard_map/all_to_all | solution.py:314
  119.4 6.4 %collective-permute-start.22 = (f32[12,128]{1,0:T(8,128)S(1)}, f32[12,128]{1,0:T(8,128)S(1)}, u32[]{:S(2)}, u32[]{:S(2)}) collective-permute-start(f32[12,128]{1,0:T(8,128)S(1)} %get-tuple-element.85), channel_id=1, source_target_pairs={{0,1},{1,0},{2,3},{3,2},{4,5},{5,4},{6,7},{7,6},{8,9},{9,8},{10,11... | collective-permute-start | bytes 18440 | tf_op jit(solution)/shard_map/ppermute | solution.py:36
  121.7 4.3 %collective-permute-start.23 = (f32[12,128]{1,0:T(8,128)S(1)}, f32[12,128]{1,0:T(8,128)S(1)}, u32[]{:S(2)}, u32[]{:S(2)}) collective-permute-start(f32[12,128]{1,0:T(8,128)S(1)} %get-tuple-element.84), channel_id=1, source_target_pairs={{0,2},{1,3},{2,4},{3,5},{4,6},{5,7},{6,0},{7,1},{8,10},{9,11},{10,... | collective-permute-start | bytes 18440 | tf_op jit(solution)/shard_map/ppermute | solution.py:36
  121.7 6.2 %collective-permute-start.24 = (f32[12,128]{1,0:T(8,128)S(1)}, f32[12,128]{1,0:T(8,128)S(1)}, u32[]{:S(2)}, u32[]{:S(2)}) collective-permute-start(f32[12,128]{1,0:T(8,128)S(1)} %get-tuple-element.83), channel_id=1, source_target_pairs={{0,3},{1,2},{2,5},{3,4},{4,7},{5,6},{6,1},{7,0},{8,11},{9,10},{10,... | collective-permute-start | bytes 18440 | tf_op jit(solution)/shard_map/ppermute | solution.py:36
  122.8 7.1 %collective-permute-start.25 = (f32[12,128]{1,0:T(8,128)S(1)}, f32[12,128]{1,0:T(8,128)S(1)}, u32[]{:S(2)}, u32[]{:S(2)}) collective-permute-start(f32[12,128]{1,0:T(8,128)S(1)} %get-tuple-element.82), channel_id=1, source_target_pairs={{0,4},{1,5},{2,6},{3,7},{4,0},{5,1},{6,2},{7,3},{8,12},{9,13},{10,... | collective-permute-start | bytes 18440 | tf_op jit(solution)/shard_map/ppermute | solution.py:36
  125.8 4.9 %collective-permute-start.26 = (f32[12,128]{1,0:T(8,128)S(1)}, f32[12,128]{1,0:T(8,128)S(1)}, u32[]{:S(2)}, u32[]{:S(2)}) collective-permute-start(f32[12,128]{1,0:T(8,128)S(1)} %get-tuple-element.81), channel_id=1, source_target_pairs={{0,5},{1,4},{2,7},{3,6},{4,1},{5,0},{6,3},{7,2},{8,13},{9,12},{10,... | collective-permute-start | bytes 18440 | tf_op jit(solution)/shard_map/ppermute | solution.py:36
  126.0 4.7 %collective-permute-start.27 = (f32[12,128]{1,0:T(8,128)S(1)}, f32[12,128]{1,0:T(8,128)S(1)}, u32[]{:S(2)}, u32[]{:S(2)}) collective-permute-start(f32[12,128]{1,0:T(8,128)S(1)} %get-tuple-element.80), channel_id=1, source_target_pairs={{0,6},{1,7},{2,0},{3,1},{4,2},{5,3},{6,4},{7,5},{8,14},{9,15},{10,... | collective-permute-start | bytes 18440 | tf_op jit(solution)/shard_map/ppermute | solution.py:36
  127.9 3.4 %collective-permute-start.28 = (f32[12,128]{1,0:T(8,128)S(1)}, f32[12,128]{1,0:T(8,128)S(1)}, u32[]{:S(2)}, u32[]{:S(2)}) collective-permute-start(f32[12,128]{1,0:T(8,128)S(1)} %get-tuple-element.79), channel_id=1, source_target_pairs={{0,7},{1,6},{2,1},{3,0},{4,3},{5,2},{6,5},{7,4},{8,15},{9,14},{10,... | collective-permute-start | bytes 18440 | tf_op jit(solution)/shard_map/ppermute | solution.py:36
  131.3 2.8 %copy-start = (bf16[1024,3072]{1,0:T(8,128)(2,1)S(1)}, bf16[1024,3072]{1,0:T(8,128)(2,1)}, u32[]{:S(2)}) copy-start(bf16[1024,3072]{1,0:T(8,128)(2,1)} %refs_5_.1) | copy-start | bytes 18874372

commit v2 on v1

--- a/solution.py
+++ b/solution.py
@@ -48,51 +48,105 @@
     return lax.dot_general(a, b, (((over_a,), (over_b,)), ((), ())), preferred_element_type=F32)
 
 
-def block_kernel(users, *refs):
-    first, second, w, cot, rows_t, proj, cot_half, key_state, query_state, intra = refs
-    total = first.shape[0]
-    size = total // users
+def message_kernel(place, inputs, grad_out, right, left, cross):
+    x, c = place[1], place[2]
+
+    def rows(user, j):
+        return inputs[user, :, j * DH : (j + 1) * DH].astype(F32)
+
+    def cot(user, dx, core):
+        head = ((x + dx) % NX) * 2 + core
+        return grad_out[user, :, pl.ds(pl.multiple_of(head * DH, DH), DH)].astype(F32)
+
+    for j in range(H):
+        right[j] = rows(0, j)
+        right[10 + j] = rows(1, j)
+        left[j] = rows(1, j)
+        left[10 + j] = rows(0, j)
+        cross[j] = rows(0, j)
+        cross[8 + j] = rows(1, j)
+    for core in range(2):
+        right[8 + core] = cot(0, 2, core)
+        left[8 + core] = cot(1, 2, core)
+        for user in range(2):
+            right[18 + 2 * core + user] = cot(user, 1, core)
+            left[18 + 2 * core + user] = cot(user, NX - 1, core)
+    for user in range(2):
+        cross[16 + user] = cot(user, 0, 1 - c)
+
+
+def messages(place, inputs, grad_out):
+    size = inputs.shape[1]
+    return pl.pallas_call(
+        message_kernel,
+        out_shape=tuple(struct((count, size, DH), F32) for count in (22, 22, 18)),
+        in_specs=[SMEM, VMEM, VMEM],
+        out_specs=(VMEM,) * 3,
+        compiler_params=pltpu.CompilerParams(vmem_limit_bytes=16 * MIB),
+        cost_estimate=pl.CostEstimate(flops=MIB, bytes_accessed=3 * MIB, transcendentals=0),
+        name="messages",
+    )(place, inputs, grad_out)
+
+
+def block_kernel(units, place, w, *refs):
+    sources, refs = refs[:-7], refs[-7:]
+    rows_t, proj, cot_half, key_state, query_state, intra, x_all = refs
+    x, c = place[1], place[2]
+    features, total = rows_t.shape
+    size = total // len(units)
     causal = lax.broadcasted_iota(jnp.int32, (size, size), 0) >= lax.broadcasted_iota(
         jnp.int32, (size, size), 1
     )
-    cot_half[...] = cot[...].astype(BF16)
-    for i, ref in enumerate((first, second)):
-        x = ref[...].astype(BF16)
-        rows_t[:, i * total : (i + 1) * total] = x.T
-        proj[i * total : (i + 1) * total, :] = dot(x, w[...], 1, 0).astype(BF16)
-        for u in range(users):
-            here = slice(i * total + u * size, i * total + (u + 1) * size)
-            q, k, v = (proj[here, part * DH : (part + 1) * DH] for part in range(3))
-            g = cot_half[here, :]
-            key_state[i, u] = dot(k, v, 0, 0)
-            query_state[i, u] = dot(q, g, 0, 0)
-            out_value = jnp.where(causal, dot(g, v, 1, 1), 0.0).astype(BF16)
-            query_key = jnp.where(causal, dot(q, k, 1, 1), 0.0).astype(BF16)
-            intra[here, :DH] = dot(out_value, k, 1, 0)
-            intra[here, DH : 2 * DH] = dot(out_value, q, 0, 0)
-            intra[here, 2 * DH :] = dot(query_key, g, 0, 0)
-
-
-def blocks(first, second, w_head, cot, users):
-    total, features = first.shape
-    return pl.pallas_call(
-        functools.partial(block_kernel, users),
+    for n, (source, start, cot_start, cot_step) in enumerate(units):
+        here = slice(n * size, (n + 1) * size)
+        if start is None:
+            x_all[here, :] = sources[source][n]
+            columns = pl.ds(pl.multiple_of((x * 2 + c) * DH, DH), DH)
+            cot_half[here, :] = sources[source + 1][n, :, columns]
+        else:
+            for j in range(features // DH):
+                x_all[here, j * DH : (j + 1) * DH] = sources[source][start + j].astype(BF16)
+            cot_half[here, :] = sources[source][cot_start + cot_step * c].astype(BF16)
+    rows = x_all[...]
+    proj[...] = dot(rows, w[...], 1, 0).astype(BF16)
+    rows_t[...] = rows.T
+    for n in range(len(units)):
+        here = slice(n * size, (n + 1) * size)
+        i, u = n // 2, n % 2
+        q, k, v = (proj[here, part * DH : (part + 1) * DH] for part in range(3))
+        g = cot_half[here, :]
+        key_state[i, u] = dot(k, v, 0, 0)
+        query_state[i, u] = dot(q, g, 0, 0)
+        out_value = jnp.where(causal, dot(g, v, 1, 1), 0.0).astype(BF16)
+        query_key = jnp.where(causal, dot(q, k, 1, 1), 0.0).astype(BF16)
+        intra[here, :DH] = dot(out_value, k, 1, 0)
+        intra[here, DH : 2 * DH] = dot(out_value, q, 0, 0)
+        intra[here, 2 * DH :] = dot(query_key, g, 0, 0)
+
+
+def blocks(place, w_head, sources, units):
+    features = w_head.shape[0]
+    size = sources[0].shape[1]
+    total = len(units) * size
+    return pl.pallas_call(
+        functools.partial(block_kernel, units),
         out_shape=(
-            struct((features, 2 * total), BF16),
-            struct((2 * total, 3 * DH), BF16),
-            struct((2 * total, DH), BF16),
-            struct((2, users, DH, DH), F32),
-            struct((2, users, DH, DH), F32),
-            struct((2 * total, 3 * DH), F32),
+            struct((features, total), BF16),
+            struct((total, 3 * DH), BF16),
+            struct((total, DH), BF16),
+            struct((2, 2, DH, DH), F32),
+            struct((2, 2, DH, DH), F32),
+            struct((total, 3 * DH), F32),
         ),
-        in_specs=[VMEM] * 4,
+        in_specs=[SMEM] + [VMEM] * (1 + len(sources)),
         out_specs=(VMEM,) * 6,
+        scratch_shapes=[pltpu.VMEM((total, features), BF16)],
         compiler_params=pltpu.CompilerParams(vmem_limit_bytes=24 * MIB),
         cost_estimate=pl.CostEstimate(
-            flops=2 * 2 * total * features * 3 * DH, bytes_accessed=4 * MIB, transcendentals=0
+            flops=2 * total * features * 3 * DH, bytes_accessed=4 * MIB, transcendentals=0
         ),
         name="blocks",
-    )(first, second, w_head, cot)
+    )(place, w_head, *sources)
 
 
 def total_kernel(place, *refs):
@@ -208,7 +262,8 @@
 
 def input_kernel(place, *refs):
     x, c = place[1], place[2]
-    keep, swap, w, out, full = refs[:NX], refs[NX], refs[NX + 1], refs[NX + 2], refs[NX + 3]
+    keep = refs[:NX]
+    swap, w, out, done, full = refs[NX:]
     total = out.shape[0]
     for dx in range(NX):
         for dc in range(2):
@@ -219,6 +274,7 @@
                 start = pl.multiple_of((part * H + head) * DH, DH)
                 full[:, pl.ds(start, DH)] = value.astype(BF16)
     out[...] = dot(full[...], w[...], 1, 1).astype(BF16)
+    done[...] = jnp.zeros(done.shape, F32)
 
 
 def input_gradient(place, keep, swap, w_qkv):
@@ -226,9 +282,9 @@
     features, width = w_qkv.shape
     return pl.pallas_call(
         input_kernel,
-        out_shape=struct((total, features), BF16),
+        out_shape=(struct((total, features), BF16), struct((8, DH), F32)),
         in_specs=[SMEM] + [VMEM] * (NX + 2),
-        out_specs=VMEM,
+        out_specs=(VMEM, VMEM),
         scratch_shapes=[pltpu.VMEM((total, width), BF16)],
         compiler_params=pltpu.CompilerParams(vmem_limit_bytes=24 * MIB),
         cost_estimate=pl.CostEstimate(
@@ -236,6 +292,74 @@
         ),
         name="input_gradient",
     )(place, *keep, swap, w_qkv)
+
+
+def fold_kernel(*refs):
+    out = refs[-1]
+    dp_count, row_block = refs[0].shape[0], refs[0].shape[1]
+    rows = out.shape[1]
+    for z in range(dp_count):
+        value = sum(ref[z] for ref in refs[:-1])
+        for t in range(GROUP):
+            out[z * GROUP + t] = value[t * rows : (t + 1) * rows, :]
+
+
+def fold(parts):
+    dp_count, row_block, width = parts[0].shape
+    return pl.pallas_call(
+        fold_kernel,
+        out_shape=struct((dp_count * GROUP, row_block // GROUP, width), F32),
+        in_specs=[VMEM] * len(parts),
+        out_specs=VMEM,
+        compiler_params=pltpu.CompilerParams(vmem_limit_bytes=8 * MIB),
+        cost_estimate=pl.CostEstimate(flops=MIB, bytes_accessed=2 * MIB, transcendentals=0),
+        name="fold",
+    )(*parts)
+
+
+def collect_kernel(got, after, weights, squares):
+    count = got.shape[0] // H
+    square = jnp.zeros((), F32)
+    for head in range(H):
+        value = sum(got[z * H + head] for z in range(count))
+        square = square + jnp.sum(value * value)
+        for part in range(3):
+            start = (part * H + head) * DH
+            weights[:, start : start + DH] = value[:, part * DH : (part + 1) * DH]
+    squares[...] = jnp.full(squares.shape, square)
+
+
+def collect(got, after, device_count):
+    rows, width = got.shape[1], got.shape[2]
+    return pl.pallas_call(
+        collect_kernel,
+        out_shape=(struct((rows, H * width), F32), struct((device_count, DH), F32)),
+        in_specs=[VMEM, pl.BlockSpec(memory_space=pl.ANY)],
+        out_specs=(VMEM, VMEM),
+        compiler_params=pltpu.CompilerParams(vmem_limit_bytes=8 * MIB),
+        cost_estimate=pl.CostEstimate(flops=MIB, bytes_accessed=MIB, transcendentals=0),
+        name="collect",
+    )(got, after)
+
+
+def clip_kernel(weights, squares, out):
+    total_sq = jnp.sum(squares[...], axis=0, keepdims=True)
+    factor = jnp.minimum(1.0, D / jnp.sqrt(total_sq + 1e-06))
+    for j in range(out.shape[1] // DH):
+        columns = slice(j * DH, (j + 1) * DH)
+        out[:, columns] = weights[:, columns] * factor
+
+
+def clip(weights, squares):
+    return pl.pallas_call(
+        clip_kernel,
+        out_shape=struct(weights.shape, F32),
+        in_specs=[VMEM, VMEM],
+        out_specs=VMEM,
+        compiler_params=pltpu.CompilerParams(vmem_limit_bytes=8 * MIB),
+        cost_estimate=pl.CostEstimate(flops=MIB, bytes_accessed=MIB, transcendentals=0),
+        name="clip",
+    )(weights, squares)
 
 
 def body(inputs, grad_out, w_qkv):
@@ -249,75 +373,54 @@
     head = x * 2 + c
     total_rows = user_count * row_count
 
-    own = inputs.reshape(total_rows, feature_count).astype(F32)
-    half = total_rows // 2
-    from_left = send(own, dx=1)
-    from_right = send(own, dx=-1)
-    other = send(own, dc=1)
-    far_low = send(from_left[:half], dx=1)
-    far_high = send(from_right[half:], dx=-1)
-    left_other = send(from_left, dc=1)
-    right_other = send(from_right, dc=1)
-    far = jnp.concatenate([far_low, far_high], axis=0)
-    far_other = send(far, dc=1)
-
-    cot = grad_out.reshape(total_rows, feature_count).astype(F32)
-    by_head = cot.reshape(total_rows, NX, 2, DH)
-    mine = lax.dynamic_index_in_dim(by_head, c, 2, False)
-    theirs = lax.dynamic_index_in_dim(by_head, 1 - c, 2, False)
-    swapped = send(theirs.reshape(total_rows, NX * DH), dc=1)
-    pair = jnp.concatenate([mine.reshape(total_rows, NX * DH), swapped], axis=0)
-    cot_pieces = [head_columns(pair, x)]
-    for dx in range(1, NX):
-        piece = send(head_columns(pair, (x + dx) % NX), dx=dx)
-        cot_pieces.append(piece)
+    to_right, to_left, to_other = messages(place, inputs, grad_out)
+    left = send(to_right, dx=1)
+    right = send(to_left, dx=-1)
+    other = send(to_other, dc=1)
+    far_low = send(left[:10], dx=1)
+    far_high = send(right[:10], dx=-1)
+    left_other = send(left, dc=1)
+    right_other = send(right, dc=1)
+    far_low_other = send(far_low, dc=1)
+    far_high_other = send(far_high, dc=1)
 
     w_head = jnp.concatenate(
         [head_columns(w_qkv, part * H + head) for part in range(3)], axis=1
     )
-    pairs = [(own, other), (from_left, left_other), (far, far_other), (from_right, right_other)]
+    own_units = ((0, None, 0, 0), (0, None, 0, 0), (2, 0, 16, 0), (2, 8, 17, 0))
+    left_units = ((0, 0, 18, 2), (0, 10, 19, 2), (1, 0, 18, 2), (1, 10, 19, 2))
+    right_units = ((0, 10, 18, 2), (0, 0, 19, 2), (1, 10, 18, 2), (1, 0, 19, 2))
+    far_units = ((0, 0, 8, 1), (1, 0, 8, 1), (2, 0, 8, 1), (3, 0, 8, 1))
+    far_sources = (far_low, far_high, far_low_other, far_high_other)
     parts = [
-        blocks(first, second, w_head, cot_piece, user_count)
-        for (first, second), cot_piece in zip(pairs, cot_pieces)
+        blocks(place, w_head, (inputs, grad_out, other), own_units),
+        blocks(place, w_head, (left, left_other), left_units),
+        blocks(place, w_head, far_sources, far_units),
+        blocks(place, w_head, (right, right_other), right_units),
     ]
     sent = totals(place, [part[3] for part in parts], [part[4] for part in parts])
     arrived = [send(sent[dy - 1], dy=dy) for dy in range(1, NY)]
     grad_proj, *pieces = gradients(place, arrived, parts, scaling, user_count, dp_count)
 
-    summed = pieces[0]
-    for dy in range(1, NY):
-        summed = summed + send(pieces[dy], dy=dy)
-    tile = jnp.sum(lax.all_to_all(summed, "dp", 0, 0), axis=0)
+    folded = fold([pieces[0]] + [send(pieces[dy], dy=dy) for dy in range(1, NY)])
+    planes = [
+        [z * NY * GROUP + plane * GROUP + t for z in range(dp_count) for t in range(GROUP)]
+        for plane in range(NY)
+    ]
+    got = lax.all_to_all(folded, ("dp", "seq"), 0, 0, axis_index_groups=planes)
 
     span = 2 * total_rows
     back = [grad_proj[:span].astype(F32)]
     for dx in range(1, NX):
         back.append(send(grad_proj[dx * span : (dx + 1) * span].astype(F32), dx=-dx))
     swap = send(jnp.stack([piece[total_rows:] for piece in back]), dc=1)
-    grad_rows = input_gradient(place, back, swap, w_qkv)
+    grad_rows, done = input_gradient(place, back, swap, w_qkv)
     grad_inputs = grad_rows.reshape(user_count, row_count, feature_count)
 
-    square = jnp.sum(tile * tile)
-    row_block = tile.shape[0]
-    out_rows = row_block // H
-    by_owner = tile.reshape(H, out_rows * 3, DH)
-    got = jnp.zeros((H, out_rows * 3, DH), F32)
-    for dx in range(NX):
-        for dc in range(2):
-            target = ((x + dx) % NX) * 2 + (c ^ dc)
-            piece = lax.dynamic_index_in_dim(by_owner, target, 0, False)
-            if dx or dc:
-                piece = send(piece, dx=dx, dc=dc)
-            source = ((x - dx) % NX) * 2 + (c ^ dc)
-            got = lax.dynamic_update_index_in_dim(got, piece, source, 0)
     device_count = dp_count * lax.axis_size("seq")
-    squares = lax.all_to_all(
-        jnp.full((device_count, DH), square), ("dp", "seq"), 0, 0, tiled=True
-    )
-    total_sq = jnp.sum(squares[:, 0])
-    factor = jnp.minimum(1.0, D / jnp.sqrt(total_sq + 1e-06))
-    weights = jnp.transpose(got.reshape(H, out_rows, 3, DH), (1, 2, 0, 3))
-    return (grad_inputs, weights.reshape(out_rows, 3 * feature_count) * factor)
+    weights, squares = collect(got, done, device_count)
+    squares = lax.all_to_all(squares, ("dp", "seq"), 0, 0, tiled=True)
+    return (grad_inputs, clip(weights, squares))
 
 
 def solution(mesh):

time: 140 us -> 138 us (0.986)
  starting transfers between devices: 68.8 us -> 43.3 us
  blocking collectives: 0 us -> 20.1 us
  waiting for transfers between devices: 35.9 us -> 47.4 us
  local copies, waits for them, and re-layouts: 14.3 us -> 6.02 us
  Pallas kernels: 13.9 us -> 18.9 us
  other arithmetic: 4.86 us -> 1.23 us
    all_to_all x0 -> x1, blocking collectives: none -> 20.1 us  [body(): squares = lax.all_to_all(squares, ('dp', 'seq'), 0, 0, tiled=True)]
    ppermute x29 -> x19, starting transfers between devices: 48.6 us -> 29.9 us  [send(): return lax.ppermute(value, 'seq', seq_perm(dy, dx, dc))]
    ppermute x29 -> x19, waiting for transfers between devices: 26.2 us -> 38.7 us  [send(): return lax.ppermute(value, 'seq', seq_perm(dy, dx, dc))]
    all_to_all x2 -> x1, starting transfers between devices: 20.2 us -> 13.3 us  [body(): got = lax.all_to_all(folded, ('dp', 'seq'), 0, 0, axis_index_groups=planes)]
    pallas_call x5 -> x9, Pallas kernels: 10.3 us -> 15.3 us  [the longest x4 8.61 us: blocks(): pl.pallas_call(functools.partial(block_kernel, units), out_shape=(struct(...]
    reduce_sum x3 -> x0, other arithmetic: 2.69 us -> none  [the longest x1 1.41 us: body(): square = jnp.sum(tile * tile)]
    concatenate x2 -> x0, local copies, waits for them, and re-layouts: 1.94 us -> none  [the longest x1 0.97 us: body(): far = jnp.concatenate([far_low, far_high], axis=0)]
    convert_element_type x1 -> x0, local copies, waits for them, and re-layouts: 1.47 us -> none  [body(): cot = grad_out.reshape(total_rows, feature_count).astype(F32)]
  transfers between devices with their start and end apart: 31 -> 20, of which waited for: 12 -> 8; matrix products, arithmetic and copies ran while one was open for 10% -> 2% of each run, Pallas kernels for 6% -> 8%
where the time goes in v2:
time: 138 us
  waiting for transfers between devices  47.4 us (34%)
  starting transfers between devices  43.3 us (31%)
  blocking collectives  20.1 us (15%)
  Pallas kernels  18.9 us (14%)
  local copies, waits for them, and re-layouts  6.02 us (4%)
    ppermute x19, waiting for transfers between devices, send(): return lax.ppermute(value, 'seq', seq_perm(dy, dx, dc))  38.7 us
    ppermute x19, starting transfers between devices, send(): return lax.ppermute(value, 'seq', seq_perm(dy, dx, dc))  29.9 us
    all_to_all x1, blocking collectives, body(): squares = lax.all_to_all(squares, ('dp', 'seq'), 0, 0, tiled=True)  20.1 us
    all_to_all x1, starting transfers between devices, body(): got = lax.all_to_all(folded, ('dp', 'seq'), 0, 0, axis_index_groups=planes)  13.3 us
    all_to_all x1, waiting for transfers between devices, body(): got = lax.all_to_all(folded, ('dp', 'seq'), 0, 0, axis_index_groups=planes)  8.72 us
    pallas_call x4, Pallas kernels, blocks(): pl.pallas_call(functools.partial(block_kernel, units), out_shape=(struct(...  8.61 us
    unnamed x10, local copies, waits for them, and re-layouts  4.69 us
    pallas_call x1, Pallas kernels, input_gradient(): pl.pallas_call(input_kernel, out_shape=(struct((total, features), BF16),...  3.54 us
  transfers between devices with their start and end apart: 20, of which 8 were waited for; matrix products, arithmetic and copies ran while one was open for 2% of the time, Pallas kernels for 8%

profile of v2, /device:TPU:1, one launch (start us, length us, event | category | flops | bytes accessed | tf_op | source)
XLA Modules:
  0.0 137.8 jit_solution(12990101710655823246)
XLA Ops:
  0.7 0.1 pad_add_fusion.place
  0.7 0.0 copy-start.1
  0.7 0.9 copy-done.1
  1.7 0.9 copy-done.3
  2.6 1.5 %messages.1 = (f32[22,64,128]{2,1,0:T(8,128)S(1)}, f32[22,64,128]{2,1,0:T(8,128)S(1)}, f32[18,64,128]{2,1,0:T(8,128)}) custom-call(s32[3]{0:T(128)S(1)} %pad_add_fusion.place, bf16[2,64,1024]{2,1,0:T(8,128)(2,1)S(1)} %copy-done.1, bf16[2,64,1024]{2,1,0:T(8,128)(2,1)S(1)} %copy-done.3), custom_call_target="tpu_custom_call" | custom-call | flops 1048576 | bytes 3145728 | tf_op jit(solution)/shard_map/messages/pallas_call | solution.py:80
  4.1 2.0 %collective-permute-start.1 = (f32[22,64,128]{2,1,0:T(8,128)S(1)}, f32[22,64,128]{2,1,0:T(8,128)S(1)}, u32[]{:S(2)}, u32[]{:S(2)}) collective-permute-start(f32[22,64,128]{2,1,0:T(8,128)S(1)} %get-tuple-element.43), channel_id=1, source_target_pairs={{0,2},{1,3},{2,4},{3,5},{4,6},{5,7},{6,0},{7,1},{8,10},{9,11},{10,... | collective-permute-start | bytes 2162696 | tf_op jit(solution)/shard_map/ppermute | solution.py:36
  6.2 1.3 collective-permute-start.4
  7.4 13.6 %collective-permute-done.1.refs_0_ = f32[22,64,128]{2,1,0:T(8,128)S(1)} collective-permute-done((f32[22,64,128]{2,1,0:T(8,128)S(1)}, f32[22,64,128]{2,1,0:T(8,128)S(1)}, u32[]{:S(2)}, u32[]{:S(2)}) %collective-permute-start.1) | collective-permute-done | bytes 720928 | tf_op jit(solution)/shard_map/ppermute | solution.py:36
  21.0 3.5 %collective-permute-start.2 = (f32[22,64,128]{2,1,0:T(8,128)S(1)}, f32[22,64,128]{2,1,0:T(8,128)S(1)}, u32[]{:S(2)}, u32[]{:S(2)}) collective-permute-start(f32[22,64,128]{2,1,0:T(8,128)S(1)} %collective-permute-done.1.refs_0_), channel_id=1, source_target_pairs={{0,1},{1,0},{2,3},{3,2},{4,5},{5,4},{6,7},{7,6},{8,9},{9,8},{10,11... | collective-permute-start | bytes 2162696 | tf_op jit(solution)/shard_map/ppermute | solution.py:36
  24.5 0.0 collective-permute-done.4.refs_0_
  24.5 0.2 collective-permute-start.8
  24.7 1.3 collective-permute-start.3
  26.1 1.5 %collective-permute-start.5 = (f32[10,64,128]{2,1,0:T(8,128)S(1)}, f32[10,64,128]{2,1,0:T(8,128)}, u32[]{:S(2)}, u32[]{:S(2)}) collective-permute-start(f32[10,64,128]{2,1,0:T(8,128)S(1)} %slice.41), channel_id=1, source_target_pairs={{0,6},{1,7},{2,0},{3,1},{4,2},{5,3},{6,4},{7,5},{8,14},{9,15},{10,... | collective-permute-start | bytes 983048 | tf_op jit(solution)/shard_map/ppermute | solution.py:36
  27.6 0.9 collective-permute-start
  28.5 6.6 %collective-permute-done.3.refs_0_ = f32[10,64,128]{2,1,0:T(8,128)} collective-permute-done((f32[10,64,128]{2,1,0:T(8,128)S(1)}, f32[10,64,128]{2,1,0:T(8,128)}, u32[]{:S(2)}, u32[]{:S(2)}) %collective-permute-start.3) | collective-permute-done | bytes 327712 | tf_op jit(solution)/shard_map/ppermute | solution.py:36
  35.1 1.1 collective-permute-start.6
  36.3 0.0 collective-permute-done.5.refs_1_
  36.3 0.1 collective-permute-start.7
  36.4 1.2 constant_dynamic-slice_fusion.2
  37.6 0.1 pad_maximum_fusion.w
  37.7 0.0 collective-permute-done.refs_2_
  37.7 0.0 copy-done.2
  37.7 0.0 copy-done.4
  37.8 2.0 %blocks.4 = (bf16[1024,256]{1,0:T(8,128)(2,1)S(1)}, bf16[256,384]{1,0:T(8,128)(2,1)S(1)}, bf16[256,128]{1,0:T(8,128)(2,1)S(1)}, f32[2,2,128,128]{3,2,1,0:T(8,128...) custom-call(s32[3]{0:T(128)S(1)} %pad_add_fusion.place, bf16[1024,384]{1,0:T(8,128)(2,1)S(1)} %pad_maximum_fusion.w, ...), custom_call_target="tpu_custom_call" | custom-call | flops 201326592 | bytes 4194304 | tf_op jit(solution)/shard_map/blocks/pallas_call | solution.py:131
  39.7 0.0 collective-permute-done.6.refs_2_
  39.7 0.0 collective-permute-done.7.refs_3_
  39.7 2.7 %blocks.6 = (bf16[1024,256]{1,0:T(8,128)(2,1)S(1)}, bf16[256,384]{1,0:T(8,128)(2,1)S(1)}, bf16[256,128]{1,0:T(8,128)(2,1)S(1)}, f32[2,2,128,128]{3,2,1,0:T(8,128...) custom-call(s32[3]{0:T(128)S(1)} %pad_add_fusion.place, bf16[1024,384]{1,0:T(8,128)(2,1)S(1)} %pad_maximum_fusion.w, ...), custom_call_target="tpu_custom_call" | custom-call | flops 201326592 | bytes 4194304 | tf_op jit(solution)/shard_map/blocks/pallas_call | solution.py:131
  42.5 0.0 collective-permute-done.2.refs_1_
  42.5 2.0 %blocks.5 = (bf16[1024,256]{1,0:T(8,128)(2,1)S(1)}, bf16[256,384]{1,0:T(8,128)(2,1)S(1)}, bf16[256,128]{1,0:T(8,128)(2,1)S(1)}, f32[2,2,128,128]{3,2,1,0:T(8,128...) custom-call(s32[3]{0:T(128)S(1)} %pad_add_fusion.place, bf16[1024,384]{1,0:T(8,128)(2,1)S(1)} %pad_maximum_fusion.w, ...), custom_call_target="tpu_custom_call" | custom-call | flops 201326592 | bytes 4194304 | tf_op jit(solution)/shard_map/blocks/pallas_call | solution.py:131
  44.4 0.0 collective-permute-done.8.refs_1_
  44.5 2.0 %blocks.7 = (bf16[1024,256]{1,0:T(8,128)(2,1)S(1)}, bf16[256,384]{1,0:T(8,128)(2,1)S(1)}, bf16[256,128]{1,0:T(8,128)(2,1)S(1)}, f32[2,2,128,128]{3,2,1,0:T(8,128...) custom-call(s32[3]{0:T(128)S(1)} %pad_add_fusion.place, bf16[1024,384]{1,0:T(8,128)(2,1)S(1)} %pad_maximum_fusion.w, ...), custom_call_target="tpu_custom_call" | custom-call | flops 201326592 | bytes 4194304 | tf_op jit(solution)/shard_map/blocks/pallas_call | solution.py:131
  46.4 0.6 totals.1
  47.1 1.4 collective-permute-start.9
  48.5 2.6 %collective-permute-start.10 = (f32[2,128,128]{2,1,0:T(8,128)S(1)}, f32[2,128,128]{2,1,0:T(8,128)S(1)}, u32[]{:S(2)}, u32[]{:S(2)}) collective-permute-start(f32[2,128,128]{2,1,0:T(8,128)S(1)} %get-tuple-element.53), channel_id=1, source_target_pairs={{0,16},{1,17},{2,18},{3,19},{4,20},{5,21},{6,22},{7,23},{8,24},{9,... | collective-permute-start | bytes 393224 | tf_op jit(solution)/shard_map/ppermute | solution.py:36
  51.1 1.1 collective-permute-start.11
  52.1 1.0 collective-permute-done.9.refs_0_
  53.2 3.9 %collective-permute-done.10.refs_1_ = f32[2,128,128]{2,1,0:T(8,128)S(1)} collective-permute-done((f32[2,128,128]{2,1,0:T(8,128)S(1)}, f32[2,128,128]{2,1,0:T(8,128)S(1)}, u32[]{:S(2)}, u32[]{:S(2)}) %collective-permute-start.10) | collective-permute-done | bytes 131104 | tf_op jit(solution)/shard_map/ppermute | solution.py:36
  57.1 0.0 collective-permute-done.11.refs_2_
  57.1 2.9 %gradients.1 = (bf16[1024,384]{1,0:T(8,128)(2,1)S(1)}, f32[8,32,384]{2,1,0:T(8,128)S(1)}, f32[8,32,384]{2,1,0:T(8,128)S(1)}, f32[8,32,384]{2,1,0:T(8,128)S(1)}, f32[8,32,384]{2,1,0:T(8,128)S(1)}) custom-call(s32[3]{0:T(128)S(1)} %pad_add_fusion.place, f32[2,128,128]{2,1,0:T(8,128)S(1)} %collective-permute-done.9.refs_0_, ...), custom_call_target="tpu_custom_call" | custom-call | flops 805306368 | bytes 10485760 | tf_op jit(solution)/shard_map/gradients/pallas_call | solution.py:242
  60.0 0.1 slice_convert_fusion
  60.1 1.5 %collective-permute-start.14 = (f32[256,384]{1,0:T(8,128)S(1)}, f32[256,384]{1,0:T(8,128)S(1)}, u32[]{:S(2)}, u32[]{:S(2)}) collective-permute-start(f32[256,384]{1,0:T(8,128)S(1)} %get-tuple-element.83), channel_id=1, source_target_pairs={{0,2},{1,3},{2,4},{3,5},{4,6},{5,7},{6,0},{7,1},{8,10},{9,11},{10,... | collective-permute-start | bytes 1179656 | tf_op jit(solution)/shard_map/ppermute | solution.py:36
  61.6 0.6 collective-permute-start.16
  62.2 2.6 %collective-permute-start.17 = (f32[8,32,384]{2,1,0:T(8,128)S(1)}, f32[8,32,384]{2,1,0:T(8,128)S(1)}, u32[]{:S(2)}, u32[]{:S(2)}) collective-permute-start(f32[8,32,384]{2,1,0:T(8,128)S(1)} %get-tuple-element.75), channel_id=1, source_target_pairs={{0,16},{1,17},{2,18},{3,19},{4,20},{5,21},{6,22},{7,23},{8,24},{9,... | collective-permute-start | bytes 1179656 | tf_op jit(solution)/shard_map/ppermute | solution.py:36
  64.8 0.9 collective-permute-start.18
  65.7 3.0 %collective-permute-start.13 = (f32[256,384]{1,0:T(8,128)S(1)}, f32[256,384]{1,0:T(8,128)S(1)}, u32[]{:S(2)}, u32[]{:S(2)}) collective-permute-start(f32[256,384]{1,0:T(8,128)S(1)} %get-tuple-element.84), channel_id=1, source_target_pairs={{0,4},{1,5},{2,6},{3,7},{4,0},{5,1},{6,2},{7,3},{8,12},{9,13},{10,... | collective-permute-start | bytes 1179656 | tf_op jit(solution)/shard_map/ppermute | solution.py:36
  68.6 3.2 %collective-permute-done.14.refs_3_ = f32[256,384]{1,0:T(8,128)S(1)} collective-permute-done((f32[256,384]{1,0:T(8,128)S(1)}, f32[256,384]{1,0:T(8,128)S(1)}, u32[]{:S(2)}, u32[]{:S(2)}) %collective-permute-start.14) | collective-permute-done | bytes 393248 | tf_op jit(solution)/shard_map/ppermute | solution.py:36
  71.8 1.4 %collective-permute-start.12 = (f32[256,384]{1,0:T(8,128)S(1)}, f32[256,384]{1,0:T(8,128)S(1)}, u32[]{:S(2)}, u32[]{:S(2)}) collective-permute-start(f32[256,384]{1,0:T(8,128)S(1)} %get-tuple-element.85), channel_id=1, source_target_pairs={{0,6},{1,7},{2,0},{3,1},{4,2},{5,3},{6,4},{7,5},{8,14},{9,15},{10,... | collective-permute-start | bytes 1179656 | tf_op jit(solution)/shard_map/ppermute | solution.py:36
  73.3 8.1 %collective-permute-done.13.refs_2_ = f32[256,384]{1,0:T(8,128)S(1)} collective-permute-done((f32[256,384]{1,0:T(8,128)S(1)}, f32[256,384]{1,0:T(8,128)S(1)}, u32[]{:S(2)}, u32[]{:S(2)}) %collective-permute-start.13) | collective-permute-done | bytes 393248 | tf_op jit(solution)/shard_map/ppermute | solution.py:36
  81.4 2.2 %collective-permute-done.12.refs_1_ = f32[256,384]{1,0:T(8,128)S(1)} collective-permute-done((f32[256,384]{1,0:T(8,128)S(1)}, f32[256,384]{1,0:T(8,128)S(1)}, u32[]{:S(2)}, u32[]{:S(2)}) %collective-permute-start.12) | collective-permute-done | bytes 393248 | tf_op jit(solution)/shard_map/ppermute | solution.py:36
  83.6 0.9 pad_maximum_fusion.1
  84.6 3.0 %collective-permute-start.15 = (f32[4,128,384]{2,1,0:T(8,128)}, f32[4,128,384]{2,1,0:T(8,128)S(1)}, u32[]{:S(2)}, u32[]{:S(2)}) collective-permute-start(f32[4,128,384]{2,1,0:T(8,128)} %pad_maximum_fusion.1), channel_id=1, source_target_pairs={{0,1},{1,0},{2,3},{3,2},{4,5},{5,4},{6,7},{7,6},{8,9},{9,8},{10,11... | collective-permute-start | bytes 2359304 | tf_op jit(solution)/shard_map/ppermute | solution.py:36
  87.6 0.0 collective-permute-done.16.refs_1_
  87.6 0.0 collective-permute-done.17.refs_2_
  87.6 0.0 collective-permute-done.18.refs_3_
  87.6 0.8 fold.1
  88.4 13.3 %all-to-all-start = ((f32[64,4,384]{2,1,0:T(4,128)}), f32[64,4,384]{2,1,0:T(4,128)S(1)}, u32[]{:S(2)}, u32[]{:S(2)}) async-start(f32[64,4,384]{2,1,0:T(4,128)} %fold.1), calls=%async_computation | async-start | bytes 786432 | tf_op jit(solution)/shard_map/all_to_all | solution.py:410
  101.7 0.0 collective-permute-done.15.refs_4_
  101.8 0.0 copy-start
  101.8 2.8 %copy-done = bf16[1024,3072]{1,0:T(8,128)(2,1)S(1)} copy-done((bf16[1024,3072]{1,0:T(8,128)(2,1)S(1)}, bf16[1024,3072]{1,0:T(8,128)(2,1)}, u32[]{:S(2)}) %copy-start) | copy-done | bytes 6291480
  104.5 3.5 %input_gradient.1 = (bf16[128,1024]{1,0:T(8,128)(2,1)}, f32[8,128]{1,0:T(8,128)S(1)}) custom-call(s32[3]{0:T(128)S(1)} %pad_add_fusion.place, f32[256,384]{1,0:T(8,128)S(1)} %get-tuple-element.86.refs_0_, f32[256,384]{1,0:T(8,128)S(1)} %collective-permute-done.12.refs_1_, f32[256,384]{1,0:T(8,128)S(1)} %collective-permute-done.13.refs_2_, ...), custom_call_target="tpu_custom_call" | custom-call | flops 805306368 | bytes 10485760 | tf_op jit(solution)/shard_map/input_gradient/pallas_call | solution.py:283
  108.1 8.7 %all-to-all-done.got = f32[64,4,384]{2,1,0:T(4,128)S(1)} async-done(((f32[64,4,384]{2,1,0:T(4,128)}), f32[64,4,384]{2,1,0:T(4,128)S(1)}, u32[]{:S(2)}, u32[]{:S(2)}) %all-to-all-start) | async-done | bytes 393248 | tf_op jit(solution)/shard_map/all_to_all | solution.py:410
  116.8 0.2 collect.1
  117.0 20.1 %all_to_all.16 = f32[256,1,128]{2,1,0:T(1,128)S(1)} all-to-all(f32[256,1,128]{2,1,0:T(1,128)S(1)} %bitcast.17), channel_id=1, replica_groups=mesh['dp'=8,'seq'=32] {'dp','seq'}, dimensions={0} | all-to-all | bytes 262144 | tf_op jit(solution)/shard_map/all_to_all | solution.py:422
  137.1 0.7 clip.1
  (9 shorter events, 0.1 us)
Async XLA Ops:
  0.7 1.0 copy-start.1
  1.7 0.9 copy-start.3
  4.1 16.9 %collective-permute-start.1 = (f32[22,64,128]{2,1,0:T(8,128)S(1)}, f32[22,64,128]{2,1,0:T(8,128)S(1)}, u32[]{:S(2)}, u32[]{:S(2)}) collective-permute-start(f32[22,64,128]{2,1,0:T(8,128)S(1)} %get-tuple-element.43), channel_id=1, source_target_pairs={{0,2},{1,3},{2,4},{3,5},{4,6},{5,7},{6,0},{7,1},{8,10},{9,11},{10,... | collective-permute-start | bytes 2162696 | tf_op jit(solution)/shard_map/ppermute | solution.py:36
  6.2 18.4 %collective-permute-start.4 = (f32[22,64,128]{2,1,0:T(8,128)S(1)}, f32[22,64,128]{2,1,0:T(8,128)S(1)}, u32[]{:S(2)}, u32[]{:S(2)}) collective-permute-start(f32[22,64,128]{2,1,0:T(8,128)S(1)} %get-tuple-element.45), channel_id=1, source_target_pairs={{0,6},{1,7},{2,0},{3,1},{4,2},{5,3},{6,4},{7,5},{8,14},{9,15},{10,... | collective-permute-start | bytes 2162696 | tf_op jit(solution)/shard_map/ppermute | solution.py:36
  21.0 21.5 %collective-permute-start.2 = (f32[22,64,128]{2,1,0:T(8,128)S(1)}, f32[22,64,128]{2,1,0:T(8,128)S(1)}, u32[]{:S(2)}, u32[]{:S(2)}) collective-permute-start(f32[22,64,128]{2,1,0:T(8,128)S(1)} %collective-permute-done.1.refs_0_), channel_id=1, source_target_pairs={{0,1},{1,0},{2,3},{3,2},{4,5},{5,4},{6,7},{7,6},{8,9},{9,8},{10,11... | collective-permute-start | bytes 2162696 | tf_op jit(solution)/shard_map/ppermute | solution.py:36
  24.5 19.9 %collective-permute-start.8 = (f32[22,64,128]{2,1,0:T(8,128)S(1)}, f32[22,64,128]{2,1,0:T(8,128)S(1)}, u32[]{:S(2)}, u32[]{:S(2)}) collective-permute-start(f32[22,64,128]{2,1,0:T(8,128)S(1)} %collective-permute-done.4.refs_0_), channel_id=1, source_target_pairs={{0,1},{1,0},{2,3},{3,2},{4,5},{5,4},{6,7},{7,6},{8,9},{9,8},{10,11... | collective-permute-start | bytes 2162696 | tf_op jit(solution)/shard_map/ppermute | solution.py:36
  24.7 10.4 %collective-permute-start.3 = (f32[10,64,128]{2,1,0:T(8,128)S(1)}, f32[10,64,128]{2,1,0:T(8,128)}, u32[]{:S(2)}, u32[]{:S(2)}) collective-permute-start(f32[10,64,128]{2,1,0:T(8,128)S(1)} %slice.40), channel_id=1, source_target_pairs={{0,2},{1,3},{2,4},{3,5},{4,6},{5,7},{6,0},{7,1},{8,10},{9,11},{10,... | collective-permute-start | bytes 983048 | tf_op jit(solution)/shard_map/ppermute | solution.py:36
  26.1 10.2 %collective-permute-start.5 = (f32[10,64,128]{2,1,0:T(8,128)S(1)}, f32[10,64,128]{2,1,0:T(8,128)}, u32[]{:S(2)}, u32[]{:S(2)}) collective-permute-start(f32[10,64,128]{2,1,0:T(8,128)S(1)} %slice.41), channel_id=1, source_target_pairs={{0,6},{1,7},{2,0},{3,1},{4,2},{5,3},{6,4},{7,5},{8,14},{9,15},{10,... | collective-permute-start | bytes 983048 | tf_op jit(solution)/shard_map/ppermute | solution.py:36
  27.6 10.1 %collective-permute-start = (f32[18,64,128]{2,1,0:T(8,128)}, f32[18,64,128]{2,1,0:T(8,128)S(1)}, u32[]{:S(2)}, u32[]{:S(2)}) collective-permute-start(f32[18,64,128]{2,1,0:T(8,128)} %get-tuple-element.41), channel_id=1, source_target_pairs={{0,1},{1,0},{2,3},{3,2},{4,5},{5,4},{6,7},{7,6},{8,9},{9,8},{10,11... | collective-permute-start | bytes 1769480 | tf_op jit(solution)/shard_map/ppermute | solution.py:36
  35.1 4.6 %collective-permute-start.6 = (f32[10,64,128]{2,1,0:T(8,128)}, f32[10,64,128]{2,1,0:T(8,128)}, u32[]{:S(2)}, u32[]{:S(2)}) collective-permute-start(f32[10,64,128]{2,1,0:T(8,128)} %collective-permute-done.3.refs_0_), channel_id=1, source_target_pairs={{0,1},{1,0},{2,3},{3,2},{4,5},{5,4},{6,7},{7,6},{8,9},{9,8},{10,11... | collective-permute-start | bytes 983048 | tf_op jit(solution)/shard_map/ppermute | solution.py:36
  36.3 3.5 %collective-permute-start.7 = (f32[10,64,128]{2,1,0:T(8,128)}, f32[10,64,128]{2,1,0:T(8,128)}, u32[]{:S(2)}, u32[]{:S(2)}) collective-permute-start(f32[10,64,128]{2,1,0:T(8,128)} %collective-permute-done.5.refs_1_), channel_id=1, source_target_pairs={{0,1},{1,0},{2,3},{3,2},{4,5},{5,4},{6,7},{7,6},{8,9},{9,8},{10,11... | collective-permute-start | bytes 983048 | tf_op jit(solution)/shard_map/ppermute | solution.py:36
  36.4 1.4 copy-start.2
  36.4 1.4 copy-start.4
  47.1 6.1 %collective-permute-start.9 = (f32[2,128,128]{2,1,0:T(8,128)S(1)}, f32[2,128,128]{2,1,0:T(8,128)S(1)}, u32[]{:S(2)}, u32[]{:S(2)}) collective-permute-start(f32[2,128,128]{2,1,0:T(8,128)S(1)} %get-tuple-element.52), channel_id=1, source_target_pairs={{0,8},{1,9},{2,10},{3,11},{4,12},{5,13},{6,14},{7,15},{8,16},{9,17... | collective-permute-start | bytes 393224 | tf_op jit(solution)/shard_map/ppermute | solution.py:36
  48.5 8.6 %collective-permute-start.10 = (f32[2,128,128]{2,1,0:T(8,128)S(1)}, f32[2,128,128]{2,1,0:T(8,128)S(1)}, u32[]{:S(2)}, u32[]{:S(2)}) collective-permute-start(f32[2,128,128]{2,1,0:T(8,128)S(1)} %get-tuple-element.53), channel_id=1, source_target_pairs={{0,16},{1,17},{2,18},{3,19},{4,20},{5,21},{6,22},{7,23},{8,24},{9,... | collective-permute-start | bytes 393224 | tf_op jit(solution)/shard_map/ppermute | solution.py:36
  51.1 6.0 %collective-permute-start.11 = (f32[2,128,128]{2,1,0:T(8,128)S(1)}, f32[2,128,128]{2,1,0:T(8,128)S(1)}, u32[]{:S(2)}, u32[]{:S(2)}) collective-permute-start(f32[2,128,128]{2,1,0:T(8,128)S(1)} %get-tuple-element.54), channel_id=1, source_target_pairs={{0,24},{1,25},{2,26},{3,27},{4,28},{5,29},{6,30},{7,31},{8,0},{9,1... | collective-permute-start | bytes 393224 | tf_op jit(solution)/shard_map/ppermute | solution.py:36
  60.1 11.7 %collective-permute-start.14 = (f32[256,384]{1,0:T(8,128)S(1)}, f32[256,384]{1,0:T(8,128)S(1)}, u32[]{:S(2)}, u32[]{:S(2)}) collective-permute-start(f32[256,384]{1,0:T(8,128)S(1)} %get-tuple-element.83), channel_id=1, source_target_pairs={{0,2},{1,3},{2,4},{3,5},{4,6},{5,7},{6,0},{7,1},{8,10},{9,11},{10,... | collective-permute-start | bytes 1179656 | tf_op jit(solution)/shard_map/ppermute | solution.py:36
  61.6 25.9 %collective-permute-start.16 = (f32[8,32,384]{2,1,0:T(8,128)S(1)}, f32[8,32,384]{2,1,0:T(8,128)S(1)}, u32[]{:S(2)}, u32[]{:S(2)}) collective-permute-start(f32[8,32,384]{2,1,0:T(8,128)S(1)} %get-tuple-element.74), channel_id=1, source_target_pairs={{0,8},{1,9},{2,10},{3,11},{4,12},{5,13},{6,14},{7,15},{8,16},{9,17... | collective-permute-start | bytes 1179656 | tf_op jit(solution)/shard_map/ppermute | solution.py:36
  62.2 25.4 %collective-permute-start.17 = (f32[8,32,384]{2,1,0:T(8,128)S(1)}, f32[8,32,384]{2,1,0:T(8,128)S(1)}, u32[]{:S(2)}, u32[]{:S(2)}) collective-permute-start(f32[8,32,384]{2,1,0:T(8,128)S(1)} %get-tuple-element.75), channel_id=1, source_target_pairs={{0,16},{1,17},{2,18},{3,19},{4,20},{5,21},{6,22},{7,23},{8,24},{9,... | collective-permute-start | bytes 1179656 | tf_op jit(solution)/shard_map/ppermute | solution.py:36
  64.8 22.8 %collective-permute-start.18 = (f32[8,32,384]{2,1,0:T(8,128)S(1)}, f32[8,32,384]{2,1,0:T(8,128)S(1)}, u32[]{:S(2)}, u32[]{:S(2)}) collective-permute-start(f32[8,32,384]{2,1,0:T(8,128)S(1)} %get-tuple-element.76), channel_id=1, source_target_pairs={{0,24},{1,25},{2,26},{3,27},{4,28},{5,29},{6,30},{7,31},{8,0},{9,1... | collective-permute-start | bytes 1179656 | tf_op jit(solution)/shard_map/ppermute | solution.py:36
  65.7 15.7 %collective-permute-start.13 = (f32[256,384]{1,0:T(8,128)S(1)}, f32[256,384]{1,0:T(8,128)S(1)}, u32[]{:S(2)}, u32[]{:S(2)}) collective-permute-start(f32[256,384]{1,0:T(8,128)S(1)} %get-tuple-element.84), channel_id=1, source_target_pairs={{0,4},{1,5},{2,6},{3,7},{4,0},{5,1},{6,2},{7,3},{8,12},{9,13},{10,... | collective-permute-start | bytes 1179656 | tf_op jit(solution)/shard_map/ppermute | solution.py:36
  71.8 11.8 %collective-permute-start.12 = (f32[256,384]{1,0:T(8,128)S(1)}, f32[256,384]{1,0:T(8,128)S(1)}, u32[]{:S(2)}, u32[]{:S(2)}) collective-permute-start(f32[256,384]{1,0:T(8,128)S(1)} %get-tuple-element.85), channel_id=1, source_target_pairs={{0,6},{1,7},{2,0},{3,1},{4,2},{5,3},{6,4},{7,5},{8,14},{9,15},{10,... | collective-permute-start | bytes 1179656 | tf_op jit(solution)/shard_map/ppermute | solution.py:36
  84.6 17.2 %collective-permute-start.15 = (f32[4,128,384]{2,1,0:T(8,128)}, f32[4,128,384]{2,1,0:T(8,128)S(1)}, u32[]{:S(2)}, u32[]{:S(2)}) collective-permute-start(f32[4,128,384]{2,1,0:T(8,128)} %pad_maximum_fusion.1), channel_id=1, source_target_pairs={{0,1},{1,0},{2,3},{3,2},{4,5},{5,4},{6,7},{7,6},{8,9},{9,8},{10,11... | collective-permute-start | bytes 2359304 | tf_op jit(solution)/shard_map/ppermute | solution.py:36
  88.4 28.4 %all-to-all-start = ((f32[64,4,384]{2,1,0:T(4,128)}), f32[64,4,384]{2,1,0:T(4,128)S(1)}, u32[]{:S(2)}, u32[]{:S(2)}) async-start(f32[64,4,384]{2,1,0:T(4,128)} %fold.1), calls=%async_computation | async-start | bytes 786432 | tf_op jit(solution)/shard_map/all_to_all | solution.py:410
  101.8 2.8 %copy-start = (bf16[1024,3072]{1,0:T(8,128)(2,1)S(1)}, bf16[1024,3072]{1,0:T(8,128)(2,1)}, u32[]{:S(2)}) copy-start(bf16[1024,3072]{1,0:T(8,128)(2,1)} %refs_5_.1) | copy-start | bytes 18874372

commit v3 on v2

--- a/solution.py
+++ b/solution.py
@@ -18,6 +18,7 @@
 F32 = jnp.float32
 VMEM = pl.BlockSpec(memory_space=pltpu.VMEM)
 SMEM = pl.BlockSpec(memory_space=pltpu.SMEM)
+ANY = pl.BlockSpec(memory_space=pl.ANY)
 MIB = 1 << 20
 
 
@@ -51,28 +52,22 @@
 def message_kernel(place, inputs, grad_out, right, left, cross):
     x, c = place[1], place[2]
 
-    def rows(user, j):
-        return inputs[user, :, j * DH : (j + 1) * DH].astype(F32)
-
     def cot(user, dx, core):
         head = ((x + dx) % NX) * 2 + core
         return grad_out[user, :, pl.ds(pl.multiple_of(head * DH, DH), DH)].astype(F32)
 
-    for j in range(H):
-        right[j] = rows(0, j)
-        right[10 + j] = rows(1, j)
-        left[j] = rows(1, j)
-        left[10 + j] = rows(0, j)
-        cross[j] = rows(0, j)
-        cross[8 + j] = rows(1, j)
-    for core in range(2):
-        right[8 + core] = cot(0, 2, core)
-        left[8 + core] = cot(1, 2, core)
-        for user in range(2):
+    for user in range(2):
+        passed, kept = (right, left) if user == 0 else (left, right)
+        for j in range(H):
+            value = inputs[user, :, j * DH : (j + 1) * DH].astype(F32)
+            passed[j] = value
+            kept[10 + j] = value
+            cross[user * H + j] = value
+        for core in range(2):
+            passed[8 + core] = cot(user, 2, core)
             right[18 + 2 * core + user] = cot(user, 1, core)
             left[18 + 2 * core + user] = cot(user, NX - 1, core)
-    for user in range(2):
-        cross[16 + user] = cot(user, 0, 1 - c)
+        cross[2 * H + user] = cot(user, 0, 1 - c)
 
 
 def messages(place, inputs, grad_out):
@@ -86,6 +81,27 @@
         cost_estimate=pl.CostEstimate(flops=MIB, bytes_accessed=3 * MIB, transcendentals=0),
         name="messages",
     )(place, inputs, grad_out)
+
+
+def relay_kernel(cuts, *refs):
+    sources, outs = refs
+    for out, source, first, last, at in cuts:
+        outs[out][at : at + last - first] = sources[source][first:last].astype(outs[out].dtype)
+
+
+def relay(sources, shapes, cuts, after=()):
+    def kernel(*refs):
+        relay_kernel(cuts, refs[: len(sources)], refs[len(sources) + len(after) :])
+
+    return pl.pallas_call(
+        kernel,
+        out_shape=tuple(struct(shape, F32) for shape in shapes),
+        in_specs=[VMEM] * len(sources) + [ANY] * len(after),
+        out_specs=(VMEM,) * len(shapes),
+        compiler_params=pltpu.CompilerParams(vmem_limit_bytes=12 * MIB),
+        cost_estimate=pl.CostEstimate(flops=MIB, bytes_accessed=2 * MIB, transcendentals=0),
+        name="relay",
+    )(*sources, *after)
 
 
 def block_kernel(units, place, w, *refs):
@@ -134,8 +150,8 @@
             struct((features, total), BF16),
             struct((total, 3 * DH), BF16),
             struct((total, DH), BF16),
-            struct((2, 2, DH, DH), F32),
-            struct((2, 2, DH, DH), F32),
+            struct((len(units) // 2, 2, DH, DH), F32),
+            struct((len(units) // 2, 2, DH, DH), F32),
             struct((total, 3 * DH), F32),
         ),
         in_specs=[SMEM] + [VMEM] * (1 + len(sources)),
@@ -150,9 +166,10 @@
 
 
 def total_kernel(place, *refs):
-    keys, queries, outs = refs[:NX], refs[NX : 2 * NX], refs[2 * NX :]
-    key_total = sum(ref[i] for ref in keys for i in range(2))
-    query_total = sum(ref[i] for ref in queries for i in range(2))
+    count = (len(refs) - NY + 1) // 2
+    keys, queries, outs = refs[:count], refs[count : 2 * count], refs[2 * count :]
+    key_total = sum(ref[i] for ref in keys for i in range(ref.shape[0]))
+    query_total = sum(ref[i] for ref in queries for i in range(ref.shape[0]))
     for dy in range(1, NY):
         outs[dy - 1][...] = jnp.where(place[0] + dy < NY, key_total, query_total)
 
@@ -162,7 +179,7 @@
     return pl.pallas_call(
         total_kernel,
         out_shape=(struct(shape, F32),) * (NY - 1),
-        in_specs=[SMEM] + [VMEM] * (2 * NX),
+        in_specs=[SMEM] + [VMEM] * (2 * len(key_states)),
         out_specs=(VMEM,) * (NY - 1),
         compiler_params=pltpu.CompilerParams(vmem_limit_bytes=16 * MIB),
         cost_estimate=pl.CostEstimate(flops=MIB, bytes_accessed=3 * MIB, transcendentals=0),
@@ -170,20 +187,23 @@
     )(place, *key_states, *query_states)
 
 
-def grad_kernel(scaling, users, dp_count, place, *refs):
+def grad_kernel(scaling, users, dp_count, count, place, *refs):
     y, x, c = place[0], place[1], place[2]
     arrived, refs = refs[: NY - 1], refs[NY - 1 :]
-    keys, refs = refs[:NX], refs[NX:]
-    queries, refs = refs[:NX], refs[NX:]
-    rows_t, refs = refs[:NX], refs[NX:]
-    proj, refs = refs[:NX], refs[NX:]
-    cots, refs = refs[:NX], refs[NX:]
-    intra, refs = refs[:NX], refs[NX:]
-    grad_proj, pieces, refs = refs[0], refs[1 : 1 + NY], refs[1 + NY :]
+    keys, refs = refs[:count], refs[count:]
+    queries, refs = refs[:count], refs[count:]
+    rows_t, refs = refs[:count], refs[count:]
+    proj, refs = refs[:count], refs[count:]
+    cots, refs = refs[:count], refs[count:]
+    intra, refs = refs[:count], refs[count:]
+    grad_proj, give, pieces, refs = refs[0], refs[1], refs[2 : 2 + NY], refs[2 + NY :]
     key_all, query_all, prior_all, later_all, product = refs
-    for dx in range(NX):
-        key_all[2 * dx : 2 * dx + 2] = keys[dx][...]
-        query_all[2 * dx : 2 * dx + 2] = queries[dx][...]
+    first = 0
+    for part in range(count):
+        last = first + keys[part].shape[0]
+        key_all[first:last] = keys[part][...]
+        query_all[first:last] = queries[part][...]
+        first = last
     prior = jnp.zeros(arrived[0].shape, F32)
     later = jnp.zeros(arrived[0].shape, F32)
     for dy in range(1, NY):
@@ -202,31 +222,36 @@
         here = slot(position)
         later_all[here] = later.astype(BF16)
         later = later + query_all[here]
-    total = proj[0].shape[0] // 2
-    size = total // users
-    for dx in range(NX):
-        for i in range(2):
+    size = intra[0].shape[0] // (keys[0].shape[0] * users)
+    block = 0
+    for part in range(count):
+        for i in range(keys[part].shape[0]):
             for u in range(users):
-                here = slice(i * total + u * size, i * total + (u + 1) * size)
-                there = slice(dx * 2 * total + here.start, dx * 2 * total + here.stop)
-                k, v = proj[dx][here, DH : 2 * DH], proj[dx][here, 2 * DH :]
-                prior_state = prior_all[2 * dx + i, u]
-                later_state = later_all[2 * dx + i, u]
-                parts = (
-                    dot(cots[dx][here, :], prior_state, 1, 1),
+                here = slice((i * users + u) * size, (i * users + u + 1) * size)
+                there = slice((block * users + u) * size, (block * users + u + 1) * size)
+                k, v = proj[part][here, DH : 2 * DH], proj[part][here, 2 * DH :]
+                prior_state, later_state = prior_all[block, u], later_all[block, u]
+                inter = (
+                    dot(cots[part][here, :], prior_state, 1, 1),
                     dot(v, later_state, 1, 1),
                     dot(k, later_state, 1, 0),
                 )
-                for part in range(3):
-                    columns = slice(part * DH, (part + 1) * DH)
+                for kind in range(3):
+                    columns = slice(kind * DH, (kind + 1) * DH)
                     grad_proj[there, columns] = (
-                        scaling * (intra[dx][here, columns] + parts[part])
+                        scaling * (intra[part][here, columns] + inter[kind])
                     ).astype(BF16)
-    span = 2 * total
-    product[...] = sum(
-        dot(rows_t[dx][...], grad_proj[dx * span : (dx + 1) * span, :], 1, 0)
-        for dx in range(NX)
-    )
+            block += 1
+    total = users * size
+    for dx in range(NX):
+        there = slice((2 * dx + 1) * total, (2 * dx + 2) * total)
+        give[dx * total : (dx + 1) * total, :] = grad_proj[there, :].astype(F32)
+    value, first = 0.0, 0
+    for part in range(count):
+        last = first + rows_t[part].shape[1]
+        value = value + dot(rows_t[part][...], grad_proj[first:last, :], 1, 0)
+        first = last
+    product[...] = value
     row_block = product.shape[0] // (dp_count * NY)
     for dy in range(NY):
         target = (y + dy) % NY
@@ -237,14 +262,16 @@
 
 def gradients(place, arrived, parts, scaling, users, dp_count):
     rows_t, proj, cots, keys, queries, intra = zip(*parts)
-    features, span = rows_t[0].shape
+    features = rows_t[0].shape[0]
+    rows = sum(part.shape[1] for part in rows_t)
     row_block = features // (dp_count * NY)
-    return pl.pallas_call(
-        functools.partial(grad_kernel, scaling, users, dp_count),
-        out_shape=(struct((NX * span, 3 * DH), BF16),)
+    count = len(parts)
+    return pl.pallas_call(
+        functools.partial(grad_kernel, scaling, users, dp_count, count),
+        out_shape=(struct((rows, 3 * DH), BF16), struct((rows // 2, 3 * DH), F32))
         + (struct((dp_count, row_block, 3 * DH), F32),) * NY,
-        in_specs=[SMEM] + [VMEM] * (NY - 1 + 6 * NX),
-        out_specs=(VMEM,) * (1 + NY),
+        in_specs=[SMEM] + [VMEM] * (NY - 1 + 6 * count),
+        out_specs=(VMEM,) * (2 + NY),
         scratch_shapes=[
             pltpu.VMEM((GROUP, users, DH, DH), F32),
             pltpu.VMEM((GROUP, users, DH, DH), F32),
@@ -254,7 +281,7 @@
         ],
         compiler_params=pltpu.CompilerParams(vmem_limit_bytes=32 * MIB),
         cost_estimate=pl.CostEstimate(
-            flops=2 * NX * span * features * 3 * DH, bytes_accessed=10 * MIB, transcendentals=0
+            flops=2 * rows * features * 3 * DH, bytes_accessed=10 * MIB, transcendentals=0
         ),
         name="gradients",
     )(place, *arrived, *keys, *queries, *rows_t, *proj, *cots, *intra)
@@ -262,83 +289,101 @@
 
 def input_kernel(place, *refs):
     x, c = place[1], place[2]
-    keep = refs[:NX]
-    swap, w, out, done, full = refs[NX:]
+    own, theirs, back = refs[0], refs[1], refs[2 : 1 + NX]
+    w, out, done, full = refs[1 + NX :]
     total = out.shape[0]
     for dx in range(NX):
         for dc in range(2):
             head = ((x + dx) % NX) * 2 + (c ^ dc)
+            source = (theirs if dc else own) if dx == 0 else back[dx - 1]
+            first = total if dx and dc else 0
             for part in range(3):
                 columns = slice(part * DH, (part + 1) * DH)
-                value = keep[dx][:total, columns] if dc == 0 else swap[dx, :, columns]
                 start = pl.multiple_of((part * H + head) * DH, DH)
-                full[:, pl.ds(start, DH)] = value.astype(BF16)
+                full[:, pl.ds(start, DH)] = source[first : first + total, columns].astype(BF16)
     out[...] = dot(full[...], w[...], 1, 1).astype(BF16)
     done[...] = jnp.zeros(done.shape, F32)
 
 
-def input_gradient(place, keep, swap, w_qkv):
-    total = swap.shape[1]
+def input_gradient(place, sources, total, w_qkv):
     features, width = w_qkv.shape
     return pl.pallas_call(
         input_kernel,
         out_shape=(struct((total, features), BF16), struct((8, DH), F32)),
-        in_specs=[SMEM] + [VMEM] * (NX + 2),
+        in_specs=[SMEM] + [VMEM] * (len(sources) + 1),
         out_specs=(VMEM, VMEM),
         scratch_shapes=[pltpu.VMEM((total, width), BF16)],
         compiler_params=pltpu.CompilerParams(vmem_limit_bytes=24 * MIB),
         cost_estimate=pl.CostEstimate(
-            flops=2 * total * features * width, bytes_accessed=10 * MIB, transcendentals=0
+            flops=16 * total * features * width, bytes_accessed=80 * MIB, transcendentals=0
         ),
         name="input_gradient",
-    )(place, *keep, swap, w_qkv)
-
-
-def fold_kernel(*refs):
+    )(place, *sources, w_qkv)
+
+
+def fold_kernel(count, *refs):
     out = refs[-1]
     dp_count, row_block = refs[0].shape[0], refs[0].shape[1]
     rows = out.shape[1]
     for z in range(dp_count):
-        value = sum(ref[z] for ref in refs[:-1])
+        value = sum(ref[z] for ref in refs[:count])
         for t in range(GROUP):
             out[z * GROUP + t] = value[t * rows : (t + 1) * rows, :]
 
 
-def fold(parts):
+def fold(parts, after):
     dp_count, row_block, width = parts[0].shape
     return pl.pallas_call(
-        fold_kernel,
+        functools.partial(fold_kernel, len(parts)),
         out_shape=struct((dp_count * GROUP, row_block // GROUP, width), F32),
-        in_specs=[VMEM] * len(parts),
+        in_specs=[VMEM] * len(parts) + [ANY],
         out_specs=VMEM,
         compiler_params=pltpu.CompilerParams(vmem_limit_bytes=8 * MIB),
         cost_estimate=pl.CostEstimate(flops=MIB, bytes_accessed=2 * MIB, transcendentals=0),
         name="fold",
-    )(*parts)
-
-
-def collect_kernel(got, after, weights, squares):
+    )(*parts, after)
+
+
+def square_kernel(got, after, squares):
     count = got.shape[0] // H
-    square = jnp.zeros((), F32)
+    lanes = jnp.zeros((1, got.shape[2]), F32)
     for head in range(H):
         value = sum(got[z * H + head] for z in range(count))
-        square = square + jnp.sum(value * value)
+        lanes = lanes + jnp.sum(value * value, axis=0, keepdims=True)
+    squares[...] = jnp.full(squares.shape, jnp.sum(lanes))
+
+
+def square_sum(got, after, device_count):
+    return pl.pallas_call(
+        square_kernel,
+        out_shape=struct((device_count, DH), F32),
+        in_specs=[VMEM, ANY],
+        out_specs=VMEM,
+        compiler_params=pltpu.CompilerParams(vmem_limit_bytes=8 * MIB),
+        cost_estimate=pl.CostEstimate(flops=MIB, bytes_accessed=MIB, transcendentals=0),
+        name="square_sum",
+    )(got, after)
+
+
+def assemble_kernel(got, after, weights):
+    count = got.shape[0] // H
+    for head in range(H):
+        value = sum(got[z * H + head] for z in range(count))
         for part in range(3):
             start = (part * H + head) * DH
             weights[:, start : start + DH] = value[:, part * DH : (part + 1) * DH]
-    squares[...] = jnp.full(squares.shape, square)
-
-
-def collect(got, after, device_count):
+
+
+def assemble(got, after):
     rows, width = got.shape[1], got.shape[2]
     return pl.pallas_call(
-        collect_kernel,
-        out_shape=(struct((rows, H * width), F32), struct((device_count, DH), F32)),
-        in_specs=[VMEM, pl.BlockSpec(memory_space=pl.ANY)],
-        out_specs=(VMEM, VMEM),
+        assemble_kernel,
+        out_shape=struct((rows, H * width), F32),
+        in_specs=[VMEM, ANY],
+        out_specs=VMEM,
         compiler_params=pltpu.CompilerParams(vmem_limit_bytes=8 * MIB),
         cost_estimate=pl.CostEstimate(flops=MIB, bytes_accessed=MIB, transcendentals=0),
-        name="collect",
+        name="assemble",
     )(got, after)
 
 
@@ -377,48 +422,70 @@
     left = send(to_right, dx=1)
     right = send(to_left, dx=-1)
     other = send(to_other, dc=1)
-    far_low = send(left[:10], dx=1)
-    far_high = send(right[:10], dx=-1)
-    left_other = send(left, dc=1)
-    right_other = send(right, dc=1)
-    far_low_other = send(far_low, dc=1)
-    far_high_other = send(far_high, dc=1)
-
     w_head = jnp.concatenate(
         [head_columns(w_qkv, part * H + head) for part in range(3)], axis=1
     )
     own_units = ((0, None, 0, 0), (0, None, 0, 0), (2, 0, 16, 0), (2, 8, 17, 0))
     left_units = ((0, 0, 18, 2), (0, 10, 19, 2), (1, 0, 18, 2), (1, 10, 19, 2))
     right_units = ((0, 10, 18, 2), (0, 0, 19, 2), (1, 10, 18, 2), (1, 0, 19, 2))
-    far_units = ((0, 0, 8, 1), (1, 0, 8, 1), (2, 0, 8, 1), (3, 0, 8, 1))
-    far_sources = (far_low, far_high, far_low_other, far_high_other)
+    far_units = ((0, 0, 8, 1), (0, 10, 18, 1))
+    own_part = blocks(place, w_head, (inputs, grad_out, other), own_units)
+
+    far_low = send(left[:10], dx=1)
+    far_high = send(right[:10], dx=-1)
+    count = left.shape[0]
+    crossing = relay(
+        (left, right),
+        (left.shape, right.shape),
+        ((0, 0, 0, count, 0), (1, 1, 0, count, 0)),
+        (own_part[3],),
+    )
+    left_other, right_other = (send(value, dc=1) for value in crossing)
+    left_part = blocks(place, w_head, (left, left_other), left_units)
+    right_part = blocks(place, w_head, (right, right_other), right_units)
+    (far,) = relay(
+        (far_low, far_high),
+        ((20,) + left.shape[1:],),
+        ((0, 0, 0, 10, 0), (0, 1, 0, 10, 10)),
+        (own_part[3], left_part[3], right_part[3]),
+    )
+    far_other = send(far, dc=1)
     parts = [
-        blocks(place, w_head, (inputs, grad_out, other), own_units),
-        blocks(place, w_head, (left, left_other), left_units),
-        blocks(place, w_head, far_sources, far_units),
-        blocks(place, w_head, (right, right_other), right_units),
+        own_part,
+        left_part,
+        blocks(place, w_head, (far,), far_units),
+        blocks(place, w_head, (far_other,), far_units),
+        right_part,
     ]
     sent = totals(place, [part[3] for part in parts], [part[4] for part in parts])
     arrived = [send(sent[dy - 1], dy=dy) for dy in range(1, NY)]
-    grad_proj, *pieces = gradients(place, arrived, parts, scaling, user_count, dp_count)
-
-    folded = fold([pieces[0]] + [send(pieces[dy], dy=dy) for dy in range(1, NY)])
+    grad_proj, give, *pieces = gradients(place, arrived, parts, scaling, user_count, dp_count)
+
+    span = 2 * total_rows
+    theirs = send(give, dc=1)
+    returns = relay(
+        (grad_proj, theirs),
+        ((span, 3 * DH),) * (NX - 1),
+        tuple((dx - 1, 0, dx * span, dx * span + total_rows, 0) for dx in range(1, NX))
+        + tuple(
+            (dx - 1, 1, dx * total_rows, (dx + 1) * total_rows, total_rows)
+            for dx in range(1, NX)
+        ),
+    )
+    back = [send(returns[dx - 1], dx=-dx) for dx in range(1, NX)]
+    summands = [pieces[0]] + [send(pieces[dy], dy=dy) for dy in range(1, NY)]
+    folded = fold(summands, returns[0])
     planes = [
         [z * NY * GROUP + plane * GROUP + t for z in range(dp_count) for t in range(GROUP)]
         for plane in range(NY)
     ]
     got = lax.all_to_all(folded, ("dp", "seq"), 0, 0, axis_index_groups=planes)
 
-    span = 2 * total_rows
-    back = [grad_proj[:span].astype(F32)]
-    for dx in range(1, NX):
-        back.append(send(grad_proj[dx * span : (dx + 1) * span].astype(F32), dx=-dx))
-    swap = send(jnp.stack([piece[total_rows:] for piece in back]), dc=1)
-    grad_rows, done = input_gradient(place, back, swap, w_qkv)
+    grad_rows, done = input_gradient(place, (grad_proj, theirs, *back), total_rows, w_qkv)
     grad_inputs = grad_rows.reshape(user_count, row_count, feature_count)
 
-    device_count = dp_count * lax.axis_size("seq")
-    weights, squares = collect(got, done, device_count)
+    squares = square_sum(got, done, dp_count * lax.axis_size("seq"))
+    weights = assemble(got, squares)
     squares = lax.all_to_all(squares, ("dp", "seq"), 0, 0, tiled=True)
     return (grad_inputs, clip(weights, squares))
 

time: 138 us -> 127 us (0.920)
  blocking collectives: 20.1 us -> 0 us
  starting transfers between devices: 43.3 us -> 50.3 us
  Pallas kernels: 18.9 us -> 21.6 us
    all_to_all x1 -> x0, blocking collectives: 20.1 us -> none  [body(): squares = lax.all_to_all(squares, ('dp', 'seq'), 0, 0, tiled=True)]
    all_to_all x0 -> x1, waiting for transfers between devices: none -> 12.9 us  [body(): squares = lax.all_to_all(squares, ('dp', 'seq'), 0, 0, tiled=True)]
    ppermute x19 -> x18, waiting for transfers between devices: 38.7 us -> 26.7 us  [send(): return lax.ppermute(value, 'seq', seq_perm(dy, dx, dc))]
    all_to_all x0 -> x1, starting transfers between devices: none -> 7.7 us  [body(): squares = lax.all_to_all(squares, ('dp', 'seq'), 0, 0, tiled=True)]
    pallas_call x3 -> x7, Pallas kernels: 3.95 us -> 5.81 us  [the longest x1 3.14 us: gradients(): pl.pallas_call(functools.partial(grad_kernel, scaling, users, dp_count, c...]
    pallas_call x4 -> x5, Pallas kernels: 8.61 us -> 8.72 us  [blocks(): pl.pallas_call(functools.partial(block_kernel, units), out_shape=(struct(...]
    ppermute x19 -> x18, starting transfers between devices: 29.9 us -> 30 us  [send(): return lax.ppermute(value, 'seq', seq_perm(dy, dx, dc))]
  transfers between devices with their start and end apart: 20 -> 20, of which waited for: 8 -> 11; matrix products, arithmetic and copies ran while one was open for 2% -> 1% of each run, Pallas kernels for 8% -> 10%
where the time goes in v3:
time: 127 us
  starting transfers between devices  50.3 us (40%)
  waiting for transfers between devices  47.9 us (38%)
  Pallas kernels  21.6 us (17%)
  local copies, waits for them, and re-layouts  5.97 us (5%)
    ppermute x18, starting transfers between devices, send(): return lax.ppermute(value, 'seq', seq_perm(dy, dx, dc))  30 us
    ppermute x18, waiting for transfers between devices, send(): return lax.ppermute(value, 'seq', seq_perm(dy, dx, dc))  26.7 us
    all_to_all x1, waiting for transfers between devices, body(): squares = lax.all_to_all(squares, ('dp', 'seq'), 0, 0, tiled=True)  12.9 us
    all_to_all x1, starting transfers between devices, body(): got = lax.all_to_all(folded, ('dp', 'seq'), 0, 0, axis_index_groups=planes)  12.6 us
    pallas_call x5, Pallas kernels, blocks(): pl.pallas_call(functools.partial(block_kernel, units), out_shape=(struct(...  8.72 us
    all_to_all x1, waiting for transfers between devices, body(): got = lax.all_to_all(folded, ('dp', 'seq'), 0, 0, axis_index_groups=planes)  8.24 us
    all_to_all x1, starting transfers between devices, body(): squares = lax.all_to_all(squares, ('dp', 'seq'), 0, 0, tiled=True)  7.7 us
    unnamed x10, local copies, waits for them, and re-layouts  4.69 us
  transfers between devices with their start and end apart: 20, of which 11 were waited for; matrix products, arithmetic and copies ran while one was open for 1% of the time, Pallas kernels for 10%

profile of v3, /device:TPU:1, one launch (start us, length us, event | category | flops | bytes accessed | tf_op | source)
XLA Modules:
  0.0 126.8 jit_solution(15869794091544088285)
XLA Ops:
  0.7 0.1 pad_add_fusion.place
  0.7 0.0 copy-start
  0.7 0.9 copy-done
  1.7 0.9 copy-done.2
  2.6 1.7 %messages.1 = (f32[22,64,128]{2,1,0:T(8,128)}, f32[22,64,128]{2,1,0:T(8,128)S(1)}, f32[18,64,128]{2,1,0:T(8,128)}) custom-call(s32[3]{0:T(128)S(1)} %pad_add_fusion.place, bf16[2,64,1024]{2,1,0:T(8,128)(2,1)S(1)} %copy-done, bf16[2,64,1024]{2,1,0:T(8,128)(2,1)S(1)} %copy-done.2), custom_call_target="tpu_custom_call" | custom-call | flops 1048576 | bytes 3145728 | tf_op jit(solution)/shard_map/messages/pallas_call | solution.py:75
  4.4 2.0 %collective-permute-start.1 = (f32[22,64,128]{2,1,0:T(8,128)}, f32[22,64,128]{2,1,0:T(8,128)S(1)}, u32[]{:S(2)}, u32[]{:S(2)}) collective-permute-start(f32[22,64,128]{2,1,0:T(8,128)} %get-tuple-element.53), channel_id=1, source_target_pairs={{0,2},{1,3},{2,4},{3,5},{4,6},{5,7},{6,0},{7,1},{8,10},{9,11},{10,... | collective-permute-start | bytes 2162696 | tf_op jit(solution)/shard_map/ppermute | solution.py:37
  6.4 1.3 %collective-permute-start.2 = (f32[22,64,128]{2,1,0:T(8,128)S(1)}, f32[22,64,128]{2,1,0:T(8,128)S(1)}, u32[]{:S(2)}, u32[]{:S(2)}) collective-permute-start(f32[22,64,128]{2,1,0:T(8,128)S(1)} %get-tuple-element.54), channel_id=1, source_target_pairs={{0,6},{1,7},{2,0},{3,1},{4,2},{5,3},{6,4},{7,5},{8,14},{9,15},{10,... | collective-permute-start | bytes 2162696 | tf_op jit(solution)/shard_map/ppermute | solution.py:37
  7.7 3.2 %collective-permute-start = (f32[18,64,128]{2,1,0:T(8,128)}, f32[18,64,128]{2,1,0:T(8,128)S(1)}, u32[]{:S(2)}, u32[]{:S(2)}) collective-permute-start(f32[18,64,128]{2,1,0:T(8,128)} %get-tuple-element.51), channel_id=1, source_target_pairs={{0,1},{1,0},{2,3},{3,2},{4,5},{5,4},{6,7},{7,6},{8,9},{9,8},{10,11... | collective-permute-start | bytes 1769480 | tf_op jit(solution)/shard_map/ppermute | solution.py:37
  10.9 1.2 constant_dynamic-slice_fusion.2
  12.1 0.1 pad_maximum_fusion.w
  12.2 0.5 collective-permute-done.refs_2_
  12.7 0.0 copy-done.1
  12.7 0.0 copy-done.3
  12.7 2.0 %blocks.5 = (bf16[1024,256]{1,0:T(8,128)(2,1)S(1)}, bf16[256,384]{1,0:T(8,128)(2,1)S(1)}, bf16[256,128]{1,0:T(8,128)(2,1)S(1)}, f32[2,2,128,128]{3,2,1,0:T(8,128...) custom-call(s32[3]{0:T(128)S(1)} %pad_add_fusion.place, bf16[1024,384]{1,0:T(8,128)(2,1)S(1)} %pad_maximum_fusion.w, ...), custom_call_target="tpu_custom_call" | custom-call | flops 201326592 | bytes 4194304 | tf_op jit(solution)/shard_map/blocks/pallas_call | solution.py:147
  14.7 6.8 %collective-permute-done.1.refs_0_ = f32[22,64,128]{2,1,0:T(8,128)S(1)} collective-permute-done((f32[22,64,128]{2,1,0:T(8,128)}, f32[22,64,128]{2,1,0:T(8,128)S(1)}, u32[]{:S(2)}, u32[]{:S(2)}) %collective-permute-start.1) | collective-permute-done | bytes 720928 | tf_op jit(solution)/shard_map/ppermute | solution.py:37
  21.5 1.4 %collective-permute-done.2.refs_1_.refs_0_ = f32[22,64,128]{2,1,0:T(8,128)S(1)} collective-permute-done((f32[22,64,128]{2,1,0:T(8,128)S(1)}, f32[22,64,128]{2,1,0:T(8,128)S(1)}, u32[]{:S(2)}, u32[]{:S(2)}) %collective-permute-start.2) | collective-permute-done | bytes 720928 | tf_op jit(solution)/shard_map/ppermute | solution.py:37
  22.8 0.1 relay.3
  22.9 2.2 %collective-permute-start.3 = (f32[22,64,128]{2,1,0:T(8,128)S(1)}, f32[22,64,128]{2,1,0:T(8,128)S(1)}, u32[]{:S(2)}, u32[]{:S(2)}) collective-permute-start(f32[22,64,128]{2,1,0:T(8,128)S(1)} %get-tuple-element.55), channel_id=1, source_target_pairs={{0,1},{1,0},{2,3},{3,2},{4,5},{5,4},{6,7},{7,6},{8,9},{9,8},{10,11... | collective-permute-start | bytes 2162696 | tf_op jit(solution)/shard_map/ppermute | solution.py:37
  25.2 0.1 collective-permute-start.6
  25.3 1.3 %collective-permute-start.4 = (f32[10,64,128]{2,1,0:T(8,128)S(1)}, f32[10,64,128]{2,1,0:T(8,128)S(1)}, u32[]{:S(2)}, u32[]{:S(2)}) collective-permute-start(f32[10,64,128]{2,1,0:T(8,128)S(1)} %slice.8), channel_id=1, source_target_pairs={{0,2},{1,3},{2,4},{3,5},{4,6},{5,7},{6,0},{7,1},{8,10},{9,11},{10,... | collective-permute-start | bytes 983048 | tf_op jit(solution)/shard_map/ppermute | solution.py:37
  26.6 1.6 %collective-permute-start.5 = (f32[10,64,128]{2,1,0:T(8,128)S(1)}, f32[10,64,128]{2,1,0:T(8,128)S(1)}, u32[]{:S(2)}, u32[]{:S(2)}) collective-permute-start(f32[10,64,128]{2,1,0:T(8,128)S(1)} %slice.9), channel_id=1, source_target_pairs={{0,6},{1,7},{2,0},{3,1},{4,2},{5,3},{6,4},{7,5},{8,14},{9,15},{10,... | collective-permute-start | bytes 983048 | tf_op jit(solution)/shard_map/ppermute | solution.py:37
  28.2 0.0 collective-permute-done.3.refs_1_
  28.2 2.0 %blocks.6 = (bf16[1024,256]{1,0:T(8,128)(2,1)S(1)}, bf16[256,384]{1,0:T(8,128)(2,1)S(1)}, bf16[256,128]{1,0:T(8,128)(2,1)S(1)}, f32[2,2,128,128]{3,2,1,0:T(8,128...) custom-call(s32[3]{0:T(128)S(1)} %pad_add_fusion.place, bf16[1024,384]{1,0:T(8,128)(2,1)S(1)} %pad_maximum_fusion.w, ...), custom_call_target="tpu_custom_call" | custom-call | flops 201326592 | bytes 4194304 | tf_op jit(solution)/shard_map/blocks/pallas_call | solution.py:147
  30.1 0.0 collective-permute-done.6.refs_1_
  30.1 2.0 %blocks.7 = (bf16[1024,256]{1,0:T(8,128)(2,1)S(1)}, bf16[256,384]{1,0:T(8,128)(2,1)S(1)}, bf16[256,128]{1,0:T(8,128)(2,1)S(1)}, f32[2,2,128,128]{3,2,1,0:T(8,128...) custom-call(s32[3]{0:T(128)S(1)} %pad_add_fusion.place, bf16[1024,384]{1,0:T(8,128)(2,1)S(1)} %pad_maximum_fusion.w, ...), custom_call_target="tpu_custom_call" | custom-call | flops 201326592 | bytes 4194304 | tf_op jit(solution)/shard_map/blocks/pallas_call | solution.py:147
  32.1 3.4 %collective-permute-done.4.refs_0_ = f32[10,64,128]{2,1,0:T(8,128)S(1)} collective-permute-done((f32[10,64,128]{2,1,0:T(8,128)S(1)}, f32[10,64,128]{2,1,0:T(8,128)S(1)}, u32[]{:S(2)}, u32[]{:S(2)}) %collective-permute-start.4) | collective-permute-done | bytes 327712 | tf_op jit(solution)/shard_map/ppermute | solution.py:37
  35.5 0.0 collective-permute-done.5.refs_1_
  35.5 1.4 %collective-permute-start.7 = (f32[20,64,128]{2,1,0:T(8,128)S(1)}, f32[20,64,128]{2,1,0:T(8,128)S(1)}, u32[]{:S(2)}, u32[]{:S(2)}) collective-permute-start(f32[20,64,128]{2,1,0:T(8,128)S(1)} %relay.4.refs_0_), channel_id=1, source_target_pairs={{0,1},{1,0},{2,3},{3,2},{4,5},{5,4},{6,7},{7,6},{8,9},{9,8},{10,11... | collective-permute-start | bytes 1966088 | tf_op jit(solution)/shard_map/ppermute | solution.py:37
  36.9 1.4 %blocks.8 = (bf16[1024,128]{1,0:T(8,128)(2,1)S(1)}, bf16[128,384]{1,0:T(8,128)(2,1)S(1)}, bf16[128,128]{1,0:T(8,128)(2,1)S(1)}, f32[1,2,128,128]{3,2,1,0:T(8,128...) custom-call(s32[3]{0:T(128)S(1)} %pad_add_fusion.place, bf16[1024,384]{1,0:T(8,128)(2,1)S(1)} %pad_maximum_fusion.w, ...), custom_call_target="tpu_custom_call" | custom-call | flops 100663296 | bytes 4194304 | tf_op jit(solution)/shard_map/blocks/pallas_call | solution.py:147
  38.4 0.3 collective-permute-done.7.refs_0_
  38.7 1.4 %blocks.9 = (bf16[1024,128]{1,0:T(8,128)(2,1)S(1)}, bf16[128,384]{1,0:T(8,128)(2,1)S(1)}, bf16[128,128]{1,0:T(8,128)(2,1)S(1)}, f32[1,2,128,128]{3,2,1,0:T(8,128...) custom-call(s32[3]{0:T(128)S(1)} %pad_add_fusion.place, bf16[1024,384]{1,0:T(8,128)(2,1)S(1)} %pad_maximum_fusion.w, ...), custom_call_target="tpu_custom_call" | custom-call | flops 100663296 | bytes 4194304 | tf_op jit(solution)/shard_map/blocks/pallas_call | solution.py:147
  40.1 0.6 totals.1
  40.7 1.5 %collective-permute-start.8 = (f32[2,128,128]{2,1,0:T(8,128)S(1)}, f32[2,128,128]{2,1,0:T(8,128)S(1)}, u32[]{:S(2)}, u32[]{:S(2)}) collective-permute-start(f32[2,128,128]{2,1,0:T(8,128)S(1)} %get-tuple-element.66), channel_id=1, source_target_pairs={{0,8},{1,9},{2,10},{3,11},{4,12},{5,13},{6,14},{7,15},{8,16},{9,17... | collective-permute-start | bytes 393224 | tf_op jit(solution)/shard_map/ppermute | solution.py:37
  42.2 2.6 %collective-permute-start.9 = (f32[2,128,128]{2,1,0:T(8,128)S(1)}, f32[2,128,128]{2,1,0:T(8,128)S(1)}, u32[]{:S(2)}, u32[]{:S(2)}) collective-permute-start(f32[2,128,128]{2,1,0:T(8,128)S(1)} %get-tuple-element.67), channel_id=1, source_target_pairs={{0,16},{1,17},{2,18},{3,19},{4,20},{5,21},{6,22},{7,23},{8,24},{9,... | collective-permute-start | bytes 393224 | tf_op jit(solution)/shard_map/ppermute | solution.py:37
  44.8 1.1 collective-permute-start.10
  45.9 1.2 collective-permute-done.8.refs_0_
  47.1 3.8 %collective-permute-done.9.refs_1_ = f32[2,128,128]{2,1,0:T(8,128)S(1)} collective-permute-done((f32[2,128,128]{2,1,0:T(8,128)S(1)}, f32[2,128,128]{2,1,0:T(8,128)S(1)}, u32[]{:S(2)}, u32[]{:S(2)}) %collective-permute-start.9) | collective-permute-done | bytes 131104 | tf_op jit(solution)/shard_map/ppermute | solution.py:37
  50.9 0.0 collective-permute-done.10.refs_2_
  50.9 3.1 %gradients.1 = (bf16[1024,384]{1,0:T(8,128)(2,1)S(1)}, f32[512,384]{1,0:T(8,128)S(1)}, f32[8,32,384]{2,1,0:T(8,128)S(1)}, f32[8,32,384]{2,1,0:T(8,128)S(1)}, f32...) custom-call(s32[3]{0:T(128)S(1)} %pad_add_fusion.place, f32[2,128,128]{2,1,0:T(8,128)S(1)} %collective-permute-done.8.refs_0_, ...), custom_call_target="tpu_custom_call" | custom-call | flops 805306368 | bytes 10485760 | tf_op jit(solution)/shard_map/gradients/pallas_call | solution.py:269
  54.0 1.3 %collective-permute-start.11 = (f32[512,384]{1,0:T(8,128)S(1)}, f32[512,384]{1,0:T(8,128)S(1)}, u32[]{:S(2)}, u32[]{:S(2)}) collective-permute-start(f32[512,384]{1,0:T(8,128)S(1)} %get-tuple-element.90), channel_id=1, source_target_pairs={{0,1},{1,0},{2,3},{3,2},{4,5},{5,4},{6,7},{7,6},{8,9},{9,8},{10,11... | collective-permute-start | bytes 2359304 | tf_op jit(solution)/shard_map/ppermute | solution.py:37
  55.3 1.0 collective-permute-start.15
  56.3 2.1 %collective-permute-start.16 = (f32[8,32,384]{2,1,0:T(8,128)S(1)}, f32[8,32,384]{2,1,0:T(8,128)S(1)}, u32[]{:S(2)}, u32[]{:S(2)}) collective-permute-start(f32[8,32,384]{2,1,0:T(8,128)S(1)} %get-tuple-element.97), channel_id=1, source_target_pairs={{0,16},{1,17},{2,18},{3,19},{4,20},{5,21},{6,22},{7,23},{8,24},{9,... | collective-permute-start | bytes 1179656 | tf_op jit(solution)/shard_map/ppermute | solution.py:37
  58.4 1.3 %collective-permute-start.17 = (f32[8,32,384]{2,1,0:T(8,128)S(1)}, f32[8,32,384]{2,1,0:T(8,128)S(1)}, u32[]{:S(2)}, u32[]{:S(2)}) collective-permute-start(f32[8,32,384]{2,1,0:T(8,128)S(1)} %get-tuple-element.98), channel_id=1, source_target_pairs={{0,24},{1,25},{2,26},{3,27},{4,28},{5,29},{6,30},{7,31},{8,0},{9,1... | collective-permute-start | bytes 1179656 | tf_op jit(solution)/shard_map/ppermute | solution.py:37
  59.7 0.0 collective-permute-done.11.refs_1_
  59.7 0.8 relay.5
  60.5 2.5 %collective-permute-start.13 = (f32[256,384]{1,0:T(8,128)}, f32[256,384]{1,0:T(8,128)S(1)}, u32[]{:S(2)}, u32[]{:S(2)}) collective-permute-start(f32[256,384]{1,0:T(8,128)} %get-tuple-element.92), channel_id=1, source_target_pairs={{0,4},{1,5},{2,6},{3,7},{4,0},{5,1},{6,2},{7,3},{8,12},{9,13},{10,... | collective-permute-start | bytes 1179656 | tf_op jit(solution)/shard_map/ppermute | solution.py:37
  63.1 0.8 collective-permute-start.14
  63.9 3.3 %collective-permute-done.15.refs_1_ = f32[8,32,384]{2,1,0:T(8,128)S(1)} collective-permute-done((f32[8,32,384]{2,1,0:T(8,128)S(1)}, f32[8,32,384]{2,1,0:T(8,128)S(1)}, u32[]{:S(2)}, u32[]{:S(2)}) %collective-permute-start.15) | collective-permute-done | bytes 393248 | tf_op jit(solution)/shard_map/ppermute | solution.py:37
  67.2 2.8 %collective-permute-start.12 = (f32[256,384]{1,0:T(8,128)S(1)}, f32[256,384]{1,0:T(8,128)}, u32[]{:S(2)}, u32[]{:S(2)}) collective-permute-start(f32[256,384]{1,0:T(8,128)S(1)} %get-tuple-element.91.refs_4_), channel_id=1, source_target_pairs={{0,6},{1,7},{2,0},{3,1},{4,2},{5,3},{6,4},{7,5},{8,14},{9,15},{10,... | collective-permute-start | bytes 1179656 | tf_op jit(solution)/shard_map/ppermute | solution.py:37
  70.0 6.0 %collective-permute-done.16.refs_2_ = f32[8,32,384]{2,1,0:T(8,128)S(1)} collective-permute-done((f32[8,32,384]{2,1,0:T(8,128)S(1)}, f32[8,32,384]{2,1,0:T(8,128)S(1)}, u32[]{:S(2)}, u32[]{:S(2)}) %collective-permute-start.16) | collective-permute-done | bytes 393248 | tf_op jit(solution)/shard_map/ppermute | solution.py:37
  76.0 0.0 collective-permute-done.17.refs_3_
  76.0 0.8 fold.1
  76.9 12.6 %all-to-all-start = ((f32[64,4,384]{2,1,0:T(4,128)}), f32[64,4,384]{2,1,0:T(4,128)S(1)}, u32[]{:S(2)}, u32[]{:S(2)}) async-start(f32[64,4,384]{2,1,0:T(4,128)} %fold.1), calls=%async_computation | async-start | bytes 786432 | tf_op jit(solution)/shard_map/all_to_all | solution.py:482
  89.5 0.0 collective-permute-done.13.refs_3_
  89.5 0.0 collective-permute-done.14.refs_4_
  89.5 0.0 collective-permute-done.12.refs_2_
  89.5 0.0 copy-start.4
  89.5 2.8 %copy-done.4 = bf16[1024,3072]{1,0:T(8,128)(2,1)S(1)} copy-done((bf16[1024,3072]{1,0:T(8,128)(2,1)S(1)}, bf16[1024,3072]{1,0:T(8,128)(2,1)}, u32[]{:S(2)}) %copy-start.4) | copy-done | bytes 6291480
  92.3 4.0 %input_gradient.1 = (bf16[128,1024]{1,0:T(8,128)(2,1)}, f32[8,128]{1,0:T(8,128)S(1)}) custom-call(s32[3]{0:T(128)S(1)} %pad_add_fusion.place, bf16[1024,384]{1,0:T(8,128)(2,1)S(1)} %get-tuple-element.89.refs_0_, f32[512,384]{1,0:T(8,128)S(1)} %collective-permute-done.11.refs_1_, f32[256,384]{1,0:T(8,128)} %collective-permute-done.12.refs_2_, ...), custom_call_target="tpu_custom_call" | custom-call | flops 6442450944 | bytes 83886080 | tf_op jit(solution)/shard_map/input_gradient/pallas_call | solution.py:310
  96.3 8.2 %all-to-all-done.got = f32[64,4,384]{2,1,0:T(4,128)S(1)} async-done(((f32[64,4,384]{2,1,0:T(4,128)}), f32[64,4,384]{2,1,0:T(4,128)S(1)}, u32[]{:S(2)}, u32[]{:S(2)}) %all-to-all-start) | async-done | bytes 393248 | tf_op jit(solution)/shard_map/all_to_all | solution.py:482
  104.6 0.8 square_sum.1.after
  105.4 7.7 %all-to-all-start.1 = ((f32[256,1,128]{2,1,0:T(1,128)}), f32[256,1,128]{2,1,0:T(1,128)S(1)}, u32[]{:S(2)}, u32[]{:S(2)}) async-start(f32[256,1,128]{2,1,0:T(1,128)} %bitcast.5), calls=%async_computation.1 | async-start | bytes 262144 | tf_op jit(solution)/shard_map/all_to_all | solution.py:489
  113.1 12.9 %all-to-all-done.1 = f32[256,1,128]{2,1,0:T(1,128)S(1)} async-done(((f32[256,1,128]{2,1,0:T(1,128)}), f32[256,1,128]{2,1,0:T(1,128)S(1)}, u32[]{:S(2)}, u32[]{:S(2)}) %all-to-all-start.1) | async-done | bytes 131104 | tf_op jit(solution)/shard_map/all_to_all | solution.py:489
  126.1 0.7 clip.1
  (7 shorter events, 0.1 us)
Async XLA Ops:
  0.7 1.0 copy-start
  1.7 0.9 copy-start.2
  4.4 17.1 %collective-permute-start.1 = (f32[22,64,128]{2,1,0:T(8,128)}, f32[22,64,128]{2,1,0:T(8,128)S(1)}, u32[]{:S(2)}, u32[]{:S(2)}) collective-permute-start(f32[22,64,128]{2,1,0:T(8,128)} %get-tuple-element.53), channel_id=1, source_target_pairs={{0,2},{1,3},{2,4},{3,5},{4,6},{5,7},{6,0},{7,1},{8,10},{9,11},{10,... | collective-permute-start | bytes 2162696 | tf_op jit(solution)/shard_map/ppermute | solution.py:37
  6.4 16.4 %collective-permute-start.2 = (f32[22,64,128]{2,1,0:T(8,128)S(1)}, f32[22,64,128]{2,1,0:T(8,128)S(1)}, u32[]{:S(2)}, u32[]{:S(2)}) collective-permute-start(f32[22,64,128]{2,1,0:T(8,128)S(1)} %get-tuple-element.54), channel_id=1, source_target_pairs={{0,6},{1,7},{2,0},{3,1},{4,2},{5,3},{6,4},{7,5},{8,14},{9,15},{10,... | collective-permute-start | bytes 2162696 | tf_op jit(solution)/shard_map/ppermute | solution.py:37
  7.7 5.0 %collective-permute-start = (f32[18,64,128]{2,1,0:T(8,128)}, f32[18,64,128]{2,1,0:T(8,128)S(1)}, u32[]{:S(2)}, u32[]{:S(2)}) collective-permute-start(f32[18,64,128]{2,1,0:T(8,128)} %get-tuple-element.51), channel_id=1, source_target_pairs={{0,1},{1,0},{2,3},{3,2},{4,5},{5,4},{6,7},{7,6},{8,9},{9,8},{10,11... | collective-permute-start | bytes 1769480 | tf_op jit(solution)/shard_map/ppermute | solution.py:37
  10.9 1.8 %copy-start.1 = (bf16[2,64,1024]{2,1,0:T(8,128)(2,1)S(1)}, bf16[2,64,1024]{2,1,0:T(8,128)(2,1)}, u32[]{:S(2)}) copy-start(bf16[2,64,1024]{2,1,0:T(8,128)(2,1)} %refs_0_.1) | copy-start | bytes 786436
  10.9 1.8 %copy-start.3 = (bf16[2,64,1024]{2,1,0:T(8,128)(2,1)S(1)}, bf16[2,64,1024]{2,1,0:T(8,128)(2,1)}, u32[]{:S(2)}) copy-start(bf16[2,64,1024]{2,1,0:T(8,128)(2,1)} %refs_1_.1) | copy-start | bytes 786436
  22.9 5.2 %collective-permute-start.3 = (f32[22,64,128]{2,1,0:T(8,128)S(1)}, f32[22,64,128]{2,1,0:T(8,128)S(1)}, u32[]{:S(2)}, u32[]{:S(2)}) collective-permute-start(f32[22,64,128]{2,1,0:T(8,128)S(1)} %get-tuple-element.55), channel_id=1, source_target_pairs={{0,1},{1,0},{2,3},{3,2},{4,5},{5,4},{6,7},{7,6},{8,9},{9,8},{10,11... | collective-permute-start | bytes 2162696 | tf_op jit(solution)/shard_map/ppermute | solution.py:37
  25.2 5.0 %collective-permute-start.6 = (f32[22,64,128]{2,1,0:T(8,128)S(1)}, f32[22,64,128]{2,1,0:T(8,128)S(1)}, u32[]{:S(2)}, u32[]{:S(2)}) collective-permute-start(f32[22,64,128]{2,1,0:T(8,128)S(1)} %get-tuple-element.57), channel_id=1, source_target_pairs={{0,1},{1,0},{2,3},{3,2},{4,5},{5,4},{6,7},{7,6},{8,9},{9,8},{10,11... | collective-permute-start | bytes 2162696 | tf_op jit(solution)/shard_map/ppermute | solution.py:37
  25.3 10.2 %collective-permute-start.4 = (f32[10,64,128]{2,1,0:T(8,128)S(1)}, f32[10,64,128]{2,1,0:T(8,128)S(1)}, u32[]{:S(2)}, u32[]{:S(2)}) collective-permute-start(f32[10,64,128]{2,1,0:T(8,128)S(1)} %slice.8), channel_id=1, source_target_pairs={{0,2},{1,3},{2,4},{3,5},{4,6},{5,7},{6,0},{7,1},{8,10},{9,11},{10,... | collective-permute-start | bytes 983048 | tf_op jit(solution)/shard_map/ppermute | solution.py:37
  26.6 8.9 %collective-permute-start.5 = (f32[10,64,128]{2,1,0:T(8,128)S(1)}, f32[10,64,128]{2,1,0:T(8,128)S(1)}, u32[]{:S(2)}, u32[]{:S(2)}) collective-permute-start(f32[10,64,128]{2,1,0:T(8,128)S(1)} %slice.9), channel_id=1, source_target_pairs={{0,6},{1,7},{2,0},{3,1},{4,2},{5,3},{6,4},{7,5},{8,14},{9,15},{10,... | collective-permute-start | bytes 983048 | tf_op jit(solution)/shard_map/ppermute | solution.py:37
  35.5 3.1 %collective-permute-start.7 = (f32[20,64,128]{2,1,0:T(8,128)S(1)}, f32[20,64,128]{2,1,0:T(8,128)S(1)}, u32[]{:S(2)}, u32[]{:S(2)}) collective-permute-start(f32[20,64,128]{2,1,0:T(8,128)S(1)} %relay.4.refs_0_), channel_id=1, source_target_pairs={{0,1},{1,0},{2,3},{3,2},{4,5},{5,4},{6,7},{7,6},{8,9},{9,8},{10,11... | collective-permute-start | bytes 1966088 | tf_op jit(solution)/shard_map/ppermute | solution.py:37
  40.7 6.4 %collective-permute-start.8 = (f32[2,128,128]{2,1,0:T(8,128)S(1)}, f32[2,128,128]{2,1,0:T(8,128)S(1)}, u32[]{:S(2)}, u32[]{:S(2)}) collective-permute-start(f32[2,128,128]{2,1,0:T(8,128)S(1)} %get-tuple-element.66), channel_id=1, source_target_pairs={{0,8},{1,9},{2,10},{3,11},{4,12},{5,13},{6,14},{7,15},{8,16},{9,17... | collective-permute-start | bytes 393224 | tf_op jit(solution)/shard_map/ppermute | solution.py:37
  42.2 8.7 %collective-permute-start.9 = (f32[2,128,128]{2,1,0:T(8,128)S(1)}, f32[2,128,128]{2,1,0:T(8,128)S(1)}, u32[]{:S(2)}, u32[]{:S(2)}) collective-permute-start(f32[2,128,128]{2,1,0:T(8,128)S(1)} %get-tuple-element.67), channel_id=1, source_target_pairs={{0,16},{1,17},{2,18},{3,19},{4,20},{5,21},{6,22},{7,23},{8,24},{9,... | collective-permute-start | bytes 393224 | tf_op jit(solution)/shard_map/ppermute | solution.py:37
  44.8 6.1 %collective-permute-start.10 = (f32[2,128,128]{2,1,0:T(8,128)S(1)}, f32[2,128,128]{2,1,0:T(8,128)S(1)}, u32[]{:S(2)}, u32[]{:S(2)}) collective-permute-start(f32[2,128,128]{2,1,0:T(8,128)S(1)} %get-tuple-element.68), channel_id=1, source_target_pairs={{0,24},{1,25},{2,26},{3,27},{4,28},{5,29},{6,30},{7,31},{8,0},{9,1... | collective-permute-start | bytes 393224 | tf_op jit(solution)/shard_map/ppermute | solution.py:37
  54.0 5.7 %collective-permute-start.11 = (f32[512,384]{1,0:T(8,128)S(1)}, f32[512,384]{1,0:T(8,128)S(1)}, u32[]{:S(2)}, u32[]{:S(2)}) collective-permute-start(f32[512,384]{1,0:T(8,128)S(1)} %get-tuple-element.90), channel_id=1, source_target_pairs={{0,1},{1,0},{2,3},{3,2},{4,5},{5,4},{6,7},{7,6},{8,9},{9,8},{10,11... | collective-permute-start | bytes 2359304 | tf_op jit(solution)/shard_map/ppermute | solution.py:37
  55.3 11.9 %collective-permute-start.15 = (f32[8,32,384]{2,1,0:T(8,128)S(1)}, f32[8,32,384]{2,1,0:T(8,128)S(1)}, u32[]{:S(2)}, u32[]{:S(2)}) collective-permute-start(f32[8,32,384]{2,1,0:T(8,128)S(1)} %get-tuple-element.96), channel_id=1, source_target_pairs={{0,8},{1,9},{2,10},{3,11},{4,12},{5,13},{6,14},{7,15},{8,16},{9,17... | collective-permute-start | bytes 1179656 | tf_op jit(solution)/shard_map/ppermute | solution.py:37
  56.3 19.7 %collective-permute-start.16 = (f32[8,32,384]{2,1,0:T(8,128)S(1)}, f32[8,32,384]{2,1,0:T(8,128)S(1)}, u32[]{:S(2)}, u32[]{:S(2)}) collective-permute-start(f32[8,32,384]{2,1,0:T(8,128)S(1)} %get-tuple-element.97), channel_id=1, source_target_pairs={{0,16},{1,17},{2,18},{3,19},{4,20},{5,21},{6,22},{7,23},{8,24},{9,... | collective-permute-start | bytes 1179656 | tf_op jit(solution)/shard_map/ppermute | solution.py:37
  58.4 17.6 %collective-permute-start.17 = (f32[8,32,384]{2,1,0:T(8,128)S(1)}, f32[8,32,384]{2,1,0:T(8,128)S(1)}, u32[]{:S(2)}, u32[]{:S(2)}) collective-permute-start(f32[8,32,384]{2,1,0:T(8,128)S(1)} %get-tuple-element.98), channel_id=1, source_target_pairs={{0,24},{1,25},{2,26},{3,27},{4,28},{5,29},{6,30},{7,31},{8,0},{9,1... | collective-permute-start | bytes 1179656 | tf_op jit(solution)/shard_map/ppermute | solution.py:37
  60.5 28.9 %collective-permute-start.13 = (f32[256,384]{1,0:T(8,128)}, f32[256,384]{1,0:T(8,128)S(1)}, u32[]{:S(2)}, u32[]{:S(2)}) collective-permute-start(f32[256,384]{1,0:T(8,128)} %get-tuple-element.92), channel_id=1, source_target_pairs={{0,4},{1,5},{2,6},{3,7},{4,0},{5,1},{6,2},{7,3},{8,12},{9,13},{10,... | collective-permute-start | bytes 1179656 | tf_op jit(solution)/shard_map/ppermute | solution.py:37
  63.1 26.4 %collective-permute-start.14 = (f32[256,384]{1,0:T(8,128)S(1)}, f32[256,384]{1,0:T(8,128)S(1)}, u32[]{:S(2)}, u32[]{:S(2)}) collective-permute-start(f32[256,384]{1,0:T(8,128)S(1)} %get-tuple-element.93), channel_id=1, source_target_pairs={{0,2},{1,3},{2,4},{3,5},{4,6},{5,7},{6,0},{7,1},{8,10},{9,11},{10,... | collective-permute-start | bytes 1179656 | tf_op jit(solution)/shard_map/ppermute | solution.py:37
  67.2 22.3 %collective-permute-start.12 = (f32[256,384]{1,0:T(8,128)S(1)}, f32[256,384]{1,0:T(8,128)}, u32[]{:S(2)}, u32[]{:S(2)}) collective-permute-start(f32[256,384]{1,0:T(8,128)S(1)} %get-tuple-element.91.refs_4_), channel_id=1, source_target_pairs={{0,6},{1,7},{2,0},{3,1},{4,2},{5,3},{6,4},{7,5},{8,14},{9,15},{10,... | collective-permute-start | bytes 1179656 | tf_op jit(solution)/shard_map/ppermute | solution.py:37
  76.9 27.7 %all-to-all-start = ((f32[64,4,384]{2,1,0:T(4,128)}), f32[64,4,384]{2,1,0:T(4,128)S(1)}, u32[]{:S(2)}, u32[]{:S(2)}) async-start(f32[64,4,384]{2,1,0:T(4,128)} %fold.1), calls=%async_computation | async-start | bytes 786432 | tf_op jit(solution)/shard_map/all_to_all | solution.py:482
  89.5 2.8 %copy-start.4 = (bf16[1024,3072]{1,0:T(8,128)(2,1)S(1)}, bf16[1024,3072]{1,0:T(8,128)(2,1)}, u32[]{:S(2)}) copy-start(bf16[1024,3072]{1,0:T(8,128)(2,1)} %refs_5_.1) | copy-start | bytes 18874372
  105.4 20.7 %all-to-all-start.1 = ((f32[256,1,128]{2,1,0:T(1,128)}), f32[256,1,128]{2,1,0:T(1,128)S(1)}, u32[]{:S(2)}, u32[]{:S(2)}) async-start(f32[256,1,128]{2,1,0:T(1,128)} %bitcast.5), calls=%async_computation.1 | async-start | bytes 262144 | tf_op jit(solution)/shard_map/all_to_all | solution.py:489

commit v4 on v3

--- a/solution.py
+++ b/solution.py
@@ -14,6 +14,7 @@
 NY = 4
 NX = 4
 GROUP = 2 * NX
+FAR_FIRST = (2, 1, 3)
 BF16 = jnp.bfloat16
 F32 = jnp.float32
 VMEM = pl.BlockSpec(memory_space=pltpu.VMEM)
@@ -170,8 +171,8 @@
     keys, queries, outs = refs[:count], refs[count : 2 * count], refs[2 * count :]
     key_total = sum(ref[i] for ref in keys for i in range(ref.shape[0]))
     query_total = sum(ref[i] for ref in queries for i in range(ref.shape[0]))
-    for dy in range(1, NY):
-        outs[dy - 1][...] = jnp.where(place[0] + dy < NY, key_total, query_total)
+    for out, dy in zip(outs, FAR_FIRST):
+        out[...] = jnp.where(place[0] + dy < NY, key_total, query_total)
 
 
 def totals(place, key_states, query_states):
@@ -206,8 +207,8 @@
         first = last
     prior = jnp.zeros(arrived[0].shape, F32)
     later = jnp.zeros(arrived[0].shape, F32)
-    for dy in range(1, NY):
-        value = arrived[dy - 1][...]
+    for ref, dy in zip(arrived, FAR_FIRST):
+        value = ref[...]
         prior = prior + jnp.where(y >= dy, value, 0.0)
         later = later + jnp.where(y >= dy, 0.0, value)
 
@@ -253,11 +254,11 @@
         first = last
     product[...] = value
     row_block = product.shape[0] // (dp_count * NY)
-    for dy in range(NY):
+    for piece, dy in zip(pieces, (0,) + FAR_FIRST):
         target = (y + dy) % NY
         for z in range(dp_count):
             start = pl.multiple_of((z * NY + target) * row_block, row_block)
-            pieces[dy][z] = product[pl.ds(start, row_block), :]
+            piece[z] = product[pl.ds(start, row_block), :]
 
 
 def gradients(place, arrived, parts, scaling, users, dp_count):
@@ -292,28 +293,39 @@
     own, theirs, back = refs[0], refs[1], refs[2 : 1 + NX]
     w, out, done, full = refs[1 + NX :]
     total = out.shape[0]
-    for dx in range(NX):
-        for dc in range(2):
-            head = ((x + dx) % NX) * 2 + (c ^ dc)
-            source = (theirs if dc else own) if dx == 0 else back[dx - 1]
-            first = total if dx and dc else 0
-            for part in range(3):
-                columns = slice(part * DH, (part + 1) * DH)
-                start = pl.multiple_of((part * H + head) * DH, DH)
-                full[:, pl.ds(start, DH)] = source[first : first + total, columns].astype(BF16)
+
+    @pl.when(pl.program_id(0) == 0)
+    def _():
+        for dx in range(NX):
+            for dc in range(2):
+                head = ((x + dx) % NX) * 2 + (c ^ dc)
+                source = (theirs if dc else own) if dx == 0 else back[dx - 1]
+                first = total if dx and dc else 0
+                for part in range(3):
+                    columns = slice(part * DH, (part + 1) * DH)
+                    start = pl.multiple_of((part * H + head) * DH, DH)
+                    full[:, pl.ds(start, DH)] = source[first : first + total, columns].astype(BF16)
+        done[...] = jnp.zeros(done.shape, F32)
+
     out[...] = dot(full[...], w[...], 1, 1).astype(BF16)
-    done[...] = jnp.zeros(done.shape, F32)
 
 
 def input_gradient(place, sources, total, w_qkv):
     features, width = w_qkv.shape
+    step = 256
     return pl.pallas_call(
         input_kernel,
+        grid=(features // step,),
         out_shape=(struct((total, features), BF16), struct((8, DH), F32)),
-        in_specs=[SMEM] + [VMEM] * (len(sources) + 1),
-        out_specs=(VMEM, VMEM),
+        in_specs=[SMEM]
+        + [VMEM] * len(sources)
+        + [pl.BlockSpec((step, width), lambda i: (i, 0))],
+        out_specs=(
+            pl.BlockSpec((total, step), lambda i: (0, i)),
+            pl.BlockSpec((8, DH), lambda i: (0, 0)),
+        ),
         scratch_shapes=[pltpu.VMEM((total, width), BF16)],
-        compiler_params=pltpu.CompilerParams(vmem_limit_bytes=24 * MIB),
+        compiler_params=pltpu.CompilerParams(vmem_limit_bytes=48 * MIB),
         cost_estimate=pl.CostEstimate(
             flops=16 * total * features * width, bytes_accessed=80 * MIB, transcendentals=0
         ),
@@ -324,18 +336,19 @@
 def fold_kernel(count, *refs):
     out = refs[-1]
     dp_count, row_block = refs[0].shape[0], refs[0].shape[1]
-    rows = out.shape[1]
+    rows = row_block // GROUP
     for z in range(dp_count):
         value = sum(ref[z] for ref in refs[:count])
         for t in range(GROUP):
-            out[z * GROUP + t] = value[t * rows : (t + 1) * rows, :]
+            to = (t // 2) * rows
+            out[2 * z + t % 2, to : to + rows, :] = value[t * rows : (t + 1) * rows, :]
 
 
 def fold(parts, after):
     dp_count, row_block, width = parts[0].shape
     return pl.pallas_call(
         functools.partial(fold_kernel, len(parts)),
-        out_shape=struct((dp_count * GROUP, row_block // GROUP, width), F32),
+        out_shape=struct((dp_count * 2, row_block // 2, width), F32),
         in_specs=[VMEM] * len(parts) + [ANY],
         out_specs=VMEM,
         compiler_params=pltpu.CompilerParams(vmem_limit_bytes=8 * MIB),
@@ -344,67 +357,60 @@
     )(*parts, after)
 
 
-def square_kernel(got, after, squares):
-    count = got.shape[0] // H
+def square_kernel(place, got, after, squares, *refs):
+    x, pieces, rows_of = place[1], refs[:NX], refs[NX]
+    count, rows = got.shape[0] // 2, got.shape[1] // NX
     lanes = jnp.zeros((1, got.shape[2]), F32)
-    for head in range(H):
-        value = sum(got[z * H + head] for z in range(count))
+    for core in range(2):
+        value = sum(got[2 * z + core] for z in range(count))
         lanes = lanes + jnp.sum(value * value, axis=0, keepdims=True)
+        for to in range(NX):
+            rows_of[to, core * rows : (core + 1) * rows, :] = value[to * rows : (to + 1) * rows, :]
     squares[...] = jnp.full(squares.shape, jnp.sum(lanes))
-
-
-def square_sum(got, after, device_count):
+    for dx in range(NX):
+        pieces[dx][...] = rows_of[(x + dx) % NX]
+
+
+def square_sum(place, got, after, device_count):
+    rows, width = 2 * got.shape[1] // NX, got.shape[2]
     return pl.pallas_call(
         square_kernel,
-        out_shape=struct((device_count, DH), F32),
-        in_specs=[VMEM, ANY],
-        out_specs=VMEM,
+        out_shape=(struct((device_count, DH), F32),) + (struct((rows, width), F32),) * NX,
+        in_specs=[SMEM, VMEM, ANY],
+        out_specs=(VMEM,) * (1 + NX),
+        scratch_shapes=[pltpu.VMEM((NX, rows, width), F32)],
         compiler_params=pltpu.CompilerParams(vmem_limit_bytes=8 * MIB),
         cost_estimate=pl.CostEstimate(flops=MIB, bytes_accessed=MIB, transcendentals=0),
         name="square_sum",
-    )(got, after)
-
-
-def assemble_kernel(got, after, weights):
-    count = got.shape[0] // H
-    for head in range(H):
-        value = sum(got[z * H + head] for z in range(count))
-        for part in range(3):
-            start = (part * H + head) * DH
-            weights[:, start : start + DH] = value[:, part * DH : (part + 1) * DH]
-
-
-def assemble(got, after):
-    rows, width = got.shape[1], got.shape[2]
-    return pl.pallas_call(
-        assemble_kernel,
-        out_shape=struct((rows, H * width), F32),
-        in_specs=[VMEM, ANY],
-        out_specs=VMEM,
-        compiler_params=pltpu.CompilerParams(vmem_limit_bytes=8 * MIB),
-        cost_estimate=pl.CostEstimate(flops=MIB, bytes_accessed=MIB, transcendentals=0),
-        name="assemble",
-    )(got, after)
-
-
-def clip_kernel(weights, squares, out):
+    )(place, got, after)
+
+
+def clip_kernel(place, squares, *refs):
+    x, pieces, out = place[1], refs[:NX], refs[NX]
+    rows = out.shape[0]
     total_sq = jnp.sum(squares[...], axis=0, keepdims=True)
     factor = jnp.minimum(1.0, D / jnp.sqrt(total_sq + 1e-06))
-    for j in range(out.shape[1] // DH):
-        columns = slice(j * DH, (j + 1) * DH)
-        out[:, columns] = weights[:, columns] * factor
-
-
-def clip(weights, squares):
+    for dx in range(NX):
+        for core in range(2):
+            head = ((x + NX - dx) % NX) * 2 + core
+            for part in range(3):
+                columns = slice(part * DH, (part + 1) * DH)
+                start = pl.multiple_of((part * H + head) * DH, DH)
+                value = pieces[dx][core * rows : (core + 1) * rows, columns]
+                out[:, pl.ds(start, DH)] = value * factor
+
+
+def clip(place, squares, pieces):
+    rows, width = pieces[0].shape[0] // 2, pieces[0].shape[1] * H
     return pl.pallas_call(
         clip_kernel,
-        out_shape=struct(weights.shape, F32),
-        in_specs=[VMEM, VMEM],
+        out_shape=struct((rows, width), F32),
+        in_specs=[SMEM] + [VMEM] * (1 + NX),
         out_specs=VMEM,
         compiler_params=pltpu.CompilerParams(vmem_limit_bytes=8 * MIB),
         cost_estimate=pl.CostEstimate(flops=MIB, bytes_accessed=MIB, transcendentals=0),
         name="clip",
-    )(weights, squares)
+    )(place, squares, *pieces)
 
 
 def body(inputs, grad_out, w_qkv):
@@ -458,7 +464,7 @@
         right_part,
     ]
     sent = totals(place, [part[3] for part in parts], [part[4] for part in parts])
-    arrived = [send(sent[dy - 1], dy=dy) for dy in range(1, NY)]
+    arrived = [send(value, dy=dy) for value, dy in zip(sent, FAR_FIRST)]
     grad_proj, give, *pieces = gradients(place, arrived, parts, scaling, user_count, dp_count)
 
     span = 2 * total_rows
@@ -473,21 +479,21 @@
         ),
     )
     back = [send(returns[dx - 1], dx=-dx) for dx in range(1, NX)]
-    summands = [pieces[0]] + [send(pieces[dy], dy=dy) for dy in range(1, NY)]
+    summands = pieces[:1] + [send(value, dy=dy) for value, dy in zip(pieces[1:], FAR_FIRST)]
     folded = fold(summands, returns[0])
-    planes = [
-        [z * NY * GROUP + plane * GROUP + t for z in range(dp_count) for t in range(GROUP)]
-        for plane in range(NY)
+    columns_of = [
+        [z * NY * GROUP + place_of + core for z in range(dp_count) for core in range(2)]
+        for place_of in range(0, NY * GROUP, 2)
     ]
-    got = lax.all_to_all(folded, ("dp", "seq"), 0, 0, axis_index_groups=planes)
-
+    got = lax.all_to_all(folded, ("dp", "seq"), 0, 0, axis_index_groups=columns_of)
     grad_rows, done = input_gradient(place, (grad_proj, theirs, *back), total_rows, w_qkv)
     grad_inputs = grad_rows.reshape(user_count, row_count, feature_count)
 
-    squares = square_sum(got, done, dp_count * lax.axis_size("seq"))
-    weights = assemble(got, squares)
+    device_count = dp_count * lax.axis_size("seq")
+    squares, *parts = square_sum(place, got, done, device_count)
     squares = lax.all_to_all(squares, ("dp", "seq"), 0, 0, tiled=True)
-    return (grad_inputs, clip(weights, squares))
+    parts = parts[:1] + [send(parts[dx], dx=dx) for dx in range(1, NX)]
+    return (grad_inputs, clip(place, squares, parts))
 
 
 def solution(mesh):

time: 127 us -> 124 us (0.976)
  waiting for transfers between devices: 47.9 us -> 42.3 us
  Pallas kernels: 21.6 us -> 24.6 us
  local copies, waits for them, and re-layouts: 5.97 us -> 3.19 us
  starting transfers between devices: 50.3 us -> 53 us
    all_to_all x1, waiting for transfers between devices: 12.9 us -> 6.2 us  [body(): squares = lax.all_to_all(squares, ('dp', 'seq'), 0, 0, tiled=True)]
    ppermute x18 -> x21, starting transfers between devices: 30 us -> 35.8 us  [send(): return lax.ppermute(value, 'seq', seq_perm(dy, dx, dc))]
    all_to_all x1, starting transfers between devices: 12.6 us -> 9.25 us  [body(): lax.all_to_all(folded, ('dp', 'seq'), 0, 0, axis_index_groups=columns_of)]
    pallas_call x4 -> x3, Pallas kernels: 5.54 us -> 8.46 us  [the longest x1 5.89 us: input_gradient(): pl.pallas_call(input_kernel, grid=(features // step,), out_shape=(struct(...]
    unnamed x10 -> x8, local copies, waits for them, and re-layouts: 4.69 us -> 1.91 us
    ppermute x18 -> x21, waiting for transfers between devices: 26.7 us -> 27.4 us  [send(): return lax.ppermute(value, 'seq', seq_perm(dy, dx, dc))]
  transfers between devices with their start and end apart: 20 -> 23, of which waited for: 11 -> 13; matrix products, arithmetic and copies ran while one was open for 1% -> 1% of each run, Pallas kernels for 10% -> 12%
where the time goes in v4:
time: 124 us
  starting transfers between devices  53 us (43%)
  waiting for transfers between devices  42.3 us (34%)
  Pallas kernels  24.6 us (20%)
  local copies, waits for them, and re-layouts  3.19 us (3%)
    ppermute x21, starting transfers between devices, send(): return lax.ppermute(value, 'seq', seq_perm(dy, dx, dc))  35.8 us
    ppermute x21, waiting for transfers between devices, send(): return lax.ppermute(value, 'seq', seq_perm(dy, dx, dc))  27.4 us
    all_to_all x1, starting transfers between devices, body(): lax.all_to_all(folded, ('dp', 'seq'), 0, 0, axis_index_groups=columns_of)  9.25 us
    pallas_call x5, Pallas kernels, blocks(): pl.pallas_call(functools.partial(block_kernel, units), out_shape=(struct(...  8.77 us
    all_to_all x1, waiting for transfers between devices, body(): lax.all_to_all(folded, ('dp', 'seq'), 0, 0, axis_index_groups=columns_of)  8.63 us
    all_to_all x1, starting transfers between devices, body(): squares = lax.all_to_all(squares, ('dp', 'seq'), 0, 0, tiled=True)  8.01 us
    all_to_all x1, waiting for transfers between devices, body(): squares = lax.all_to_all(squares, ('dp', 'seq'), 0, 0, tiled=True)  6.2 us
    pallas_call x1, Pallas kernels, input_gradient(): pl.pallas_call(input_kernel, grid=(features // step,), out_shape=(struct(...  5.89 us
  transfers between devices with their start and end apart: 23, of which 13 were waited for; matrix products, arithmetic and copies ran while one was open for 1% of the time, Pallas kernels for 12%

profile of v4, /device:TPU:1, one launch (start us, length us, event | category | flops | bytes accessed | tf_op | source)
XLA Modules:
  0.0 124.0 jit_solution(12270457344401808960)
XLA Ops:
  0.7 0.1 pad_add_fusion.place
  0.7 0.9 copy-done
  1.7 0.9 copy-done.2
  2.6 1.8 %messages.1 = (f32[22,64,128]{2,1,0:T(8,128)}, f32[22,64,128]{2,1,0:T(8,128)S(1)}, f32[18,64,128]{2,1,0:T(8,128)}) custom-call(s32[3]{0:T(128)S(1)} %pad_add_fusion.place, bf16[2,64,1024]{2,1,0:T(8,128)(2,1)S(1)} %copy-done, bf16[2,64,1024]{2,1,0:T(8,128)(2,1)S(1)} %copy-done.2), custom_call_target="tpu_custom_call" | custom-call | flops 1048576 | bytes 3145728 | tf_op jit(solution)/shard_map/messages/pallas_call | solution.py:76
  4.4 2.0 %collective-permute-start.1 = (f32[22,64,128]{2,1,0:T(8,128)}, f32[22,64,128]{2,1,0:T(8,128)S(1)}, u32[]{:S(2)}, u32[]{:S(2)}) collective-permute-start(f32[22,64,128]{2,1,0:T(8,128)} %get-tuple-element.58), channel_id=1, source_target_pairs={{0,2},{1,3},{2,4},{3,5},{4,6},{5,7},{6,0},{7,1},{8,10},{9,11},{10,... | collective-permute-start | bytes 2162696 | tf_op jit(solution)/shard_map/ppermute | solution.py:38
  6.4 1.3 %collective-permute-start.2 = (f32[22,64,128]{2,1,0:T(8,128)S(1)}, f32[22,64,128]{2,1,0:T(8,128)S(1)}, u32[]{:S(2)}, u32[]{:S(2)}) collective-permute-start(f32[22,64,128]{2,1,0:T(8,128)S(1)} %get-tuple-element.59), channel_id=1, source_target_pairs={{0,6},{1,7},{2,0},{3,1},{4,2},{5,3},{6,4},{7,5},{8,14},{9,15},{10,... | collective-permute-start | bytes 2162696 | tf_op jit(solution)/shard_map/ppermute | solution.py:38
  7.7 3.2 %collective-permute-start = (f32[18,64,128]{2,1,0:T(8,128)}, f32[18,64,128]{2,1,0:T(8,128)S(1)}, u32[]{:S(2)}, u32[]{:S(2)}) collective-permute-start(f32[18,64,128]{2,1,0:T(8,128)} %get-tuple-element.56), channel_id=1, source_target_pairs={{0,1},{1,0},{2,3},{3,2},{4,5},{5,4},{6,7},{7,6},{8,9},{9,8},{10,11... | collective-permute-start | bytes 1769480 | tf_op jit(solution)/shard_map/ppermute | solution.py:38
  10.9 1.2 constant_dynamic-slice_fusion.2
  12.1 0.1 pad_maximum_fusion.w
  12.2 0.5 collective-permute-done.refs_2_
  12.7 2.0 %blocks.5 = (bf16[1024,256]{1,0:T(8,128)(2,1)S(1)}, bf16[256,384]{1,0:T(8,128)(2,1)S(1)}, bf16[256,128]{1,0:T(8,128)(2,1)S(1)}, f32[2,2,128,128]{3,2,1,0:T(8,128...) custom-call(s32[3]{0:T(128)S(1)} %pad_add_fusion.place, bf16[1024,384]{1,0:T(8,128)(2,1)S(1)} %pad_maximum_fusion.w, ...), custom_call_target="tpu_custom_call" | custom-call | flops 201326592 | bytes 4194304 | tf_op jit(solution)/shard_map/blocks/pallas_call | solution.py:148
  14.7 6.8 %collective-permute-done.1.refs_0_ = f32[22,64,128]{2,1,0:T(8,128)S(1)} collective-permute-done((f32[22,64,128]{2,1,0:T(8,128)}, f32[22,64,128]{2,1,0:T(8,128)S(1)}, u32[]{:S(2)}, u32[]{:S(2)}) %collective-permute-start.1) | collective-permute-done | bytes 720928 | tf_op jit(solution)/shard_map/ppermute | solution.py:38
  21.5 1.4 %collective-permute-done.2.refs_1_.refs_0_ = f32[22,64,128]{2,1,0:T(8,128)S(1)} collective-permute-done((f32[22,64,128]{2,1,0:T(8,128)S(1)}, f32[22,64,128]{2,1,0:T(8,128)S(1)}, u32[]{:S(2)}, u32[]{:S(2)}) %collective-permute-start.2) | collective-permute-done | bytes 720928 | tf_op jit(solution)/shard_map/ppermute | solution.py:38
  22.9 0.1 relay.3
  23.0 2.2 %collective-permute-start.3 = (f32[22,64,128]{2,1,0:T(8,128)S(1)}, f32[22,64,128]{2,1,0:T(8,128)S(1)}, u32[]{:S(2)}, u32[]{:S(2)}) collective-permute-start(f32[22,64,128]{2,1,0:T(8,128)S(1)} %get-tuple-element.60), channel_id=1, source_target_pairs={{0,1},{1,0},{2,3},{3,2},{4,5},{5,4},{6,7},{7,6},{8,9},{9,8},{10,11... | collective-permute-start | bytes 2162696 | tf_op jit(solution)/shard_map/ppermute | solution.py:38
  25.2 0.1 collective-permute-start.6
  25.3 1.3 %collective-permute-start.4 = (f32[10,64,128]{2,1,0:T(8,128)S(1)}, f32[10,64,128]{2,1,0:T(8,128)S(1)}, u32[]{:S(2)}, u32[]{:S(2)}) collective-permute-start(f32[10,64,128]{2,1,0:T(8,128)S(1)} %slice.8), channel_id=1, source_target_pairs={{0,2},{1,3},{2,4},{3,5},{4,6},{5,7},{6,0},{7,1},{8,10},{9,11},{10,... | collective-permute-start | bytes 983048 | tf_op jit(solution)/shard_map/ppermute | solution.py:38
  26.6 1.6 %collective-permute-start.5 = (f32[10,64,128]{2,1,0:T(8,128)S(1)}, f32[10,64,128]{2,1,0:T(8,128)S(1)}, u32[]{:S(2)}, u32[]{:S(2)}) collective-permute-start(f32[10,64,128]{2,1,0:T(8,128)S(1)} %slice.9), channel_id=1, source_target_pairs={{0,6},{1,7},{2,0},{3,1},{4,2},{5,3},{6,4},{7,5},{8,14},{9,15},{10,... | collective-permute-start | bytes 983048 | tf_op jit(solution)/shard_map/ppermute | solution.py:38
  28.2 0.0 collective-permute-done.3.refs_1_
  28.2 2.0 %blocks.6 = (bf16[1024,256]{1,0:T(8,128)(2,1)S(1)}, bf16[256,384]{1,0:T(8,128)(2,1)S(1)}, bf16[256,128]{1,0:T(8,128)(2,1)S(1)}, f32[2,2,128,128]{3,2,1,0:T(8,128...) custom-call(s32[3]{0:T(128)S(1)} %pad_add_fusion.place, bf16[1024,384]{1,0:T(8,128)(2,1)S(1)} %pad_maximum_fusion.w, ...), custom_call_target="tpu_custom_call" | custom-call | flops 201326592 | bytes 4194304 | tf_op jit(solution)/shard_map/blocks/pallas_call | solution.py:148
  30.2 0.0 collective-permute-done.6.refs_1_
  30.2 2.0 %blocks.7 = (bf16[1024,256]{1,0:T(8,128)(2,1)S(1)}, bf16[256,384]{1,0:T(8,128)(2,1)S(1)}, bf16[256,128]{1,0:T(8,128)(2,1)S(1)}, f32[2,2,128,128]{3,2,1,0:T(8,128...) custom-call(s32[3]{0:T(128)S(1)} %pad_add_fusion.place, bf16[1024,384]{1,0:T(8,128)(2,1)S(1)} %pad_maximum_fusion.w, ...), custom_call_target="tpu_custom_call" | custom-call | flops 201326592 | bytes 4194304 | tf_op jit(solution)/shard_map/blocks/pallas_call | solution.py:148
  32.2 3.3 %collective-permute-done.4.refs_0_ = f32[10,64,128]{2,1,0:T(8,128)S(1)} collective-permute-done((f32[10,64,128]{2,1,0:T(8,128)S(1)}, f32[10,64,128]{2,1,0:T(8,128)S(1)}, u32[]{:S(2)}, u32[]{:S(2)}) %collective-permute-start.4) | collective-permute-done | bytes 327712 | tf_op jit(solution)/shard_map/ppermute | solution.py:38
  35.5 0.0 collective-permute-done.5.refs_1_
  35.5 1.4 %collective-permute-start.7 = (f32[20,64,128]{2,1,0:T(8,128)S(1)}, f32[20,64,128]{2,1,0:T(8,128)S(1)}, u32[]{:S(2)}, u32[]{:S(2)}) collective-permute-start(f32[20,64,128]{2,1,0:T(8,128)S(1)} %relay.4.refs_0_), channel_id=1, source_target_pairs={{0,1},{1,0},{2,3},{3,2},{4,5},{5,4},{6,7},{7,6},{8,9},{9,8},{10,11... | collective-permute-start | bytes 1966088 | tf_op jit(solution)/shard_map/ppermute | solution.py:38
  37.0 1.4 %blocks.8 = (bf16[1024,128]{1,0:T(8,128)(2,1)S(1)}, bf16[128,384]{1,0:T(8,128)(2,1)S(1)}, bf16[128,128]{1,0:T(8,128)(2,1)S(1)}, f32[1,2,128,128]{3,2,1,0:T(8,128...) custom-call(s32[3]{0:T(128)S(1)} %pad_add_fusion.place, bf16[1024,384]{1,0:T(8,128)(2,1)S(1)} %pad_maximum_fusion.w, ...), custom_call_target="tpu_custom_call" | custom-call | flops 100663296 | bytes 4194304 | tf_op jit(solution)/shard_map/blocks/pallas_call | solution.py:148
  38.4 0.3 collective-permute-done.7.refs_0_
  38.7 1.4 %blocks.9 = (bf16[1024,128]{1,0:T(8,128)(2,1)S(1)}, bf16[128,384]{1,0:T(8,128)(2,1)S(1)}, bf16[128,128]{1,0:T(8,128)(2,1)S(1)}, f32[1,2,128,128]{3,2,1,0:T(8,128...) custom-call(s32[3]{0:T(128)S(1)} %pad_add_fusion.place, bf16[1024,384]{1,0:T(8,128)(2,1)S(1)} %pad_maximum_fusion.w, ...), custom_call_target="tpu_custom_call" | custom-call | flops 100663296 | bytes 4194304 | tf_op jit(solution)/shard_map/blocks/pallas_call | solution.py:148
  40.1 0.6 totals.1
  40.8 3.1 %collective-permute-start.8 = (f32[2,128,128]{2,1,0:T(8,128)S(1)}, f32[2,128,128]{2,1,0:T(8,128)S(1)}, u32[]{:S(2)}, u32[]{:S(2)}) collective-permute-start(f32[2,128,128]{2,1,0:T(8,128)S(1)} %get-tuple-element.71), channel_id=1, source_target_pairs={{0,16},{1,17},{2,18},{3,19},{4,20},{5,21},{6,22},{7,23},{8,24},{9,... | collective-permute-start | bytes 393224 | tf_op jit(solution)/shard_map/ppermute | solution.py:38
  43.9 0.4 collective-permute-start.9
  44.3 2.3 %collective-permute-start.10 = (f32[2,128,128]{2,1,0:T(8,128)S(1)}, f32[2,128,128]{2,1,0:T(8,128)S(1)}, u32[]{:S(2)}, u32[]{:S(2)}) collective-permute-start(f32[2,128,128]{2,1,0:T(8,128)S(1)} %get-tuple-element.73), channel_id=1, source_target_pairs={{0,24},{1,25},{2,26},{3,27},{4,28},{5,29},{6,30},{7,31},{8,0},{9,1... | collective-permute-start | bytes 393224 | tf_op jit(solution)/shard_map/ppermute | solution.py:38
  46.5 0.6 collective-permute-done.8.refs_0_
  47.2 3.2 %collective-permute-done.9.refs_1_ = f32[2,128,128]{2,1,0:T(8,128)S(1)} collective-permute-done((f32[2,128,128]{2,1,0:T(8,128)S(1)}, f32[2,128,128]{2,1,0:T(8,128)S(1)}, u32[]{:S(2)}, u32[]{:S(2)}) %collective-permute-start.9) | collective-permute-done | bytes 131104 | tf_op jit(solution)/shard_map/ppermute | solution.py:38
  50.4 0.0 collective-permute-done.10.refs_2_
  50.4 3.2 %gradients.1 = (bf16[1024,384]{1,0:T(8,128)(2,1)S(1)}, f32[512,384]{1,0:T(8,128)S(1)}, f32[8,32,384]{2,1,0:T(8,128)S(1)}, f32[8,32,384]{2,1,0:T(8,128)S(1)}, f32...) custom-call(s32[3]{0:T(128)S(1)} %pad_add_fusion.place, f32[2,128,128]{2,1,0:T(8,128)S(1)} %collective-permute-done.8.refs_0_, ...), custom_call_target="tpu_custom_call" | custom-call | flops 805306368 | bytes 10485760 | tf_op jit(solution)/shard_map/gradients/pallas_call | solution.py:270
  53.5 1.3 %collective-permute-start.11 = (f32[512,384]{1,0:T(8,128)S(1)}, f32[512,384]{1,0:T(8,128)S(1)}, u32[]{:S(2)}, u32[]{:S(2)}) collective-permute-start(f32[512,384]{1,0:T(8,128)S(1)} %get-tuple-element.95), channel_id=1, source_target_pairs={{0,1},{1,0},{2,3},{3,2},{4,5},{5,4},{6,7},{7,6},{8,9},{9,8},{10,11... | collective-permute-start | bytes 2359304 | tf_op jit(solution)/shard_map/ppermute | solution.py:38
  54.8 1.8 %collective-permute-start.15 = (f32[8,32,384]{2,1,0:T(8,128)S(1)}, f32[8,32,384]{2,1,0:T(8,128)S(1)}, u32[]{:S(2)}, u32[]{:S(2)}) collective-permute-start(f32[8,32,384]{2,1,0:T(8,128)S(1)} %get-tuple-element.101), channel_id=1, source_target_pairs={{0,16},{1,17},{2,18},{3,19},{4,20},{5,21},{6,22},{7,23},{8,24},{9,... | collective-permute-start | bytes 1179656 | tf_op jit(solution)/shard_map/ppermute | solution.py:38
  56.6 1.5 %collective-permute-start.16 = (f32[8,32,384]{2,1,0:T(8,128)S(1)}, f32[8,32,384]{2,1,0:T(8,128)S(1)}, u32[]{:S(2)}, u32[]{:S(2)}) collective-permute-start(f32[8,32,384]{2,1,0:T(8,128)S(1)} %get-tuple-element.102), channel_id=1, source_target_pairs={{0,8},{1,9},{2,10},{3,11},{4,12},{5,13},{6,14},{7,15},{8,16},{9,17... | collective-permute-start | bytes 1179656 | tf_op jit(solution)/shard_map/ppermute | solution.py:38
  58.0 1.2 collective-permute-start.17
  59.3 0.0 collective-permute-done.11.refs_1_
  59.3 0.8 relay.5
  60.1 2.5 %collective-permute-start.13 = (f32[256,384]{1,0:T(8,128)}, f32[256,384]{1,0:T(8,128)S(1)}, u32[]{:S(2)}, u32[]{:S(2)}) collective-permute-start(f32[256,384]{1,0:T(8,128)} %get-tuple-element.97), channel_id=1, source_target_pairs={{0,4},{1,5},{2,6},{3,7},{4,0},{5,1},{6,2},{7,3},{8,12},{9,13},{10,... | collective-permute-start | bytes 1179656 | tf_op jit(solution)/shard_map/ppermute | solution.py:38
  62.6 0.8 collective-permute-start.14
  63.5 3.6 %collective-permute-done.15.refs_1_ = f32[8,32,384]{2,1,0:T(8,128)S(1)} collective-permute-done((f32[8,32,384]{2,1,0:T(8,128)S(1)}, f32[8,32,384]{2,1,0:T(8,128)S(1)}, u32[]{:S(2)}, u32[]{:S(2)}) %collective-permute-start.15) | collective-permute-done | bytes 393248 | tf_op jit(solution)/shard_map/ppermute | solution.py:38
  67.0 2.8 %collective-permute-start.12 = (f32[256,384]{1,0:T(8,128)S(1)}, f32[256,384]{1,0:T(8,128)}, u32[]{:S(2)}, u32[]{:S(2)}) collective-permute-start(f32[256,384]{1,0:T(8,128)S(1)} %get-tuple-element.96.refs_4_), channel_id=1, source_target_pairs={{0,6},{1,7},{2,0},{3,1},{4,2},{5,3},{6,4},{7,5},{8,14},{9,15},{10,... | collective-permute-start | bytes 1179656 | tf_op jit(solution)/shard_map/ppermute | solution.py:38
  69.8 6.0 %collective-permute-done.16.refs_2_ = f32[8,32,384]{2,1,0:T(8,128)S(1)} collective-permute-done((f32[8,32,384]{2,1,0:T(8,128)S(1)}, f32[8,32,384]{2,1,0:T(8,128)S(1)}, u32[]{:S(2)}, u32[]{:S(2)}) %collective-permute-start.16) | collective-permute-done | bytes 393248 | tf_op jit(solution)/shard_map/ppermute | solution.py:38
  75.8 0.0 collective-permute-done.17.refs_3_
  75.8 0.8 fold.1
  76.6 9.2 %all-to-all-start = ((f32[16,16,384]{2,1,0:T(8,128)}), f32[16,16,384]{2,1,0:T(8,128)S(1)}, u32[]{:S(2)}, u32[]{:S(2)}) async-start(f32[16,16,384]{2,1,0:T(8,128)} %fold.1), calls=%async_computation | async-start | bytes 786432 | tf_op jit(solution)/shard_map/all_to_all | solution.py:488
  85.9 0.0 collective-permute-done.13.refs_3_
  85.9 0.0 collective-permute-done.12.refs_2_
  85.9 5.9 %input_gradient.1 = (bf16[128,1024]{1,0:T(8,128)(2,1)}, f32[8,128]{1,0:T(8,128)S(1)}) custom-call(s32[3]{0:T(128)S(1)} %pad_add_fusion.place, bf16[1024,384]{1,0:T(8,128)(2,1)S(1)} %get-tuple-element.94.refs_0_, f32[512,384]{1,0:T(8,128)S(1)} %collective-permute-done.11.refs_1_, f32[256,384]{1,0:T(8,128)} %collective-permute-done.12.refs_2_, ...), custom_call_target="tpu_custom_call" | custom-call | flops 6442450944 | bytes 83886080 | tf_op jit(solution)/shard_map/input_gradient/pallas_call | solution.py:316
  91.8 8.6 %all-to-all-done.got = f32[16,16,384]{2,1,0:T(8,128)S(1)} async-done(((f32[16,16,384]{2,1,0:T(8,128)}), f32[16,16,384]{2,1,0:T(8,128)S(1)}, u32[]{:S(2)}, u32[]{:S(2)}) %all-to-all-start) | async-done | bytes 393248 | tf_op jit(solution)/shard_map/all_to_all | solution.py:488
  100.4 1.3 %square_sum.1 = (f32[256,128]{1,0:T(8,128)}, f32[8,384]{1,0:T(8,128)S(1)}, f32[8,384]{1,0:T(8,128)S(1)}, f32[8,384]{1,0:T(8,128)S(1)}, f32[8,384]{1,0:T(8,128)S(1)}) custom-call(s32[3]{0:T(128)S(1)} %pad_add_fusion.place, f32[16,16,384]{2,1,0:T(8,128)S(1)} %all-to-all-done.got, f32[8,128]{1,0:T(8,128)S(1)} %get-tuple-element.104.after), custom_call_target="tpu_custom_call" | custom-call | flops 1048576 | bytes 1048576 | tf_op jit(solution)/shard_map/square_sum/pallas_call | solution.py:376
  101.8 8.0 %all-to-all-start.1 = ((f32[256,1,128]{2,1,0:T(1,128)}), f32[256,1,128]{2,1,0:T(1,128)S(1)}, u32[]{:S(2)}, u32[]{:S(2)}) async-start(f32[256,1,128]{2,1,0:T(1,128)} %bitcast.5), calls=%async_computation.1 | async-start | bytes 262144 | tf_op jit(solution)/shard_map/all_to_all | solution.py:494
  109.8 1.5 %collective-permute-start.18 = (f32[8,384]{1,0:T(8,128)S(1)}, f32[8,384]{1,0:T(8,128)S(1)}, u32[]{:S(2)}, u32[]{:S(2)}) collective-permute-start(f32[8,384]{1,0:T(8,128)S(1)} %get-tuple-element.107), channel_id=1, source_target_pairs={{0,2},{1,3},{2,4},{3,5},{4,6},{5,7},{6,0},{7,1},{8,10},{9,11},{10,... | collective-permute-start | bytes 36872 | tf_op jit(solution)/shard_map/ppermute | solution.py:38
  111.3 2.4 %collective-permute-start.19 = (f32[8,384]{1,0:T(8,128)S(1)}, f32[8,384]{1,0:T(8,128)S(1)}, u32[]{:S(2)}, u32[]{:S(2)}) collective-permute-start(f32[8,384]{1,0:T(8,128)S(1)} %get-tuple-element.108), channel_id=1, source_target_pairs={{0,4},{1,5},{2,6},{3,7},{4,0},{5,1},{6,2},{7,3},{8,12},{9,13},{10,... | collective-permute-start | bytes 36872 | tf_op jit(solution)/shard_map/ppermute | solution.py:38
  113.7 1.2 collective-permute-start.20
  114.8 0.0 collective-permute-done.18.refs_1_
  114.8 0.8 collective-permute-done.19.refs_2_
  115.6 0.9 collective-permute-done.20.refs_3_
  116.6 6.2 %all-to-all-done.1 = f32[256,1,128]{2,1,0:T(1,128)S(1)} async-done(((f32[256,1,128]{2,1,0:T(1,128)}), f32[256,1,128]{2,1,0:T(1,128)S(1)}, u32[]{:S(2)}, u32[]{:S(2)}) %all-to-all-start.1) | async-done | bytes 131104 | tf_op jit(solution)/shard_map/all_to_all | solution.py:494
  122.8 1.2 clip.1
  (10 shorter events, 0.1 us)
Async XLA Ops:
  0.7 1.0 copy-start
  1.7 0.9 copy-start.2
  4.4 17.1 %collective-permute-start.1 = (f32[22,64,128]{2,1,0:T(8,128)}, f32[22,64,128]{2,1,0:T(8,128)S(1)}, u32[]{:S(2)}, u32[]{:S(2)}) collective-permute-start(f32[22,64,128]{2,1,0:T(8,128)} %get-tuple-element.58), channel_id=1, source_target_pairs={{0,2},{1,3},{2,4},{3,5},{4,6},{5,7},{6,0},{7,1},{8,10},{9,11},{10,... | collective-permute-start | bytes 2162696 | tf_op jit(solution)/shard_map/ppermute | solution.py:38
  6.4 16.4 %collective-permute-start.2 = (f32[22,64,128]{2,1,0:T(8,128)S(1)}, f32[22,64,128]{2,1,0:T(8,128)S(1)}, u32[]{:S(2)}, u32[]{:S(2)}) collective-permute-start(f32[22,64,128]{2,1,0:T(8,128)S(1)} %get-tuple-element.59), channel_id=1, source_target_pairs={{0,6},{1,7},{2,0},{3,1},{4,2},{5,3},{6,4},{7,5},{8,14},{9,15},{10,... | collective-permute-start | bytes 2162696 | tf_op jit(solution)/shard_map/ppermute | solution.py:38
  7.7 5.0 %collective-permute-start = (f32[18,64,128]{2,1,0:T(8,128)}, f32[18,64,128]{2,1,0:T(8,128)S(1)}, u32[]{:S(2)}, u32[]{:S(2)}) collective-permute-start(f32[18,64,128]{2,1,0:T(8,128)} %get-tuple-element.56), channel_id=1, source_target_pairs={{0,1},{1,0},{2,3},{3,2},{4,5},{5,4},{6,7},{7,6},{8,9},{9,8},{10,11... | collective-permute-start | bytes 1769480 | tf_op jit(solution)/shard_map/ppermute | solution.py:38
  10.9 1.8 %copy-start.1 = (bf16[2,64,1024]{2,1,0:T(8,128)(2,1)S(1)}, bf16[2,64,1024]{2,1,0:T(8,128)(2,1)}, u32[]{:S(2)}) copy-start(bf16[2,64,1024]{2,1,0:T(8,128)(2,1)} %refs_0_.1) | copy-start | bytes 786436
  10.9 1.8 %copy-start.3 = (bf16[2,64,1024]{2,1,0:T(8,128)(2,1)S(1)}, bf16[2,64,1024]{2,1,0:T(8,128)(2,1)}, u32[]{:S(2)}) copy-start(bf16[2,64,1024]{2,1,0:T(8,128)(2,1)} %refs_1_.1) | copy-start | bytes 786436
  23.0 5.2 %collective-permute-start.3 = (f32[22,64,128]{2,1,0:T(8,128)S(1)}, f32[22,64,128]{2,1,0:T(8,128)S(1)}, u32[]{:S(2)}, u32[]{:S(2)}) collective-permute-start(f32[22,64,128]{2,1,0:T(8,128)S(1)} %get-tuple-element.60), channel_id=1, source_target_pairs={{0,1},{1,0},{2,3},{3,2},{4,5},{5,4},{6,7},{7,6},{8,9},{9,8},{10,11... | collective-permute-start | bytes 2162696 | tf_op jit(solution)/shard_map/ppermute | solution.py:38
  25.2 5.0 %collective-permute-start.6 = (f32[22,64,128]{2,1,0:T(8,128)S(1)}, f32[22,64,128]{2,1,0:T(8,128)S(1)}, u32[]{:S(2)}, u32[]{:S(2)}) collective-permute-start(f32[22,64,128]{2,1,0:T(8,128)S(1)} %get-tuple-element.62), channel_id=1, source_target_pairs={{0,1},{1,0},{2,3},{3,2},{4,5},{5,4},{6,7},{7,6},{8,9},{9,8},{10,11... | collective-permute-start | bytes 2162696 | tf_op jit(solution)/shard_map/ppermute | solution.py:38
  25.3 10.2 %collective-permute-start.4 = (f32[10,64,128]{2,1,0:T(8,128)S(1)}, f32[10,64,128]{2,1,0:T(8,128)S(1)}, u32[]{:S(2)}, u32[]{:S(2)}) collective-permute-start(f32[10,64,128]{2,1,0:T(8,128)S(1)} %slice.8), channel_id=1, source_target_pairs={{0,2},{1,3},{2,4},{3,5},{4,6},{5,7},{6,0},{7,1},{8,10},{9,11},{10,... | collective-permute-start | bytes 983048 | tf_op jit(solution)/shard_map/ppermute | solution.py:38
  26.6 8.9 %collective-permute-start.5 = (f32[10,64,128]{2,1,0:T(8,128)S(1)}, f32[10,64,128]{2,1,0:T(8,128)S(1)}, u32[]{:S(2)}, u32[]{:S(2)}) collective-permute-start(f32[10,64,128]{2,1,0:T(8,128)S(1)} %slice.9), channel_id=1, source_target_pairs={{0,6},{1,7},{2,0},{3,1},{4,2},{5,3},{6,4},{7,5},{8,14},{9,15},{10,... | collective-permute-start | bytes 983048 | tf_op jit(solution)/shard_map/ppermute | solution.py:38
  35.5 3.1 %collective-permute-start.7 = (f32[20,64,128]{2,1,0:T(8,128)S(1)}, f32[20,64,128]{2,1,0:T(8,128)S(1)}, u32[]{:S(2)}, u32[]{:S(2)}) collective-permute-start(f32[20,64,128]{2,1,0:T(8,128)S(1)} %relay.4.refs_0_), channel_id=1, source_target_pairs={{0,1},{1,0},{2,3},{3,2},{4,5},{5,4},{6,7},{7,6},{8,9},{9,8},{10,11... | collective-permute-start | bytes 1966088 | tf_op jit(solution)/shard_map/ppermute | solution.py:38
  40.8 6.4 %collective-permute-start.8 = (f32[2,128,128]{2,1,0:T(8,128)S(1)}, f32[2,128,128]{2,1,0:T(8,128)S(1)}, u32[]{:S(2)}, u32[]{:S(2)}) collective-permute-start(f32[2,128,128]{2,1,0:T(8,128)S(1)} %get-tuple-element.71), channel_id=1, source_target_pairs={{0,16},{1,17},{2,18},{3,19},{4,20},{5,21},{6,22},{7,23},{8,24},{9,... | collective-permute-start | bytes 393224 | tf_op jit(solution)/shard_map/ppermute | solution.py:38
  43.9 6.5 %collective-permute-start.9 = (f32[2,128,128]{2,1,0:T(8,128)S(1)}, f32[2,128,128]{2,1,0:T(8,128)S(1)}, u32[]{:S(2)}, u32[]{:S(2)}) collective-permute-start(f32[2,128,128]{2,1,0:T(8,128)S(1)} %get-tuple-element.72), channel_id=1, source_target_pairs={{0,8},{1,9},{2,10},{3,11},{4,12},{5,13},{6,14},{7,15},{8,16},{9,17... | collective-permute-start | bytes 393224 | tf_op jit(solution)/shard_map/ppermute | solution.py:38
  44.3 6.1 %collective-permute-start.10 = (f32[2,128,128]{2,1,0:T(8,128)S(1)}, f32[2,128,128]{2,1,0:T(8,128)S(1)}, u32[]{:S(2)}, u32[]{:S(2)}) collective-permute-start(f32[2,128,128]{2,1,0:T(8,128)S(1)} %get-tuple-element.73), channel_id=1, source_target_pairs={{0,24},{1,25},{2,26},{3,27},{4,28},{5,29},{6,30},{7,31},{8,0},{9,1... | collective-permute-start | bytes 393224 | tf_op jit(solution)/shard_map/ppermute | solution.py:38
  53.5 5.8 %collective-permute-start.11 = (f32[512,384]{1,0:T(8,128)S(1)}, f32[512,384]{1,0:T(8,128)S(1)}, u32[]{:S(2)}, u32[]{:S(2)}) collective-permute-start(f32[512,384]{1,0:T(8,128)S(1)} %get-tuple-element.95), channel_id=1, source_target_pairs={{0,1},{1,0},{2,3},{3,2},{4,5},{5,4},{6,7},{7,6},{8,9},{9,8},{10,11... | collective-permute-start | bytes 2359304 | tf_op jit(solution)/shard_map/ppermute | solution.py:38
  54.8 12.2 %collective-permute-start.15 = (f32[8,32,384]{2,1,0:T(8,128)S(1)}, f32[8,32,384]{2,1,0:T(8,128)S(1)}, u32[]{:S(2)}, u32[]{:S(2)}) collective-permute-start(f32[8,32,384]{2,1,0:T(8,128)S(1)} %get-tuple-element.101), channel_id=1, source_target_pairs={{0,16},{1,17},{2,18},{3,19},{4,20},{5,21},{6,22},{7,23},{8,24},{9,... | collective-permute-start | bytes 1179656 | tf_op jit(solution)/shard_map/ppermute | solution.py:38
  56.6 19.2 %collective-permute-start.16 = (f32[8,32,384]{2,1,0:T(8,128)S(1)}, f32[8,32,384]{2,1,0:T(8,128)S(1)}, u32[]{:S(2)}, u32[]{:S(2)}) collective-permute-start(f32[8,32,384]{2,1,0:T(8,128)S(1)} %get-tuple-element.102), channel_id=1, source_target_pairs={{0,8},{1,9},{2,10},{3,11},{4,12},{5,13},{6,14},{7,15},{8,16},{9,17... | collective-permute-start | bytes 1179656 | tf_op jit(solution)/shard_map/ppermute | solution.py:38
  58.0 17.8 %collective-permute-start.17 = (f32[8,32,384]{2,1,0:T(8,128)S(1)}, f32[8,32,384]{2,1,0:T(8,128)S(1)}, u32[]{:S(2)}, u32[]{:S(2)}) collective-permute-start(f32[8,32,384]{2,1,0:T(8,128)S(1)} %get-tuple-element.103), channel_id=1, source_target_pairs={{0,24},{1,25},{2,26},{3,27},{4,28},{5,29},{6,30},{7,31},{8,0},{9,1... | collective-permute-start | bytes 1179656 | tf_op jit(solution)/shard_map/ppermute | solution.py:38
  60.1 25.8 %collective-permute-start.13 = (f32[256,384]{1,0:T(8,128)}, f32[256,384]{1,0:T(8,128)S(1)}, u32[]{:S(2)}, u32[]{:S(2)}) collective-permute-start(f32[256,384]{1,0:T(8,128)} %get-tuple-element.97), channel_id=1, source_target_pairs={{0,4},{1,5},{2,6},{3,7},{4,0},{5,1},{6,2},{7,3},{8,12},{9,13},{10,... | collective-permute-start | bytes 1179656 | tf_op jit(solution)/shard_map/ppermute | solution.py:38
  62.6 23.3 %collective-permute-start.14 = (f32[256,384]{1,0:T(8,128)S(1)}, f32[256,384]{1,0:T(8,128)S(1)}, u32[]{:S(2)}, u32[]{:S(2)}) collective-permute-start(f32[256,384]{1,0:T(8,128)S(1)} %get-tuple-element.98), channel_id=1, source_target_pairs={{0,2},{1,3},{2,4},{3,5},{4,6},{5,7},{6,0},{7,1},{8,10},{9,11},{10,... | collective-permute-start | bytes 1179656 | tf_op jit(solution)/shard_map/ppermute | solution.py:38
  67.0 18.9 %collective-permute-start.12 = (f32[256,384]{1,0:T(8,128)S(1)}, f32[256,384]{1,0:T(8,128)}, u32[]{:S(2)}, u32[]{:S(2)}) collective-permute-start(f32[256,384]{1,0:T(8,128)S(1)} %get-tuple-element.96.refs_4_), channel_id=1, source_target_pairs={{0,6},{1,7},{2,0},{3,1},{4,2},{5,3},{6,4},{7,5},{8,14},{9,15},{10,... | collective-permute-start | bytes 1179656 | tf_op jit(solution)/shard_map/ppermute | solution.py:38
  76.6 23.8 %all-to-all-start = ((f32[16,16,384]{2,1,0:T(8,128)}), f32[16,16,384]{2,1,0:T(8,128)S(1)}, u32[]{:S(2)}, u32[]{:S(2)}) async-start(f32[16,16,384]{2,1,0:T(8,128)} %fold.1), calls=%async_computation | async-start | bytes 786432 | tf_op jit(solution)/shard_map/all_to_all | solution.py:488
  101.8 21.0 %all-to-all-start.1 = ((f32[256,1,128]{2,1,0:T(1,128)}), f32[256,1,128]{2,1,0:T(1,128)S(1)}, u32[]{:S(2)}, u32[]{:S(2)}) async-start(f32[256,1,128]{2,1,0:T(1,128)} %bitcast.5), calls=%async_computation.1 | async-start | bytes 262144 | tf_op jit(solution)/shard_map/all_to_all | solution.py:494
  109.8 5.0 %collective-permute-start.18 = (f32[8,384]{1,0:T(8,128)S(1)}, f32[8,384]{1,0:T(8,128)S(1)}, u32[]{:S(2)}, u32[]{:S(2)}) collective-permute-start(f32[8,384]{1,0:T(8,128)S(1)} %get-tuple-element.107), channel_id=1, source_target_pairs={{0,2},{1,3},{2,4},{3,5},{4,6},{5,7},{6,0},{7,1},{8,10},{9,11},{10,... | collective-permute-start | bytes 36872 | tf_op jit(solution)/shard_map/ppermute | solution.py:38
  111.3 4.4 %collective-permute-start.19 = (f32[8,384]{1,0:T(8,128)S(1)}, f32[8,384]{1,0:T(8,128)S(1)}, u32[]{:S(2)}, u32[]{:S(2)}) collective-permute-start(f32[8,384]{1,0:T(8,128)S(1)} %get-tuple-element.108), channel_id=1, source_target_pairs={{0,4},{1,5},{2,6},{3,7},{4,0},{5,1},{6,2},{7,3},{8,12},{9,13},{10,... | collective-permute-start | bytes 36872 | tf_op jit(solution)/shard_map/ppermute | solution.py:38
  113.7 2.9 %collective-permute-start.20 = (f32[8,384]{1,0:T(8,128)S(1)}, f32[8,384]{1,0:T(8,128)S(1)}, u32[]{:S(2)}, u32[]{:S(2)}) collective-permute-start(f32[8,384]{1,0:T(8,128)S(1)} %get-tuple-element.109), channel_id=1, source_target_pairs={{0,6},{1,7},{2,0},{3,1},{4,2},{5,3},{6,4},{7,5},{8,14},{9,15},{10,... | collective-permute-start | bytes 36872 | tf_op jit(solution)/shard_map/ppermute | solution.py:38

commit v5 on v4

--- a/solution.py
+++ b/solution.py
@@ -335,20 +335,14 @@
 
 def fold_kernel(count, *refs):
     out = refs[-1]
-    dp_count, row_block = refs[0].shape[0], refs[0].shape[1]
-    rows = row_block // GROUP
-    for z in range(dp_count):
-        value = sum(ref[z] for ref in refs[:count])
-        for t in range(GROUP):
-            to = (t // 2) * rows
-            out[2 * z + t % 2, to : to + rows, :] = value[t * rows : (t + 1) * rows, :]
+    for z in range(out.shape[0]):
+        out[z] = sum(ref[z] for ref in refs[:count])
 
 
 def fold(parts, after):
-    dp_count, row_block, width = parts[0].shape
     return pl.pallas_call(
         functools.partial(fold_kernel, len(parts)),
-        out_shape=struct((dp_count * 2, row_block // 2, width), F32),
+        out_shape=struct(parts[0].shape, F32),
         in_specs=[VMEM] * len(parts) + [ANY],
         out_specs=VMEM,
         compiler_params=pltpu.CompilerParams(vmem_limit_bytes=8 * MIB),
@@ -357,42 +351,80 @@
     )(*parts, after)
 
 
-def square_kernel(place, got, after, squares, *refs):
-    x, pieces, rows_of = place[1], refs[:NX], refs[NX]
-    count, rows = got.shape[0] // 2, got.shape[1] // NX
-    lanes = jnp.zeros((1, got.shape[2]), F32)
-    for core in range(2):
-        value = sum(got[2 * z + core] for z in range(count))
-        lanes = lanes + jnp.sum(value * value, axis=0, keepdims=True)
-        for to in range(NX):
-            rows_of[to, core * rows : (core + 1) * rows, :] = value[to * rows : (to + 1) * rows, :]
-    squares[...] = jnp.full(squares.shape, jnp.sum(lanes))
-    for dx in range(NX):
-        pieces[dx][...] = rows_of[(x + dx) % NX]
-
-
-def square_sum(place, got, after, device_count):
-    rows, width = 2 * got.shape[1] // NX, got.shape[2]
+def square_kernel(place, got, after, squares, own, theirs, rows_of):
+    c = place[2]
+    count, rows = got.shape[0], own.shape[0] // NX
+    value = sum(got[z] for z in range(count))
+    for to in range(GROUP):
+        there = slice((to // 2) * rows, (to // 2 + 1) * rows)
+        rows_of[to % 2, there, :] = value[to * rows : (to + 1) * rows, :]
+    squares[...] = jnp.full(squares.shape, jnp.sum(jnp.sum(value * value, axis=0, keepdims=True)))
+    own[...] = rows_of[c]
+    theirs[...] = rows_of[1 - c]
+
+
+def square_sum(place, got, after, copies):
+    rows, width = got.shape[1] // 2, got.shape[2]
     return pl.pallas_call(
         square_kernel,
-        out_shape=(struct((device_count, DH), F32),) + (struct((rows, width), F32),) * NX,
+        out_shape=(struct((copies, DH), F32),) + (struct((rows, width), F32),) * 2,
         in_specs=[SMEM, VMEM, ANY],
-        out_specs=(VMEM,) * (1 + NX),
-        scratch_shapes=[pltpu.VMEM((NX, rows, width), F32)],
+        out_specs=(VMEM,) * 3,
+        scratch_shapes=[pltpu.VMEM((2, rows, width), F32)],
         compiler_params=pltpu.CompilerParams(vmem_limit_bytes=8 * MIB),
         cost_estimate=pl.CostEstimate(flops=MIB, bytes_accessed=MIB, transcendentals=0),
         name="square_sum",
     )(place, got, after)
 
 
+def total_square_kernel(squares, out):
+    out[...] = jnp.broadcast_to(jnp.sum(squares[...], axis=0, keepdims=True), out.shape)
+
+
+def total_square(squares, count):
+    return pl.pallas_call(
+        total_square_kernel,
+        out_shape=struct((count, DH), F32),
+        in_specs=[VMEM],
+        out_specs=VMEM,
+        compiler_params=pltpu.CompilerParams(vmem_limit_bytes=4 * MIB),
+        cost_estimate=pl.CostEstimate(flops=4096, bytes_accessed=16384, transcendentals=0),
+        name="total_square",
+    )(squares)
+
+
+def pair_kernel(place, own, theirs, *refs):
+    x, pieces, rows_of = place[1], refs[:NX], refs[NX]
+    rows = own.shape[0] // NX
+    for to in range(NX):
+        rows_of[to, :rows, :] = own[to * rows : (to + 1) * rows, :]
+        rows_of[to, rows:, :] = theirs[to * rows : (to + 1) * rows, :]
+    for dx in range(NX):
+        pieces[dx][...] = rows_of[(x + dx) % NX]
+
+
+def pair_rows(place, own, theirs):
+    rows, width = 2 * own.shape[0] // NX, own.shape[1]
+    return pl.pallas_call(
+        pair_kernel,
+        out_shape=(struct((rows, width), F32),) * NX,
+        in_specs=[SMEM, VMEM, VMEM],
+        out_specs=(VMEM,) * NX,
+        scratch_shapes=[pltpu.VMEM((NX, rows, width), F32)],
+        compiler_params=pltpu.CompilerParams(vmem_limit_bytes=8 * MIB),
+        cost_estimate=pl.CostEstimate(flops=MIB, bytes_accessed=MIB, transcendentals=0),
+        name="pair_rows",
+    )(place, own, theirs)
+
+
 def clip_kernel(place, squares, *refs):
-    x, pieces, out = place[1], refs[:NX], refs[NX]
+    x, c, pieces, out = place[1], place[2], refs[:NX], refs[NX]
     rows = out.shape[0]
     total_sq = jnp.sum(squares[...], axis=0, keepdims=True)
     factor = jnp.minimum(1.0, D / jnp.sqrt(total_sq + 1e-06))
     for dx in range(NX):
         for core in range(2):
-            head = ((x + NX - dx) % NX) * 2 + core
+            head = ((x + NX - dx) % NX) * 2 + (c ^ core)
             for part in range(3):
                 columns = slice(part * DH, (part + 1) * DH)
                 start = pl.multiple_of((part * H + head) * DH, DH)
@@ -481,18 +513,16 @@
     back = [send(returns[dx - 1], dx=-dx) for dx in range(1, NX)]
     summands = pieces[:1] + [send(value, dy=dy) for value, dy in zip(pieces[1:], FAR_FIRST)]
     folded = fold(summands, returns[0])
-    columns_of = [
-        [z * NY * GROUP + place_of + core for z in range(dp_count) for core in range(2)]
-        for place_of in range(0, NY * GROUP, 2)
-    ]
-    got = lax.all_to_all(folded, ("dp", "seq"), 0, 0, axis_index_groups=columns_of)
+    got = lax.all_to_all(folded, "dp", 0, 0)
     grad_rows, done = input_gradient(place, (grad_proj, theirs, *back), total_rows, w_qkv)
     grad_inputs = grad_rows.reshape(user_count, row_count, feature_count)
 
-    device_count = dp_count * lax.axis_size("seq")
-    squares, *parts = square_sum(place, got, done, device_count)
-    squares = lax.all_to_all(squares, ("dp", "seq"), 0, 0, tiled=True)
-    parts = parts[:1] + [send(parts[dx], dx=dx) for dx in range(1, NX)]
+    squares, own, theirs = square_sum(place, got, done, dp_count)
+    squares = lax.all_to_all(squares, "dp", 0, 0, tiled=True)
+    parts = pair_rows(place, own, send(theirs, dc=1))
+    squares = total_square(squares, lax.axis_size("seq"))
+    squares = lax.all_to_all(squares, "seq", 0, 0, tiled=True)
+    parts = parts[:1] + tuple(send(parts[dx], dx=dx) for dx in range(1, NX))
     return (grad_inputs, clip(place, squares, parts))
 
 

time: 124 us -> 128 us (1.032)
  blocking collectives: 0 us -> 8.88 us
  waiting for transfers between devices: 42.3 us -> 35 us
    all_to_all x0 -> x1, blocking collectives: none -> 8.88 us  [body(): squares = lax.all_to_all(squares, 'dp', 0, 0, tiled=True)]
    all_to_all x2, waiting for transfers between devices: 14.8 us -> 8.91 us  [the longest x1 7.67 us: body(): got = lax.all_to_all(folded, 'dp', 0, 0)]
    ppermute x21 -> x22, starting transfers between devices: 35.8 us -> 37.9 us  [send(): return lax.ppermute(value, 'seq', seq_perm(dy, dx, dc))]
    ppermute x21 -> x22, waiting for transfers between devices: 27.4 us -> 26.1 us  [send(): return lax.ppermute(value, 'seq', seq_perm(dy, dx, dc))]
  transfers between devices with their start and end apart: 23 -> 24, of which waited for: 13 -> 12; matrix products, arithmetic and copies ran while one was open for 1% -> 1% of each run, Pallas kernels for 12% -> 13%
where the time goes in v5:
time: 128 us; the launch traced here: 127 us
  starting transfers between devices  54.2 us (42%)
  waiting for transfers between devices  35 us (27%)
  Pallas kernels  25.1 us (20%)
  blocking collectives  8.88 us (7%)
  local copies, waits for them, and re-layouts  3.19 us (2%)
    ppermute x22, starting transfers between devices, send(): return lax.ppermute(value, 'seq', seq_perm(dy, dx, dc))  37.9 us
    ppermute x22, waiting for transfers between devices, send(): return lax.ppermute(value, 'seq', seq_perm(dy, dx, dc))  26.1 us
    all_to_all x1, blocking collectives, body(): squares = lax.all_to_all(squares, 'dp', 0, 0, tiled=True)  8.88 us
    pallas_call x5, Pallas kernels, blocks(): pl.pallas_call(functools.partial(block_kernel, units), out_shape=(struct(...  8.77 us
    all_to_all x1, starting transfers between devices, body(): got = lax.all_to_all(folded, 'dp', 0, 0)  8.19 us
    all_to_all x1, starting transfers between devices, body(): squares = lax.all_to_all(squares, 'seq', 0, 0, tiled=True)  8.11 us
    all_to_all x1, waiting for transfers between devices, body(): got = lax.all_to_all(folded, 'dp', 0, 0)  7.67 us
    pallas_call x1, Pallas kernels, input_gradient(): pl.pallas_call(input_kernel, grid=(features // step,), out_shape=(struct(...  5.9 us
  transfers between devices with their start and end apart: 24, of which 12 were waited for; matrix products, arithmetic and copies ran while one was open for 1% of the time, Pallas kernels for 13%

profile of v5, /device:TPU:1, one launch (start us, length us, event | category | flops | bytes accessed | tf_op | source)
XLA Modules:
  0.0 127.4 jit_solution(2007895005446001676)
XLA Ops:
  0.7 0.1 pad_add_fusion.place
  0.7 0.9 copy-done
  1.7 0.9 copy-done.2
  2.6 1.8 %messages.1 = (f32[22,64,128]{2,1,0:T(8,128)}, f32[22,64,128]{2,1,0:T(8,128)S(1)}, f32[18,64,128]{2,1,0:T(8,128)}) custom-call(s32[3]{0:T(128)S(1)} %pad_add_fusion.place, bf16[2,64,1024]{2,1,0:T(8,128)(2,1)S(1)} %copy-done, bf16[2,64,1024]{2,1,0:T(8,128)(2,1)S(1)} %copy-done.2), custom_call_target="tpu_custom_call" | custom-call | flops 1048576 | bytes 3145728 | tf_op jit(solution)/shard_map/messages/pallas_call | solution.py:76
  4.4 2.0 %collective-permute-start.1 = (f32[22,64,128]{2,1,0:T(8,128)}, f32[22,64,128]{2,1,0:T(8,128)S(1)}, u32[]{:S(2)}, u32[]{:S(2)}) collective-permute-start(f32[22,64,128]{2,1,0:T(8,128)} %get-tuple-element.60), channel_id=1, source_target_pairs={{0,2},{1,3},{2,4},{3,5},{4,6},{5,7},{6,0},{7,1},{8,10},{9,11},{10,... | collective-permute-start | bytes 2162696 | tf_op jit(solution)/shard_map/ppermute | solution.py:38
  6.4 1.3 collective-permute-start.2
  7.7 3.2 %collective-permute-start = (f32[18,64,128]{2,1,0:T(8,128)}, f32[18,64,128]{2,1,0:T(8,128)S(1)}, u32[]{:S(2)}, u32[]{:S(2)}) collective-permute-start(f32[18,64,128]{2,1,0:T(8,128)} %get-tuple-element.58), channel_id=1, source_target_pairs={{0,1},{1,0},{2,3},{3,2},{4,5},{5,4},{6,7},{7,6},{8,9},{9,8},{10,11... | collective-permute-start | bytes 1769480 | tf_op jit(solution)/shard_map/ppermute | solution.py:38
  10.9 1.2 constant_dynamic-slice_fusion.2
  12.1 0.1 pad_maximum_fusion.w
  12.2 0.5 collective-permute-done.refs_2_
  12.7 2.0 %blocks.5 = (bf16[1024,256]{1,0:T(8,128)(2,1)S(1)}, bf16[256,384]{1,0:T(8,128)(2,1)S(1)}, bf16[256,128]{1,0:T(8,128)(2,1)S(1)}, f32[2,2,128,128]{3,2,1,0:T(8,128...) custom-call(s32[3]{0:T(128)S(1)} %pad_add_fusion.place, bf16[1024,384]{1,0:T(8,128)(2,1)S(1)} %pad_maximum_fusion.w, ...), custom_call_target="tpu_custom_call" | custom-call | flops 201326592 | bytes 4194304 | tf_op jit(solution)/shard_map/blocks/pallas_call | solution.py:148
  14.7 6.8 %collective-permute-done.1.refs_0_ = f32[22,64,128]{2,1,0:T(8,128)S(1)} collective-permute-done((f32[22,64,128]{2,1,0:T(8,128)}, f32[22,64,128]{2,1,0:T(8,128)S(1)}, u32[]{:S(2)}, u32[]{:S(2)}) %collective-permute-start.1) | collective-permute-done | bytes 720928 | tf_op jit(solution)/shard_map/ppermute | solution.py:38
  21.5 1.4 %collective-permute-done.2.refs_1_.refs_0_ = f32[22,64,128]{2,1,0:T(8,128)S(1)} collective-permute-done((f32[22,64,128]{2,1,0:T(8,128)S(1)}, f32[22,64,128]{2,1,0:T(8,128)S(1)}, u32[]{:S(2)}, u32[]{:S(2)}) %collective-permute-start.2) | collective-permute-done | bytes 720928 | tf_op jit(solution)/shard_map/ppermute | solution.py:38
  22.9 0.1 relay.3
  23.0 2.2 %collective-permute-start.3 = (f32[22,64,128]{2,1,0:T(8,128)S(1)}, f32[22,64,128]{2,1,0:T(8,128)S(1)}, u32[]{:S(2)}, u32[]{:S(2)}) collective-permute-start(f32[22,64,128]{2,1,0:T(8,128)S(1)} %get-tuple-element.62), channel_id=1, source_target_pairs={{0,1},{1,0},{2,3},{3,2},{4,5},{5,4},{6,7},{7,6},{8,9},{9,8},{10,11... | collective-permute-start | bytes 2162696 | tf_op jit(solution)/shard_map/ppermute | solution.py:38
  25.2 0.1 collective-permute-start.6
  25.3 1.3 collective-permute-start.4
  26.6 1.6 %collective-permute-start.5 = (f32[10,64,128]{2,1,0:T(8,128)S(1)}, f32[10,64,128]{2,1,0:T(8,128)S(1)}, u32[]{:S(2)}, u32[]{:S(2)}) collective-permute-start(f32[10,64,128]{2,1,0:T(8,128)S(1)} %slice.9), channel_id=1, source_target_pairs={{0,6},{1,7},{2,0},{3,1},{4,2},{5,3},{6,4},{7,5},{8,14},{9,15},{10,... | collective-permute-start | bytes 983048 | tf_op jit(solution)/shard_map/ppermute | solution.py:38
  28.2 0.0 collective-permute-done.3.refs_1_
  28.2 2.0 %blocks.6 = (bf16[1024,256]{1,0:T(8,128)(2,1)S(1)}, bf16[256,384]{1,0:T(8,128)(2,1)S(1)}, bf16[256,128]{1,0:T(8,128)(2,1)S(1)}, f32[2,2,128,128]{3,2,1,0:T(8,128...) custom-call(s32[3]{0:T(128)S(1)} %pad_add_fusion.place, bf16[1024,384]{1,0:T(8,128)(2,1)S(1)} %pad_maximum_fusion.w, ...), custom_call_target="tpu_custom_call" | custom-call | flops 201326592 | bytes 4194304 | tf_op jit(solution)/shard_map/blocks/pallas_call | solution.py:148
  30.2 2.0 %blocks.7 = (bf16[1024,256]{1,0:T(8,128)(2,1)S(1)}, bf16[256,384]{1,0:T(8,128)(2,1)S(1)}, bf16[256,128]{1,0:T(8,128)(2,1)S(1)}, f32[2,2,128,128]{3,2,1,0:T(8,128...) custom-call(s32[3]{0:T(128)S(1)} %pad_add_fusion.place, bf16[1024,384]{1,0:T(8,128)(2,1)S(1)} %pad_maximum_fusion.w, ...), custom_call_target="tpu_custom_call" | custom-call | flops 201326592 | bytes 4194304 | tf_op jit(solution)/shard_map/blocks/pallas_call | solution.py:148
  32.2 3.3 %collective-permute-done.4.refs_0_ = f32[10,64,128]{2,1,0:T(8,128)S(1)} collective-permute-done((f32[10,64,128]{2,1,0:T(8,128)S(1)}, f32[10,64,128]{2,1,0:T(8,128)S(1)}, u32[]{:S(2)}, u32[]{:S(2)}) %collective-permute-start.4) | collective-permute-done | bytes 327712 | tf_op jit(solution)/shard_map/ppermute | solution.py:38
  35.5 0.0 collective-permute-done.5.refs_1_
  35.6 1.4 %collective-permute-start.7 = (f32[20,64,128]{2,1,0:T(8,128)S(1)}, f32[20,64,128]{2,1,0:T(8,128)S(1)}, u32[]{:S(2)}, u32[]{:S(2)}) collective-permute-start(f32[20,64,128]{2,1,0:T(8,128)S(1)} %relay.4.refs_0_), channel_id=1, source_target_pairs={{0,1},{1,0},{2,3},{3,2},{4,5},{5,4},{6,7},{7,6},{8,9},{9,8},{10,11... | collective-permute-start | bytes 1966088 | tf_op jit(solution)/shard_map/ppermute | solution.py:38
  37.0 1.4 %blocks.8 = (bf16[1024,128]{1,0:T(8,128)(2,1)S(1)}, bf16[128,384]{1,0:T(8,128)(2,1)S(1)}, bf16[128,128]{1,0:T(8,128)(2,1)S(1)}, f32[1,2,128,128]{3,2,1,0:T(8,128...) custom-call(s32[3]{0:T(128)S(1)} %pad_add_fusion.place, bf16[1024,384]{1,0:T(8,128)(2,1)S(1)} %pad_maximum_fusion.w, ...), custom_call_target="tpu_custom_call" | custom-call | flops 100663296 | bytes 4194304 | tf_op jit(solution)/shard_map/blocks/pallas_call | solution.py:148
  38.4 0.3 collective-permute-done.7.refs_0_
  38.7 1.4 %blocks.9 = (bf16[1024,128]{1,0:T(8,128)(2,1)S(1)}, bf16[128,384]{1,0:T(8,128)(2,1)S(1)}, bf16[128,128]{1,0:T(8,128)(2,1)S(1)}, f32[1,2,128,128]{3,2,1,0:T(8,128...) custom-call(s32[3]{0:T(128)S(1)} %pad_add_fusion.place, bf16[1024,384]{1,0:T(8,128)(2,1)S(1)} %pad_maximum_fusion.w, ...), custom_call_target="tpu_custom_call" | custom-call | flops 100663296 | bytes 4194304 | tf_op jit(solution)/shard_map/blocks/pallas_call | solution.py:148
  40.1 0.6 totals.1
  40.8 3.1 %collective-permute-start.8 = (f32[2,128,128]{2,1,0:T(8,128)S(1)}, f32[2,128,128]{2,1,0:T(8,128)S(1)}, u32[]{:S(2)}, u32[]{:S(2)}) collective-permute-start(f32[2,128,128]{2,1,0:T(8,128)S(1)} %get-tuple-element.73), channel_id=1, source_target_pairs={{0,16},{1,17},{2,18},{3,19},{4,20},{5,21},{6,22},{7,23},{8,24},{9,... | collective-permute-start | bytes 393224 | tf_op jit(solution)/shard_map/ppermute | solution.py:38
  43.9 0.4 collective-permute-start.9
  44.3 2.3 %collective-permute-start.10 = (f32[2,128,128]{2,1,0:T(8,128)S(1)}, f32[2,128,128]{2,1,0:T(8,128)S(1)}, u32[]{:S(2)}, u32[]{:S(2)}) collective-permute-start(f32[2,128,128]{2,1,0:T(8,128)S(1)} %get-tuple-element.75), channel_id=1, source_target_pairs={{0,24},{1,25},{2,26},{3,27},{4,28},{5,29},{6,30},{7,31},{8,0},{9,1... | collective-permute-start | bytes 393224 | tf_op jit(solution)/shard_map/ppermute | solution.py:38
  46.6 0.6 collective-permute-done.8.refs_0_
  47.2 3.2 %collective-permute-done.9.refs_1_ = f32[2,128,128]{2,1,0:T(8,128)S(1)} collective-permute-done((f32[2,128,128]{2,1,0:T(8,128)S(1)}, f32[2,128,128]{2,1,0:T(8,128)S(1)}, u32[]{:S(2)}, u32[]{:S(2)}) %collective-permute-start.9) | collective-permute-done | bytes 131104 | tf_op jit(solution)/shard_map/ppermute | solution.py:38
  50.4 3.2 %gradients.1 = (bf16[1024,384]{1,0:T(8,128)(2,1)S(1)}, f32[512,384]{1,0:T(8,128)S(1)}, f32[8,32,384]{2,1,0:T(8,128)S(1)}, f32[8,32,384]{2,1,0:T(8,128)S(1)}, f32...) custom-call(s32[3]{0:T(128)S(1)} %pad_add_fusion.place, f32[2,128,128]{2,1,0:T(8,128)S(1)} %collective-permute-done.8.refs_0_, ...), custom_call_target="tpu_custom_call" | custom-call | flops 805306368 | bytes 10485760 | tf_op jit(solution)/shard_map/gradients/pallas_call | solution.py:270
  53.5 1.3 collective-permute-start.11
  54.8 1.8 %collective-permute-start.15 = (f32[8,32,384]{2,1,0:T(8,128)S(1)}, f32[8,32,384]{2,1,0:T(8,128)S(1)}, u32[]{:S(2)}, u32[]{:S(2)}) collective-permute-start(f32[8,32,384]{2,1,0:T(8,128)S(1)} %get-tuple-element.103), channel_id=1, source_target_pairs={{0,16},{1,17},{2,18},{3,19},{4,20},{5,21},{6,22},{7,23},{8,24},{9,... | collective-permute-start | bytes 1179656 | tf_op jit(solution)/shard_map/ppermute | solution.py:38
  56.6 1.5 %collective-permute-start.16 = (f32[8,32,384]{2,1,0:T(8,128)S(1)}, f32[8,32,384]{2,1,0:T(8,128)S(1)}, u32[]{:S(2)}, u32[]{:S(2)}) collective-permute-start(f32[8,32,384]{2,1,0:T(8,128)S(1)} %get-tuple-element.104), channel_id=1, source_target_pairs={{0,8},{1,9},{2,10},{3,11},{4,12},{5,13},{6,14},{7,15},{8,16},{9,17... | collective-permute-start | bytes 1179656 | tf_op jit(solution)/shard_map/ppermute | solution.py:38
  58.1 1.2 collective-permute-start.17
  59.3 0.0 collective-permute-done.11.refs_1_
  59.3 0.8 relay.5
  60.1 2.5 %collective-permute-start.13 = (f32[256,384]{1,0:T(8,128)}, f32[256,384]{1,0:T(8,128)S(1)}, u32[]{:S(2)}, u32[]{:S(2)}) collective-permute-start(f32[256,384]{1,0:T(8,128)} %get-tuple-element.99), channel_id=1, source_target_pairs={{0,4},{1,5},{2,6},{3,7},{4,0},{5,1},{6,2},{7,3},{8,12},{9,13},{10,... | collective-permute-start | bytes 1179656 | tf_op jit(solution)/shard_map/ppermute | solution.py:38
  62.6 0.8 collective-permute-start.14
  63.5 3.6 %collective-permute-done.15.refs_1_ = f32[8,32,384]{2,1,0:T(8,128)S(1)} collective-permute-done((f32[8,32,384]{2,1,0:T(8,128)S(1)}, f32[8,32,384]{2,1,0:T(8,128)S(1)}, u32[]{:S(2)}, u32[]{:S(2)}) %collective-permute-start.15) | collective-permute-done | bytes 393248 | tf_op jit(solution)/shard_map/ppermute | solution.py:38
  67.0 2.8 %collective-permute-start.12 = (f32[256,384]{1,0:T(8,128)S(1)}, f32[256,384]{1,0:T(8,128)}, u32[]{:S(2)}, u32[]{:S(2)}) collective-permute-start(f32[256,384]{1,0:T(8,128)S(1)} %get-tuple-element.98.refs_4_), channel_id=1, source_target_pairs={{0,6},{1,7},{2,0},{3,1},{4,2},{5,3},{6,4},{7,5},{8,14},{9,15},{10,... | collective-permute-start | bytes 1179656 | tf_op jit(solution)/shard_map/ppermute | solution.py:38
  69.8 6.0 %collective-permute-done.16.refs_2_ = f32[8,32,384]{2,1,0:T(8,128)S(1)} collective-permute-done((f32[8,32,384]{2,1,0:T(8,128)S(1)}, f32[8,32,384]{2,1,0:T(8,128)S(1)}, u32[]{:S(2)}, u32[]{:S(2)}) %collective-permute-start.16) | collective-permute-done | bytes 393248 | tf_op jit(solution)/shard_map/ppermute | solution.py:38
  75.8 0.0 collective-permute-done.17.refs_3_
  75.8 0.8 fold.1
  76.6 8.2 %all-to-all-start = ((f32[8,32,384]{2,1,0:T(8,128)}), f32[8,32,384]{2,1,0:T(8,128)S(1)}, u32[]{:S(2)}, u32[]{:S(2)}) async-start(f32[8,32,384]{2,1,0:T(8,128)} %fold.1), calls=%async_computation | async-start | bytes 786432 | tf_op jit(solution)/shard_map/all_to_all | solution.py:516
  84.8 0.0 collective-permute-done.13.refs_3_
  84.8 0.0 collective-permute-done.12.refs_2_
  84.9 5.9 %input_gradient.1 = (bf16[128,1024]{1,0:T(8,128)(2,1)}, f32[8,128]{1,0:T(8,128)S(1)}) custom-call(s32[3]{0:T(128)S(1)} %pad_add_fusion.place, bf16[1024,384]{1,0:T(8,128)(2,1)S(1)} %get-tuple-element.96.refs_0_, f32[512,384]{1,0:T(8,128)S(1)} %collective-permute-done.11.refs_1_, f32[256,384]{1,0:T(8,128)} %collective-permute-done.12.refs_2_, ...), custom_call_target="tpu_custom_call" | custom-call | flops 6442450944 | bytes 83886080 | tf_op jit(solution)/shard_map/input_gradient/pallas_call | solution.py:316
  90.8 7.7 %all-to-all-done.got = f32[8,32,384]{2,1,0:T(8,128)S(1)} async-done(((f32[8,32,384]{2,1,0:T(8,128)}), f32[8,32,384]{2,1,0:T(8,128)S(1)}, u32[]{:S(2)}, u32[]{:S(2)}) %all-to-all-start) | async-done | bytes 393248 | tf_op jit(solution)/shard_map/all_to_all | solution.py:516
  98.4 0.7 square_sum.1
  99.1 2.1 %collective-permute-start.18 = (f32[16,384]{1,0:T(8,128)S(1)}, f32[16,384]{1,0:T(8,128)S(1)}, u32[]{:S(2)}, u32[]{:S(2)}) collective-permute-start(f32[16,384]{1,0:T(8,128)S(1)} %get-tuple-element.109), channel_id=1, source_target_pairs={{0,1},{1,0},{2,3},{3,2},{4,5},{5,4},{6,7},{7,6},{8,9},{9,8},{10,11... | collective-permute-start | bytes 73736 | tf_op jit(solution)/shard_map/ppermute | solution.py:38
  101.3 8.9 %all_to_all.27 = f32[8,1,128]{2,1,0:T(1,128)S(1)} all-to-all(f32[8,1,128]{2,1,0:T(1,128)S(1)} %bitcast.14), channel_id=1, replica_groups=mesh['dp'=8,'seq'=32] {'dp'}, dimensions={0} | all-to-all | bytes 8192 | tf_op jit(solution)/shard_map/all_to_all | solution.py:521
  110.1 0.6 total_square.1
  110.7 8.1 %all-to-all-start.2 = ((f32[32,1,128]{2,1,0:T(1,128)}), f32[32,1,128]{2,1,0:T(1,128)S(1)}, u32[]{:S(2)}, u32[]{:S(2)}) async-start(f32[32,1,128]{2,1,0:T(1,128)} %bitcast.8), calls=%async_computation.2 | async-start | bytes 32768 | tf_op jit(solution)/shard_map/all_to_all | solution.py:524
  118.9 0.6 pair_rows.1
  119.5 1.5 %collective-permute-start.19 = (f32[8,384]{1,0:T(8,128)S(1)}, f32[8,384]{1,0:T(8,128)S(1)}, u32[]{:S(2)}, u32[]{:S(2)}) collective-permute-start(f32[8,384]{1,0:T(8,128)S(1)} %get-tuple-element.111), channel_id=1, source_target_pairs={{0,2},{1,3},{2,4},{3,5},{4,6},{5,7},{6,0},{7,1},{8,10},{9,11},{10,... | collective-permute-start | bytes 36872 | tf_op jit(solution)/shard_map/ppermute | solution.py:38
  120.9 2.4 %collective-permute-start.20 = (f32[8,384]{1,0:T(8,128)S(1)}, f32[8,384]{1,0:T(8,128)S(1)}, u32[]{:S(2)}, u32[]{:S(2)}) collective-permute-start(f32[8,384]{1,0:T(8,128)S(1)} %get-tuple-element.112), channel_id=1, source_target_pairs={{0,4},{1,5},{2,6},{3,7},{4,0},{5,1},{6,2},{7,3},{8,12},{9,13},{10,... | collective-permute-start | bytes 36872 | tf_op jit(solution)/shard_map/ppermute | solution.py:38
  123.3 1.2 collective-permute-start.21
  124.5 1.2 all-to-all-done.2
  125.7 0.4 collective-permute-done.21.refs_3_
  126.2 1.2 clip.1
  (15 shorter events, 0.1 us)
Async XLA Ops:
  0.7 1.0 copy-start
  1.7 0.9 copy-start.2
  4.4 17.1 %collective-permute-start.1 = (f32[22,64,128]{2,1,0:T(8,128)}, f32[22,64,128]{2,1,0:T(8,128)S(1)}, u32[]{:S(2)}, u32[]{:S(2)}) collective-permute-start(f32[22,64,128]{2,1,0:T(8,128)} %get-tuple-element.60), channel_id=1, source_target_pairs={{0,2},{1,3},{2,4},{3,5},{4,6},{5,7},{6,0},{7,1},{8,10},{9,11},{10,... | collective-permute-start | bytes 2162696 | tf_op jit(solution)/shard_map/ppermute | solution.py:38
  6.4 16.4 %collective-permute-start.2 = (f32[22,64,128]{2,1,0:T(8,128)S(1)}, f32[22,64,128]{2,1,0:T(8,128)S(1)}, u32[]{:S(2)}, u32[]{:S(2)}) collective-permute-start(f32[22,64,128]{2,1,0:T(8,128)S(1)} %get-tuple-element.61), channel_id=1, source_target_pairs={{0,6},{1,7},{2,0},{3,1},{4,2},{5,3},{6,4},{7,5},{8,14},{9,15},{10,... | collective-permute-start | bytes 2162696 | tf_op jit(solution)/shard_map/ppermute | solution.py:38
  7.7 5.0 %collective-permute-start = (f32[18,64,128]{2,1,0:T(8,128)}, f32[18,64,128]{2,1,0:T(8,128)S(1)}, u32[]{:S(2)}, u32[]{:S(2)}) collective-permute-start(f32[18,64,128]{2,1,0:T(8,128)} %get-tuple-element.58), channel_id=1, source_target_pairs={{0,1},{1,0},{2,3},{3,2},{4,5},{5,4},{6,7},{7,6},{8,9},{9,8},{10,11... | collective-permute-start | bytes 1769480 | tf_op jit(solution)/shard_map/ppermute | solution.py:38
  10.9 1.8 %copy-start.1 = (bf16[2,64,1024]{2,1,0:T(8,128)(2,1)S(1)}, bf16[2,64,1024]{2,1,0:T(8,128)(2,1)}, u32[]{:S(2)}) copy-start(bf16[2,64,1024]{2,1,0:T(8,128)(2,1)} %refs_0_.1) | copy-start | bytes 786436
  10.9 1.8 %copy-start.3 = (bf16[2,64,1024]{2,1,0:T(8,128)(2,1)S(1)}, bf16[2,64,1024]{2,1,0:T(8,128)(2,1)}, u32[]{:S(2)}) copy-start(bf16[2,64,1024]{2,1,0:T(8,128)(2,1)} %refs_1_.1) | copy-start | bytes 786436
  23.0 5.2 %collective-permute-start.3 = (f32[22,64,128]{2,1,0:T(8,128)S(1)}, f32[22,64,128]{2,1,0:T(8,128)S(1)}, u32[]{:S(2)}, u32[]{:S(2)}) collective-permute-start(f32[22,64,128]{2,1,0:T(8,128)S(1)} %get-tuple-element.62), channel_id=1, source_target_pairs={{0,1},{1,0},{2,3},{3,2},{4,5},{5,4},{6,7},{7,6},{8,9},{9,8},{10,11... | collective-permute-start | bytes 2162696 | tf_op jit(solution)/shard_map/ppermute | solution.py:38
  25.2 5.0 %collective-permute-start.6 = (f32[22,64,128]{2,1,0:T(8,128)S(1)}, f32[22,64,128]{2,1,0:T(8,128)S(1)}, u32[]{:S(2)}, u32[]{:S(2)}) collective-permute-start(f32[22,64,128]{2,1,0:T(8,128)S(1)} %get-tuple-element.64), channel_id=1, source_target_pairs={{0,1},{1,0},{2,3},{3,2},{4,5},{5,4},{6,7},{7,6},{8,9},{9,8},{10,11... | collective-permute-start | bytes 2162696 | tf_op jit(solution)/shard_map/ppermute | solution.py:38
  25.3 10.2 %collective-permute-start.4 = (f32[10,64,128]{2,1,0:T(8,128)S(1)}, f32[10,64,128]{2,1,0:T(8,128)S(1)}, u32[]{:S(2)}, u32[]{:S(2)}) collective-permute-start(f32[10,64,128]{2,1,0:T(8,128)S(1)} %slice.8), channel_id=1, source_target_pairs={{0,2},{1,3},{2,4},{3,5},{4,6},{5,7},{6,0},{7,1},{8,10},{9,11},{10,... | collective-permute-start | bytes 983048 | tf_op jit(solution)/shard_map/ppermute | solution.py:38
  26.6 8.9 %collective-permute-start.5 = (f32[10,64,128]{2,1,0:T(8,128)S(1)}, f32[10,64,128]{2,1,0:T(8,128)S(1)}, u32[]{:S(2)}, u32[]{:S(2)}) collective-permute-start(f32[10,64,128]{2,1,0:T(8,128)S(1)} %slice.9), channel_id=1, source_target_pairs={{0,6},{1,7},{2,0},{3,1},{4,2},{5,3},{6,4},{7,5},{8,14},{9,15},{10,... | collective-permute-start | bytes 983048 | tf_op jit(solution)/shard_map/ppermute | solution.py:38
  35.6 3.1 %collective-permute-start.7 = (f32[20,64,128]{2,1,0:T(8,128)S(1)}, f32[20,64,128]{2,1,0:T(8,128)S(1)}, u32[]{:S(2)}, u32[]{:S(2)}) collective-permute-start(f32[20,64,128]{2,1,0:T(8,128)S(1)} %relay.4.refs_0_), channel_id=1, source_target_pairs={{0,1},{1,0},{2,3},{3,2},{4,5},{5,4},{6,7},{7,6},{8,9},{9,8},{10,11... | collective-permute-start | bytes 1966088 | tf_op jit(solution)/shard_map/ppermute | solution.py:38
  40.8 6.4 %collective-permute-start.8 = (f32[2,128,128]{2,1,0:T(8,128)S(1)}, f32[2,128,128]{2,1,0:T(8,128)S(1)}, u32[]{:S(2)}, u32[]{:S(2)}) collective-permute-start(f32[2,128,128]{2,1,0:T(8,128)S(1)} %get-tuple-element.73), channel_id=1, source_target_pairs={{0,16},{1,17},{2,18},{3,19},{4,20},{5,21},{6,22},{7,23},{8,24},{9,... | collective-permute-start | bytes 393224 | tf_op jit(solution)/shard_map/ppermute | solution.py:38
  43.9 6.5 %collective-permute-start.9 = (f32[2,128,128]{2,1,0:T(8,128)S(1)}, f32[2,128,128]{2,1,0:T(8,128)S(1)}, u32[]{:S(2)}, u32[]{:S(2)}) collective-permute-start(f32[2,128,128]{2,1,0:T(8,128)S(1)} %get-tuple-element.74), channel_id=1, source_target_pairs={{0,8},{1,9},{2,10},{3,11},{4,12},{5,13},{6,14},{7,15},{8,16},{9,17... | collective-permute-start | bytes 393224 | tf_op jit(solution)/shard_map/ppermute | solution.py:38
  44.3 6.1 %collective-permute-start.10 = (f32[2,128,128]{2,1,0:T(8,128)S(1)}, f32[2,128,128]{2,1,0:T(8,128)S(1)}, u32[]{:S(2)}, u32[]{:S(2)}) collective-permute-start(f32[2,128,128]{2,1,0:T(8,128)S(1)} %get-tuple-element.75), channel_id=1, source_target_pairs={{0,24},{1,25},{2,26},{3,27},{4,28},{5,29},{6,30},{7,31},{8,0},{9,1... | collective-permute-start | bytes 393224 | tf_op jit(solution)/shard_map/ppermute | solution.py:38
  53.5 5.8 %collective-permute-start.11 = (f32[512,384]{1,0:T(8,128)S(1)}, f32[512,384]{1,0:T(8,128)S(1)}, u32[]{:S(2)}, u32[]{:S(2)}) collective-permute-start(f32[512,384]{1,0:T(8,128)S(1)} %get-tuple-element.97), channel_id=1, source_target_pairs={{0,1},{1,0},{2,3},{3,2},{4,5},{5,4},{6,7},{7,6},{8,9},{9,8},{10,11... | collective-permute-start | bytes 2359304 | tf_op jit(solution)/shard_map/ppermute | solution.py:38
  54.8 12.2 %collective-permute-start.15 = (f32[8,32,384]{2,1,0:T(8,128)S(1)}, f32[8,32,384]{2,1,0:T(8,128)S(1)}, u32[]{:S(2)}, u32[]{:S(2)}) collective-permute-start(f32[8,32,384]{2,1,0:T(8,128)S(1)} %get-tuple-element.103), channel_id=1, source_target_pairs={{0,16},{1,17},{2,18},{3,19},{4,20},{5,21},{6,22},{7,23},{8,24},{9,... | collective-permute-start | bytes 1179656 | tf_op jit(solution)/shard_map/ppermute | solution.py:38
  56.6 19.2 %collective-permute-start.16 = (f32[8,32,384]{2,1,0:T(8,128)S(1)}, f32[8,32,384]{2,1,0:T(8,128)S(1)}, u32[]{:S(2)}, u32[]{:S(2)}) collective-permute-start(f32[8,32,384]{2,1,0:T(8,128)S(1)} %get-tuple-element.104), channel_id=1, source_target_pairs={{0,8},{1,9},{2,10},{3,11},{4,12},{5,13},{6,14},{7,15},{8,16},{9,17... | collective-permute-start | bytes 1179656 | tf_op jit(solution)/shard_map/ppermute | solution.py:38
  58.1 17.8 %collective-permute-start.17 = (f32[8,32,384]{2,1,0:T(8,128)S(1)}, f32[8,32,384]{2,1,0:T(8,128)S(1)}, u32[]{:S(2)}, u32[]{:S(2)}) collective-permute-start(f32[8,32,384]{2,1,0:T(8,128)S(1)} %get-tuple-element.105), channel_id=1, source_target_pairs={{0,24},{1,25},{2,26},{3,27},{4,28},{5,29},{6,30},{7,31},{8,0},{9,1... | collective-permute-start | bytes 1179656 | tf_op jit(solution)/shard_map/ppermute | solution.py:38
  60.1 24.7 %collective-permute-start.13 = (f32[256,384]{1,0:T(8,128)}, f32[256,384]{1,0:T(8,128)S(1)}, u32[]{:S(2)}, u32[]{:S(2)}) collective-permute-start(f32[256,384]{1,0:T(8,128)} %get-tuple-element.99), channel_id=1, source_target_pairs={{0,4},{1,5},{2,6},{3,7},{4,0},{5,1},{6,2},{7,3},{8,12},{9,13},{10,... | collective-permute-start | bytes 1179656 | tf_op jit(solution)/shard_map/ppermute | solution.py:38
  62.6 22.2 %collective-permute-start.14 = (f32[256,384]{1,0:T(8,128)S(1)}, f32[256,384]{1,0:T(8,128)S(1)}, u32[]{:S(2)}, u32[]{:S(2)}) collective-permute-start(f32[256,384]{1,0:T(8,128)S(1)} %get-tuple-element.100), channel_id=1, source_target_pairs={{0,2},{1,3},{2,4},{3,5},{4,6},{5,7},{6,0},{7,1},{8,10},{9,11},{10,... | collective-permute-start | bytes 1179656 | tf_op jit(solution)/shard_map/ppermute | solution.py:38
  67.0 17.8 %collective-permute-start.12 = (f32[256,384]{1,0:T(8,128)S(1)}, f32[256,384]{1,0:T(8,128)}, u32[]{:S(2)}, u32[]{:S(2)}) collective-permute-start(f32[256,384]{1,0:T(8,128)S(1)} %get-tuple-element.98.refs_4_), channel_id=1, source_target_pairs={{0,6},{1,7},{2,0},{3,1},{4,2},{5,3},{6,4},{7,5},{8,14},{9,15},{10,... | collective-permute-start | bytes 1179656 | tf_op jit(solution)/shard_map/ppermute | solution.py:38
  76.6 21.8 %all-to-all-start = ((f32[8,32,384]{2,1,0:T(8,128)}), f32[8,32,384]{2,1,0:T(8,128)S(1)}, u32[]{:S(2)}, u32[]{:S(2)}) async-start(f32[8,32,384]{2,1,0:T(8,128)} %fold.1), calls=%async_computation | async-start | bytes 786432 | tf_op jit(solution)/shard_map/all_to_all | solution.py:516
  99.1 19.7 %collective-permute-start.18 = (f32[16,384]{1,0:T(8,128)S(1)}, f32[16,384]{1,0:T(8,128)S(1)}, u32[]{:S(2)}, u32[]{:S(2)}) collective-permute-start(f32[16,384]{1,0:T(8,128)S(1)} %get-tuple-element.109), channel_id=1, source_target_pairs={{0,1},{1,0},{2,3},{3,2},{4,5},{5,4},{6,7},{7,6},{8,9},{9,8},{10,11... | collective-permute-start | bytes 73736 | tf_op jit(solution)/shard_map/ppermute | solution.py:38
  110.7 15.0 %all-to-all-start.2 = ((f32[32,1,128]{2,1,0:T(1,128)}), f32[32,1,128]{2,1,0:T(1,128)S(1)}, u32[]{:S(2)}, u32[]{:S(2)}) async-start(f32[32,1,128]{2,1,0:T(1,128)} %bitcast.8), calls=%async_computation.2 | async-start | bytes 32768 | tf_op jit(solution)/shard_map/all_to_all | solution.py:524
  119.5 6.3 %collective-permute-start.19 = (f32[8,384]{1,0:T(8,128)S(1)}, f32[8,384]{1,0:T(8,128)S(1)}, u32[]{:S(2)}, u32[]{:S(2)}) collective-permute-start(f32[8,384]{1,0:T(8,128)S(1)} %get-tuple-element.111), channel_id=1, source_target_pairs={{0,2},{1,3},{2,4},{3,5},{4,6},{5,7},{6,0},{7,1},{8,10},{9,11},{10,... | collective-permute-start | bytes 36872 | tf_op jit(solution)/shard_map/ppermute | solution.py:38
  120.9 4.8 %collective-permute-start.20 = (f32[8,384]{1,0:T(8,128)S(1)}, f32[8,384]{1,0:T(8,128)S(1)}, u32[]{:S(2)}, u32[]{:S(2)}) collective-permute-start(f32[8,384]{1,0:T(8,128)S(1)} %get-tuple-element.112), channel_id=1, source_target_pairs={{0,4},{1,5},{2,6},{3,7},{4,0},{5,1},{6,2},{7,3},{8,12},{9,13},{10,... | collective-permute-start | bytes 36872 | tf_op jit(solution)/shard_map/ppermute | solution.py:38
  123.3 2.8 %collective-permute-start.21 = (f32[8,384]{1,0:T(8,128)S(1)}, f32[8,384]{1,0:T(8,128)S(1)}, u32[]{:S(2)}, u32[]{:S(2)}) collective-permute-start(f32[8,384]{1,0:T(8,128)S(1)} %get-tuple-element.113), channel_id=1, source_target_pairs={{0,6},{1,7},{2,0},{3,1},{4,2},{5,3},{6,4},{7,5},{8,14},{9,15},{10,... | collective-permute-start | bytes 36872 | tf_op jit(solution)/shard_map/ppermute | solution.py:38

commit v6 on v5

--- a/solution.py
+++ b/solution.py
@@ -333,22 +333,24 @@
     )(place, *sources, w_qkv)
 
 
-def fold_kernel(count, *refs):
+def fold_kernel(count, place, *refs):
     out = refs[-1]
+    half = out.shape[0] // 2
     for z in range(out.shape[0]):
-        out[z] = sum(ref[z] for ref in refs[:count])
-
-
-def fold(parts, after):
+        to = jnp.where(place[2] == 0, z, (z + half) % out.shape[0])
+        out[to] = sum(ref[z] for ref in refs[:count])
+
+
+def fold(place, parts, after):
     return pl.pallas_call(
         functools.partial(fold_kernel, len(parts)),
         out_shape=struct(parts[0].shape, F32),
-        in_specs=[VMEM] * len(parts) + [ANY],
+        in_specs=[SMEM] + [VMEM] * len(parts) + [ANY],
         out_specs=VMEM,
         compiler_params=pltpu.CompilerParams(vmem_limit_bytes=8 * MIB),
         cost_estimate=pl.CostEstimate(flops=MIB, bytes_accessed=2 * MIB, transcendentals=0),
         name="fold",
-    )(*parts, after)
+    )(place, *parts, after)
 
 
 def square_kernel(place, got, after, squares, own, theirs, rows_of):
@@ -375,22 +377,6 @@
         cost_estimate=pl.CostEstimate(flops=MIB, bytes_accessed=MIB, transcendentals=0),
         name="square_sum",
     )(place, got, after)
-
-
-def total_square_kernel(squares, out):
-    out[...] = jnp.broadcast_to(jnp.sum(squares[...], axis=0, keepdims=True), out.shape)
-
-
-def total_square(squares, count):
-    return pl.pallas_call(
-        total_square_kernel,
-        out_shape=struct((count, DH), F32),
-        in_specs=[VMEM],
-        out_specs=VMEM,
-        compiler_params=pltpu.CompilerParams(vmem_limit_bytes=4 * MIB),
-        cost_estimate=pl.CostEstimate(flops=4096, bytes_accessed=16384, transcendentals=0),
-        name="total_square",
-    )(squares)
 
 
 def pair_kernel(place, own, theirs, *refs):
@@ -512,16 +498,19 @@
     )
     back = [send(returns[dx - 1], dx=-dx) for dx in range(1, NX)]
     summands = pieces[:1] + [send(value, dy=dy) for value, dy in zip(pieces[1:], FAR_FIRST)]
-    folded = fold(summands, returns[0])
-    got = lax.all_to_all(folded, "dp", 0, 0)
+    folded = fold(place, summands, returns[0])
+    columns_of = []
+    for column in range(NY * GROUP):
+        turn = column % 2 * (dp_count // 2)
+        order = [(z + turn) % dp_count for z in range(dp_count)]
+        columns_of.append([z * NY * GROUP + column for z in order])
+    got = lax.all_to_all(folded, ("dp", "seq"), 0, 0, axis_index_groups=columns_of)
     grad_rows, done = input_gradient(place, (grad_proj, theirs, *back), total_rows, w_qkv)
     grad_inputs = grad_rows.reshape(user_count, row_count, feature_count)
 
-    squares, own, theirs = square_sum(place, got, done, dp_count)
-    squares = lax.all_to_all(squares, "dp", 0, 0, tiled=True)
+    squares, own, theirs = square_sum(place, got, done, dp_count * lax.axis_size("seq"))
+    squares = lax.all_to_all(squares, ("dp", "seq"), 0, 0, tiled=True)
     parts = pair_rows(place, own, send(theirs, dc=1))
-    squares = total_square(squares, lax.axis_size("seq"))
-    squares = lax.all_to_all(squares, "seq", 0, 0, tiled=True)
     parts = parts[:1] + tuple(send(parts[dx], dx=dx) for dx in range(1, NX))
     return (grad_inputs, clip(place, squares, parts))
 

time: 128 us -> 125 us (0.977)
  blocking collectives: 8.88 us -> 0 us
  starting transfers between devices: 54.2 us -> 59.5 us
    all_to_all x1 -> x0, blocking collectives: 8.88 us -> none  [body(): squares = lax.all_to_all(squares, 'dp', 0, 0, tiled=True)]
    all_to_all x2, starting transfers between devices: 16.3 us -> 23.3 us  [the longest x1 13 us: body(): squares = lax.all_to_all(squares, ('dp', 'seq'), 0, 0, tiled=True)]
    ppermute x22, waiting for transfers between devices: 26.1 us -> 28.2 us  [send(): return lax.ppermute(value, 'seq', seq_perm(dy, dx, dc))]
    ppermute x22, starting transfers between devices: 37.9 us -> 36.2 us  [send(): return lax.ppermute(value, 'seq', seq_perm(dy, dx, dc))]
    all_to_all x2, waiting for transfers between devices: 8.91 us -> 7.27 us  [the longest x1 4.38 us: body(): squares = lax.all_to_all(squares, ('dp', 'seq'), 0, 0, tiled=True)]
  transfers between devices with their start and end apart: 24 -> 24, of which waited for: 12 -> 15; matrix products, arithmetic and copies ran while one was open for 1% -> 1% of each run, Pallas kernels for 13% -> 13%
where the time goes in v6:
time: 125 us
  starting transfers between devices  59.5 us (48%)
  waiting for transfers between devices  35.5 us (28%)
  Pallas kernels  25.7 us (21%)
  local copies, waits for them, and re-layouts  3.19 us (3%)
    ppermute x22, starting transfers between devices, send(): return lax.ppermute(value, 'seq', seq_perm(dy, dx, dc))  36.2 us
    ppermute x22, waiting for transfers between devices, send(): return lax.ppermute(value, 'seq', seq_perm(dy, dx, dc))  28.2 us
    all_to_all x1, starting transfers between devices, body(): squares = lax.all_to_all(squares, ('dp', 'seq'), 0, 0, tiled=True)  13 us
    all_to_all x1, starting transfers between devices, body(): lax.all_to_all(folded, ('dp', 'seq'), 0, 0, axis_index_groups=columns_of)  10.3 us
    pallas_call x5, Pallas kernels, blocks(): pl.pallas_call(functools.partial(block_kernel, units), out_shape=(struct(...  8.77 us
    pallas_call x1, Pallas kernels, input_gradient(): pl.pallas_call(input_kernel, grid=(features // step,), out_shape=(struct(...  5.89 us
    all_to_all x1, waiting for transfers between devices, body(): squares = lax.all_to_all(squares, ('dp', 'seq'), 0, 0, tiled=True)  4.38 us
    pallas_call x1, Pallas kernels, gradients(): pl.pallas_call(functools.partial(grad_kernel, scaling, users, dp_count, c...  3.16 us
  transfers between devices with their start and end apart: 24, of which 15 were waited for; matrix products, arithmetic and copies ran while one was open for 1% of the time, Pallas kernels for 13%

profile of v6, /device:TPU:1, one launch (start us, length us, event | category | flops | bytes accessed | tf_op | source)
XLA Modules:
  0.0 124.9 jit_solution(2148350765830314609)
XLA Ops:
  0.7 0.1 pad_add_fusion.place
  0.7 0.9 copy-done
  1.7 0.9 copy-done.2
  2.6 1.8 %messages.1 = (f32[22,64,128]{2,1,0:T(8,128)}, f32[22,64,128]{2,1,0:T(8,128)S(1)}, f32[18,64,128]{2,1,0:T(8,128)}) custom-call(s32[3]{0:T(128)S(1)} %pad_add_fusion.place, bf16[2,64,1024]{2,1,0:T(8,128)(2,1)S(1)} %copy-done, bf16[2,64,1024]{2,1,0:T(8,128)(2,1)S(1)} %copy-done.2), custom_call_target="tpu_custom_call" | custom-call | flops 1048576 | bytes 3145728 | tf_op jit(solution)/shard_map/messages/pallas_call | solution.py:76
  4.4 2.0 %collective-permute-start.1 = (f32[22,64,128]{2,1,0:T(8,128)}, f32[22,64,128]{2,1,0:T(8,128)S(1)}, u32[]{:S(2)}, u32[]{:S(2)}) collective-permute-start(f32[22,64,128]{2,1,0:T(8,128)} %get-tuple-element.60), channel_id=1, source_target_pairs={{0,2},{1,3},{2,4},{3,5},{4,6},{5,7},{6,0},{7,1},{8,10},{9,11},{10,... | collective-permute-start | bytes 2162696 | tf_op jit(solution)/shard_map/ppermute | solution.py:38
  6.4 1.3 %collective-permute-start.2 = (f32[22,64,128]{2,1,0:T(8,128)S(1)}, f32[22,64,128]{2,1,0:T(8,128)S(1)}, u32[]{:S(2)}, u32[]{:S(2)}) collective-permute-start(f32[22,64,128]{2,1,0:T(8,128)S(1)} %get-tuple-element.61), channel_id=1, source_target_pairs={{0,6},{1,7},{2,0},{3,1},{4,2},{5,3},{6,4},{7,5},{8,14},{9,15},{10,... | collective-permute-start | bytes 2162696 | tf_op jit(solution)/shard_map/ppermute | solution.py:38
  7.7 3.2 %collective-permute-start = (f32[18,64,128]{2,1,0:T(8,128)}, f32[18,64,128]{2,1,0:T(8,128)S(1)}, u32[]{:S(2)}, u32[]{:S(2)}) collective-permute-start(f32[18,64,128]{2,1,0:T(8,128)} %get-tuple-element.58), channel_id=1, source_target_pairs={{0,1},{1,0},{2,3},{3,2},{4,5},{5,4},{6,7},{7,6},{8,9},{9,8},{10,11... | collective-permute-start | bytes 1769480 | tf_op jit(solution)/shard_map/ppermute | solution.py:38
  10.9 1.2 constant_dynamic-slice_fusion.2
  12.1 0.1 pad_maximum_fusion.w
  12.2 0.5 collective-permute-done.refs_2_
  12.7 2.0 %blocks.5 = (bf16[1024,256]{1,0:T(8,128)(2,1)S(1)}, bf16[256,384]{1,0:T(8,128)(2,1)S(1)}, bf16[256,128]{1,0:T(8,128)(2,1)S(1)}, f32[2,2,128,128]{3,2,1,0:T(8,128...) custom-call(s32[3]{0:T(128)S(1)} %pad_add_fusion.place, bf16[1024,384]{1,0:T(8,128)(2,1)S(1)} %pad_maximum_fusion.w, ...), custom_call_target="tpu_custom_call" | custom-call | flops 201326592 | bytes 4194304 | tf_op jit(solution)/shard_map/blocks/pallas_call | solution.py:148
  14.7 6.8 %collective-permute-done.1.refs_0_ = f32[22,64,128]{2,1,0:T(8,128)S(1)} collective-permute-done((f32[22,64,128]{2,1,0:T(8,128)}, f32[22,64,128]{2,1,0:T(8,128)S(1)}, u32[]{:S(2)}, u32[]{:S(2)}) %collective-permute-start.1) | collective-permute-done | bytes 720928 | tf_op jit(solution)/shard_map/ppermute | solution.py:38
  21.5 1.4 %collective-permute-done.2.refs_1_.refs_0_ = f32[22,64,128]{2,1,0:T(8,128)S(1)} collective-permute-done((f32[22,64,128]{2,1,0:T(8,128)S(1)}, f32[22,64,128]{2,1,0:T(8,128)S(1)}, u32[]{:S(2)}, u32[]{:S(2)}) %collective-permute-start.2) | collective-permute-done | bytes 720928 | tf_op jit(solution)/shard_map/ppermute | solution.py:38
  22.9 0.1 relay.3
  23.0 2.2 %collective-permute-start.3 = (f32[22,64,128]{2,1,0:T(8,128)S(1)}, f32[22,64,128]{2,1,0:T(8,128)S(1)}, u32[]{:S(2)}, u32[]{:S(2)}) collective-permute-start(f32[22,64,128]{2,1,0:T(8,128)S(1)} %get-tuple-element.62), channel_id=1, source_target_pairs={{0,1},{1,0},{2,3},{3,2},{4,5},{5,4},{6,7},{7,6},{8,9},{9,8},{10,11... | collective-permute-start | bytes 2162696 | tf_op jit(solution)/shard_map/ppermute | solution.py:38
  25.2 0.1 collective-permute-start.6
  25.3 1.3 %collective-permute-start.4 = (f32[10,64,128]{2,1,0:T(8,128)S(1)}, f32[10,64,128]{2,1,0:T(8,128)S(1)}, u32[]{:S(2)}, u32[]{:S(2)}) collective-permute-start(f32[10,64,128]{2,1,0:T(8,128)S(1)} %slice.8), channel_id=1, source_target_pairs={{0,2},{1,3},{2,4},{3,5},{4,6},{5,7},{6,0},{7,1},{8,10},{9,11},{10,... | collective-permute-start | bytes 983048 | tf_op jit(solution)/shard_map/ppermute | solution.py:38
  26.6 1.6 %collective-permute-start.5 = (f32[10,64,128]{2,1,0:T(8,128)S(1)}, f32[10,64,128]{2,1,0:T(8,128)S(1)}, u32[]{:S(2)}, u32[]{:S(2)}) collective-permute-start(f32[10,64,128]{2,1,0:T(8,128)S(1)} %slice.9), channel_id=1, source_target_pairs={{0,6},{1,7},{2,0},{3,1},{4,2},{5,3},{6,4},{7,5},{8,14},{9,15},{10,... | collective-permute-start | bytes 983048 | tf_op jit(solution)/shard_map/ppermute | solution.py:38
  28.2 0.0 collective-permute-done.3.refs_1_
  28.2 2.0 %blocks.6 = (bf16[1024,256]{1,0:T(8,128)(2,1)S(1)}, bf16[256,384]{1,0:T(8,128)(2,1)S(1)}, bf16[256,128]{1,0:T(8,128)(2,1)S(1)}, f32[2,2,128,128]{3,2,1,0:T(8,128...) custom-call(s32[3]{0:T(128)S(1)} %pad_add_fusion.place, bf16[1024,384]{1,0:T(8,128)(2,1)S(1)} %pad_maximum_fusion.w, ...), custom_call_target="tpu_custom_call" | custom-call | flops 201326592 | bytes 4194304 | tf_op jit(solution)/shard_map/blocks/pallas_call | solution.py:148
  30.2 0.0 collective-permute-done.6.refs_1_
  30.2 2.0 %blocks.7 = (bf16[1024,256]{1,0:T(8,128)(2,1)S(1)}, bf16[256,384]{1,0:T(8,128)(2,1)S(1)}, bf16[256,128]{1,0:T(8,128)(2,1)S(1)}, f32[2,2,128,128]{3,2,1,0:T(8,128...) custom-call(s32[3]{0:T(128)S(1)} %pad_add_fusion.place, bf16[1024,384]{1,0:T(8,128)(2,1)S(1)} %pad_maximum_fusion.w, ...), custom_call_target="tpu_custom_call" | custom-call | flops 201326592 | bytes 4194304 | tf_op jit(solution)/shard_map/blocks/pallas_call | solution.py:148
  32.2 3.3 %collective-permute-done.4.refs_0_ = f32[10,64,128]{2,1,0:T(8,128)S(1)} collective-permute-done((f32[10,64,128]{2,1,0:T(8,128)S(1)}, f32[10,64,128]{2,1,0:T(8,128)S(1)}, u32[]{:S(2)}, u32[]{:S(2)}) %collective-permute-start.4) | collective-permute-done | bytes 327712 | tf_op jit(solution)/shard_map/ppermute | solution.py:38
  35.6 1.4 %collective-permute-start.7 = (f32[20,64,128]{2,1,0:T(8,128)S(1)}, f32[20,64,128]{2,1,0:T(8,128)S(1)}, u32[]{:S(2)}, u32[]{:S(2)}) collective-permute-start(f32[20,64,128]{2,1,0:T(8,128)S(1)} %relay.4.refs_0_), channel_id=1, source_target_pairs={{0,1},{1,0},{2,3},{3,2},{4,5},{5,4},{6,7},{7,6},{8,9},{9,8},{10,11... | collective-permute-start | bytes 1966088 | tf_op jit(solution)/shard_map/ppermute | solution.py:38
  37.0 1.4 %blocks.8 = (bf16[1024,128]{1,0:T(8,128)(2,1)S(1)}, bf16[128,384]{1,0:T(8,128)(2,1)S(1)}, bf16[128,128]{1,0:T(8,128)(2,1)S(1)}, f32[1,2,128,128]{3,2,1,0:T(8,128...) custom-call(s32[3]{0:T(128)S(1)} %pad_add_fusion.place, bf16[1024,384]{1,0:T(8,128)(2,1)S(1)} %pad_maximum_fusion.w, ...), custom_call_target="tpu_custom_call" | custom-call | flops 100663296 | bytes 4194304 | tf_op jit(solution)/shard_map/blocks/pallas_call | solution.py:148
  38.4 0.3 collective-permute-done.7.refs_0_
  38.7 1.4 %blocks.9 = (bf16[1024,128]{1,0:T(8,128)(2,1)S(1)}, bf16[128,384]{1,0:T(8,128)(2,1)S(1)}, bf16[128,128]{1,0:T(8,128)(2,1)S(1)}, f32[1,2,128,128]{3,2,1,0:T(8,128...) custom-call(s32[3]{0:T(128)S(1)} %pad_add_fusion.place, bf16[1024,384]{1,0:T(8,128)(2,1)S(1)} %pad_maximum_fusion.w, ...), custom_call_target="tpu_custom_call" | custom-call | flops 100663296 | bytes 4194304 | tf_op jit(solution)/shard_map/blocks/pallas_call | solution.py:148
  40.1 0.6 totals.1
  40.8 3.1 %collective-permute-start.8 = (f32[2,128,128]{2,1,0:T(8,128)S(1)}, f32[2,128,128]{2,1,0:T(8,128)S(1)}, u32[]{:S(2)}, u32[]{:S(2)}) collective-permute-start(f32[2,128,128]{2,1,0:T(8,128)S(1)} %get-tuple-element.73), channel_id=1, source_target_pairs={{0,16},{1,17},{2,18},{3,19},{4,20},{5,21},{6,22},{7,23},{8,24},{9,... | collective-permute-start | bytes 393224 | tf_op jit(solution)/shard_map/ppermute | solution.py:38
  43.9 0.4 collective-permute-start.9
  44.3 2.3 %collective-permute-start.10 = (f32[2,128,128]{2,1,0:T(8,128)S(1)}, f32[2,128,128]{2,1,0:T(8,128)S(1)}, u32[]{:S(2)}, u32[]{:S(2)}) collective-permute-start(f32[2,128,128]{2,1,0:T(8,128)S(1)} %get-tuple-element.75), channel_id=1, source_target_pairs={{0,24},{1,25},{2,26},{3,27},{4,28},{5,29},{6,30},{7,31},{8,0},{9,1... | collective-permute-start | bytes 393224 | tf_op jit(solution)/shard_map/ppermute | solution.py:38
  46.6 0.6 collective-permute-done.8.refs_0_
  47.2 3.2 %collective-permute-done.9.refs_1_ = f32[2,128,128]{2,1,0:T(8,128)S(1)} collective-permute-done((f32[2,128,128]{2,1,0:T(8,128)S(1)}, f32[2,128,128]{2,1,0:T(8,128)S(1)}, u32[]{:S(2)}, u32[]{:S(2)}) %collective-permute-start.9) | collective-permute-done | bytes 131104 | tf_op jit(solution)/shard_map/ppermute | solution.py:38
  50.4 0.0 collective-permute-done.10.refs_2_
  50.4 3.2 %gradients.1 = (bf16[1024,384]{1,0:T(8,128)(2,1)S(1)}, f32[512,384]{1,0:T(8,128)S(1)}, f32[8,32,384]{2,1,0:T(8,128)S(1)}, f32[8,32,384]{2,1,0:T(8,128)S(1)}, f32...) custom-call(s32[3]{0:T(128)S(1)} %pad_add_fusion.place, f32[2,128,128]{2,1,0:T(8,128)S(1)} %collective-permute-done.8.refs_0_, ...), custom_call_target="tpu_custom_call" | custom-call | flops 805306368 | bytes 10485760 | tf_op jit(solution)/shard_map/gradients/pallas_call | solution.py:270
  53.5 1.3 %collective-permute-start.11 = (f32[512,384]{1,0:T(8,128)S(1)}, f32[512,384]{1,0:T(8,128)S(1)}, u32[]{:S(2)}, u32[]{:S(2)}) collective-permute-start(f32[512,384]{1,0:T(8,128)S(1)} %get-tuple-element.97), channel_id=1, source_target_pairs={{0,1},{1,0},{2,3},{3,2},{4,5},{5,4},{6,7},{7,6},{8,9},{9,8},{10,11... | collective-permute-start | bytes 2359304 | tf_op jit(solution)/shard_map/ppermute | solution.py:38
  54.8 1.8 %collective-permute-start.15 = (f32[8,32,384]{2,1,0:T(8,128)S(1)}, f32[8,32,384]{2,1,0:T(8,128)S(1)}, u32[]{:S(2)}, u32[]{:S(2)}) collective-permute-start(f32[8,32,384]{2,1,0:T(8,128)S(1)} %get-tuple-element.103), channel_id=1, source_target_pairs={{0,16},{1,17},{2,18},{3,19},{4,20},{5,21},{6,22},{7,23},{8,24},{9,... | collective-permute-start | bytes 1179656 | tf_op jit(solution)/shard_map/ppermute | solution.py:38
  56.6 1.5 %collective-permute-start.16 = (f32[8,32,384]{2,1,0:T(8,128)S(1)}, f32[8,32,384]{2,1,0:T(8,128)S(1)}, u32[]{:S(2)}, u32[]{:S(2)}) collective-permute-start(f32[8,32,384]{2,1,0:T(8,128)S(1)} %get-tuple-element.104), channel_id=1, source_target_pairs={{0,8},{1,9},{2,10},{3,11},{4,12},{5,13},{6,14},{7,15},{8,16},{9,17... | collective-permute-start | bytes 1179656 | tf_op jit(solution)/shard_map/ppermute | solution.py:38
  58.1 1.2 collective-permute-start.17
  59.3 0.8 relay.5
  60.1 2.5 %collective-permute-start.13 = (f32[256,384]{1,0:T(8,128)}, f32[256,384]{1,0:T(8,128)S(1)}, u32[]{:S(2)}, u32[]{:S(2)}) collective-permute-start(f32[256,384]{1,0:T(8,128)} %get-tuple-element.99), channel_id=1, source_target_pairs={{0,4},{1,5},{2,6},{3,7},{4,0},{5,1},{6,2},{7,3},{8,12},{9,13},{10,... | collective-permute-start | bytes 1179656 | tf_op jit(solution)/shard_map/ppermute | solution.py:38
  62.6 0.8 collective-permute-start.14
  63.5 3.6 %collective-permute-done.15.refs_1_ = f32[8,32,384]{2,1,0:T(8,128)S(1)} collective-permute-done((f32[8,32,384]{2,1,0:T(8,128)S(1)}, f32[8,32,384]{2,1,0:T(8,128)S(1)}, u32[]{:S(2)}, u32[]{:S(2)}) %collective-permute-start.15) | collective-permute-done | bytes 393248 | tf_op jit(solution)/shard_map/ppermute | solution.py:38
  67.0 2.8 %collective-permute-start.12 = (f32[256,384]{1,0:T(8,128)S(1)}, f32[256,384]{1,0:T(8,128)}, u32[]{:S(2)}, u32[]{:S(2)}) collective-permute-start(f32[256,384]{1,0:T(8,128)S(1)} %get-tuple-element.98.refs_4_), channel_id=1, source_target_pairs={{0,6},{1,7},{2,0},{3,1},{4,2},{5,3},{6,4},{7,5},{8,14},{9,15},{10,... | collective-permute-start | bytes 1179656 | tf_op jit(solution)/shard_map/ppermute | solution.py:38
  69.8 6.0 %collective-permute-done.16.refs_2_ = f32[8,32,384]{2,1,0:T(8,128)S(1)} collective-permute-done((f32[8,32,384]{2,1,0:T(8,128)S(1)}, f32[8,32,384]{2,1,0:T(8,128)S(1)}, u32[]{:S(2)}, u32[]{:S(2)}) %collective-permute-start.16) | collective-permute-done | bytes 393248 | tf_op jit(solution)/shard_map/ppermute | solution.py:38
  75.8 0.0 collective-permute-done.17.refs_3_
  75.8 1.4 %fold.1 = f32[8,32,384]{2,1,0:T(8,128)} custom-call(s32[3]{0:T(128)S(1)} %pad_add_fusion.place, f32[8,32,384]{2,1,0:T(8,128)S(1)} %get-tuple-element.102.refs_0_, f32[8,32,384]{2,1,0:T(8,128)S(1)} %collective-permute-done.15.refs_1_, f32[8,32,384]{2,1,0:T(8,128)S(1)} %collective-permute-done.16.refs_2_, f32[8,32,384]{2,1,0:T(8,128)S(1)} %collective-permute-done.17.refs_3_, ...), custom_call_target="tpu_custom_call" | custom-call | flops 1048576 | bytes 2097152 | tf_op jit(solution)/shard_map/fold/pallas_call | solution.py:345
  77.2 10.3 %all-to-all-start = ((f32[8,32,384]{2,1,0:T(8,128)}), f32[8,32,384]{2,1,0:T(8,128)S(1)}, u32[]{:S(2)}, u32[]{:S(2)}) async-start(f32[8,32,384]{2,1,0:T(8,128)} %fold.1), calls=%async_computation | async-start | bytes 786432 | tf_op jit(solution)/shard_map/all_to_all | solution.py:507
  87.5 0.0 collective-permute-done.13.refs_3_
  87.5 5.9 %input_gradient.1 = (bf16[128,1024]{1,0:T(8,128)(2,1)}, f32[8,128]{1,0:T(8,128)S(1)}) custom-call(s32[3]{0:T(128)S(1)} %pad_add_fusion.place, bf16[1024,384]{1,0:T(8,128)(2,1)S(1)} %get-tuple-element.96.refs_0_, f32[512,384]{1,0:T(8,128)S(1)} %collective-permute-done.11.refs_1_, f32[256,384]{1,0:T(8,128)} %collective-permute-done.12.refs_2_, ...), custom_call_target="tpu_custom_call" | custom-call | flops 6442450944 | bytes 83886080 | tf_op jit(solution)/shard_map/input_gradient/pallas_call | solution.py:316
  93.4 2.9 %all-to-all-done.got = f32[8,32,384]{2,1,0:T(8,128)S(1)} async-done(((f32[8,32,384]{2,1,0:T(8,128)}), f32[8,32,384]{2,1,0:T(8,128)S(1)}, u32[]{:S(2)}, u32[]{:S(2)}) %all-to-all-start) | async-done | bytes 393248 | tf_op jit(solution)/shard_map/all_to_all | solution.py:507
  96.3 1.3 %square_sum.1 = (f32[256,128]{1,0:T(8,128)}, f32[16,384]{1,0:T(8,128)S(1)}, f32[16,384]{1,0:T(8,128)S(1)}) custom-call(s32[3]{0:T(128)S(1)} %pad_add_fusion.place, f32[8,32,384]{2,1,0:T(8,128)S(1)} %all-to-all-done.got, f32[8,128]{1,0:T(8,128)S(1)} %get-tuple-element.106.after), custom_call_target="tpu_custom_call" | custom-call | flops 1048576 | bytes 1048576 | tf_op jit(solution)/shard_map/square_sum/pallas_call | solution.py:370
  97.6 13.0 %all-to-all-start.1 = ((f32[256,1,128]{2,1,0:T(1,128)}), f32[256,1,128]{2,1,0:T(1,128)S(1)}, u32[]{:S(2)}, u32[]{:S(2)}) async-start(f32[256,1,128]{2,1,0:T(1,128)} %bitcast.5), calls=%async_computation.1 | async-start | bytes 262144 | tf_op jit(solution)/shard_map/all_to_all | solution.py:512
  110.7 2.2 %collective-permute-start.18 = (f32[16,384]{1,0:T(8,128)S(1)}, f32[16,384]{1,0:T(8,128)S(1)}, u32[]{:S(2)}, u32[]{:S(2)}) collective-permute-start(f32[16,384]{1,0:T(8,128)S(1)} %get-tuple-element.109), channel_id=1, source_target_pairs={{0,1},{1,0},{2,3},{3,2},{4,5},{5,4},{6,7},{7,6},{8,9},{9,8},{10,11... | collective-permute-start | bytes 73736 | tf_op jit(solution)/shard_map/ppermute | solution.py:38
  112.9 0.8 collective-permute-done.18.theirs
  113.7 0.6 pair_rows.1
  114.3 0.1 collective-permute-start.19
  114.4 2.0 %collective-permute-start.20 = (f32[8,384]{1,0:T(8,128)S(1)}, f32[8,384]{1,0:T(8,128)S(1)}, u32[]{:S(2)}, u32[]{:S(2)}) collective-permute-start(f32[8,384]{1,0:T(8,128)S(1)} %get-tuple-element.112), channel_id=1, source_target_pairs={{0,4},{1,5},{2,6},{3,7},{4,0},{5,1},{6,2},{7,3},{8,12},{9,13},{10,... | collective-permute-start | bytes 36872 | tf_op jit(solution)/shard_map/ppermute | solution.py:38
  116.4 1.2 collective-permute-start.21
  117.6 0.9 collective-permute-done.19.refs_1_
  118.5 0.4 collective-permute-done.20.refs_2_
  118.9 0.4 collective-permute-done.21.refs_3_
  119.2 4.4 %all-to-all-done.1 = f32[256,1,128]{2,1,0:T(1,128)S(1)} async-done(((f32[256,1,128]{2,1,0:T(1,128)}), f32[256,1,128]{2,1,0:T(1,128)S(1)}, u32[]{:S(2)}, u32[]{:S(2)}) %all-to-all-start.1) | async-done | bytes 131104 | tf_op jit(solution)/shard_map/all_to_all | solution.py:512
  123.6 1.2 clip.1
  (13 shorter events, 0.1 us)
Async XLA Ops:
  0.7 1.0 copy-start
  1.7 0.9 copy-start.2
  4.4 17.1 %collective-permute-start.1 = (f32[22,64,128]{2,1,0:T(8,128)}, f32[22,64,128]{2,1,0:T(8,128)S(1)}, u32[]{:S(2)}, u32[]{:S(2)}) collective-permute-start(f32[22,64,128]{2,1,0:T(8,128)} %get-tuple-element.60), channel_id=1, source_target_pairs={{0,2},{1,3},{2,4},{3,5},{4,6},{5,7},{6,0},{7,1},{8,10},{9,11},{10,... | collective-permute-start | bytes 2162696 | tf_op jit(solution)/shard_map/ppermute | solution.py:38
  6.4 16.4 %collective-permute-start.2 = (f32[22,64,128]{2,1,0:T(8,128)S(1)}, f32[22,64,128]{2,1,0:T(8,128)S(1)}, u32[]{:S(2)}, u32[]{:S(2)}) collective-permute-start(f32[22,64,128]{2,1,0:T(8,128)S(1)} %get-tuple-element.61), channel_id=1, source_target_pairs={{0,6},{1,7},{2,0},{3,1},{4,2},{5,3},{6,4},{7,5},{8,14},{9,15},{10,... | collective-permute-start | bytes 2162696 | tf_op jit(solution)/shard_map/ppermute | solution.py:38
  7.7 5.0 %collective-permute-start = (f32[18,64,128]{2,1,0:T(8,128)}, f32[18,64,128]{2,1,0:T(8,128)S(1)}, u32[]{:S(2)}, u32[]{:S(2)}) collective-permute-start(f32[18,64,128]{2,1,0:T(8,128)} %get-tuple-element.58), channel_id=1, source_target_pairs={{0,1},{1,0},{2,3},{3,2},{4,5},{5,4},{6,7},{7,6},{8,9},{9,8},{10,11... | collective-permute-start | bytes 1769480 | tf_op jit(solution)/shard_map/ppermute | solution.py:38
  10.9 1.8 %copy-start.1 = (bf16[2,64,1024]{2,1,0:T(8,128)(2,1)S(1)}, bf16[2,64,1024]{2,1,0:T(8,128)(2,1)}, u32[]{:S(2)}) copy-start(bf16[2,64,1024]{2,1,0:T(8,128)(2,1)} %refs_0_.1) | copy-start | bytes 786436
  10.9 1.8 %copy-start.3 = (bf16[2,64,1024]{2,1,0:T(8,128)(2,1)S(1)}, bf16[2,64,1024]{2,1,0:T(8,128)(2,1)}, u32[]{:S(2)}) copy-start(bf16[2,64,1024]{2,1,0:T(8,128)(2,1)} %refs_1_.1) | copy-start | bytes 786436
  23.0 5.2 %collective-permute-start.3 = (f32[22,64,128]{2,1,0:T(8,128)S(1)}, f32[22,64,128]{2,1,0:T(8,128)S(1)}, u32[]{:S(2)}, u32[]{:S(2)}) collective-permute-start(f32[22,64,128]{2,1,0:T(8,128)S(1)} %get-tuple-element.62), channel_id=1, source_target_pairs={{0,1},{1,0},{2,3},{3,2},{4,5},{5,4},{6,7},{7,6},{8,9},{9,8},{10,11... | collective-permute-start | bytes 2162696 | tf_op jit(solution)/shard_map/ppermute | solution.py:38
  25.2 5.0 %collective-permute-start.6 = (f32[22,64,128]{2,1,0:T(8,128)S(1)}, f32[22,64,128]{2,1,0:T(8,128)S(1)}, u32[]{:S(2)}, u32[]{:S(2)}) collective-permute-start(f32[22,64,128]{2,1,0:T(8,128)S(1)} %get-tuple-element.64), channel_id=1, source_target_pairs={{0,1},{1,0},{2,3},{3,2},{4,5},{5,4},{6,7},{7,6},{8,9},{9,8},{10,11... | collective-permute-start | bytes 2162696 | tf_op jit(solution)/shard_map/ppermute | solution.py:38
  25.3 10.2 %collective-permute-start.4 = (f32[10,64,128]{2,1,0:T(8,128)S(1)}, f32[10,64,128]{2,1,0:T(8,128)S(1)}, u32[]{:S(2)}, u32[]{:S(2)}) collective-permute-start(f32[10,64,128]{2,1,0:T(8,128)S(1)} %slice.8), channel_id=1, source_target_pairs={{0,2},{1,3},{2,4},{3,5},{4,6},{5,7},{6,0},{7,1},{8,10},{9,11},{10,... | collective-permute-start | bytes 983048 | tf_op jit(solution)/shard_map/ppermute | solution.py:38
  26.6 8.9 %collective-permute-start.5 = (f32[10,64,128]{2,1,0:T(8,128)S(1)}, f32[10,64,128]{2,1,0:T(8,128)S(1)}, u32[]{:S(2)}, u32[]{:S(2)}) collective-permute-start(f32[10,64,128]{2,1,0:T(8,128)S(1)} %slice.9), channel_id=1, source_target_pairs={{0,6},{1,7},{2,0},{3,1},{4,2},{5,3},{6,4},{7,5},{8,14},{9,15},{10,... | collective-permute-start | bytes 983048 | tf_op jit(solution)/shard_map/ppermute | solution.py:38
  35.6 3.1 %collective-permute-start.7 = (f32[20,64,128]{2,1,0:T(8,128)S(1)}, f32[20,64,128]{2,1,0:T(8,128)S(1)}, u32[]{:S(2)}, u32[]{:S(2)}) collective-permute-start(f32[20,64,128]{2,1,0:T(8,128)S(1)} %relay.4.refs_0_), channel_id=1, source_target_pairs={{0,1},{1,0},{2,3},{3,2},{4,5},{5,4},{6,7},{7,6},{8,9},{9,8},{10,11... | collective-permute-start | bytes 1966088 | tf_op jit(solution)/shard_map/ppermute | solution.py:38
  40.8 6.4 %collective-permute-start.8 = (f32[2,128,128]{2,1,0:T(8,128)S(1)}, f32[2,128,128]{2,1,0:T(8,128)S(1)}, u32[]{:S(2)}, u32[]{:S(2)}) collective-permute-start(f32[2,128,128]{2,1,0:T(8,128)S(1)} %get-tuple-element.73), channel_id=1, source_target_pairs={{0,16},{1,17},{2,18},{3,19},{4,20},{5,21},{6,22},{7,23},{8,24},{9,... | collective-permute-start | bytes 393224 | tf_op jit(solution)/shard_map/ppermute | solution.py:38
  43.9 6.5 %collective-permute-start.9 = (f32[2,128,128]{2,1,0:T(8,128)S(1)}, f32[2,128,128]{2,1,0:T(8,128)S(1)}, u32[]{:S(2)}, u32[]{:S(2)}) collective-permute-start(f32[2,128,128]{2,1,0:T(8,128)S(1)} %get-tuple-element.74), channel_id=1, source_target_pairs={{0,8},{1,9},{2,10},{3,11},{4,12},{5,13},{6,14},{7,15},{8,16},{9,17... | collective-permute-start | bytes 393224 | tf_op jit(solution)/shard_map/ppermute | solution.py:38
  44.3 6.1 %collective-permute-start.10 = (f32[2,128,128]{2,1,0:T(8,128)S(1)}, f32[2,128,128]{2,1,0:T(8,128)S(1)}, u32[]{:S(2)}, u32[]{:S(2)}) collective-permute-start(f32[2,128,128]{2,1,0:T(8,128)S(1)} %get-tuple-element.75), channel_id=1, source_target_pairs={{0,24},{1,25},{2,26},{3,27},{4,28},{5,29},{6,30},{7,31},{8,0},{9,1... | collective-permute-start | bytes 393224 | tf_op jit(solution)/shard_map/ppermute | solution.py:38
  53.5 5.8 %collective-permute-start.11 = (f32[512,384]{1,0:T(8,128)S(1)}, f32[512,384]{1,0:T(8,128)S(1)}, u32[]{:S(2)}, u32[]{:S(2)}) collective-permute-start(f32[512,384]{1,0:T(8,128)S(1)} %get-tuple-element.97), channel_id=1, source_target_pairs={{0,1},{1,0},{2,3},{3,2},{4,5},{5,4},{6,7},{7,6},{8,9},{9,8},{10,11... | collective-permute-start | bytes 2359304 | tf_op jit(solution)/shard_map/ppermute | solution.py:38
  54.8 12.2 %collective-permute-start.15 = (f32[8,32,384]{2,1,0:T(8,128)S(1)}, f32[8,32,384]{2,1,0:T(8,128)S(1)}, u32[]{:S(2)}, u32[]{:S(2)}) collective-permute-start(f32[8,32,384]{2,1,0:T(8,128)S(1)} %get-tuple-element.103), channel_id=1, source_target_pairs={{0,16},{1,17},{2,18},{3,19},{4,20},{5,21},{6,22},{7,23},{8,24},{9,... | collective-permute-start | bytes 1179656 | tf_op jit(solution)/shard_map/ppermute | solution.py:38
  56.6 19.2 %collective-permute-start.16 = (f32[8,32,384]{2,1,0:T(8,128)S(1)}, f32[8,32,384]{2,1,0:T(8,128)S(1)}, u32[]{:S(2)}, u32[]{:S(2)}) collective-permute-start(f32[8,32,384]{2,1,0:T(8,128)S(1)} %get-tuple-element.104), channel_id=1, source_target_pairs={{0,8},{1,9},{2,10},{3,11},{4,12},{5,13},{6,14},{7,15},{8,16},{9,17... | collective-permute-start | bytes 1179656 | tf_op jit(solution)/shard_map/ppermute | solution.py:38
  58.1 17.8 %collective-permute-start.17 = (f32[8,32,384]{2,1,0:T(8,128)S(1)}, f32[8,32,384]{2,1,0:T(8,128)S(1)}, u32[]{:S(2)}, u32[]{:S(2)}) collective-permute-start(f32[8,32,384]{2,1,0:T(8,128)S(1)} %get-tuple-element.105), channel_id=1, source_target_pairs={{0,24},{1,25},{2,26},{3,27},{4,28},{5,29},{6,30},{7,31},{8,0},{9,1... | collective-permute-start | bytes 1179656 | tf_op jit(solution)/shard_map/ppermute | solution.py:38
  60.1 27.4 %collective-permute-start.13 = (f32[256,384]{1,0:T(8,128)}, f32[256,384]{1,0:T(8,128)S(1)}, u32[]{:S(2)}, u32[]{:S(2)}) collective-permute-start(f32[256,384]{1,0:T(8,128)} %get-tuple-element.99), channel_id=1, source_target_pairs={{0,4},{1,5},{2,6},{3,7},{4,0},{5,1},{6,2},{7,3},{8,12},{9,13},{10,... | collective-permute-start | bytes 1179656 | tf_op jit(solution)/shard_map/ppermute | solution.py:38
  62.6 24.8 %collective-permute-start.14 = (f32[256,384]{1,0:T(8,128)S(1)}, f32[256,384]{1,0:T(8,128)S(1)}, u32[]{:S(2)}, u32[]{:S(2)}) collective-permute-start(f32[256,384]{1,0:T(8,128)S(1)} %get-tuple-element.100), channel_id=1, source_target_pairs={{0,2},{1,3},{2,4},{3,5},{4,6},{5,7},{6,0},{7,1},{8,10},{9,11},{10,... | collective-permute-start | bytes 1179656 | tf_op jit(solution)/shard_map/ppermute | solution.py:38
  67.0 20.5 %collective-permute-start.12 = (f32[256,384]{1,0:T(8,128)S(1)}, f32[256,384]{1,0:T(8,128)}, u32[]{:S(2)}, u32[]{:S(2)}) collective-permute-start(f32[256,384]{1,0:T(8,128)S(1)} %get-tuple-element.98.refs_4_), channel_id=1, source_target_pairs={{0,6},{1,7},{2,0},{3,1},{4,2},{5,3},{6,4},{7,5},{8,14},{9,15},{10,... | collective-permute-start | bytes 1179656 | tf_op jit(solution)/shard_map/ppermute | solution.py:38
  77.2 19.1 %all-to-all-start = ((f32[8,32,384]{2,1,0:T(8,128)}), f32[8,32,384]{2,1,0:T(8,128)S(1)}, u32[]{:S(2)}, u32[]{:S(2)}) async-start(f32[8,32,384]{2,1,0:T(8,128)} %fold.1), calls=%async_computation | async-start | bytes 786432 | tf_op jit(solution)/shard_map/all_to_all | solution.py:507
  97.6 26.0 %all-to-all-start.1 = ((f32[256,1,128]{2,1,0:T(1,128)}), f32[256,1,128]{2,1,0:T(1,128)S(1)}, u32[]{:S(2)}, u32[]{:S(2)}) async-start(f32[256,1,128]{2,1,0:T(1,128)} %bitcast.5), calls=%async_computation.1 | async-start | bytes 262144 | tf_op jit(solution)/shard_map/all_to_all | solution.py:512
  110.7 3.1 %collective-permute-start.18 = (f32[16,384]{1,0:T(8,128)S(1)}, f32[16,384]{1,0:T(8,128)S(1)}, u32[]{:S(2)}, u32[]{:S(2)}) collective-permute-start(f32[16,384]{1,0:T(8,128)S(1)} %get-tuple-element.109), channel_id=1, source_target_pairs={{0,1},{1,0},{2,3},{3,2},{4,5},{5,4},{6,7},{7,6},{8,9},{9,8},{10,11... | collective-permute-start | bytes 73736 | tf_op jit(solution)/shard_map/ppermute | solution.py:38
  114.3 4.2 %collective-permute-start.19 = (f32[8,384]{1,0:T(8,128)S(1)}, f32[8,384]{1,0:T(8,128)S(1)}, u32[]{:S(2)}, u32[]{:S(2)}) collective-permute-start(f32[8,384]{1,0:T(8,128)S(1)} %get-tuple-element.111), channel_id=1, source_target_pairs={{0,2},{1,3},{2,4},{3,5},{4,6},{5,7},{6,0},{7,1},{8,10},{9,11},{10,... | collective-permute-start | bytes 36872 | tf_op jit(solution)/shard_map/ppermute | solution.py:38
  114.4 4.5 %collective-permute-start.20 = (f32[8,384]{1,0:T(8,128)S(1)}, f32[8,384]{1,0:T(8,128)S(1)}, u32[]{:S(2)}, u32[]{:S(2)}) collective-permute-start(f32[8,384]{1,0:T(8,128)S(1)} %get-tuple-element.112), channel_id=1, source_target_pairs={{0,4},{1,5},{2,6},{3,7},{4,0},{5,1},{6,2},{7,3},{8,12},{9,13},{10,... | collective-permute-start | bytes 36872 | tf_op jit(solution)/shard_map/ppermute | solution.py:38
  116.4 2.9 %collective-permute-start.21 = (f32[8,384]{1,0:T(8,128)S(1)}, f32[8,384]{1,0:T(8,128)S(1)}, u32[]{:S(2)}, u32[]{:S(2)}) collective-permute-start(f32[8,384]{1,0:T(8,128)S(1)} %get-tuple-element.113), channel_id=1, source_target_pairs={{0,6},{1,7},{2,0},{3,1},{4,2},{5,3},{6,4},{7,5},{8,14},{9,15},{10,... | collective-permute-start | bytes 36872 | tf_op jit(solution)/shard_map/ppermute | solution.py:38

commit v7 on v6

--- a/solution.py
+++ b/solution.py
@@ -353,82 +353,86 @@
     )(place, *parts, after)
 
 
-def square_kernel(place, got, after, squares, own, theirs, rows_of):
-    c = place[2]
-    count, rows = got.shape[0], own.shape[0] // NX
-    value = sum(got[z] for z in range(count))
-    for to in range(GROUP):
-        there = slice((to // 2) * rows, (to // 2 + 1) * rows)
-        rows_of[to % 2, there, :] = value[to * rows : (to + 1) * rows, :]
-    squares[...] = jnp.full(squares.shape, jnp.sum(jnp.sum(value * value, axis=0, keepdims=True)))
-    own[...] = rows_of[c]
+def square_kernel(place, got, after, *refs):
+    x, pieces, rows_of = place[1], refs[:NX], refs[NX]
+    rows, width = rows_of.shape[1], rows_of.shape[2]
+    value = sum(got[z] for z in range(got.shape[0]))
+    square = jnp.sum(jnp.sum(value * value, axis=0, keepdims=True))
+    for to in range(NX):
+        rows_of[to] = value[to * rows : (to + 1) * rows, :]
+    for dx in range(NX):
+        pieces[dx][:rows, :] = rows_of[(x + dx) % NX]
+        pieces[dx][rows:, :] = jnp.full((rows, width), square)
+
+
+def square_sum(place, got, after):
+    rows, width = got.shape[1] // NX, got.shape[2]
+    return pl.pallas_call(
+        square_kernel,
+        out_shape=(struct((2 * rows, width), F32),) * NX,
+        in_specs=[SMEM, VMEM, ANY],
+        out_specs=(VMEM,) * NX,
+        scratch_shapes=[pltpu.VMEM((NX, rows, width), F32)],
+        compiler_params=pltpu.CompilerParams(vmem_limit_bytes=8 * MIB),
+        cost_estimate=pl.CostEstimate(flops=MIB, bytes_accessed=MIB, transcendentals=0),
+        name="square_sum",
+    )(place, got, after)
+
+
+def core_kernel(place, *refs):
+    c, pieces = place[2], refs[:NX]
+    squares, mine, theirs, rows_of = refs[NX:]
+    rows = mine.shape[0] // NX
+    for dx in range(NX):
+        for core in range(2):
+            there = slice(dx * rows, (dx + 1) * rows)
+            rows_of[core, there, :] = pieces[dx][core * rows : (core + 1) * rows, :]
+    mine[...] = rows_of[c]
     theirs[...] = rows_of[1 - c]
-
-
-def square_sum(place, got, after, copies):
-    rows, width = got.shape[1] // 2, got.shape[2]
-    return pl.pallas_call(
-        square_kernel,
+    square = sum(piece[2 * rows : 2 * rows + 1, :DH] for piece in pieces)
+    squares[...] = jnp.broadcast_to(square, squares.shape)
+
+
+def by_core(place, pieces, copies):
+    rows, width = NX * pieces[0].shape[0] // 4, pieces[0].shape[1]
+    return pl.pallas_call(
+        core_kernel,
         out_shape=(struct((copies, DH), F32),) + (struct((rows, width), F32),) * 2,
-        in_specs=[SMEM, VMEM, ANY],
+        in_specs=[SMEM] + [VMEM] * NX,
         out_specs=(VMEM,) * 3,
         scratch_shapes=[pltpu.VMEM((2, rows, width), F32)],
         compiler_params=pltpu.CompilerParams(vmem_limit_bytes=8 * MIB),
         cost_estimate=pl.CostEstimate(flops=MIB, bytes_accessed=MIB, transcendentals=0),
-        name="square_sum",
-    )(place, got, after)
-
-
-def pair_kernel(place, own, theirs, *refs):
-    x, pieces, rows_of = place[1], refs[:NX], refs[NX]
-    rows = own.shape[0] // NX
-    for to in range(NX):
-        rows_of[to, :rows, :] = own[to * rows : (to + 1) * rows, :]
-        rows_of[to, rows:, :] = theirs[to * rows : (to + 1) * rows, :]
-    for dx in range(NX):
-        pieces[dx][...] = rows_of[(x + dx) % NX]
-
-
-def pair_rows(place, own, theirs):
-    rows, width = 2 * own.shape[0] // NX, own.shape[1]
-    return pl.pallas_call(
-        pair_kernel,
-        out_shape=(struct((rows, width), F32),) * NX,
-        in_specs=[SMEM, VMEM, VMEM],
-        out_specs=(VMEM,) * NX,
-        scratch_shapes=[pltpu.VMEM((NX, rows, width), F32)],
-        compiler_params=pltpu.CompilerParams(vmem_limit_bytes=8 * MIB),
-        cost_estimate=pl.CostEstimate(flops=MIB, bytes_accessed=MIB, transcendentals=0),
-        name="pair_rows",
-    )(place, own, theirs)
-
-
-def clip_kernel(place, squares, *refs):
-    x, c, pieces, out = place[1], place[2], refs[:NX], refs[NX]
+        name="by_core",
+    )(place, *pieces)
+
+
+def clip_kernel(place, squares, mine, theirs, out):
+    x, c = place[1], place[2]
     rows = out.shape[0]
     total_sq = jnp.sum(squares[...], axis=0, keepdims=True)
     factor = jnp.minimum(1.0, D / jnp.sqrt(total_sq + 1e-06))
     for dx in range(NX):
-        for core in range(2):
+        for core, source in enumerate((mine, theirs)):
             head = ((x + NX - dx) % NX) * 2 + (c ^ core)
             for part in range(3):
                 columns = slice(part * DH, (part + 1) * DH)
                 start = pl.multiple_of((part * H + head) * DH, DH)
-                value = pieces[dx][core * rows : (core + 1) * rows, columns]
+                value = source[dx * rows : (dx + 1) * rows, columns]
                 out[:, pl.ds(start, DH)] = value * factor
 
 
-def clip(place, squares, pieces):
-    rows, width = pieces[0].shape[0] // 2, pieces[0].shape[1] * H
+def clip(place, squares, mine, theirs):
+    rows, width = mine.shape[0] // NX, mine.shape[1] * H
     return pl.pallas_call(
         clip_kernel,
         out_shape=struct((rows, width), F32),
-        in_specs=[SMEM] + [VMEM] * (1 + NX),
+        in_specs=[SMEM] + [VMEM] * 3,
         out_specs=VMEM,
         compiler_params=pltpu.CompilerParams(vmem_limit_bytes=8 * MIB),
         cost_estimate=pl.CostEstimate(flops=MIB, bytes_accessed=MIB, transcendentals=0),
         name="clip",
-    )(place, squares, *pieces)
+    )(place, squares, mine, theirs)
 
 
 def body(inputs, grad_out, w_qkv):
@@ -508,11 +512,23 @@
     grad_rows, done = input_gradient(place, (grad_proj, theirs, *back), total_rows, w_qkv)
     grad_inputs = grad_rows.reshape(user_count, row_count, feature_count)
 
-    squares, own, theirs = square_sum(place, got, done, dp_count * lax.axis_size("seq"))
-    squares = lax.all_to_all(squares, ("dp", "seq"), 0, 0, tiled=True)
-    parts = pair_rows(place, own, send(theirs, dc=1))
-    parts = parts[:1] + tuple(send(parts[dx], dx=dx) for dx in range(1, NX))
-    return (grad_inputs, clip(place, squares, parts))
+    parts = square_sum(place, got, done)
+    arrived_rows = {dx: send(parts[dx], dx=dx) for dx in FAR_FIRST}
+    pieces = [parts[0]] + [arrived_rows[dx] for dx in range(1, NX)]
+    squares, mine, theirs = by_core(place, pieces, 2 * dp_count * NY)
+    slabs = [
+        [
+            (z * NY + y_of) * GROUP + 2 * x_of + core
+            for z in range(dp_count)
+            for y_of in range(NY)
+            for core in range(2)
+        ]
+        for x_of in range(NX)
+    ]
+    squares = lax.all_to_all(
+        squares, ("dp", "seq"), 0, 0, axis_index_groups=slabs, tiled=True
+    )
+    return (grad_inputs, clip(place, squares, mine, send(theirs, dc=1)))
 
 
 def solution(mesh):

time: 125 us -> 128 us (1.024)
  waiting for transfers between devices: 35.5 us -> 39.8 us
  starting transfers between devices: 59.5 us -> 58.1 us
    all_to_all x1, waiting for transfers between devices: 4.38 us -> 7.91 us  [body(): lax.all_to_all(squares, ('dp', 'seq'), 0, 0, axis_index_groups=slabs, til...]
  transfers between devices with their start and end apart: 24 -> 24, of which waited for: 15 -> 14; matrix products, arithmetic and copies ran while one was open for 1% -> 1% of each run, Pallas kernels for 13% -> 12%
where the time goes in v7:
time: 128 us
  starting transfers between devices  58.1 us (45%)
  waiting for transfers between devices  39.8 us (31%)
  Pallas kernels  25.6 us (20%)
  local copies, waits for them, and re-layouts  3.19 us (2%)
    ppermute x22, starting transfers between devices, send(): return lax.ppermute(value, 'seq', seq_perm(dy, dx, dc))  35.9 us
    ppermute x22, waiting for transfers between devices, send(): return lax.ppermute(value, 'seq', seq_perm(dy, dx, dc))  29 us
    all_to_all x1, starting transfers between devices, body(): lax.all_to_all(squares, ('dp', 'seq'), 0, 0, axis_index_groups=slabs, til...  11.8 us
    all_to_all x1, starting transfers between devices, body(): lax.all_to_all(folded, ('dp', 'seq'), 0, 0, axis_index_groups=columns_of)  10.3 us
    pallas_call x5, Pallas kernels, blocks(): pl.pallas_call(functools.partial(block_kernel, units), out_shape=(struct(...  8.77 us
    all_to_all x1, waiting for transfers between devices, body(): lax.all_to_all(squares, ('dp', 'seq'), 0, 0, axis_index_groups=slabs, til...  7.91 us
    pallas_call x1, Pallas kernels, input_gradient(): pl.pallas_call(input_kernel, grid=(features // step,), out_shape=(struct(...  5.89 us
    pallas_call x1, Pallas kernels, gradients(): pl.pallas_call(functools.partial(grad_kernel, scaling, users, dp_count, c...  3.16 us
  transfers between devices with their start and end apart: 24, of which 14 were waited for; matrix products, arithmetic and copies ran while one was open for 1% of the time, Pallas kernels for 12%

profile of v7, /device:TPU:1, one launch (start us, length us, event | category | flops | bytes accessed | tf_op | source)
XLA Modules:
  0.0 127.6 jit_solution(13495984671146947460)
XLA Ops:
  0.7 0.1 pad_add_fusion.place
  0.7 0.9 copy-done
  1.7 0.9 copy-done.2
  2.6 1.8 %messages.1 = (f32[22,64,128]{2,1,0:T(8,128)}, f32[22,64,128]{2,1,0:T(8,128)S(1)}, f32[18,64,128]{2,1,0:T(8,128)}) custom-call(s32[3]{0:T(128)S(1)} %pad_add_fusion.place, bf16[2,64,1024]{2,1,0:T(8,128)(2,1)S(1)} %copy-done, bf16[2,64,1024]{2,1,0:T(8,128)(2,1)S(1)} %copy-done.2), custom_call_target="tpu_custom_call" | custom-call | flops 1048576 | bytes 3145728 | tf_op jit(solution)/shard_map/messages/pallas_call | solution.py:76
  4.4 2.0 %collective-permute-start.1 = (f32[22,64,128]{2,1,0:T(8,128)}, f32[22,64,128]{2,1,0:T(8,128)S(1)}, u32[]{:S(2)}, u32[]{:S(2)}) collective-permute-start(f32[22,64,128]{2,1,0:T(8,128)} %get-tuple-element.60), channel_id=1, source_target_pairs={{0,2},{1,3},{2,4},{3,5},{4,6},{5,7},{6,0},{7,1},{8,10},{9,11},{10,... | collective-permute-start | bytes 2162696 | tf_op jit(solution)/shard_map/ppermute | solution.py:38
  6.4 1.3 collective-permute-start.2
  7.7 3.2 %collective-permute-start = (f32[18,64,128]{2,1,0:T(8,128)}, f32[18,64,128]{2,1,0:T(8,128)S(1)}, u32[]{:S(2)}, u32[]{:S(2)}) collective-permute-start(f32[18,64,128]{2,1,0:T(8,128)} %get-tuple-element.58), channel_id=1, source_target_pairs={{0,1},{1,0},{2,3},{3,2},{4,5},{5,4},{6,7},{7,6},{8,9},{9,8},{10,11... | collective-permute-start | bytes 1769480 | tf_op jit(solution)/shard_map/ppermute | solution.py:38
  10.9 1.2 constant_dynamic-slice_fusion.2
  12.1 0.1 pad_maximum_fusion.w
  12.2 0.5 collective-permute-done.refs_2_
  12.7 2.0 %blocks.5 = (bf16[1024,256]{1,0:T(8,128)(2,1)S(1)}, bf16[256,384]{1,0:T(8,128)(2,1)S(1)}, bf16[256,128]{1,0:T(8,128)(2,1)S(1)}, f32[2,2,128,128]{3,2,1,0:T(8,128...) custom-call(s32[3]{0:T(128)S(1)} %pad_add_fusion.place, bf16[1024,384]{1,0:T(8,128)(2,1)S(1)} %pad_maximum_fusion.w, ...), custom_call_target="tpu_custom_call" | custom-call | flops 201326592 | bytes 4194304 | tf_op jit(solution)/shard_map/blocks/pallas_call | solution.py:148
  14.7 6.8 %collective-permute-done.1.refs_0_ = f32[22,64,128]{2,1,0:T(8,128)S(1)} collective-permute-done((f32[22,64,128]{2,1,0:T(8,128)}, f32[22,64,128]{2,1,0:T(8,128)S(1)}, u32[]{:S(2)}, u32[]{:S(2)}) %collective-permute-start.1) | collective-permute-done | bytes 720928 | tf_op jit(solution)/shard_map/ppermute | solution.py:38
  21.5 1.4 %collective-permute-done.2.refs_1_.refs_0_ = f32[22,64,128]{2,1,0:T(8,128)S(1)} collective-permute-done((f32[22,64,128]{2,1,0:T(8,128)S(1)}, f32[22,64,128]{2,1,0:T(8,128)S(1)}, u32[]{:S(2)}, u32[]{:S(2)}) %collective-permute-start.2) | collective-permute-done | bytes 720928 | tf_op jit(solution)/shard_map/ppermute | solution.py:38
  22.9 0.1 relay.3
  23.0 2.2 %collective-permute-start.3 = (f32[22,64,128]{2,1,0:T(8,128)S(1)}, f32[22,64,128]{2,1,0:T(8,128)S(1)}, u32[]{:S(2)}, u32[]{:S(2)}) collective-permute-start(f32[22,64,128]{2,1,0:T(8,128)S(1)} %get-tuple-element.62), channel_id=1, source_target_pairs={{0,1},{1,0},{2,3},{3,2},{4,5},{5,4},{6,7},{7,6},{8,9},{9,8},{10,11... | collective-permute-start | bytes 2162696 | tf_op jit(solution)/shard_map/ppermute | solution.py:38
  25.2 0.1 collective-permute-start.6
  25.3 1.3 collective-permute-start.4
  26.6 1.6 %collective-permute-start.5 = (f32[10,64,128]{2,1,0:T(8,128)S(1)}, f32[10,64,128]{2,1,0:T(8,128)S(1)}, u32[]{:S(2)}, u32[]{:S(2)}) collective-permute-start(f32[10,64,128]{2,1,0:T(8,128)S(1)} %slice.9), channel_id=1, source_target_pairs={{0,6},{1,7},{2,0},{3,1},{4,2},{5,3},{6,4},{7,5},{8,14},{9,15},{10,... | collective-permute-start | bytes 983048 | tf_op jit(solution)/shard_map/ppermute | solution.py:38
  28.2 0.0 collective-permute-done.3.refs_1_
  28.2 2.0 %blocks.6 = (bf16[1024,256]{1,0:T(8,128)(2,1)S(1)}, bf16[256,384]{1,0:T(8,128)(2,1)S(1)}, bf16[256,128]{1,0:T(8,128)(2,1)S(1)}, f32[2,2,128,128]{3,2,1,0:T(8,128...) custom-call(s32[3]{0:T(128)S(1)} %pad_add_fusion.place, bf16[1024,384]{1,0:T(8,128)(2,1)S(1)} %pad_maximum_fusion.w, ...), custom_call_target="tpu_custom_call" | custom-call | flops 201326592 | bytes 4194304 | tf_op jit(solution)/shard_map/blocks/pallas_call | solution.py:148
  30.2 2.0 %blocks.7 = (bf16[1024,256]{1,0:T(8,128)(2,1)S(1)}, bf16[256,384]{1,0:T(8,128)(2,1)S(1)}, bf16[256,128]{1,0:T(8,128)(2,1)S(1)}, f32[2,2,128,128]{3,2,1,0:T(8,128...) custom-call(s32[3]{0:T(128)S(1)} %pad_add_fusion.place, bf16[1024,384]{1,0:T(8,128)(2,1)S(1)} %pad_maximum_fusion.w, ...), custom_call_target="tpu_custom_call" | custom-call | flops 201326592 | bytes 4194304 | tf_op jit(solution)/shard_map/blocks/pallas_call | solution.py:148
  32.2 3.3 %collective-permute-done.4.refs_0_ = f32[10,64,128]{2,1,0:T(8,128)S(1)} collective-permute-done((f32[10,64,128]{2,1,0:T(8,128)S(1)}, f32[10,64,128]{2,1,0:T(8,128)S(1)}, u32[]{:S(2)}, u32[]{:S(2)}) %collective-permute-start.4) | collective-permute-done | bytes 327712 | tf_op jit(solution)/shard_map/ppermute | solution.py:38
  35.5 0.0 collective-permute-done.5.refs_1_
  35.6 1.4 %collective-permute-start.7 = (f32[20,64,128]{2,1,0:T(8,128)S(1)}, f32[20,64,128]{2,1,0:T(8,128)S(1)}, u32[]{:S(2)}, u32[]{:S(2)}) collective-permute-start(f32[20,64,128]{2,1,0:T(8,128)S(1)} %relay.4.refs_0_), channel_id=1, source_target_pairs={{0,1},{1,0},{2,3},{3,2},{4,5},{5,4},{6,7},{7,6},{8,9},{9,8},{10,11... | collective-permute-start | bytes 1966088 | tf_op jit(solution)/shard_map/ppermute | solution.py:38
  37.0 1.4 %blocks.8 = (bf16[1024,128]{1,0:T(8,128)(2,1)S(1)}, bf16[128,384]{1,0:T(8,128)(2,1)S(1)}, bf16[128,128]{1,0:T(8,128)(2,1)S(1)}, f32[1,2,128,128]{3,2,1,0:T(8,128...) custom-call(s32[3]{0:T(128)S(1)} %pad_add_fusion.place, bf16[1024,384]{1,0:T(8,128)(2,1)S(1)} %pad_maximum_fusion.w, ...), custom_call_target="tpu_custom_call" | custom-call | flops 100663296 | bytes 4194304 | tf_op jit(solution)/shard_map/blocks/pallas_call | solution.py:148
  38.4 0.3 collective-permute-done.7.refs_0_
  38.7 1.4 %blocks.9 = (bf16[1024,128]{1,0:T(8,128)(2,1)S(1)}, bf16[128,384]{1,0:T(8,128)(2,1)S(1)}, bf16[128,128]{1,0:T(8,128)(2,1)S(1)}, f32[1,2,128,128]{3,2,1,0:T(8,128...) custom-call(s32[3]{0:T(128)S(1)} %pad_add_fusion.place, bf16[1024,384]{1,0:T(8,128)(2,1)S(1)} %pad_maximum_fusion.w, ...), custom_call_target="tpu_custom_call" | custom-call | flops 100663296 | bytes 4194304 | tf_op jit(solution)/shard_map/blocks/pallas_call | solution.py:148
  40.1 0.6 totals.1
  40.8 3.1 %collective-permute-start.8 = (f32[2,128,128]{2,1,0:T(8,128)S(1)}, f32[2,128,128]{2,1,0:T(8,128)S(1)}, u32[]{:S(2)}, u32[]{:S(2)}) collective-permute-start(f32[2,128,128]{2,1,0:T(8,128)S(1)} %get-tuple-element.73), channel_id=1, source_target_pairs={{0,16},{1,17},{2,18},{3,19},{4,20},{5,21},{6,22},{7,23},{8,24},{9,... | collective-permute-start | bytes 393224 | tf_op jit(solution)/shard_map/ppermute | solution.py:38
  43.9 0.4 collective-permute-start.9
  44.3 2.3 %collective-permute-start.10 = (f32[2,128,128]{2,1,0:T(8,128)S(1)}, f32[2,128,128]{2,1,0:T(8,128)S(1)}, u32[]{:S(2)}, u32[]{:S(2)}) collective-permute-start(f32[2,128,128]{2,1,0:T(8,128)S(1)} %get-tuple-element.75), channel_id=1, source_target_pairs={{0,24},{1,25},{2,26},{3,27},{4,28},{5,29},{6,30},{7,31},{8,0},{9,1... | collective-permute-start | bytes 393224 | tf_op jit(solution)/shard_map/ppermute | solution.py:38
  46.6 0.6 collective-permute-done.8.refs_0_
  47.2 3.2 %collective-permute-done.9.refs_1_ = f32[2,128,128]{2,1,0:T(8,128)S(1)} collective-permute-done((f32[2,128,128]{2,1,0:T(8,128)S(1)}, f32[2,128,128]{2,1,0:T(8,128)S(1)}, u32[]{:S(2)}, u32[]{:S(2)}) %collective-permute-start.9) | collective-permute-done | bytes 131104 | tf_op jit(solution)/shard_map/ppermute | solution.py:38
  50.4 0.0 collective-permute-done.10.refs_2_
  50.4 3.2 %gradients.1 = (bf16[1024,384]{1,0:T(8,128)(2,1)S(1)}, f32[512,384]{1,0:T(8,128)S(1)}, f32[8,32,384]{2,1,0:T(8,128)S(1)}, f32[8,32,384]{2,1,0:T(8,128)S(1)}, f32...) custom-call(s32[3]{0:T(128)S(1)} %pad_add_fusion.place, f32[2,128,128]{2,1,0:T(8,128)S(1)} %collective-permute-done.8.refs_0_, ...), custom_call_target="tpu_custom_call" | custom-call | flops 805306368 | bytes 10485760 | tf_op jit(solution)/shard_map/gradients/pallas_call | solution.py:270
  53.5 1.3 collective-permute-start.11
  54.8 1.8 %collective-permute-start.15 = (f32[8,32,384]{2,1,0:T(8,128)S(1)}, f32[8,32,384]{2,1,0:T(8,128)S(1)}, u32[]{:S(2)}, u32[]{:S(2)}) collective-permute-start(f32[8,32,384]{2,1,0:T(8,128)S(1)} %get-tuple-element.103), channel_id=1, source_target_pairs={{0,16},{1,17},{2,18},{3,19},{4,20},{5,21},{6,22},{7,23},{8,24},{9,... | collective-permute-start | bytes 1179656 | tf_op jit(solution)/shard_map/ppermute | solution.py:38
  56.6 1.5 %collective-permute-start.16 = (f32[8,32,384]{2,1,0:T(8,128)S(1)}, f32[8,32,384]{2,1,0:T(8,128)S(1)}, u32[]{:S(2)}, u32[]{:S(2)}) collective-permute-start(f32[8,32,384]{2,1,0:T(8,128)S(1)} %get-tuple-element.104), channel_id=1, source_target_pairs={{0,8},{1,9},{2,10},{3,11},{4,12},{5,13},{6,14},{7,15},{8,16},{9,17... | collective-permute-start | bytes 1179656 | tf_op jit(solution)/shard_map/ppermute | solution.py:38
  58.1 1.2 collective-permute-start.17
  59.3 0.0 collective-permute-done.11.refs_1_
  59.3 0.8 relay.5
  60.1 2.5 %collective-permute-start.13 = (f32[256,384]{1,0:T(8,128)}, f32[256,384]{1,0:T(8,128)S(1)}, u32[]{:S(2)}, u32[]{:S(2)}) collective-permute-start(f32[256,384]{1,0:T(8,128)} %get-tuple-element.99), channel_id=1, source_target_pairs={{0,4},{1,5},{2,6},{3,7},{4,0},{5,1},{6,2},{7,3},{8,12},{9,13},{10,... | collective-permute-start | bytes 1179656 | tf_op jit(solution)/shard_map/ppermute | solution.py:38
  62.6 0.8 collective-permute-start.14
  63.5 3.6 %collective-permute-done.15.refs_1_ = f32[8,32,384]{2,1,0:T(8,128)S(1)} collective-permute-done((f32[8,32,384]{2,1,0:T(8,128)S(1)}, f32[8,32,384]{2,1,0:T(8,128)S(1)}, u32[]{:S(2)}, u32[]{:S(2)}) %collective-permute-start.15) | collective-permute-done | bytes 393248 | tf_op jit(solution)/shard_map/ppermute | solution.py:38
  67.0 2.8 %collective-permute-start.12 = (f32[256,384]{1,0:T(8,128)S(1)}, f32[256,384]{1,0:T(8,128)}, u32[]{:S(2)}, u32[]{:S(2)}) collective-permute-start(f32[256,384]{1,0:T(8,128)S(1)} %get-tuple-element.98.refs_4_), channel_id=1, source_target_pairs={{0,6},{1,7},{2,0},{3,1},{4,2},{5,3},{6,4},{7,5},{8,14},{9,15},{10,... | collective-permute-start | bytes 1179656 | tf_op jit(solution)/shard_map/ppermute | solution.py:38
  69.8 6.0 %collective-permute-done.16.refs_2_ = f32[8,32,384]{2,1,0:T(8,128)S(1)} collective-permute-done((f32[8,32,384]{2,1,0:T(8,128)S(1)}, f32[8,32,384]{2,1,0:T(8,128)S(1)}, u32[]{:S(2)}, u32[]{:S(2)}) %collective-permute-start.16) | collective-permute-done | bytes 393248 | tf_op jit(solution)/shard_map/ppermute | solution.py:38
  75.8 0.0 collective-permute-done.17.refs_3_
  75.8 1.4 %fold.1 = f32[8,32,384]{2,1,0:T(8,128)} custom-call(s32[3]{0:T(128)S(1)} %pad_add_fusion.place, f32[8,32,384]{2,1,0:T(8,128)S(1)} %get-tuple-element.102.refs_0_, f32[8,32,384]{2,1,0:T(8,128)S(1)} %collective-permute-done.15.refs_1_, f32[8,32,384]{2,1,0:T(8,128)S(1)} %collective-permute-done.16.refs_2_, f32[8,32,384]{2,1,0:T(8,128)S(1)} %collective-permute-done.17.refs_3_, ...), custom_call_target="tpu_custom_call" | custom-call | flops 1048576 | bytes 2097152 | tf_op jit(solution)/shard_map/fold/pallas_call | solution.py:345
  77.2 10.3 %all-to-all-start = ((f32[8,32,384]{2,1,0:T(8,128)}), f32[8,32,384]{2,1,0:T(8,128)S(1)}, u32[]{:S(2)}, u32[]{:S(2)}) async-start(f32[8,32,384]{2,1,0:T(8,128)} %fold.1), calls=%async_computation | async-start | bytes 786432 | tf_op jit(solution)/shard_map/all_to_all | solution.py:511
  87.5 0.0 collective-permute-done.12.refs_2_
  87.5 5.9 %input_gradient.1 = (bf16[128,1024]{1,0:T(8,128)(2,1)}, f32[8,128]{1,0:T(8,128)S(1)}) custom-call(s32[3]{0:T(128)S(1)} %pad_add_fusion.place, bf16[1024,384]{1,0:T(8,128)(2,1)S(1)} %get-tuple-element.96.refs_0_, f32[512,384]{1,0:T(8,128)S(1)} %collective-permute-done.11.refs_1_, f32[256,384]{1,0:T(8,128)} %collective-permute-done.12.refs_2_, ...), custom_call_target="tpu_custom_call" | custom-call | flops 6442450944 | bytes 83886080 | tf_op jit(solution)/shard_map/input_gradient/pallas_call | solution.py:316
  93.4 2.9 %all-to-all-done.got = f32[8,32,384]{2,1,0:T(8,128)S(1)} async-done(((f32[8,32,384]{2,1,0:T(8,128)}), f32[8,32,384]{2,1,0:T(8,128)S(1)}, u32[]{:S(2)}, u32[]{:S(2)}) %all-to-all-start) | async-done | bytes 393248 | tf_op jit(solution)/shard_map/all_to_all | solution.py:511
  96.3 0.7 square_sum.1
  97.0 0.9 collective-permute-start.18
  97.8 3.2 %collective-permute-start.19 = (f32[16,384]{1,0:T(8,128)S(1)}, f32[16,384]{1,0:T(8,128)S(1)}, u32[]{:S(2)}, u32[]{:S(2)}) collective-permute-start(f32[16,384]{1,0:T(8,128)S(1)} %get-tuple-element.109), channel_id=1, source_target_pairs={{0,4},{1,5},{2,6},{3,7},{4,0},{5,1},{6,2},{7,3},{8,12},{9,13},{10,... | collective-permute-start | bytes 73736 | tf_op jit(solution)/shard_map/ppermute | solution.py:38
  101.1 0.6 collective-permute-start.20
  101.7 0.9 collective-permute-done.19.refs_2_
  102.6 1.5 %collective-permute-done.20.refs_3_ = f32[16,384]{1,0:T(8,128)S(1)} collective-permute-done((f32[16,384]{1,0:T(8,128)S(1)}, f32[16,384]{1,0:T(8,128)S(1)}, u32[]{:S(2)}, u32[]{:S(2)}) %collective-permute-start.20) | collective-permute-done | bytes 24608 | tf_op jit(solution)/shard_map/ppermute | solution.py:38
  104.1 1.2 by_core.1
  105.2 11.8 %all-to-all-start.1 = ((f32[64,1,128]{2,1,0:T(1,128)}), f32[64,1,128]{2,1,0:T(1,128)S(1)}, u32[]{:S(2)}, u32[]{:S(2)}) async-start(f32[64,1,128]{2,1,0:T(1,128)} %bitcast.5), calls=%async_computation.1 | async-start | bytes 65536 | tf_op jit(solution)/shard_map/all_to_all | solution.py:528
  117.1 0.5 collective-permute-start.21
  117.6 0.8 collective-permute-done.21.theirs
  118.5 7.9 %all-to-all-done.1 = f32[64,1,128]{2,1,0:T(1,128)S(1)} async-done(((f32[64,1,128]{2,1,0:T(1,128)}), f32[64,1,128]{2,1,0:T(1,128)S(1)}, u32[]{:S(2)}, u32[]{:S(2)}) %all-to-all-start.1) | async-done | bytes 32800 | tf_op jit(solution)/shard_map/all_to_all | solution.py:528
  126.4 1.2 clip.1
  (13 shorter events, 0.1 us)
Async XLA Ops:
  0.7 1.0 copy-start
  1.7 0.9 copy-start.2
  4.4 17.1 %collective-permute-start.1 = (f32[22,64,128]{2,1,0:T(8,128)}, f32[22,64,128]{2,1,0:T(8,128)S(1)}, u32[]{:S(2)}, u32[]{:S(2)}) collective-permute-start(f32[22,64,128]{2,1,0:T(8,128)} %get-tuple-element.60), channel_id=1, source_target_pairs={{0,2},{1,3},{2,4},{3,5},{4,6},{5,7},{6,0},{7,1},{8,10},{9,11},{10,... | collective-permute-start | bytes 2162696 | tf_op jit(solution)/shard_map/ppermute | solution.py:38
  6.4 16.4 %collective-permute-start.2 = (f32[22,64,128]{2,1,0:T(8,128)S(1)}, f32[22,64,128]{2,1,0:T(8,128)S(1)}, u32[]{:S(2)}, u32[]{:S(2)}) collective-permute-start(f32[22,64,128]{2,1,0:T(8,128)S(1)} %get-tuple-element.61), channel_id=1, source_target_pairs={{0,6},{1,7},{2,0},{3,1},{4,2},{5,3},{6,4},{7,5},{8,14},{9,15},{10,... | collective-permute-start | bytes 2162696 | tf_op jit(solution)/shard_map/ppermute | solution.py:38
  7.7 5.0 %collective-permute-start = (f32[18,64,128]{2,1,0:T(8,128)}, f32[18,64,128]{2,1,0:T(8,128)S(1)}, u32[]{:S(2)}, u32[]{:S(2)}) collective-permute-start(f32[18,64,128]{2,1,0:T(8,128)} %get-tuple-element.58), channel_id=1, source_target_pairs={{0,1},{1,0},{2,3},{3,2},{4,5},{5,4},{6,7},{7,6},{8,9},{9,8},{10,11... | collective-permute-start | bytes 1769480 | tf_op jit(solution)/shard_map/ppermute | solution.py:38
  10.9 1.8 %copy-start.1 = (bf16[2,64,1024]{2,1,0:T(8,128)(2,1)S(1)}, bf16[2,64,1024]{2,1,0:T(8,128)(2,1)}, u32[]{:S(2)}) copy-start(bf16[2,64,1024]{2,1,0:T(8,128)(2,1)} %refs_0_.1) | copy-start | bytes 786436
  10.9 1.8 %copy-start.3 = (bf16[2,64,1024]{2,1,0:T(8,128)(2,1)S(1)}, bf16[2,64,1024]{2,1,0:T(8,128)(2,1)}, u32[]{:S(2)}) copy-start(bf16[2,64,1024]{2,1,0:T(8,128)(2,1)} %refs_1_.1) | copy-start | bytes 786436
  23.0 5.2 %collective-permute-start.3 = (f32[22,64,128]{2,1,0:T(8,128)S(1)}, f32[22,64,128]{2,1,0:T(8,128)S(1)}, u32[]{:S(2)}, u32[]{:S(2)}) collective-permute-start(f32[22,64,128]{2,1,0:T(8,128)S(1)} %get-tuple-element.62), channel_id=1, source_target_pairs={{0,1},{1,0},{2,3},{3,2},{4,5},{5,4},{6,7},{7,6},{8,9},{9,8},{10,11... | collective-permute-start | bytes 2162696 | tf_op jit(solution)/shard_map/ppermute | solution.py:38
  25.2 5.0 %collective-permute-start.6 = (f32[22,64,128]{2,1,0:T(8,128)S(1)}, f32[22,64,128]{2,1,0:T(8,128)S(1)}, u32[]{:S(2)}, u32[]{:S(2)}) collective-permute-start(f32[22,64,128]{2,1,0:T(8,128)S(1)} %get-tuple-element.64), channel_id=1, source_target_pairs={{0,1},{1,0},{2,3},{3,2},{4,5},{5,4},{6,7},{7,6},{8,9},{9,8},{10,11... | collective-permute-start | bytes 2162696 | tf_op jit(solution)/shard_map/ppermute | solution.py:38
  25.3 10.2 %collective-permute-start.4 = (f32[10,64,128]{2,1,0:T(8,128)S(1)}, f32[10,64,128]{2,1,0:T(8,128)S(1)}, u32[]{:S(2)}, u32[]{:S(2)}) collective-permute-start(f32[10,64,128]{2,1,0:T(8,128)S(1)} %slice.8), channel_id=1, source_target_pairs={{0,2},{1,3},{2,4},{3,5},{4,6},{5,7},{6,0},{7,1},{8,10},{9,11},{10,... | collective-permute-start | bytes 983048 | tf_op jit(solution)/shard_map/ppermute | solution.py:38
  26.6 8.9 %collective-permute-start.5 = (f32[10,64,128]{2,1,0:T(8,128)S(1)}, f32[10,64,128]{2,1,0:T(8,128)S(1)}, u32[]{:S(2)}, u32[]{:S(2)}) collective-permute-start(f32[10,64,128]{2,1,0:T(8,128)S(1)} %slice.9), channel_id=1, source_target_pairs={{0,6},{1,7},{2,0},{3,1},{4,2},{5,3},{6,4},{7,5},{8,14},{9,15},{10,... | collective-permute-start | bytes 983048 | tf_op jit(solution)/shard_map/ppermute | solution.py:38
  35.6 3.1 %collective-permute-start.7 = (f32[20,64,128]{2,1,0:T(8,128)S(1)}, f32[20,64,128]{2,1,0:T(8,128)S(1)}, u32[]{:S(2)}, u32[]{:S(2)}) collective-permute-start(f32[20,64,128]{2,1,0:T(8,128)S(1)} %relay.4.refs_0_), channel_id=1, source_target_pairs={{0,1},{1,0},{2,3},{3,2},{4,5},{5,4},{6,7},{7,6},{8,9},{9,8},{10,11... | collective-permute-start | bytes 1966088 | tf_op jit(solution)/shard_map/ppermute | solution.py:38
  40.8 6.4 %collective-permute-start.8 = (f32[2,128,128]{2,1,0:T(8,128)S(1)}, f32[2,128,128]{2,1,0:T(8,128)S(1)}, u32[]{:S(2)}, u32[]{:S(2)}) collective-permute-start(f32[2,128,128]{2,1,0:T(8,128)S(1)} %get-tuple-element.73), channel_id=1, source_target_pairs={{0,16},{1,17},{2,18},{3,19},{4,20},{5,21},{6,22},{7,23},{8,24},{9,... | collective-permute-start | bytes 393224 | tf_op jit(solution)/shard_map/ppermute | solution.py:38
  43.9 6.5 %collective-permute-start.9 = (f32[2,128,128]{2,1,0:T(8,128)S(1)}, f32[2,128,128]{2,1,0:T(8,128)S(1)}, u32[]{:S(2)}, u32[]{:S(2)}) collective-permute-start(f32[2,128,128]{2,1,0:T(8,128)S(1)} %get-tuple-element.74), channel_id=1, source_target_pairs={{0,8},{1,9},{2,10},{3,11},{4,12},{5,13},{6,14},{7,15},{8,16},{9,17... | collective-permute-start | bytes 393224 | tf_op jit(solution)/shard_map/ppermute | solution.py:38
  44.3 6.1 %collective-permute-start.10 = (f32[2,128,128]{2,1,0:T(8,128)S(1)}, f32[2,128,128]{2,1,0:T(8,128)S(1)}, u32[]{:S(2)}, u32[]{:S(2)}) collective-permute-start(f32[2,128,128]{2,1,0:T(8,128)S(1)} %get-tuple-element.75), channel_id=1, source_target_pairs={{0,24},{1,25},{2,26},{3,27},{4,28},{5,29},{6,30},{7,31},{8,0},{9,1... | collective-permute-start | bytes 393224 | tf_op jit(solution)/shard_map/ppermute | solution.py:38
  53.5 5.8 %collective-permute-start.11 = (f32[512,384]{1,0:T(8,128)S(1)}, f32[512,384]{1,0:T(8,128)S(1)}, u32[]{:S(2)}, u32[]{:S(2)}) collective-permute-start(f32[512,384]{1,0:T(8,128)S(1)} %get-tuple-element.97), channel_id=1, source_target_pairs={{0,1},{1,0},{2,3},{3,2},{4,5},{5,4},{6,7},{7,6},{8,9},{9,8},{10,11... | collective-permute-start | bytes 2359304 | tf_op jit(solution)/shard_map/ppermute | solution.py:38
  54.8 12.2 %collective-permute-start.15 = (f32[8,32,384]{2,1,0:T(8,128)S(1)}, f32[8,32,384]{2,1,0:T(8,128)S(1)}, u32[]{:S(2)}, u32[]{:S(2)}) collective-permute-start(f32[8,32,384]{2,1,0:T(8,128)S(1)} %get-tuple-element.103), channel_id=1, source_target_pairs={{0,16},{1,17},{2,18},{3,19},{4,20},{5,21},{6,22},{7,23},{8,24},{9,... | collective-permute-start | bytes 1179656 | tf_op jit(solution)/shard_map/ppermute | solution.py:38
  56.6 19.2 %collective-permute-start.16 = (f32[8,32,384]{2,1,0:T(8,128)S(1)}, f32[8,32,384]{2,1,0:T(8,128)S(1)}, u32[]{:S(2)}, u32[]{:S(2)}) collective-permute-start(f32[8,32,384]{2,1,0:T(8,128)S(1)} %get-tuple-element.104), channel_id=1, source_target_pairs={{0,8},{1,9},{2,10},{3,11},{4,12},{5,13},{6,14},{7,15},{8,16},{9,17... | collective-permute-start | bytes 1179656 | tf_op jit(solution)/shard_map/ppermute | solution.py:38
  58.1 17.8 %collective-permute-start.17 = (f32[8,32,384]{2,1,0:T(8,128)S(1)}, f32[8,32,384]{2,1,0:T(8,128)S(1)}, u32[]{:S(2)}, u32[]{:S(2)}) collective-permute-start(f32[8,32,384]{2,1,0:T(8,128)S(1)} %get-tuple-element.105), channel_id=1, source_target_pairs={{0,24},{1,25},{2,26},{3,27},{4,28},{5,29},{6,30},{7,31},{8,0},{9,1... | collective-permute-start | bytes 1179656 | tf_op jit(solution)/shard_map/ppermute | solution.py:38
  60.1 27.4 %collective-permute-start.13 = (f32[256,384]{1,0:T(8,128)}, f32[256,384]{1,0:T(8,128)S(1)}, u32[]{:S(2)}, u32[]{:S(2)}) collective-permute-start(f32[256,384]{1,0:T(8,128)} %get-tuple-element.99), channel_id=1, source_target_pairs={{0,4},{1,5},{2,6},{3,7},{4,0},{5,1},{6,2},{7,3},{8,12},{9,13},{10,... | collective-permute-start | bytes 1179656 | tf_op jit(solution)/shard_map/ppermute | solution.py:38
  62.6 24.8 %collective-permute-start.14 = (f32[256,384]{1,0:T(8,128)S(1)}, f32[256,384]{1,0:T(8,128)S(1)}, u32[]{:S(2)}, u32[]{:S(2)}) collective-permute-start(f32[256,384]{1,0:T(8,128)S(1)} %get-tuple-element.100), channel_id=1, source_target_pairs={{0,2},{1,3},{2,4},{3,5},{4,6},{5,7},{6,0},{7,1},{8,10},{9,11},{10,... | collective-permute-start | bytes 1179656 | tf_op jit(solution)/shard_map/ppermute | solution.py:38
  67.0 20.5 %collective-permute-start.12 = (f32[256,384]{1,0:T(8,128)S(1)}, f32[256,384]{1,0:T(8,128)}, u32[]{:S(2)}, u32[]{:S(2)}) collective-permute-start(f32[256,384]{1,0:T(8,128)S(1)} %get-tuple-element.98.refs_4_), channel_id=1, source_target_pairs={{0,6},{1,7},{2,0},{3,1},{4,2},{5,3},{6,4},{7,5},{8,14},{9,15},{10,... | collective-permute-start | bytes 1179656 | tf_op jit(solution)/shard_map/ppermute | solution.py:38
  77.2 19.1 %all-to-all-start = ((f32[8,32,384]{2,1,0:T(8,128)}), f32[8,32,384]{2,1,0:T(8,128)S(1)}, u32[]{:S(2)}, u32[]{:S(2)}) async-start(f32[8,32,384]{2,1,0:T(8,128)} %fold.1), calls=%async_computation | async-start | bytes 786432 | tf_op jit(solution)/shard_map/all_to_all | solution.py:511
  97.0 4.7 %collective-permute-start.18 = (f32[16,384]{1,0:T(8,128)S(1)}, f32[16,384]{1,0:T(8,128)S(1)}, u32[]{:S(2)}, u32[]{:S(2)}) collective-permute-start(f32[16,384]{1,0:T(8,128)S(1)} %get-tuple-element.108), channel_id=1, source_target_pairs={{0,2},{1,3},{2,4},{3,5},{4,6},{5,7},{6,0},{7,1},{8,10},{9,11},{10,... | collective-permute-start | bytes 73736 | tf_op jit(solution)/shard_map/ppermute | solution.py:38
  97.8 4.7 %collective-permute-start.19 = (f32[16,384]{1,0:T(8,128)S(1)}, f32[16,384]{1,0:T(8,128)S(1)}, u32[]{:S(2)}, u32[]{:S(2)}) collective-permute-start(f32[16,384]{1,0:T(8,128)S(1)} %get-tuple-element.109), channel_id=1, source_target_pairs={{0,4},{1,5},{2,6},{3,7},{4,0},{5,1},{6,2},{7,3},{8,12},{9,13},{10,... | collective-permute-start | bytes 73736 | tf_op jit(solution)/shard_map/ppermute | solution.py:38
  101.1 3.0 %collective-permute-start.20 = (f32[16,384]{1,0:T(8,128)S(1)}, f32[16,384]{1,0:T(8,128)S(1)}, u32[]{:S(2)}, u32[]{:S(2)}) collective-permute-start(f32[16,384]{1,0:T(8,128)S(1)} %get-tuple-element.110), channel_id=1, source_target_pairs={{0,6},{1,7},{2,0},{3,1},{4,2},{5,3},{6,4},{7,5},{8,14},{9,15},{10,... | collective-permute-start | bytes 73736 | tf_op jit(solution)/shard_map/ppermute | solution.py:38
  105.2 21.1 %all-to-all-start.1 = ((f32[64,1,128]{2,1,0:T(1,128)}), f32[64,1,128]{2,1,0:T(1,128)S(1)}, u32[]{:S(2)}, u32[]{:S(2)}) async-start(f32[64,1,128]{2,1,0:T(1,128)} %bitcast.5), calls=%async_computation.1 | async-start | bytes 65536 | tf_op jit(solution)/shard_map/all_to_all | solution.py:528
  117.1 1.4 %collective-permute-start.21 = (f32[16,384]{1,0:T(8,128)S(1)}, f32[16,384]{1,0:T(8,128)S(1)}, u32[]{:S(2)}, u32[]{:S(2)}) collective-permute-start(f32[16,384]{1,0:T(8,128)S(1)} %get-tuple-element.113), channel_id=1, source_target_pairs={{0,1},{1,0},{2,3},{3,2},{4,5},{5,4},{6,7},{7,6},{8,9},{9,8},{10,11... | collective-permute-start | bytes 73736 | tf_op jit(solution)/shard_map/ppermute | solution.py:38

commit v8 on v7

--- a/solution.py
+++ b/solution.py
@@ -197,8 +197,7 @@
     proj, refs = refs[:count], refs[count:]
     cots, refs = refs[:count], refs[count:]
     intra, refs = refs[:count], refs[count:]
-    grad_proj, give, pieces, refs = refs[0], refs[1], refs[2 : 2 + NY], refs[2 + NY :]
-    key_all, query_all, prior_all, later_all, product = refs
+    grad_proj, give, piece, key_all, query_all, prior_all, later_all, picked = refs
     first = 0
     for part in range(count):
         last = first + keys[part].shape[0]
@@ -247,18 +246,44 @@
     for dx in range(NX):
         there = slice((2 * dx + 1) * total, (2 * dx + 2) * total)
         give[dx * total : (dx + 1) * total, :] = grad_proj[there, :].astype(F32)
-    value, first = 0.0, 0
-    for part in range(count):
-        last = first + rows_t[part].shape[1]
-        value = value + dot(rows_t[part][...], grad_proj[first:last, :], 1, 0)
-        first = last
-    product[...] = value
-    row_block = product.shape[0] // (dp_count * NY)
-    for piece, dy in zip(pieces, (0,) + FAR_FIRST):
-        target = (y + dy) % NY
+    rows_for(y, FAR_FIRST[0], rows_t, grad_proj, picked, piece)
+
+
+def rows_for(y, dy, rows_t, grad_proj, picked, piece):
+    dp_count, row_block = piece.shape[0], piece.shape[1]
+    target = (y + dy) % NY
+    first = 0
+    for part in rows_t:
+        last = first + part.shape[1]
         for z in range(dp_count):
             start = pl.multiple_of((z * NY + target) * row_block, row_block)
-            piece[z] = product[pl.ds(start, row_block), :]
+            picked[z * row_block : (z + 1) * row_block, first:last] = part[
+                pl.ds(start, row_block), :
+            ]
+        first = last
+    value = dot(picked[...], grad_proj[...], 1, 0)
+    for z in range(dp_count):
+        piece[z] = value[z * row_block : (z + 1) * row_block, :]
+
+
+def rest_kernel(place, *refs):
+    rows_t, grad_proj, refs = refs[: -1 - NY], refs[-1 - NY], refs[-NY:]
+    for piece, dy in zip(refs, FAR_FIRST[1:] + (0,)):
+        rows_for(place[0], dy, rows_t, grad_proj, refs[-1], piece)
+
+
+def rest_of_rows(place, rows_t, grad_proj, shape):
+    tokens = grad_proj.shape[0]
+    return pl.pallas_call(
+        rest_kernel,
+        out_shape=(struct(shape, F32),) * (NY - 1),
+        in_specs=[SMEM] + [VMEM] * (len(rows_t) + 1),
+        out_specs=(VMEM,) * (NY - 1),
+        scratch_shapes=[pltpu.VMEM((shape[0] * shape[1], tokens), BF16)],
+        compiler_params=pltpu.CompilerParams(vmem_limit_bytes=24 * MIB),
+        cost_estimate=pl.CostEstimate(flops=MIB, bytes_accessed=4 * MIB, transcendentals=0),
+        name="rest_of_rows",
+    )(place, *rows_t, grad_proj)
 
 
 def gradients(place, arrived, parts, scaling, users, dp_count):
@@ -270,15 +295,15 @@
     return pl.pallas_call(
         functools.partial(grad_kernel, scaling, users, dp_count, count),
         out_shape=(struct((rows, 3 * DH), BF16), struct((rows // 2, 3 * DH), F32))
-        + (struct((dp_count, row_block, 3 * DH), F32),) * NY,
+        + (struct((dp_count, row_block, 3 * DH), F32),),
         in_specs=[SMEM] + [VMEM] * (NY - 1 + 6 * count),
-        out_specs=(VMEM,) * (2 + NY),
+        out_specs=(VMEM,) * 3,
         scratch_shapes=[
             pltpu.VMEM((GROUP, users, DH, DH), F32),
             pltpu.VMEM((GROUP, users, DH, DH), F32),
             pltpu.VMEM((GROUP, users, DH, DH), BF16),
             pltpu.VMEM((GROUP, users, DH, DH), BF16),
-            pltpu.VMEM((features, 3 * DH), F32),
+            pltpu.VMEM((dp_count * row_block, rows), BF16),
         ],
         compiler_params=pltpu.CompilerParams(vmem_limit_bytes=32 * MIB),
         cost_estimate=pl.CostEstimate(
@@ -335,10 +360,14 @@
 
 def fold_kernel(count, place, *refs):
     out = refs[-1]
-    half = out.shape[0] // 2
-    for z in range(out.shape[0]):
-        to = jnp.where(place[2] == 0, z, (z + half) % out.shape[0])
-        out[to] = sum(ref[z] for ref in refs[:count])
+    dp_count = out.shape[0]
+    for core in range(2):
+
+        @pl.when(place[2] == core)
+        def _():
+            for z in range(dp_count):
+                to = (z + core * (dp_count // 2)) % dp_count
+                out[to] = sum(ref[z] for ref in refs[:count])
 
 
 def fold(place, parts, after):
@@ -353,25 +382,24 @@
     )(place, *parts, after)
 
 
-def square_kernel(place, got, after, *refs):
+def square_kernel(place, got, after, squares, *refs):
     x, pieces, rows_of = place[1], refs[:NX], refs[NX]
-    rows, width = rows_of.shape[1], rows_of.shape[2]
+    rows = rows_of.shape[1]
     value = sum(got[z] for z in range(got.shape[0]))
-    square = jnp.sum(jnp.sum(value * value, axis=0, keepdims=True))
+    squares[...] = jnp.full(squares.shape, jnp.sum(jnp.sum(value * value, axis=0, keepdims=True)))
     for to in range(NX):
         rows_of[to] = value[to * rows : (to + 1) * rows, :]
     for dx in range(NX):
-        pieces[dx][:rows, :] = rows_of[(x + dx) % NX]
-        pieces[dx][rows:, :] = jnp.full((rows, width), square)
-
-
-def square_sum(place, got, after):
+        pieces[dx][...] = rows_of[(x + dx) % NX]
+
+
+def square_sum(place, got, after, copies):
     rows, width = got.shape[1] // NX, got.shape[2]
     return pl.pallas_call(
         square_kernel,
-        out_shape=(struct((2 * rows, width), F32),) * NX,
+        out_shape=(struct((copies, DH), F32),) + (struct((rows, width), F32),) * NX,
         in_specs=[SMEM, VMEM, ANY],
-        out_specs=(VMEM,) * NX,
+        out_specs=(VMEM,) * (1 + NX),
         scratch_shapes=[pltpu.VMEM((NX, rows, width), F32)],
         compiler_params=pltpu.CompilerParams(vmem_limit_bytes=8 * MIB),
         cost_estimate=pl.CostEstimate(flops=MIB, bytes_accessed=MIB, transcendentals=0),
@@ -381,7 +409,7 @@
 
 def core_kernel(place, *refs):
     c, pieces = place[2], refs[:NX]
-    squares, mine, theirs, rows_of = refs[NX:]
+    mine, theirs, rows_of = refs[NX:]
     rows = mine.shape[0] // NX
     for dx in range(NX):
         for core in range(2):
@@ -389,17 +417,15 @@
             rows_of[core, there, :] = pieces[dx][core * rows : (core + 1) * rows, :]
     mine[...] = rows_of[c]
     theirs[...] = rows_of[1 - c]
-    square = sum(piece[2 * rows : 2 * rows + 1, :DH] for piece in pieces)
-    squares[...] = jnp.broadcast_to(square, squares.shape)
-
-
-def by_core(place, pieces, copies):
-    rows, width = NX * pieces[0].shape[0] // 4, pieces[0].shape[1]
+
+
+def by_core(place, pieces):
+    rows, width = NX * pieces[0].shape[0] // 2, pieces[0].shape[1]
     return pl.pallas_call(
         core_kernel,
-        out_shape=(struct((copies, DH), F32),) + (struct((rows, width), F32),) * 2,
+        out_shape=(struct((rows, width), F32),) * 2,
         in_specs=[SMEM] + [VMEM] * NX,
-        out_specs=(VMEM,) * 3,
+        out_specs=(VMEM,) * 2,
         scratch_shapes=[pltpu.VMEM((2, rows, width), F32)],
         compiler_params=pltpu.CompilerParams(vmem_limit_bytes=8 * MIB),
         cost_estimate=pl.CostEstimate(flops=MIB, bytes_accessed=MIB, transcendentals=0),
@@ -487,7 +513,9 @@
     ]
     sent = totals(place, [part[3] for part in parts], [part[4] for part in parts])
     arrived = [send(value, dy=dy) for value, dy in zip(sent, FAR_FIRST)]
-    grad_proj, give, *pieces = gradients(place, arrived, parts, scaling, user_count, dp_count)
+    grad_proj, give, far_piece = gradients(
+        place, arrived, parts, scaling, user_count, dp_count
+    )
 
     span = 2 * total_rows
     theirs = send(give, dc=1)
@@ -501,7 +529,9 @@
         ),
     )
     back = [send(returns[dx - 1], dx=-dx) for dx in range(1, NX)]
-    summands = pieces[:1] + [send(value, dy=dy) for value, dy in zip(pieces[1:], FAR_FIRST)]
+    *near, kept = rest_of_rows(place, [part[0] for part in parts], grad_proj, far_piece.shape)
+    summands = [send(value, dy=dy) for value, dy in zip([far_piece] + near, FAR_FIRST)]
+    summands.append(kept)
     folded = fold(place, summands, returns[0])
     columns_of = []
     for column in range(NY * GROUP):
@@ -512,22 +542,10 @@
     grad_rows, done = input_gradient(place, (grad_proj, theirs, *back), total_rows, w_qkv)
     grad_inputs = grad_rows.reshape(user_count, row_count, feature_count)
 
-    parts = square_sum(place, got, done)
+    squares, *parts = square_sum(place, got, done, dp_count * lax.axis_size("seq"))
+    squares = lax.all_to_all(squares, ("dp", "seq"), 0, 0, tiled=True)
     arrived_rows = {dx: send(parts[dx], dx=dx) for dx in FAR_FIRST}
-    pieces = [parts[0]] + [arrived_rows[dx] for dx in range(1, NX)]
-    squares, mine, theirs = by_core(place, pieces, 2 * dp_count * NY)
-    slabs = [
-        [
-            (z * NY + y_of) * GROUP + 2 * x_of + core
-            for z in range(dp_count)
-            for y_of in range(NY)
-            for core in range(2)
-        ]
-        for x_of in range(NX)
-    ]
-    squares = lax.all_to_all(
-        squares, ("dp", "seq"), 0, 0, axis_index_groups=slabs, tiled=True
-    )
+    mine, theirs = by_core(place, [parts[0]] + [arrived_rows[dx] for dx in range(1, NX)])
     return (grad_inputs, clip(place, squares, mine, send(theirs, dc=1)))
 
 

time: 128 us -> 124 us (0.969)
  waiting for transfers between devices: 39.8 us -> 32.5 us
  starting transfers between devices: 58.1 us -> 61 us
    all_to_all x1, waiting for transfers between devices: 7.91 us -> 3 us  [body(): squares = lax.all_to_all(squares, ('dp', 'seq'), 0, 0, tiled=True)]
    ppermute x22, waiting for transfers between devices: 29 us -> 26.6 us  [send(): return lax.ppermute(value, 'seq', seq_perm(dy, dx, dc))]
    ppermute x22, starting transfers between devices: 35.9 us -> 37.7 us  [send(): return lax.ppermute(value, 'seq', seq_perm(dy, dx, dc))]
    pallas_call x2 -> x3, Pallas kernels: 1.86 us -> 3.46 us  [the longest x1 1.56 us: rest_of_rows(): pl.pallas_call(rest_kernel, out_shape=(struct(shape, F32),) * (NY - 1), i...]
  transfers between devices with their start and end apart: 24 -> 24, of which waited for: 14 -> 14; matrix products, arithmetic and copies ran while one was open for 1% -> 1% of each run, Pallas kernels for 12% -> 14%
where the time goes in v8:
time: 124 us
  starting transfers between devices  61 us (49%)
  waiting for transfers between devices  32.5 us (26%)
  Pallas kernels  26.1 us (21%)
  local copies, waits for them, and re-layouts  3.19 us (3%)
    ppermute x22, starting transfers between devices, send(): return lax.ppermute(value, 'seq', seq_perm(dy, dx, dc))  37.7 us
    ppermute x22, waiting for transfers between devices, send(): return lax.ppermute(value, 'seq', seq_perm(dy, dx, dc))  26.6 us
    all_to_all x1, starting transfers between devices, body(): squares = lax.all_to_all(squares, ('dp', 'seq'), 0, 0, tiled=True)  13.1 us
    all_to_all x1, starting transfers between devices, body(): lax.all_to_all(folded, ('dp', 'seq'), 0, 0, axis_index_groups=columns_of)  10.3 us
    pallas_call x5, Pallas kernels, blocks(): pl.pallas_call(functools.partial(block_kernel, units), out_shape=(struct(...  8.76 us
    pallas_call x1, Pallas kernels, input_gradient(): pl.pallas_call(input_kernel, grid=(features // step,), out_shape=(struct(...  5.89 us
    all_to_all x1, waiting for transfers between devices, body(): squares = lax.all_to_all(squares, ('dp', 'seq'), 0, 0, tiled=True)  3 us
    all_to_all x1, waiting for transfers between devices, body(): lax.all_to_all(folded, ('dp', 'seq'), 0, 0, axis_index_groups=columns_of)  2.9 us
  transfers between devices with their start and end apart: 24, of which 14 were waited for; matrix products, arithmetic and copies ran while one was open for 1% of the time, Pallas kernels for 14%

profile of v8, /device:TPU:1, one launch (start us, length us, event | category | flops | bytes accessed | tf_op | source)
XLA Modules:
  0.0 123.8 jit_solution(4114274540952693239)
XLA Ops:
  0.7 0.1 pad_add_fusion.place
  0.7 0.9 copy-done
  1.7 0.9 copy-done.2
  2.6 1.8 %messages.1 = (f32[22,64,128]{2,1,0:T(8,128)}, f32[22,64,128]{2,1,0:T(8,128)S(1)}, f32[18,64,128]{2,1,0:T(8,128)}) custom-call(s32[3]{0:T(128)S(1)} %pad_add_fusion.place, bf16[2,64,1024]{2,1,0:T(8,128)(2,1)S(1)} %copy-done, bf16[2,64,1024]{2,1,0:T(8,128)(2,1)S(1)} %copy-done.2), custom_call_target="tpu_custom_call" | custom-call | flops 1048576 | bytes 3145728 | tf_op jit(solution)/shard_map/messages/pallas_call | solution.py:76
  4.4 2.0 %collective-permute-start.1 = (f32[22,64,128]{2,1,0:T(8,128)}, f32[22,64,128]{2,1,0:T(8,128)S(1)}, u32[]{:S(2)}, u32[]{:S(2)}) collective-permute-start(f32[22,64,128]{2,1,0:T(8,128)} %get-tuple-element.60), channel_id=1, source_target_pairs={{0,2},{1,3},{2,4},{3,5},{4,6},{5,7},{6,0},{7,1},{8,10},{9,11},{10,... | collective-permute-start | bytes 2162696 | tf_op jit(solution)/shard_map/ppermute | solution.py:38
  6.4 1.3 %collective-permute-start.2 = (f32[22,64,128]{2,1,0:T(8,128)S(1)}, f32[22,64,128]{2,1,0:T(8,128)S(1)}, u32[]{:S(2)}, u32[]{:S(2)}) collective-permute-start(f32[22,64,128]{2,1,0:T(8,128)S(1)} %get-tuple-element.61), channel_id=1, source_target_pairs={{0,6},{1,7},{2,0},{3,1},{4,2},{5,3},{6,4},{7,5},{8,14},{9,15},{10,... | collective-permute-start | bytes 2162696 | tf_op jit(solution)/shard_map/ppermute | solution.py:38
  7.7 3.2 %collective-permute-start = (f32[18,64,128]{2,1,0:T(8,128)}, f32[18,64,128]{2,1,0:T(8,128)S(1)}, u32[]{:S(2)}, u32[]{:S(2)}) collective-permute-start(f32[18,64,128]{2,1,0:T(8,128)} %get-tuple-element.58), channel_id=1, source_target_pairs={{0,1},{1,0},{2,3},{3,2},{4,5},{5,4},{6,7},{7,6},{8,9},{9,8},{10,11... | collective-permute-start | bytes 1769480 | tf_op jit(solution)/shard_map/ppermute | solution.py:38
  10.9 1.2 constant_dynamic-slice_fusion.2
  12.1 0.1 pad_maximum_fusion.w
  12.2 0.5 collective-permute-done.refs_2_
  12.7 2.0 %blocks.5 = (bf16[1024,256]{1,0:T(8,128)(2,1)S(1)}, bf16[256,384]{1,0:T(8,128)(2,1)S(1)}, bf16[256,128]{1,0:T(8,128)(2,1)S(1)}, f32[2,2,128,128]{3,2,1,0:T(8,128...) custom-call(s32[3]{0:T(128)S(1)} %pad_add_fusion.place, bf16[1024,384]{1,0:T(8,128)(2,1)S(1)} %pad_maximum_fusion.w, ...), custom_call_target="tpu_custom_call" | custom-call | flops 201326592 | bytes 4194304 | tf_op jit(solution)/shard_map/blocks/pallas_call | solution.py:148
  14.7 6.8 %collective-permute-done.1.refs_0_ = f32[22,64,128]{2,1,0:T(8,128)S(1)} collective-permute-done((f32[22,64,128]{2,1,0:T(8,128)}, f32[22,64,128]{2,1,0:T(8,128)S(1)}, u32[]{:S(2)}, u32[]{:S(2)}) %collective-permute-start.1) | collective-permute-done | bytes 720928 | tf_op jit(solution)/shard_map/ppermute | solution.py:38
  21.5 1.4 %collective-permute-done.2.refs_1_.refs_0_ = f32[22,64,128]{2,1,0:T(8,128)S(1)} collective-permute-done((f32[22,64,128]{2,1,0:T(8,128)S(1)}, f32[22,64,128]{2,1,0:T(8,128)S(1)}, u32[]{:S(2)}, u32[]{:S(2)}) %collective-permute-start.2) | collective-permute-done | bytes 720928 | tf_op jit(solution)/shard_map/ppermute | solution.py:38
  22.9 0.1 relay.3
  23.0 2.2 %collective-permute-start.3 = (f32[22,64,128]{2,1,0:T(8,128)S(1)}, f32[22,64,128]{2,1,0:T(8,128)S(1)}, u32[]{:S(2)}, u32[]{:S(2)}) collective-permute-start(f32[22,64,128]{2,1,0:T(8,128)S(1)} %get-tuple-element.62), channel_id=1, source_target_pairs={{0,1},{1,0},{2,3},{3,2},{4,5},{5,4},{6,7},{7,6},{8,9},{9,8},{10,11... | collective-permute-start | bytes 2162696 | tf_op jit(solution)/shard_map/ppermute | solution.py:38
  25.2 0.1 collective-permute-start.6
  25.3 1.3 %collective-permute-start.4 = (f32[10,64,128]{2,1,0:T(8,128)S(1)}, f32[10,64,128]{2,1,0:T(8,128)S(1)}, u32[]{:S(2)}, u32[]{:S(2)}) collective-permute-start(f32[10,64,128]{2,1,0:T(8,128)S(1)} %slice.8), channel_id=1, source_target_pairs={{0,2},{1,3},{2,4},{3,5},{4,6},{5,7},{6,0},{7,1},{8,10},{9,11},{10,... | collective-permute-start | bytes 983048 | tf_op jit(solution)/shard_map/ppermute | solution.py:38
  26.6 1.6 %collective-permute-start.5 = (f32[10,64,128]{2,1,0:T(8,128)S(1)}, f32[10,64,128]{2,1,0:T(8,128)S(1)}, u32[]{:S(2)}, u32[]{:S(2)}) collective-permute-start(f32[10,64,128]{2,1,0:T(8,128)S(1)} %slice.9), channel_id=1, source_target_pairs={{0,6},{1,7},{2,0},{3,1},{4,2},{5,3},{6,4},{7,5},{8,14},{9,15},{10,... | collective-permute-start | bytes 983048 | tf_op jit(solution)/shard_map/ppermute | solution.py:38
  28.2 0.0 collective-permute-done.3.refs_1_
  28.2 2.0 %blocks.6 = (bf16[1024,256]{1,0:T(8,128)(2,1)S(1)}, bf16[256,384]{1,0:T(8,128)(2,1)S(1)}, bf16[256,128]{1,0:T(8,128)(2,1)S(1)}, f32[2,2,128,128]{3,2,1,0:T(8,128...) custom-call(s32[3]{0:T(128)S(1)} %pad_add_fusion.place, bf16[1024,384]{1,0:T(8,128)(2,1)S(1)} %pad_maximum_fusion.w, ...), custom_call_target="tpu_custom_call" | custom-call | flops 201326592 | bytes 4194304 | tf_op jit(solution)/shard_map/blocks/pallas_call | solution.py:148
  30.2 2.0 %blocks.7 = (bf16[1024,256]{1,0:T(8,128)(2,1)S(1)}, bf16[256,384]{1,0:T(8,128)(2,1)S(1)}, bf16[256,128]{1,0:T(8,128)(2,1)S(1)}, f32[2,2,128,128]{3,2,1,0:T(8,128...) custom-call(s32[3]{0:T(128)S(1)} %pad_add_fusion.place, bf16[1024,384]{1,0:T(8,128)(2,1)S(1)} %pad_maximum_fusion.w, ...), custom_call_target="tpu_custom_call" | custom-call | flops 201326592 | bytes 4194304 | tf_op jit(solution)/shard_map/blocks/pallas_call | solution.py:148
  32.2 3.3 %collective-permute-done.4.refs_0_ = f32[10,64,128]{2,1,0:T(8,128)S(1)} collective-permute-done((f32[10,64,128]{2,1,0:T(8,128)S(1)}, f32[10,64,128]{2,1,0:T(8,128)S(1)}, u32[]{:S(2)}, u32[]{:S(2)}) %collective-permute-start.4) | collective-permute-done | bytes 327712 | tf_op jit(solution)/shard_map/ppermute | solution.py:38
  35.5 0.0 collective-permute-done.5.refs_1_
  35.5 1.4 %collective-permute-start.7 = (f32[20,64,128]{2,1,0:T(8,128)S(1)}, f32[20,64,128]{2,1,0:T(8,128)S(1)}, u32[]{:S(2)}, u32[]{:S(2)}) collective-permute-start(f32[20,64,128]{2,1,0:T(8,128)S(1)} %relay.4.refs_0_), channel_id=1, source_target_pairs={{0,1},{1,0},{2,3},{3,2},{4,5},{5,4},{6,7},{7,6},{8,9},{9,8},{10,11... | collective-permute-start | bytes 1966088 | tf_op jit(solution)/shard_map/ppermute | solution.py:38
  37.0 1.4 %blocks.8 = (bf16[1024,128]{1,0:T(8,128)(2,1)S(1)}, bf16[128,384]{1,0:T(8,128)(2,1)S(1)}, bf16[128,128]{1,0:T(8,128)(2,1)S(1)}, f32[1,2,128,128]{3,2,1,0:T(8,128...) custom-call(s32[3]{0:T(128)S(1)} %pad_add_fusion.place, bf16[1024,384]{1,0:T(8,128)(2,1)S(1)} %pad_maximum_fusion.w, ...), custom_call_target="tpu_custom_call" | custom-call | flops 100663296 | bytes 4194304 | tf_op jit(solution)/shard_map/blocks/pallas_call | solution.py:148
  38.4 0.3 collective-permute-done.7.refs_0_
  38.7 1.4 %blocks.9 = (bf16[1024,128]{1,0:T(8,128)(2,1)S(1)}, bf16[128,384]{1,0:T(8,128)(2,1)S(1)}, bf16[128,128]{1,0:T(8,128)(2,1)S(1)}, f32[1,2,128,128]{3,2,1,0:T(8,128...) custom-call(s32[3]{0:T(128)S(1)} %pad_add_fusion.place, bf16[1024,384]{1,0:T(8,128)(2,1)S(1)} %pad_maximum_fusion.w, ...), custom_call_target="tpu_custom_call" | custom-call | flops 100663296 | bytes 4194304 | tf_op jit(solution)/shard_map/blocks/pallas_call | solution.py:148
  40.1 0.6 totals.1
  40.8 3.1 %collective-permute-start.8 = (f32[2,128,128]{2,1,0:T(8,128)S(1)}, f32[2,128,128]{2,1,0:T(8,128)S(1)}, u32[]{:S(2)}, u32[]{:S(2)}) collective-permute-start(f32[2,128,128]{2,1,0:T(8,128)S(1)} %get-tuple-element.73), channel_id=1, source_target_pairs={{0,16},{1,17},{2,18},{3,19},{4,20},{5,21},{6,22},{7,23},{8,24},{9,... | collective-permute-start | bytes 393224 | tf_op jit(solution)/shard_map/ppermute | solution.py:38
  43.9 0.4 collective-permute-start.9
  44.3 2.3 %collective-permute-start.10 = (f32[2,128,128]{2,1,0:T(8,128)S(1)}, f32[2,128,128]{2,1,0:T(8,128)S(1)}, u32[]{:S(2)}, u32[]{:S(2)}) collective-permute-start(f32[2,128,128]{2,1,0:T(8,128)S(1)} %get-tuple-element.75), channel_id=1, source_target_pairs={{0,24},{1,25},{2,26},{3,27},{4,28},{5,29},{6,30},{7,31},{8,0},{9,1... | collective-permute-start | bytes 393224 | tf_op jit(solution)/shard_map/ppermute | solution.py:38
  46.5 0.6 collective-permute-done.8.refs_0_
  47.2 3.2 %collective-permute-done.9.refs_1_ = f32[2,128,128]{2,1,0:T(8,128)S(1)} collective-permute-done((f32[2,128,128]{2,1,0:T(8,128)S(1)}, f32[2,128,128]{2,1,0:T(8,128)S(1)}, u32[]{:S(2)}, u32[]{:S(2)}) %collective-permute-start.9) | collective-permute-done | bytes 131104 | tf_op jit(solution)/shard_map/ppermute | solution.py:38
  50.3 2.1 %gradients.1 = (bf16[1024,384]{1,0:T(8,128)(2,1)S(1)}, f32[512,384]{1,0:T(8,128)S(1)}, f32[8,32,384]{2,1,0:T(8,128)S(1)}) custom-call(s32[3]{0:T(128)S(1)} %pad_add_fusion.place, f32[2,128,128]{2,1,0:T(8,128)S(1)} %collective-permute-done.8.refs_0_, f32[2,128,128]{2,1,0:T(8,128)S(1)} %collective-permute-done.9.refs_1_, ...), custom_call_target="tpu_custom_call" | custom-call | flops 805306368 | bytes 10485760 | tf_op jit(solution)/shard_map/gradients/pallas_call | solution.py:295
  52.4 1.3 %collective-permute-start.11 = (f32[512,384]{1,0:T(8,128)S(1)}, f32[512,384]{1,0:T(8,128)S(1)}, u32[]{:S(2)}, u32[]{:S(2)}) collective-permute-start(f32[512,384]{1,0:T(8,128)S(1)} %get-tuple-element.97), channel_id=1, source_target_pairs={{0,1},{1,0},{2,3},{3,2},{4,5},{5,4},{6,7},{7,6},{8,9},{9,8},{10,11... | collective-permute-start | bytes 2359304 | tf_op jit(solution)/shard_map/ppermute | solution.py:38
  53.7 1.8 %collective-permute-start.15 = (f32[8,32,384]{2,1,0:T(8,128)S(1)}, f32[8,32,384]{2,1,0:T(8,128)S(1)}, u32[]{:S(2)}, u32[]{:S(2)}) collective-permute-start(f32[8,32,384]{2,1,0:T(8,128)S(1)} %get-tuple-element.102), channel_id=1, source_target_pairs={{0,16},{1,17},{2,18},{3,19},{4,20},{5,21},{6,22},{7,23},{8,24},{9,... | collective-permute-start | bytes 1179656 | tf_op jit(solution)/shard_map/ppermute | solution.py:38
  55.5 1.6 %rest_of_rows.1 = (f32[8,32,384]{2,1,0:T(8,128)S(1)}, f32[8,32,384]{2,1,0:T(8,128)S(1)}, f32[8,32,384]{2,1,0:T(8,128)S(1)}) custom-call(s32[3]{0:T(128)S(1)} %pad_add_fusion.place, bf16[1024,256]{1,0:T(8,128)(2,1)S(1)} %get-tuple-element.76.refs_13_.refs_0_, bf16[1024,256]{1,0:T(8,128)(2,1)S(1)} %get-tuple-element.77.refs_14_.refs_1_, ...), custom_call_target="tpu_custom_call" | custom-call | flops 1048576 | bytes 4194304 | tf_op jit(solution)/shard_map/rest_of_rows/pallas_call | solution.py:277
  57.1 1.6 %collective-permute-start.16 = (f32[8,32,384]{2,1,0:T(8,128)S(1)}, f32[8,32,384]{2,1,0:T(8,128)S(1)}, u32[]{:S(2)}, u32[]{:S(2)}) collective-permute-start(f32[8,32,384]{2,1,0:T(8,128)S(1)} %get-tuple-element.103), channel_id=1, source_target_pairs={{0,8},{1,9},{2,10},{3,11},{4,12},{5,13},{6,14},{7,15},{8,16},{9,17... | collective-permute-start | bytes 1179656 | tf_op jit(solution)/shard_map/ppermute | solution.py:38
  58.6 1.2 collective-permute-start.17
  59.8 0.8 relay.5
  60.7 2.5 %collective-permute-start.13 = (f32[256,384]{1,0:T(8,128)}, f32[256,384]{1,0:T(8,128)S(1)}, u32[]{:S(2)}, u32[]{:S(2)}) collective-permute-start(f32[256,384]{1,0:T(8,128)} %get-tuple-element.99), channel_id=1, source_target_pairs={{0,4},{1,5},{2,6},{3,7},{4,0},{5,1},{6,2},{7,3},{8,12},{9,13},{10,... | collective-permute-start | bytes 1179656 | tf_op jit(solution)/shard_map/ppermute | solution.py:38
  63.2 0.8 collective-permute-start.14
  64.0 1.9 %collective-permute-done.15.refs_0_ = f32[8,32,384]{2,1,0:T(8,128)S(1)} collective-permute-done((f32[8,32,384]{2,1,0:T(8,128)S(1)}, f32[8,32,384]{2,1,0:T(8,128)S(1)}, u32[]{:S(2)}, u32[]{:S(2)}) %collective-permute-start.15) | collective-permute-done | bytes 393248 | tf_op jit(solution)/shard_map/ppermute | solution.py:38
  65.9 2.8 %collective-permute-start.12 = (f32[256,384]{1,0:T(8,128)S(1)}, f32[256,384]{1,0:T(8,128)}, u32[]{:S(2)}, u32[]{:S(2)}) collective-permute-start(f32[256,384]{1,0:T(8,128)S(1)} %get-tuple-element.98.refs_4_), channel_id=1, source_target_pairs={{0,6},{1,7},{2,0},{3,1},{4,2},{5,3},{6,4},{7,5},{8,14},{9,15},{10,... | collective-permute-start | bytes 1179656 | tf_op jit(solution)/shard_map/ppermute | solution.py:38
  68.7 6.0 %collective-permute-done.16.refs_1_ = f32[8,32,384]{2,1,0:T(8,128)S(1)} collective-permute-done((f32[8,32,384]{2,1,0:T(8,128)S(1)}, f32[8,32,384]{2,1,0:T(8,128)S(1)}, u32[]{:S(2)}, u32[]{:S(2)}) %collective-permute-start.16) | collective-permute-done | bytes 393248 | tf_op jit(solution)/shard_map/ppermute | solution.py:38
  74.7 0.0 collective-permute-done.17.refs_2_
  74.7 1.4 %fold.1 = f32[8,32,384]{2,1,0:T(8,128)} custom-call(s32[3]{0:T(128)S(1)} %pad_add_fusion.place, f32[8,32,384]{2,1,0:T(8,128)S(1)} %collective-permute-done.15.refs_0_, f32[8,32,384]{2,1,0:T(8,128)S(1)} %collective-permute-done.16.refs_1_, f32[8,32,384]{2,1,0:T(8,128)S(1)} %collective-permute-done.17.refs_2_, f32[8,32,384]{2,1,0:T(8,128)S(1)} %get-tuple-element.105.refs_3_, ...), custom_call_target="tpu_custom_call" | custom-call | flops 1048576 | bytes 2097152 | tf_op jit(solution)/shard_map/fold/pallas_call | solution.py:374
  76.1 10.3 %all-to-all-start = ((f32[8,32,384]{2,1,0:T(8,128)}), f32[8,32,384]{2,1,0:T(8,128)S(1)}, u32[]{:S(2)}, u32[]{:S(2)}) async-start(f32[8,32,384]{2,1,0:T(8,128)} %fold.1), calls=%async_computation | async-start | bytes 786432 | tf_op jit(solution)/shard_map/all_to_all | solution.py:541
  86.4 0.0 collective-permute-done.13.refs_3_
  86.4 0.0 collective-permute-done.14.refs_4_
  86.4 5.9 %input_gradient.1 = (bf16[128,1024]{1,0:T(8,128)(2,1)}, f32[8,128]{1,0:T(8,128)S(1)}) custom-call(s32[3]{0:T(128)S(1)} %pad_add_fusion.place, bf16[1024,384]{1,0:T(8,128)(2,1)S(1)} %get-tuple-element.96.refs_0_.refs_5_, f32[512,384]{1,0:T(8,128)S(1)} %collective-permute-done.11.refs_1_, f32[256,384]{1,0:T(8,128)} %collective-permute-done.12.refs_2_, ...), custom_call_target="tpu_custom_call" | custom-call | flops 6442450944 | bytes 83886080 | tf_op jit(solution)/shard_map/input_gradient/pallas_call | solution.py:341
  92.3 2.9 %all-to-all-done.got = f32[8,32,384]{2,1,0:T(8,128)S(1)} async-done(((f32[8,32,384]{2,1,0:T(8,128)}), f32[8,32,384]{2,1,0:T(8,128)S(1)}, u32[]{:S(2)}, u32[]{:S(2)}) %all-to-all-start) | async-done | bytes 393248 | tf_op jit(solution)/shard_map/all_to_all | solution.py:541
  95.2 1.3 %square_sum.1 = (f32[256,128]{1,0:T(8,128)}, f32[8,384]{1,0:T(8,128)S(1)}, f32[8,384]{1,0:T(8,128)S(1)}, f32[8,384]{1,0:T(8,128)S(1)}, f32[8,384]{1,0:T(8,128)S(1)}) custom-call(s32[3]{0:T(128)S(1)} %pad_add_fusion.place, f32[8,32,384]{2,1,0:T(8,128)S(1)} %all-to-all-done.got, f32[8,128]{1,0:T(8,128)S(1)} %get-tuple-element.106.after), custom_call_target="tpu_custom_call" | custom-call | flops 1048576 | bytes 1048576 | tf_op jit(solution)/shard_map/square_sum/pallas_call | solution.py:398
  96.5 13.1 %all-to-all-start.1 = ((f32[256,1,128]{2,1,0:T(1,128)}), f32[256,1,128]{2,1,0:T(1,128)S(1)}, u32[]{:S(2)}, u32[]{:S(2)}) async-start(f32[256,1,128]{2,1,0:T(1,128)} %bitcast.5), calls=%async_computation.1 | async-start | bytes 262144 | tf_op jit(solution)/shard_map/all_to_all | solution.py:546
  109.6 1.5 %collective-permute-start.18 = (f32[8,384]{1,0:T(8,128)S(1)}, f32[8,384]{1,0:T(8,128)S(1)}, u32[]{:S(2)}, u32[]{:S(2)}) collective-permute-start(f32[8,384]{1,0:T(8,128)S(1)} %get-tuple-element.109), channel_id=1, source_target_pairs={{0,2},{1,3},{2,4},{3,5},{4,6},{5,7},{6,0},{7,1},{8,10},{9,11},{10,... | collective-permute-start | bytes 36872 | tf_op jit(solution)/shard_map/ppermute | solution.py:38
  111.0 2.4 %collective-permute-start.19 = (f32[8,384]{1,0:T(8,128)S(1)}, f32[8,384]{1,0:T(8,128)S(1)}, u32[]{:S(2)}, u32[]{:S(2)}) collective-permute-start(f32[8,384]{1,0:T(8,128)S(1)} %get-tuple-element.110), channel_id=1, source_target_pairs={{0,4},{1,5},{2,6},{3,7},{4,0},{5,1},{6,2},{7,3},{8,12},{9,13},{10,... | collective-permute-start | bytes 36872 | tf_op jit(solution)/shard_map/ppermute | solution.py:38
  113.4 1.2 collective-permute-start.20
  114.6 0.8 collective-permute-done.19.refs_2_
  115.4 0.9 collective-permute-done.20.refs_3_
  116.3 0.6 by_core.1
  116.9 1.8 %collective-permute-start.21 = (f32[16,384]{1,0:T(8,128)S(1)}, f32[16,384]{1,0:T(8,128)S(1)}, u32[]{:S(2)}, u32[]{:S(2)}) collective-permute-start(f32[16,384]{1,0:T(8,128)S(1)} %get-tuple-element.113), channel_id=1, source_target_pairs={{0,1},{1,0},{2,3},{3,2},{4,5},{5,4},{6,7},{7,6},{8,9},{9,8},{10,11... | collective-permute-start | bytes 73736 | tf_op jit(solution)/shard_map/ppermute | solution.py:38
  118.7 0.8 collective-permute-done.21.theirs
  119.6 3.0 %all-to-all-done.1 = f32[256,1,128]{2,1,0:T(1,128)S(1)} async-done(((f32[256,1,128]{2,1,0:T(1,128)}), f32[256,1,128]{2,1,0:T(1,128)S(1)}, u32[]{:S(2)}, u32[]{:S(2)}) %all-to-all-start.1) | async-done | bytes 131104 | tf_op jit(solution)/shard_map/all_to_all | solution.py:546
  122.6 1.2 clip.1
  (14 shorter events, 0.1 us)
Async XLA Ops:
  0.7 1.0 copy-start
  1.7 0.9 copy-start.2
  4.4 17.1 %collective-permute-start.1 = (f32[22,64,128]{2,1,0:T(8,128)}, f32[22,64,128]{2,1,0:T(8,128)S(1)}, u32[]{:S(2)}, u32[]{:S(2)}) collective-permute-start(f32[22,64,128]{2,1,0:T(8,128)} %get-tuple-element.60), channel_id=1, source_target_pairs={{0,2},{1,3},{2,4},{3,5},{4,6},{5,7},{6,0},{7,1},{8,10},{9,11},{10,... | collective-permute-start | bytes 2162696 | tf_op jit(solution)/shard_map/ppermute | solution.py:38
  6.4 16.4 %collective-permute-start.2 = (f32[22,64,128]{2,1,0:T(8,128)S(1)}, f32[22,64,128]{2,1,0:T(8,128)S(1)}, u32[]{:S(2)}, u32[]{:S(2)}) collective-permute-start(f32[22,64,128]{2,1,0:T(8,128)S(1)} %get-tuple-element.61), channel_id=1, source_target_pairs={{0,6},{1,7},{2,0},{3,1},{4,2},{5,3},{6,4},{7,5},{8,14},{9,15},{10,... | collective-permute-start | bytes 2162696 | tf_op jit(solution)/shard_map/ppermute | solution.py:38
  7.7 5.0 %collective-permute-start = (f32[18,64,128]{2,1,0:T(8,128)}, f32[18,64,128]{2,1,0:T(8,128)S(1)}, u32[]{:S(2)}, u32[]{:S(2)}) collective-permute-start(f32[18,64,128]{2,1,0:T(8,128)} %get-tuple-element.58), channel_id=1, source_target_pairs={{0,1},{1,0},{2,3},{3,2},{4,5},{5,4},{6,7},{7,6},{8,9},{9,8},{10,11... | collective-permute-start | bytes 1769480 | tf_op jit(solution)/shard_map/ppermute | solution.py:38
  10.9 1.8 %copy-start.1 = (bf16[2,64,1024]{2,1,0:T(8,128)(2,1)S(1)}, bf16[2,64,1024]{2,1,0:T(8,128)(2,1)}, u32[]{:S(2)}) copy-start(bf16[2,64,1024]{2,1,0:T(8,128)(2,1)} %refs_0_.1) | copy-start | bytes 786436
  10.9 1.8 %copy-start.3 = (bf16[2,64,1024]{2,1,0:T(8,128)(2,1)S(1)}, bf16[2,64,1024]{2,1,0:T(8,128)(2,1)}, u32[]{:S(2)}) copy-start(bf16[2,64,1024]{2,1,0:T(8,128)(2,1)} %refs_1_.1) | copy-start | bytes 786436
  23.0 5.2 %collective-permute-start.3 = (f32[22,64,128]{2,1,0:T(8,128)S(1)}, f32[22,64,128]{2,1,0:T(8,128)S(1)}, u32[]{:S(2)}, u32[]{:S(2)}) collective-permute-start(f32[22,64,128]{2,1,0:T(8,128)S(1)} %get-tuple-element.62), channel_id=1, source_target_pairs={{0,1},{1,0},{2,3},{3,2},{4,5},{5,4},{6,7},{7,6},{8,9},{9,8},{10,11... | collective-permute-start | bytes 2162696 | tf_op jit(solution)/shard_map/ppermute | solution.py:38
  25.2 5.0 %collective-permute-start.6 = (f32[22,64,128]{2,1,0:T(8,128)S(1)}, f32[22,64,128]{2,1,0:T(8,128)S(1)}, u32[]{:S(2)}, u32[]{:S(2)}) collective-permute-start(f32[22,64,128]{2,1,0:T(8,128)S(1)} %get-tuple-element.64), channel_id=1, source_target_pairs={{0,1},{1,0},{2,3},{3,2},{4,5},{5,4},{6,7},{7,6},{8,9},{9,8},{10,11... | collective-permute-start | bytes 2162696 | tf_op jit(solution)/shard_map/ppermute | solution.py:38
  25.3 10.2 %collective-permute-start.4 = (f32[10,64,128]{2,1,0:T(8,128)S(1)}, f32[10,64,128]{2,1,0:T(8,128)S(1)}, u32[]{:S(2)}, u32[]{:S(2)}) collective-permute-start(f32[10,64,128]{2,1,0:T(8,128)S(1)} %slice.8), channel_id=1, source_target_pairs={{0,2},{1,3},{2,4},{3,5},{4,6},{5,7},{6,0},{7,1},{8,10},{9,11},{10,... | collective-permute-start | bytes 983048 | tf_op jit(solution)/shard_map/ppermute | solution.py:38
  26.6 8.9 %collective-permute-start.5 = (f32[10,64,128]{2,1,0:T(8,128)S(1)}, f32[10,64,128]{2,1,0:T(8,128)S(1)}, u32[]{:S(2)}, u32[]{:S(2)}) collective-permute-start(f32[10,64,128]{2,1,0:T(8,128)S(1)} %slice.9), channel_id=1, source_target_pairs={{0,6},{1,7},{2,0},{3,1},{4,2},{5,3},{6,4},{7,5},{8,14},{9,15},{10,... | collective-permute-start | bytes 983048 | tf_op jit(solution)/shard_map/ppermute | solution.py:38
  35.5 3.1 %collective-permute-start.7 = (f32[20,64,128]{2,1,0:T(8,128)S(1)}, f32[20,64,128]{2,1,0:T(8,128)S(1)}, u32[]{:S(2)}, u32[]{:S(2)}) collective-permute-start(f32[20,64,128]{2,1,0:T(8,128)S(1)} %relay.4.refs_0_), channel_id=1, source_target_pairs={{0,1},{1,0},{2,3},{3,2},{4,5},{5,4},{6,7},{7,6},{8,9},{9,8},{10,11... | collective-permute-start | bytes 1966088 | tf_op jit(solution)/shard_map/ppermute | solution.py:38
  40.8 6.4 %collective-permute-start.8 = (f32[2,128,128]{2,1,0:T(8,128)S(1)}, f32[2,128,128]{2,1,0:T(8,128)S(1)}, u32[]{:S(2)}, u32[]{:S(2)}) collective-permute-start(f32[2,128,128]{2,1,0:T(8,128)S(1)} %get-tuple-element.73), channel_id=1, source_target_pairs={{0,16},{1,17},{2,18},{3,19},{4,20},{5,21},{6,22},{7,23},{8,24},{9,... | collective-permute-start | bytes 393224 | tf_op jit(solution)/shard_map/ppermute | solution.py:38
  43.9 6.5 %collective-permute-start.9 = (f32[2,128,128]{2,1,0:T(8,128)S(1)}, f32[2,128,128]{2,1,0:T(8,128)S(1)}, u32[]{:S(2)}, u32[]{:S(2)}) collective-permute-start(f32[2,128,128]{2,1,0:T(8,128)S(1)} %get-tuple-element.74), channel_id=1, source_target_pairs={{0,8},{1,9},{2,10},{3,11},{4,12},{5,13},{6,14},{7,15},{8,16},{9,17... | collective-permute-start | bytes 393224 | tf_op jit(solution)/shard_map/ppermute | solution.py:38
  44.3 6.1 %collective-permute-start.10 = (f32[2,128,128]{2,1,0:T(8,128)S(1)}, f32[2,128,128]{2,1,0:T(8,128)S(1)}, u32[]{:S(2)}, u32[]{:S(2)}) collective-permute-start(f32[2,128,128]{2,1,0:T(8,128)S(1)} %get-tuple-element.75), channel_id=1, source_target_pairs={{0,24},{1,25},{2,26},{3,27},{4,28},{5,29},{6,30},{7,31},{8,0},{9,1... | collective-permute-start | bytes 393224 | tf_op jit(solution)/shard_map/ppermute | solution.py:38
  52.4 7.4 %collective-permute-start.11 = (f32[512,384]{1,0:T(8,128)S(1)}, f32[512,384]{1,0:T(8,128)S(1)}, u32[]{:S(2)}, u32[]{:S(2)}) collective-permute-start(f32[512,384]{1,0:T(8,128)S(1)} %get-tuple-element.97), channel_id=1, source_target_pairs={{0,1},{1,0},{2,3},{3,2},{4,5},{5,4},{6,7},{7,6},{8,9},{9,8},{10,11... | collective-permute-start | bytes 2359304 | tf_op jit(solution)/shard_map/ppermute | solution.py:38
  53.7 12.2 %collective-permute-start.15 = (f32[8,32,384]{2,1,0:T(8,128)S(1)}, f32[8,32,384]{2,1,0:T(8,128)S(1)}, u32[]{:S(2)}, u32[]{:S(2)}) collective-permute-start(f32[8,32,384]{2,1,0:T(8,128)S(1)} %get-tuple-element.102), channel_id=1, source_target_pairs={{0,16},{1,17},{2,18},{3,19},{4,20},{5,21},{6,22},{7,23},{8,24},{9,... | collective-permute-start | bytes 1179656 | tf_op jit(solution)/shard_map/ppermute | solution.py:38
  57.1 17.6 %collective-permute-start.16 = (f32[8,32,384]{2,1,0:T(8,128)S(1)}, f32[8,32,384]{2,1,0:T(8,128)S(1)}, u32[]{:S(2)}, u32[]{:S(2)}) collective-permute-start(f32[8,32,384]{2,1,0:T(8,128)S(1)} %get-tuple-element.103), channel_id=1, source_target_pairs={{0,8},{1,9},{2,10},{3,11},{4,12},{5,13},{6,14},{7,15},{8,16},{9,17... | collective-permute-start | bytes 1179656 | tf_op jit(solution)/shard_map/ppermute | solution.py:38
  58.6 16.1 %collective-permute-start.17 = (f32[8,32,384]{2,1,0:T(8,128)S(1)}, f32[8,32,384]{2,1,0:T(8,128)S(1)}, u32[]{:S(2)}, u32[]{:S(2)}) collective-permute-start(f32[8,32,384]{2,1,0:T(8,128)S(1)} %get-tuple-element.104), channel_id=1, source_target_pairs={{0,24},{1,25},{2,26},{3,27},{4,28},{5,29},{6,30},{7,31},{8,0},{9,1... | collective-permute-start | bytes 1179656 | tf_op jit(solution)/shard_map/ppermute | solution.py:38
  60.7 25.7 %collective-permute-start.13 = (f32[256,384]{1,0:T(8,128)}, f32[256,384]{1,0:T(8,128)S(1)}, u32[]{:S(2)}, u32[]{:S(2)}) collective-permute-start(f32[256,384]{1,0:T(8,128)} %get-tuple-element.99), channel_id=1, source_target_pairs={{0,4},{1,5},{2,6},{3,7},{4,0},{5,1},{6,2},{7,3},{8,12},{9,13},{10,... | collective-permute-start | bytes 1179656 | tf_op jit(solution)/shard_map/ppermute | solution.py:38
  63.2 23.2 %collective-permute-start.14 = (f32[256,384]{1,0:T(8,128)S(1)}, f32[256,384]{1,0:T(8,128)S(1)}, u32[]{:S(2)}, u32[]{:S(2)}) collective-permute-start(f32[256,384]{1,0:T(8,128)S(1)} %get-tuple-element.100), channel_id=1, source_target_pairs={{0,2},{1,3},{2,4},{3,5},{4,6},{5,7},{6,0},{7,1},{8,10},{9,11},{10,... | collective-permute-start | bytes 1179656 | tf_op jit(solution)/shard_map/ppermute | solution.py:38
  65.9 20.5 %collective-permute-start.12 = (f32[256,384]{1,0:T(8,128)S(1)}, f32[256,384]{1,0:T(8,128)}, u32[]{:S(2)}, u32[]{:S(2)}) collective-permute-start(f32[256,384]{1,0:T(8,128)S(1)} %get-tuple-element.98.refs_4_), channel_id=1, source_target_pairs={{0,6},{1,7},{2,0},{3,1},{4,2},{5,3},{6,4},{7,5},{8,14},{9,15},{10,... | collective-permute-start | bytes 1179656 | tf_op jit(solution)/shard_map/ppermute | solution.py:38
  76.1 19.1 %all-to-all-start = ((f32[8,32,384]{2,1,0:T(8,128)}), f32[8,32,384]{2,1,0:T(8,128)S(1)}, u32[]{:S(2)}, u32[]{:S(2)}) async-start(f32[8,32,384]{2,1,0:T(8,128)} %fold.1), calls=%async_computation | async-start | bytes 786432 | tf_op jit(solution)/shard_map/all_to_all | solution.py:541
  96.5 26.1 %all-to-all-start.1 = ((f32[256,1,128]{2,1,0:T(1,128)}), f32[256,1,128]{2,1,0:T(1,128)S(1)}, u32[]{:S(2)}, u32[]{:S(2)}) async-start(f32[256,1,128]{2,1,0:T(1,128)} %bitcast.5), calls=%async_computation.1 | async-start | bytes 262144 | tf_op jit(solution)/shard_map/all_to_all | solution.py:546
  109.6 5.0 %collective-permute-start.18 = (f32[8,384]{1,0:T(8,128)S(1)}, f32[8,384]{1,0:T(8,128)S(1)}, u32[]{:S(2)}, u32[]{:S(2)}) collective-permute-start(f32[8,384]{1,0:T(8,128)S(1)} %get-tuple-element.109), channel_id=1, source_target_pairs={{0,2},{1,3},{2,4},{3,5},{4,6},{5,7},{6,0},{7,1},{8,10},{9,11},{10,... | collective-permute-start | bytes 36872 | tf_op jit(solution)/shard_map/ppermute | solution.py:38
  111.0 4.4 %collective-permute-start.19 = (f32[8,384]{1,0:T(8,128)S(1)}, f32[8,384]{1,0:T(8,128)S(1)}, u32[]{:S(2)}, u32[]{:S(2)}) collective-permute-start(f32[8,384]{1,0:T(8,128)S(1)} %get-tuple-element.110), channel_id=1, source_target_pairs={{0,4},{1,5},{2,6},{3,7},{4,0},{5,1},{6,2},{7,3},{8,12},{9,13},{10,... | collective-permute-start | bytes 36872 | tf_op jit(solution)/shard_map/ppermute | solution.py:38
  113.4 2.9 %collective-permute-start.20 = (f32[8,384]{1,0:T(8,128)S(1)}, f32[8,384]{1,0:T(8,128)S(1)}, u32[]{:S(2)}, u32[]{:S(2)}) collective-permute-start(f32[8,384]{1,0:T(8,128)S(1)} %get-tuple-element.111), channel_id=1, source_target_pairs={{0,6},{1,7},{2,0},{3,1},{4,2},{5,3},{6,4},{7,5},{8,14},{9,15},{10,... | collective-permute-start | bytes 36872 | tf_op jit(solution)/shard_map/ppermute | solution.py:38
  116.9 2.7 %collective-permute-start.21 = (f32[16,384]{1,0:T(8,128)S(1)}, f32[16,384]{1,0:T(8,128)S(1)}, u32[]{:S(2)}, u32[]{:S(2)}) collective-permute-start(f32[16,384]{1,0:T(8,128)S(1)} %get-tuple-element.113), channel_id=1, source_target_pairs={{0,1},{1,0},{2,3},{3,2},{4,5},{5,4},{6,7},{7,6},{8,9},{9,8},{10,11... | collective-permute-start | bytes 73736 | tf_op jit(solution)/shard_map/ppermute | solution.py:38

commit v9 on v8

--- a/solution.py
+++ b/solution.py
@@ -382,83 +382,71 @@
     )(place, *parts, after)
 
 
-def square_kernel(place, got, after, squares, *refs):
-    x, pieces, rows_of = place[1], refs[:NX], refs[NX]
-    rows = rows_of.shape[1]
+def square_kernel(got, after, out):
+    count, width = out.shape[0], got.shape[2] // DH
+    rows = got.shape[1] // count
     value = sum(got[z] for z in range(got.shape[0]))
-    squares[...] = jnp.full(squares.shape, jnp.sum(jnp.sum(value * value, axis=0, keepdims=True)))
-    for to in range(NX):
-        rows_of[to] = value[to * rows : (to + 1) * rows, :]
-    for dx in range(NX):
-        pieces[dx][...] = rows_of[(x + dx) % NX]
-
-
-def square_sum(place, got, after, copies):
-    rows, width = got.shape[1] // NX, got.shape[2]
+    square = jnp.sum(jnp.sum(value * value, axis=0, keepdims=True))
+    for to in range(count):
+        for part in range(width):
+            out[to, part * rows : (part + 1) * rows, :] = value[
+                to * rows : (to + 1) * rows, part * DH : (part + 1) * DH
+            ]
+        out[to, width * rows :, :] = jnp.full((rows, DH), square)
+
+
+def square_sum(got, after):
+    rows = (got.shape[2] // DH + 1) * got.shape[1] // GROUP
     return pl.pallas_call(
         square_kernel,
-        out_shape=(struct((copies, DH), F32),) + (struct((rows, width), F32),) * NX,
-        in_specs=[SMEM, VMEM, ANY],
-        out_specs=(VMEM,) * (1 + NX),
-        scratch_shapes=[pltpu.VMEM((NX, rows, width), F32)],
+        out_shape=struct((GROUP, rows, DH), F32),
+        in_specs=[VMEM, ANY],
+        out_specs=VMEM,
         compiler_params=pltpu.CompilerParams(vmem_limit_bytes=8 * MIB),
         cost_estimate=pl.CostEstimate(flops=MIB, bytes_accessed=MIB, transcendentals=0),
         name="square_sum",
-    )(place, got, after)
-
-
-def core_kernel(place, *refs):
-    c, pieces = place[2], refs[:NX]
-    mine, theirs, rows_of = refs[NX:]
-    rows = mine.shape[0] // NX
-    for dx in range(NX):
-        for core in range(2):
-            there = slice(dx * rows, (dx + 1) * rows)
-            rows_of[core, there, :] = pieces[dx][core * rows : (core + 1) * rows, :]
-    mine[...] = rows_of[c]
-    theirs[...] = rows_of[1 - c]
-
-
-def by_core(place, pieces):
-    rows, width = NX * pieces[0].shape[0] // 2, pieces[0].shape[1]
-    return pl.pallas_call(
-        core_kernel,
-        out_shape=(struct((rows, width), F32),) * 2,
-        in_specs=[SMEM] + [VMEM] * NX,
-        out_specs=(VMEM,) * 2,
-        scratch_shapes=[pltpu.VMEM((2, rows, width), F32)],
+    )(got, after)
+
+
+def group_square_kernel(parts, out):
+    last = parts.shape[1] - 1
+    square = sum(parts[i, last : last + 1, :] for i in range(parts.shape[0]))
+    out[...] = jnp.broadcast_to(square, out.shape)
+
+
+def group_square(parts, copies):
+    return pl.pallas_call(
+        group_square_kernel,
+        out_shape=struct((copies, DH), F32),
+        in_specs=[VMEM],
+        out_specs=VMEM,
         compiler_params=pltpu.CompilerParams(vmem_limit_bytes=8 * MIB),
         cost_estimate=pl.CostEstimate(flops=MIB, bytes_accessed=MIB, transcendentals=0),
-        name="by_core",
-    )(place, *pieces)
-
-
-def clip_kernel(place, squares, mine, theirs, out):
-    x, c = place[1], place[2]
+        name="group_square",
+    )(parts)
+
+
+def clip_kernel(squares, parts, out):
     rows = out.shape[0]
     total_sq = jnp.sum(squares[...], axis=0, keepdims=True)
     factor = jnp.minimum(1.0, D / jnp.sqrt(total_sq + 1e-06))
-    for dx in range(NX):
-        for core, source in enumerate((mine, theirs)):
-            head = ((x + NX - dx) % NX) * 2 + (c ^ core)
-            for part in range(3):
-                columns = slice(part * DH, (part + 1) * DH)
-                start = pl.multiple_of((part * H + head) * DH, DH)
-                value = source[dx * rows : (dx + 1) * rows, columns]
-                out[:, pl.ds(start, DH)] = value * factor
-
-
-def clip(place, squares, mine, theirs):
-    rows, width = mine.shape[0] // NX, mine.shape[1] * H
+    for head in range(H):
+        for part in range(3):
+            start = (part * H + head) * DH
+            out[:, start : start + DH] = parts[head, part * rows : (part + 1) * rows, :] * factor
+
+
+def clip(squares, parts):
+    rows = parts.shape[1] // 4
     return pl.pallas_call(
         clip_kernel,
-        out_shape=struct((rows, width), F32),
-        in_specs=[SMEM] + [VMEM] * 3,
+        out_shape=struct((rows, 3 * H * DH), F32),
+        in_specs=[VMEM, VMEM],
         out_specs=VMEM,
         compiler_params=pltpu.CompilerParams(vmem_limit_bytes=8 * MIB),
         cost_estimate=pl.CostEstimate(flops=MIB, bytes_accessed=MIB, transcendentals=0),
         name="clip",
-    )(place, squares, mine, theirs)
+    )(squares, parts)
 
 
 def body(inputs, grad_out, w_qkv):
@@ -542,11 +530,23 @@
     grad_rows, done = input_gradient(place, (grad_proj, theirs, *back), total_rows, w_qkv)
     grad_inputs = grad_rows.reshape(user_count, row_count, feature_count)
 
-    squares, *parts = square_sum(place, got, done, dp_count * lax.axis_size("seq"))
-    squares = lax.all_to_all(squares, ("dp", "seq"), 0, 0, tiled=True)
-    arrived_rows = {dx: send(parts[dx], dx=dx) for dx in FAR_FIRST}
-    mine, theirs = by_core(place, [parts[0]] + [arrived_rows[dx] for dx in range(1, NX)])
-    return (grad_inputs, clip(place, squares, mine, send(theirs, dc=1)))
+    seq_count = lax.axis_size("seq")
+    groups = [
+        [first + t for t in range(GROUP)] for first in range(0, dp_count * seq_count, GROUP)
+    ]
+    across = [[t + first[0] for first in groups] for t in range(GROUP)]
+    parts = lax.all_to_all(
+        square_sum(got, done), ("dp", "seq"), 0, 0, axis_index_groups=groups
+    )
+    squares = lax.all_to_all(
+        group_square(parts, dp_count * NY),
+        ("dp", "seq"),
+        0,
+        0,
+        axis_index_groups=across,
+        tiled=True,
+    )
+    return (grad_inputs, clip(squares, parts))
 
 
 def solution(mesh):

time: 124 us -> 124 us (level)
  blocking collectives: 0 us -> 27.4 us
  starting transfers between devices: 61 us -> 41.1 us
  waiting for transfers between devices: 32.5 us -> 26.9 us
  Pallas kernels: 26.1 us -> 23.9 us
    all_to_all x0 -> x2, blocking collectives: none -> 27.4 us  [the longest x1 16.6 us: body(): lax.all_to_all(group_square(parts, dp_count * NY), ('dp', 'seq'), 0, 0, a...]
    all_to_all x1 -> x0, starting transfers between devices: 13.1 us -> none  [body(): squares = lax.all_to_all(squares, ('dp', 'seq'), 0, 0, tiled=True)]
    ppermute x22 -> x18, starting transfers between devices: 37.7 us -> 30.8 us  [send(): return lax.ppermute(value, 'seq', seq_perm(dy, dx, dc))]
    all_to_all x1 -> x0, waiting for transfers between devices: 3 us -> none  [body(): squares = lax.all_to_all(squares, ('dp', 'seq'), 0, 0, tiled=True)]
    ppermute x22 -> x18, waiting for transfers between devices: 26.6 us -> 24 us  [send(): return lax.ppermute(value, 'seq', seq_perm(dy, dx, dc))]
    pallas_call x3, Pallas kernels: 3.13 us -> 0.81 us  [the longest x1 0.65 us: clip(): pl.pallas_call(clip_kernel, out_shape=struct((rows, 3 * H * DH), F32), in...]
  transfers between devices with their start and end apart: 24 -> 19, of which waited for: 14 -> 10; matrix products, arithmetic and copies ran while one was open for 1% -> 1% of each run, Pallas kernels for 14% -> 14%
where the time goes in v9:
time: 124 us; the launch traced here: 123 us
  starting transfers between devices  41.1 us (33%)
  blocking collectives  27.4 us (22%)
  waiting for transfers between devices  26.9 us (22%)
  Pallas kernels  23.9 us (19%)
  local copies, waits for them, and re-layouts  3.19 us (3%)
    ppermute x18, starting transfers between devices, send(): return lax.ppermute(value, 'seq', seq_perm(dy, dx, dc))  30.8 us
    ppermute x18, waiting for transfers between devices, send(): return lax.ppermute(value, 'seq', seq_perm(dy, dx, dc))  24 us
    all_to_all x1, blocking collectives, body(): lax.all_to_all(group_square(parts, dp_count * NY), ('dp', 'seq'), 0, 0, a...  16.6 us
    all_to_all x1, blocking collectives, body(): lax.all_to_all(square_sum(got, done), ('dp', 'seq'), 0, 0, axis_index_gro...  10.8 us
    all_to_all x1, starting transfers between devices, body(): lax.all_to_all(folded, ('dp', 'seq'), 0, 0, axis_index_groups=columns_of)  10.3 us
    pallas_call x5, Pallas kernels, blocks(): pl.pallas_call(functools.partial(block_kernel, units), out_shape=(struct(...  8.75 us
    pallas_call x1, Pallas kernels, input_gradient(): pl.pallas_call(input_kernel, grid=(features // step,), out_shape=(struct(...  5.9 us
    all_to_all x1, waiting for transfers between devices, body(): lax.all_to_all(folded, ('dp', 'seq'), 0, 0, axis_index_groups=columns_of)  2.89 us
  transfers between devices with their start and end apart: 19, of which 10 were waited for; matrix products, arithmetic and copies ran while one was open for 1% of the time, Pallas kernels for 14%

profile of v9, /device:TPU:1, one launch (start us, length us, event | category | flops | bytes accessed | tf_op | source)
XLA Modules:
  0.0 123.4 jit_solution(765569528707772001)
XLA Ops:
  0.7 0.1 pad_add_fusion.place
  0.7 0.0 copy-start
  0.7 0.9 copy-done
  1.7 0.0 copy-start.2
  1.7 0.9 copy-done.2
  2.6 1.7 %messages.1 = (f32[22,64,128]{2,1,0:T(8,128)}, f32[22,64,128]{2,1,0:T(8,128)S(1)}, f32[18,64,128]{2,1,0:T(8,128)}) custom-call(s32[3]{0:T(128)S(1)} %pad_add_fusion.place, bf16[2,64,1024]{2,1,0:T(8,128)(2,1)S(1)} %copy-done, bf16[2,64,1024]{2,1,0:T(8,128)(2,1)S(1)} %copy-done.2), custom_call_target="tpu_custom_call" | custom-call | flops 1048576 | bytes 3145728 | tf_op jit(solution)/shard_map/messages/pallas_call | solution.py:76
  4.4 2.0 %collective-permute-start.1 = (f32[22,64,128]{2,1,0:T(8,128)}, f32[22,64,128]{2,1,0:T(8,128)S(1)}, u32[]{:S(2)}, u32[]{:S(2)}) collective-permute-start(f32[22,64,128]{2,1,0:T(8,128)} %get-tuple-element.53), channel_id=1, source_target_pairs={{0,2},{1,3},{2,4},{3,5},{4,6},{5,7},{6,0},{7,1},{8,10},{9,11},{10,... | collective-permute-start | bytes 2162696 | tf_op jit(solution)/shard_map/ppermute | solution.py:38
  6.4 1.3 %collective-permute-start.2 = (f32[22,64,128]{2,1,0:T(8,128)S(1)}, f32[22,64,128]{2,1,0:T(8,128)S(1)}, u32[]{:S(2)}, u32[]{:S(2)}) collective-permute-start(f32[22,64,128]{2,1,0:T(8,128)S(1)} %get-tuple-element.54), channel_id=1, source_target_pairs={{0,6},{1,7},{2,0},{3,1},{4,2},{5,3},{6,4},{7,5},{8,14},{9,15},{10,... | collective-permute-start | bytes 2162696 | tf_op jit(solution)/shard_map/ppermute | solution.py:38
  7.7 3.2 %collective-permute-start = (f32[18,64,128]{2,1,0:T(8,128)}, f32[18,64,128]{2,1,0:T(8,128)S(1)}, u32[]{:S(2)}, u32[]{:S(2)}) collective-permute-start(f32[18,64,128]{2,1,0:T(8,128)} %get-tuple-element.51), channel_id=1, source_target_pairs={{0,1},{1,0},{2,3},{3,2},{4,5},{5,4},{6,7},{7,6},{8,9},{9,8},{10,11... | collective-permute-start | bytes 1769480 | tf_op jit(solution)/shard_map/ppermute | solution.py:38
  10.9 1.2 constant_dynamic-slice_fusion.2
  12.1 0.1 pad_maximum_fusion.w
  12.2 0.5 collective-permute-done.refs_2_
  12.7 0.0 copy-done.1
  12.7 0.0 copy-done.3
  12.7 2.0 %blocks.5 = (bf16[1024,256]{1,0:T(8,128)(2,1)S(1)}, bf16[256,384]{1,0:T(8,128)(2,1)S(1)}, bf16[256,128]{1,0:T(8,128)(2,1)S(1)}, f32[2,2,128,128]{3,2,1,0:T(8,128...) custom-call(s32[3]{0:T(128)S(1)} %pad_add_fusion.place, bf16[1024,384]{1,0:T(8,128)(2,1)S(1)} %pad_maximum_fusion.w, ...), custom_call_target="tpu_custom_call" | custom-call | flops 201326592 | bytes 4194304 | tf_op jit(solution)/shard_map/blocks/pallas_call | solution.py:148
  14.7 6.8 %collective-permute-done.1.refs_0_ = f32[22,64,128]{2,1,0:T(8,128)S(1)} collective-permute-done((f32[22,64,128]{2,1,0:T(8,128)}, f32[22,64,128]{2,1,0:T(8,128)S(1)}, u32[]{:S(2)}, u32[]{:S(2)}) %collective-permute-start.1) | collective-permute-done | bytes 720928 | tf_op jit(solution)/shard_map/ppermute | solution.py:38
  21.5 1.4 %collective-permute-done.2.refs_1_.refs_0_ = f32[22,64,128]{2,1,0:T(8,128)S(1)} collective-permute-done((f32[22,64,128]{2,1,0:T(8,128)S(1)}, f32[22,64,128]{2,1,0:T(8,128)S(1)}, u32[]{:S(2)}, u32[]{:S(2)}) %collective-permute-start.2) | collective-permute-done | bytes 720928 | tf_op jit(solution)/shard_map/ppermute | solution.py:38
  22.9 0.1 relay.3
  23.0 2.2 %collective-permute-start.3 = (f32[22,64,128]{2,1,0:T(8,128)S(1)}, f32[22,64,128]{2,1,0:T(8,128)S(1)}, u32[]{:S(2)}, u32[]{:S(2)}) collective-permute-start(f32[22,64,128]{2,1,0:T(8,128)S(1)} %get-tuple-element.55), channel_id=1, source_target_pairs={{0,1},{1,0},{2,3},{3,2},{4,5},{5,4},{6,7},{7,6},{8,9},{9,8},{10,11... | collective-permute-start | bytes 2162696 | tf_op jit(solution)/shard_map/ppermute | solution.py:38
  25.2 0.1 collective-permute-start.6
  25.3 1.3 %collective-permute-start.4 = (f32[10,64,128]{2,1,0:T(8,128)S(1)}, f32[10,64,128]{2,1,0:T(8,128)S(1)}, u32[]{:S(2)}, u32[]{:S(2)}) collective-permute-start(f32[10,64,128]{2,1,0:T(8,128)S(1)} %slice.8), channel_id=1, source_target_pairs={{0,2},{1,3},{2,4},{3,5},{4,6},{5,7},{6,0},{7,1},{8,10},{9,11},{10,... | collective-permute-start | bytes 983048 | tf_op jit(solution)/shard_map/ppermute | solution.py:38
  26.6 1.6 %collective-permute-start.5 = (f32[10,64,128]{2,1,0:T(8,128)S(1)}, f32[10,64,128]{2,1,0:T(8,128)S(1)}, u32[]{:S(2)}, u32[]{:S(2)}) collective-permute-start(f32[10,64,128]{2,1,0:T(8,128)S(1)} %slice.9), channel_id=1, source_target_pairs={{0,6},{1,7},{2,0},{3,1},{4,2},{5,3},{6,4},{7,5},{8,14},{9,15},{10,... | collective-permute-start | bytes 983048 | tf_op jit(solution)/shard_map/ppermute | solution.py:38
  28.2 0.0 collective-permute-done.3.refs_1_
  28.2 2.0 %blocks.6 = (bf16[1024,256]{1,0:T(8,128)(2,1)S(1)}, bf16[256,384]{1,0:T(8,128)(2,1)S(1)}, bf16[256,128]{1,0:T(8,128)(2,1)S(1)}, f32[2,2,128,128]{3,2,1,0:T(8,128...) custom-call(s32[3]{0:T(128)S(1)} %pad_add_fusion.place, bf16[1024,384]{1,0:T(8,128)(2,1)S(1)} %pad_maximum_fusion.w, ...), custom_call_target="tpu_custom_call" | custom-call | flops 201326592 | bytes 4194304 | tf_op jit(solution)/shard_map/blocks/pallas_call | solution.py:148
  30.1 0.0 collective-permute-done.6.refs_1_
  30.2 2.0 %blocks.7 = (bf16[1024,256]{1,0:T(8,128)(2,1)S(1)}, bf16[256,384]{1,0:T(8,128)(2,1)S(1)}, bf16[256,128]{1,0:T(8,128)(2,1)S(1)}, f32[2,2,128,128]{3,2,1,0:T(8,128...) custom-call(s32[3]{0:T(128)S(1)} %pad_add_fusion.place, bf16[1024,384]{1,0:T(8,128)(2,1)S(1)} %pad_maximum_fusion.w, ...), custom_call_target="tpu_custom_call" | custom-call | flops 201326592 | bytes 4194304 | tf_op jit(solution)/shard_map/blocks/pallas_call | solution.py:148
  32.1 3.3 %collective-permute-done.4.refs_0_ = f32[10,64,128]{2,1,0:T(8,128)S(1)} collective-permute-done((f32[10,64,128]{2,1,0:T(8,128)S(1)}, f32[10,64,128]{2,1,0:T(8,128)S(1)}, u32[]{:S(2)}, u32[]{:S(2)}) %collective-permute-start.4) | collective-permute-done | bytes 327712 | tf_op jit(solution)/shard_map/ppermute | solution.py:38
  35.5 0.0 collective-permute-done.5.refs_1_
  35.5 1.4 %collective-permute-start.7 = (f32[20,64,128]{2,1,0:T(8,128)S(1)}, f32[20,64,128]{2,1,0:T(8,128)S(1)}, u32[]{:S(2)}, u32[]{:S(2)}) collective-permute-start(f32[20,64,128]{2,1,0:T(8,128)S(1)} %relay.4.refs_0_), channel_id=1, source_target_pairs={{0,1},{1,0},{2,3},{3,2},{4,5},{5,4},{6,7},{7,6},{8,9},{9,8},{10,11... | collective-permute-start | bytes 1966088 | tf_op jit(solution)/shard_map/ppermute | solution.py:38
  36.9 1.4 %blocks.8 = (bf16[1024,128]{1,0:T(8,128)(2,1)S(1)}, bf16[128,384]{1,0:T(8,128)(2,1)S(1)}, bf16[128,128]{1,0:T(8,128)(2,1)S(1)}, f32[1,2,128,128]{3,2,1,0:T(8,128...) custom-call(s32[3]{0:T(128)S(1)} %pad_add_fusion.place, bf16[1024,384]{1,0:T(8,128)(2,1)S(1)} %pad_maximum_fusion.w, ...), custom_call_target="tpu_custom_call" | custom-call | flops 100663296 | bytes 4194304 | tf_op jit(solution)/shard_map/blocks/pallas_call | solution.py:148
  38.4 0.3 collective-permute-done.7.refs_0_
  38.7 1.4 %blocks.9 = (bf16[1024,128]{1,0:T(8,128)(2,1)S(1)}, bf16[128,384]{1,0:T(8,128)(2,1)S(1)}, bf16[128,128]{1,0:T(8,128)(2,1)S(1)}, f32[1,2,128,128]{3,2,1,0:T(8,128...) custom-call(s32[3]{0:T(128)S(1)} %pad_add_fusion.place, bf16[1024,384]{1,0:T(8,128)(2,1)S(1)} %pad_maximum_fusion.w, ...), custom_call_target="tpu_custom_call" | custom-call | flops 100663296 | bytes 4194304 | tf_op jit(solution)/shard_map/blocks/pallas_call | solution.py:148
  40.1 0.6 totals.1
  40.7 3.1 %collective-permute-start.8 = (f32[2,128,128]{2,1,0:T(8,128)S(1)}, f32[2,128,128]{2,1,0:T(8,128)S(1)}, u32[]{:S(2)}, u32[]{:S(2)}) collective-permute-start(f32[2,128,128]{2,1,0:T(8,128)S(1)} %get-tuple-element.66), channel_id=1, source_target_pairs={{0,16},{1,17},{2,18},{3,19},{4,20},{5,21},{6,22},{7,23},{8,24},{9,... | collective-permute-start | bytes 393224 | tf_op jit(solution)/shard_map/ppermute | solution.py:38
  43.9 0.4 collective-permute-start.9
  44.3 2.3 %collective-permute-start.10 = (f32[2,128,128]{2,1,0:T(8,128)S(1)}, f32[2,128,128]{2,1,0:T(8,128)S(1)}, u32[]{:S(2)}, u32[]{:S(2)}) collective-permute-start(f32[2,128,128]{2,1,0:T(8,128)S(1)} %get-tuple-element.68), channel_id=1, source_target_pairs={{0,24},{1,25},{2,26},{3,27},{4,28},{5,29},{6,30},{7,31},{8,0},{9,1... | collective-permute-start | bytes 393224 | tf_op jit(solution)/shard_map/ppermute | solution.py:38
  46.5 0.6 collective-permute-done.8.refs_0_
  47.2 3.2 %collective-permute-done.9.refs_1_ = f32[2,128,128]{2,1,0:T(8,128)S(1)} collective-permute-done((f32[2,128,128]{2,1,0:T(8,128)S(1)}, f32[2,128,128]{2,1,0:T(8,128)S(1)}, u32[]{:S(2)}, u32[]{:S(2)}) %collective-permute-start.9) | collective-permute-done | bytes 131104 | tf_op jit(solution)/shard_map/ppermute | solution.py:38
  50.3 0.0 collective-permute-done.10.refs_2_
  50.3 2.1 %gradients.1 = (bf16[1024,384]{1,0:T(8,128)(2,1)S(1)}, f32[512,384]{1,0:T(8,128)S(1)}, f32[8,32,384]{2,1,0:T(8,128)S(1)}) custom-call(s32[3]{0:T(128)S(1)} %pad_add_fusion.place, f32[2,128,128]{2,1,0:T(8,128)S(1)} %collective-permute-done.8.refs_0_, f32[2,128,128]{2,1,0:T(8,128)S(1)} %collective-permute-done.9.refs_1_, ...), custom_call_target="tpu_custom_call" | custom-call | flops 805306368 | bytes 10485760 | tf_op jit(solution)/shard_map/gradients/pallas_call | solution.py:295
  52.4 1.3 %collective-permute-start.11 = (f32[512,384]{1,0:T(8,128)S(1)}, f32[512,384]{1,0:T(8,128)S(1)}, u32[]{:S(2)}, u32[]{:S(2)}) collective-permute-start(f32[512,384]{1,0:T(8,128)S(1)} %get-tuple-element.90), channel_id=1, source_target_pairs={{0,1},{1,0},{2,3},{3,2},{4,5},{5,4},{6,7},{7,6},{8,9},{9,8},{10,11... | collective-permute-start | bytes 2359304 | tf_op jit(solution)/shard_map/ppermute | solution.py:38
  53.7 1.8 %collective-permute-start.15 = (f32[8,32,384]{2,1,0:T(8,128)S(1)}, f32[8,32,384]{2,1,0:T(8,128)S(1)}, u32[]{:S(2)}, u32[]{:S(2)}) collective-permute-start(f32[8,32,384]{2,1,0:T(8,128)S(1)} %get-tuple-element.95), channel_id=1, source_target_pairs={{0,16},{1,17},{2,18},{3,19},{4,20},{5,21},{6,22},{7,23},{8,24},{9,... | collective-permute-start | bytes 1179656 | tf_op jit(solution)/shard_map/ppermute | solution.py:38
  55.5 1.6 %rest_of_rows.1 = (f32[8,32,384]{2,1,0:T(8,128)S(1)}, f32[8,32,384]{2,1,0:T(8,128)S(1)}, f32[8,32,384]{2,1,0:T(8,128)S(1)}) custom-call(s32[3]{0:T(128)S(1)} %pad_add_fusion.place, bf16[1024,256]{1,0:T(8,128)(2,1)S(1)} %get-tuple-element.69.refs_13_.refs_0_, bf16[1024,256]{1,0:T(8,128)(2,1)S(1)} %get-tuple-element.70.refs_14_.refs_1_, ...), custom_call_target="tpu_custom_call" | custom-call | flops 1048576 | bytes 4194304 | tf_op jit(solution)/shard_map/rest_of_rows/pallas_call | solution.py:277
  57.1 1.5 %collective-permute-start.16 = (f32[8,32,384]{2,1,0:T(8,128)S(1)}, f32[8,32,384]{2,1,0:T(8,128)S(1)}, u32[]{:S(2)}, u32[]{:S(2)}) collective-permute-start(f32[8,32,384]{2,1,0:T(8,128)S(1)} %get-tuple-element.96), channel_id=1, source_target_pairs={{0,8},{1,9},{2,10},{3,11},{4,12},{5,13},{6,14},{7,15},{8,16},{9,17... | collective-permute-start | bytes 1179656 | tf_op jit(solution)/shard_map/ppermute | solution.py:38
  58.6 1.2 collective-permute-start.17
  59.8 0.0 collective-permute-done.11.refs_1_
  59.8 0.8 relay.5
  60.7 2.5 %collective-permute-start.13 = (f32[256,384]{1,0:T(8,128)}, f32[256,384]{1,0:T(8,128)S(1)}, u32[]{:S(2)}, u32[]{:S(2)}) collective-permute-start(f32[256,384]{1,0:T(8,128)} %get-tuple-element.92), channel_id=1, source_target_pairs={{0,4},{1,5},{2,6},{3,7},{4,0},{5,1},{6,2},{7,3},{8,12},{9,13},{10,... | collective-permute-start | bytes 1179656 | tf_op jit(solution)/shard_map/ppermute | solution.py:38
  63.2 0.8 collective-permute-start.14
  64.0 1.9 %collective-permute-done.15.refs_0_ = f32[8,32,384]{2,1,0:T(8,128)S(1)} collective-permute-done((f32[8,32,384]{2,1,0:T(8,128)S(1)}, f32[8,32,384]{2,1,0:T(8,128)S(1)}, u32[]{:S(2)}, u32[]{:S(2)}) %collective-permute-start.15) | collective-permute-done | bytes 393248 | tf_op jit(solution)/shard_map/ppermute | solution.py:38
  65.9 2.8 %collective-permute-start.12 = (f32[256,384]{1,0:T(8,128)S(1)}, f32[256,384]{1,0:T(8,128)}, u32[]{:S(2)}, u32[]{:S(2)}) collective-permute-start(f32[256,384]{1,0:T(8,128)S(1)} %get-tuple-element.91.refs_4_), channel_id=1, source_target_pairs={{0,6},{1,7},{2,0},{3,1},{4,2},{5,3},{6,4},{7,5},{8,14},{9,15},{10,... | collective-permute-start | bytes 1179656 | tf_op jit(solution)/shard_map/ppermute | solution.py:38
  68.7 6.0 %collective-permute-done.16.refs_1_ = f32[8,32,384]{2,1,0:T(8,128)S(1)} collective-permute-done((f32[8,32,384]{2,1,0:T(8,128)S(1)}, f32[8,32,384]{2,1,0:T(8,128)S(1)}, u32[]{:S(2)}, u32[]{:S(2)}) %collective-permute-start.16) | collective-permute-done | bytes 393248 | tf_op jit(solution)/shard_map/ppermute | solution.py:38
  74.7 0.0 collective-permute-done.17.refs_2_
  74.7 1.4 %fold.1 = f32[8,32,384]{2,1,0:T(8,128)} custom-call(s32[3]{0:T(128)S(1)} %pad_add_fusion.place, f32[8,32,384]{2,1,0:T(8,128)S(1)} %collective-permute-done.15.refs_0_, f32[8,32,384]{2,1,0:T(8,128)S(1)} %collective-permute-done.16.refs_1_, f32[8,32,384]{2,1,0:T(8,128)S(1)} %collective-permute-done.17.refs_2_, f32[8,32,384]{2,1,0:T(8,128)S(1)} %get-tuple-element.98.refs_3_, ...), custom_call_target="tpu_custom_call" | custom-call | flops 1048576 | bytes 2097152 | tf_op jit(solution)/shard_map/fold/pallas_call | solution.py:374
  76.1 10.3 %all-to-all-start = ((f32[8,32,384]{2,1,0:T(8,128)}), f32[8,32,384]{2,1,0:T(8,128)S(1)}, u32[]{:S(2)}, u32[]{:S(2)}) async-start(f32[8,32,384]{2,1,0:T(8,128)} %fold.1), calls=%async_computation | async-start | bytes 786432 | tf_op jit(solution)/shard_map/all_to_all | solution.py:529
  86.4 0.0 collective-permute-done.13.refs_3_
  86.4 0.0 collective-permute-done.14.refs_4_
  86.4 0.0 collective-permute-done.12.refs_2_
  86.4 5.9 %input_gradient.1 = (bf16[128,1024]{1,0:T(8,128)(2,1)}, f32[8,128]{1,0:T(8,128)S(1)}) custom-call(s32[3]{0:T(128)S(1)} %pad_add_fusion.place, bf16[1024,384]{1,0:T(8,128)(2,1)S(1)} %get-tuple-element.89.refs_0_.refs_5_, f32[512,384]{1,0:T(8,128)S(1)} %collective-permute-done.11.refs_1_, f32[256,384]{1,0:T(8,128)} %collective-permute-done.12.refs_2_, ...), custom_call_target="tpu_custom_call" | custom-call | flops 6442450944 | bytes 83886080 | tf_op jit(solution)/shard_map/input_gradient/pallas_call | solution.py:341
  92.3 2.9 %all-to-all-done.got = f32[8,32,384]{2,1,0:T(8,128)S(1)} async-done(((f32[8,32,384]{2,1,0:T(8,128)}), f32[8,32,384]{2,1,0:T(8,128)S(1)}, u32[]{:S(2)}, u32[]{:S(2)}) %all-to-all-start) | async-done | bytes 393248 | tf_op jit(solution)/shard_map/all_to_all | solution.py:529
  95.2 0.1 square_sum.1
  95.3 10.8 %all_to_all.21.parts = f32[8,16,128]{2,1,0:T(8,128)S(1)} all-to-all(f32[8,16,128]{2,1,0:T(8,128)S(1)} %square_sum.1), channel_id=1, replica_groups={{0,1,2,3,4,5,6,7},{8,9,10,11,12,13,14,15},{16,17,18,19,20,21,22,23},{24..., dimensions={0} | all-to-all | bytes 131072 | tf_op jit(solution)/shard_map/all_to_all | solution.py:538
  106.2 16.6 %all_to_all.22 = f32[32,1,128]{2,1,0:T(1,128)S(1)} all-to-all(f32[32,1,128]{2,1,0:T(1,128)S(1)} %bitcast.8), channel_id=1, replica_groups={{0,8,16,24,32,40,48,56,64,72,80,88,96,104,112,120,128,136,144,152,160,1..., dimensions={0} | all-to-all | bytes 32768 | tf_op jit(solution)/shard_map/all_to_all | solution.py:541
  122.8 0.7 clip.1
  (6 shorter events, 0.1 us)
Async XLA Ops:
  0.7 1.0 copy-start
  1.7 0.9 copy-start.2
  4.4 17.1 %collective-permute-start.1 = (f32[22,64,128]{2,1,0:T(8,128)}, f32[22,64,128]{2,1,0:T(8,128)S(1)}, u32[]{:S(2)}, u32[]{:S(2)}) collective-permute-start(f32[22,64,128]{2,1,0:T(8,128)} %get-tuple-element.53), channel_id=1, source_target_pairs={{0,2},{1,3},{2,4},{3,5},{4,6},{5,7},{6,0},{7,1},{8,10},{9,11},{10,... | collective-permute-start | bytes 2162696 | tf_op jit(solution)/shard_map/ppermute | solution.py:38
  6.4 16.4 %collective-permute-start.2 = (f32[22,64,128]{2,1,0:T(8,128)S(1)}, f32[22,64,128]{2,1,0:T(8,128)S(1)}, u32[]{:S(2)}, u32[]{:S(2)}) collective-permute-start(f32[22,64,128]{2,1,0:T(8,128)S(1)} %get-tuple-element.54), channel_id=1, source_target_pairs={{0,6},{1,7},{2,0},{3,1},{4,2},{5,3},{6,4},{7,5},{8,14},{9,15},{10,... | collective-permute-start | bytes 2162696 | tf_op jit(solution)/shard_map/ppermute | solution.py:38
  7.7 5.0 %collective-permute-start = (f32[18,64,128]{2,1,0:T(8,128)}, f32[18,64,128]{2,1,0:T(8,128)S(1)}, u32[]{:S(2)}, u32[]{:S(2)}) collective-permute-start(f32[18,64,128]{2,1,0:T(8,128)} %get-tuple-element.51), channel_id=1, source_target_pairs={{0,1},{1,0},{2,3},{3,2},{4,5},{5,4},{6,7},{7,6},{8,9},{9,8},{10,11... | collective-permute-start | bytes 1769480 | tf_op jit(solution)/shard_map/ppermute | solution.py:38
  10.9 1.8 %copy-start.1 = (bf16[2,64,1024]{2,1,0:T(8,128)(2,1)S(1)}, bf16[2,64,1024]{2,1,0:T(8,128)(2,1)}, u32[]{:S(2)}) copy-start(bf16[2,64,1024]{2,1,0:T(8,128)(2,1)} %refs_0_.1) | copy-start | bytes 786436
  10.9 1.8 %copy-start.3 = (bf16[2,64,1024]{2,1,0:T(8,128)(2,1)S(1)}, bf16[2,64,1024]{2,1,0:T(8,128)(2,1)}, u32[]{:S(2)}) copy-start(bf16[2,64,1024]{2,1,0:T(8,128)(2,1)} %refs_1_.1) | copy-start | bytes 786436
  23.0 5.2 %collective-permute-start.3 = (f32[22,64,128]{2,1,0:T(8,128)S(1)}, f32[22,64,128]{2,1,0:T(8,128)S(1)}, u32[]{:S(2)}, u32[]{:S(2)}) collective-permute-start(f32[22,64,128]{2,1,0:T(8,128)S(1)} %get-tuple-element.55), channel_id=1, source_target_pairs={{0,1},{1,0},{2,3},{3,2},{4,5},{5,4},{6,7},{7,6},{8,9},{9,8},{10,11... | collective-permute-start | bytes 2162696 | tf_op jit(solution)/shard_map/ppermute | solution.py:38
  25.2 5.0 %collective-permute-start.6 = (f32[22,64,128]{2,1,0:T(8,128)S(1)}, f32[22,64,128]{2,1,0:T(8,128)S(1)}, u32[]{:S(2)}, u32[]{:S(2)}) collective-permute-start(f32[22,64,128]{2,1,0:T(8,128)S(1)} %get-tuple-element.57), channel_id=1, source_target_pairs={{0,1},{1,0},{2,3},{3,2},{4,5},{5,4},{6,7},{7,6},{8,9},{9,8},{10,11... | collective-permute-start | bytes 2162696 | tf_op jit(solution)/shard_map/ppermute | solution.py:38
  25.3 10.2 %collective-permute-start.4 = (f32[10,64,128]{2,1,0:T(8,128)S(1)}, f32[10,64,128]{2,1,0:T(8,128)S(1)}, u32[]{:S(2)}, u32[]{:S(2)}) collective-permute-start(f32[10,64,128]{2,1,0:T(8,128)S(1)} %slice.8), channel_id=1, source_target_pairs={{0,2},{1,3},{2,4},{3,5},{4,6},{5,7},{6,0},{7,1},{8,10},{9,11},{10,... | collective-permute-start | bytes 983048 | tf_op jit(solution)/shard_map/ppermute | solution.py:38
  26.6 8.9 %collective-permute-start.5 = (f32[10,64,128]{2,1,0:T(8,128)S(1)}, f32[10,64,128]{2,1,0:T(8,128)S(1)}, u32[]{:S(2)}, u32[]{:S(2)}) collective-permute-start(f32[10,64,128]{2,1,0:T(8,128)S(1)} %slice.9), channel_id=1, source_target_pairs={{0,6},{1,7},{2,0},{3,1},{4,2},{5,3},{6,4},{7,5},{8,14},{9,15},{10,... | collective-permute-start | bytes 983048 | tf_op jit(solution)/shard_map/ppermute | solution.py:38
  35.5 3.1 %collective-permute-start.7 = (f32[20,64,128]{2,1,0:T(8,128)S(1)}, f32[20,64,128]{2,1,0:T(8,128)S(1)}, u32[]{:S(2)}, u32[]{:S(2)}) collective-permute-start(f32[20,64,128]{2,1,0:T(8,128)S(1)} %relay.4.refs_0_), channel_id=1, source_target_pairs={{0,1},{1,0},{2,3},{3,2},{4,5},{5,4},{6,7},{7,6},{8,9},{9,8},{10,11... | collective-permute-start | bytes 1966088 | tf_op jit(solution)/shard_map/ppermute | solution.py:38
  40.7 6.4 %collective-permute-start.8 = (f32[2,128,128]{2,1,0:T(8,128)S(1)}, f32[2,128,128]{2,1,0:T(8,128)S(1)}, u32[]{:S(2)}, u32[]{:S(2)}) collective-permute-start(f32[2,128,128]{2,1,0:T(8,128)S(1)} %get-tuple-element.66), channel_id=1, source_target_pairs={{0,16},{1,17},{2,18},{3,19},{4,20},{5,21},{6,22},{7,23},{8,24},{9,... | collective-permute-start | bytes 393224 | tf_op jit(solution)/shard_map/ppermute | solution.py:38
  43.9 6.5 %collective-permute-start.9 = (f32[2,128,128]{2,1,0:T(8,128)S(1)}, f32[2,128,128]{2,1,0:T(8,128)S(1)}, u32[]{:S(2)}, u32[]{:S(2)}) collective-permute-start(f32[2,128,128]{2,1,0:T(8,128)S(1)} %get-tuple-element.67), channel_id=1, source_target_pairs={{0,8},{1,9},{2,10},{3,11},{4,12},{5,13},{6,14},{7,15},{8,16},{9,17... | collective-permute-start | bytes 393224 | tf_op jit(solution)/shard_map/ppermute | solution.py:38
  44.3 6.1 %collective-permute-start.10 = (f32[2,128,128]{2,1,0:T(8,128)S(1)}, f32[2,128,128]{2,1,0:T(8,128)S(1)}, u32[]{:S(2)}, u32[]{:S(2)}) collective-permute-start(f32[2,128,128]{2,1,0:T(8,128)S(1)} %get-tuple-element.68), channel_id=1, source_target_pairs={{0,24},{1,25},{2,26},{3,27},{4,28},{5,29},{6,30},{7,31},{8,0},{9,1... | collective-permute-start | bytes 393224 | tf_op jit(solution)/shard_map/ppermute | solution.py:38
  52.4 7.4 %collective-permute-start.11 = (f32[512,384]{1,0:T(8,128)S(1)}, f32[512,384]{1,0:T(8,128)S(1)}, u32[]{:S(2)}, u32[]{:S(2)}) collective-permute-start(f32[512,384]{1,0:T(8,128)S(1)} %get-tuple-element.90), channel_id=1, source_target_pairs={{0,1},{1,0},{2,3},{3,2},{4,5},{5,4},{6,7},{7,6},{8,9},{9,8},{10,11... | collective-permute-start | bytes 2359304 | tf_op jit(solution)/shard_map/ppermute | solution.py:38
  53.7 12.2 %collective-permute-start.15 = (f32[8,32,384]{2,1,0:T(8,128)S(1)}, f32[8,32,384]{2,1,0:T(8,128)S(1)}, u32[]{:S(2)}, u32[]{:S(2)}) collective-permute-start(f32[8,32,384]{2,1,0:T(8,128)S(1)} %get-tuple-element.95), channel_id=1, source_target_pairs={{0,16},{1,17},{2,18},{3,19},{4,20},{5,21},{6,22},{7,23},{8,24},{9,... | collective-permute-start | bytes 1179656 | tf_op jit(solution)/shard_map/ppermute | solution.py:38
  57.1 17.6 %collective-permute-start.16 = (f32[8,32,384]{2,1,0:T(8,128)S(1)}, f32[8,32,384]{2,1,0:T(8,128)S(1)}, u32[]{:S(2)}, u32[]{:S(2)}) collective-permute-start(f32[8,32,384]{2,1,0:T(8,128)S(1)} %get-tuple-element.96), channel_id=1, source_target_pairs={{0,8},{1,9},{2,10},{3,11},{4,12},{5,13},{6,14},{7,15},{8,16},{9,17... | collective-permute-start | bytes 1179656 | tf_op jit(solution)/shard_map/ppermute | solution.py:38
  58.6 16.1 %collective-permute-start.17 = (f32[8,32,384]{2,1,0:T(8,128)S(1)}, f32[8,32,384]{2,1,0:T(8,128)S(1)}, u32[]{:S(2)}, u32[]{:S(2)}) collective-permute-start(f32[8,32,384]{2,1,0:T(8,128)S(1)} %get-tuple-element.97), channel_id=1, source_target_pairs={{0,24},{1,25},{2,26},{3,27},{4,28},{5,29},{6,30},{7,31},{8,0},{9,1... | collective-permute-start | bytes 1179656 | tf_op jit(solution)/shard_map/ppermute | solution.py:38
  60.7 25.7 %collective-permute-start.13 = (f32[256,384]{1,0:T(8,128)}, f32[256,384]{1,0:T(8,128)S(1)}, u32[]{:S(2)}, u32[]{:S(2)}) collective-permute-start(f32[256,384]{1,0:T(8,128)} %get-tuple-element.92), channel_id=1, source_target_pairs={{0,4},{1,5},{2,6},{3,7},{4,0},{5,1},{6,2},{7,3},{8,12},{9,13},{10,... | collective-permute-start | bytes 1179656 | tf_op jit(solution)/shard_map/ppermute | solution.py:38
  63.2 23.2 %collective-permute-start.14 = (f32[256,384]{1,0:T(8,128)S(1)}, f32[256,384]{1,0:T(8,128)S(1)}, u32[]{:S(2)}, u32[]{:S(2)}) collective-permute-start(f32[256,384]{1,0:T(8,128)S(1)} %get-tuple-element.93), channel_id=1, source_target_pairs={{0,2},{1,3},{2,4},{3,5},{4,6},{5,7},{6,0},{7,1},{8,10},{9,11},{10,... | collective-permute-start | bytes 1179656 | tf_op jit(solution)/shard_map/ppermute | solution.py:38
  65.9 20.5 %collective-permute-start.12 = (f32[256,384]{1,0:T(8,128)S(1)}, f32[256,384]{1,0:T(8,128)}, u32[]{:S(2)}, u32[]{:S(2)}) collective-permute-start(f32[256,384]{1,0:T(8,128)S(1)} %get-tuple-element.91.refs_4_), channel_id=1, source_target_pairs={{0,6},{1,7},{2,0},{3,1},{4,2},{5,3},{6,4},{7,5},{8,14},{9,15},{10,... | collective-permute-start | bytes 1179656 | tf_op jit(solution)/shard_map/ppermute | solution.py:38
  76.1 19.1 %all-to-all-start = ((f32[8,32,384]{2,1,0:T(8,128)}), f32[8,32,384]{2,1,0:T(8,128)S(1)}, u32[]{:S(2)}, u32[]{:S(2)}) async-start(f32[8,32,384]{2,1,0:T(8,128)} %fold.1), calls=%async_computation | async-start | bytes 786432 | tf_op jit(solution)/shard_map/all_to_all | solution.py:529

commit v10 on v9

--- a/solution.py
+++ b/solution.py
@@ -534,7 +534,9 @@
     groups = [
         [first + t for t in range(GROUP)] for first in range(0, dp_count * seq_count, GROUP)
     ]
-    across = [[t + first[0] for first in groups] for t in range(GROUP)]
+    half = len(groups) // 2
+    turned = (groups, groups[half:] + groups[:half])
+    across = [[t + first[0] for first in turned[t % 2]] for t in range(GROUP)]
     parts = lax.all_to_all(
         square_sum(got, done), ("dp", "seq"), 0, 0, axis_index_groups=groups
     )

time: 124 us -> 124 us (level)
  the two profiles are of different devices: /device:TPU:1 before, /device:TPU:2 now
where the time goes in v10:
time: 124 us; the launch traced here: 123 us
  waiting for transfers between devices  38.4 us (31%)
  starting transfers between devices  29.5 us (24%)
  blocking collectives  27.3 us (22%)
  Pallas kernels  23.9 us (19%)
  local copies, waits for them, and re-layouts  3.19 us (3%)
    ppermute x18, waiting for transfers between devices, send(): return lax.ppermute(value, 'seq', seq_perm(dy, dx, dc))  32.7 us
    ppermute x18, starting transfers between devices, send(): return lax.ppermute(value, 'seq', seq_perm(dy, dx, dc))  21 us
    all_to_all x1, blocking collectives, body(): lax.all_to_all(group_square(parts, dp_count * NY), ('dp', 'seq'), 0, 0, a...  18 us
    all_to_all x1, blocking collectives, body(): lax.all_to_all(square_sum(got, done), ('dp', 'seq'), 0, 0, axis_index_gro...  9.29 us
    pallas_call x5, Pallas kernels, blocks(): pl.pallas_call(functools.partial(block_kernel, units), out_shape=(struct(...  8.76 us
    all_to_all x1, starting transfers between devices, body(): lax.all_to_all(folded, ('dp', 'seq'), 0, 0, axis_index_groups=columns_of)  8.47 us
    pallas_call x1, Pallas kernels, input_gradient(): pl.pallas_call(input_kernel, grid=(features // step,), out_shape=(struct(...  5.9 us
    all_to_all x1, waiting for transfers between devices, body(): lax.all_to_all(folded, ('dp', 'seq'), 0, 0, axis_index_groups=columns_of)  5.7 us
  transfers between devices with their start and end apart: 19, of which 12 were waited for; matrix products, arithmetic and copies ran while one was open for 1% of the time, Pallas kernels for 14%

profile of v10, /device:TPU:2, one launch (start us, length us, event | category | flops | bytes accessed | tf_op | source)
XLA Modules:
  0.0 123.2 jit_solution(427068341375778370)
XLA Ops:
  0.7 0.1 pad_add_fusion.place
  0.7 0.0 copy-start
  0.7 0.9 copy-done
  1.7 0.9 copy-done.2
  2.6 1.7 %messages.1 = (f32[22,64,128]{2,1,0:T(8,128)}, f32[22,64,128]{2,1,0:T(8,128)S(1)}, f32[18,64,128]{2,1,0:T(8,128)}) custom-call(s32[3]{0:T(128)S(1)} %pad_add_fusion.place, bf16[2,64,1024]{2,1,0:T(8,128)(2,1)S(1)} %copy-done, bf16[2,64,1024]{2,1,0:T(8,128)(2,1)S(1)} %copy-done.2), custom_call_target="tpu_custom_call" | custom-call | flops 1048576 | bytes 3145728 | tf_op jit(solution)/shard_map/messages/pallas_call | solution.py:76
  4.4 1.5 %collective-permute-start.1 = (f32[22,64,128]{2,1,0:T(8,128)}, f32[22,64,128]{2,1,0:T(8,128)S(1)}, u32[]{:S(2)}, u32[]{:S(2)}) collective-permute-start(f32[22,64,128]{2,1,0:T(8,128)} %get-tuple-element.53), channel_id=1, source_target_pairs={{0,2},{1,3},{2,4},{3,5},{4,6},{5,7},{6,0},{7,1},{8,10},{9,11},{10,... | collective-permute-start | bytes 2162696 | tf_op jit(solution)/shard_map/ppermute | solution.py:38
  5.9 0.8 collective-permute-start.2
  6.7 0.0 collective-permute-start
  6.7 0.0 copy-start.1
  6.7 1.2 %constant_dynamic-slice_fusion.2 = (bf16[1024,128]{1,0:T(8,128)(2,1)S(1)}, bf16[1024,128]{1,0:T(8,128)(2,1)S(1)}, bf16[1024,128]{1,0:T(8,128)(2,1)S(1)}) fusion(bf16[1024,3072]{1,0:T(8,128)(2,1)} %refs_5_.1, s32[]{:T(128)S(6)} %select_n.31, s32[]{:T(128)S(6)} %select_n.32, s32[]{:T(128)S(6)} %select_n.33), kind=kLoop, calls=%fused_computation.3 | loop fusion | bytes 1572876 | tf_op jit(solution)/shard_map/dynamic_slice | solution.py:42
  7.9 0.1 pad_maximum_fusion.w
  8.0 0.9 collective-permute-done.refs_2_
  8.9 0.0 copy-done.1
  8.9 0.0 copy-done.3
  8.9 2.0 %blocks.5 = (bf16[1024,256]{1,0:T(8,128)(2,1)S(1)}, bf16[256,384]{1,0:T(8,128)(2,1)S(1)}, bf16[256,128]{1,0:T(8,128)(2,1)S(1)}, f32[2,2,128,128]{3,2,1,0:T(8,128...) custom-call(s32[3]{0:T(128)S(1)} %pad_add_fusion.place, bf16[1024,384]{1,0:T(8,128)(2,1)S(1)} %pad_maximum_fusion.w, ...), custom_call_target="tpu_custom_call" | custom-call | flops 201326592 | bytes 4194304 | tf_op jit(solution)/shard_map/blocks/pallas_call | solution.py:148
  10.9 11.6 %collective-permute-done.1.refs_0_ = f32[22,64,128]{2,1,0:T(8,128)S(1)} collective-permute-done((f32[22,64,128]{2,1,0:T(8,128)}, f32[22,64,128]{2,1,0:T(8,128)S(1)}, u32[]{:S(2)}, u32[]{:S(2)}) %collective-permute-start.1) | collective-permute-done | bytes 720928 | tf_op jit(solution)/shard_map/ppermute | solution.py:38
  22.5 1.0 collective-permute-done.2.refs_1_.refs_0_
  23.5 0.1 relay.3
  23.6 0.1 collective-permute-start.3
  23.7 0.5 collective-permute-start.6
  24.2 1.3 %collective-permute-start.4 = (f32[10,64,128]{2,1,0:T(8,128)S(1)}, f32[10,64,128]{2,1,0:T(8,128)S(1)}, u32[]{:S(2)}, u32[]{:S(2)}) collective-permute-start(f32[10,64,128]{2,1,0:T(8,128)S(1)} %slice.8), channel_id=1, source_target_pairs={{0,2},{1,3},{2,4},{3,5},{4,6},{5,7},{6,0},{7,1},{8,10},{9,11},{10,... | collective-permute-start | bytes 983048 | tf_op jit(solution)/shard_map/ppermute | solution.py:38
  25.5 0.9 collective-permute-start.5
  26.4 0.0 collective-permute-done.3.refs_1_
  26.4 2.0 %blocks.6 = (bf16[1024,256]{1,0:T(8,128)(2,1)S(1)}, bf16[256,384]{1,0:T(8,128)(2,1)S(1)}, bf16[256,128]{1,0:T(8,128)(2,1)S(1)}, f32[2,2,128,128]{3,2,1,0:T(8,128...) custom-call(s32[3]{0:T(128)S(1)} %pad_add_fusion.place, bf16[1024,384]{1,0:T(8,128)(2,1)S(1)} %pad_maximum_fusion.w, ...), custom_call_target="tpu_custom_call" | custom-call | flops 201326592 | bytes 4194304 | tf_op jit(solution)/shard_map/blocks/pallas_call | solution.py:148
  28.4 0.0 collective-permute-done.6.refs_1_
  28.4 2.0 %blocks.7 = (bf16[1024,256]{1,0:T(8,128)(2,1)S(1)}, bf16[256,384]{1,0:T(8,128)(2,1)S(1)}, bf16[256,128]{1,0:T(8,128)(2,1)S(1)}, f32[2,2,128,128]{3,2,1,0:T(8,128...) custom-call(s32[3]{0:T(128)S(1)} %pad_add_fusion.place, bf16[1024,384]{1,0:T(8,128)(2,1)S(1)} %pad_maximum_fusion.w, ...), custom_call_target="tpu_custom_call" | custom-call | flops 201326592 | bytes 4194304 | tf_op jit(solution)/shard_map/blocks/pallas_call | solution.py:148
  30.4 3.6 %collective-permute-done.4.refs_0_ = f32[10,64,128]{2,1,0:T(8,128)S(1)} collective-permute-done((f32[10,64,128]{2,1,0:T(8,128)S(1)}, f32[10,64,128]{2,1,0:T(8,128)S(1)}, u32[]{:S(2)}, u32[]{:S(2)}) %collective-permute-start.4) | collective-permute-done | bytes 327712 | tf_op jit(solution)/shard_map/ppermute | solution.py:38
  34.0 1.0 collective-permute-done.5.refs_1_
  35.1 0.1 collective-permute-start.7
  35.2 1.4 %blocks.8 = (bf16[1024,128]{1,0:T(8,128)(2,1)S(1)}, bf16[128,384]{1,0:T(8,128)(2,1)S(1)}, bf16[128,128]{1,0:T(8,128)(2,1)S(1)}, f32[1,2,128,128]{3,2,1,0:T(8,128...) custom-call(s32[3]{0:T(128)S(1)} %pad_add_fusion.place, bf16[1024,384]{1,0:T(8,128)(2,1)S(1)} %pad_maximum_fusion.w, ...), custom_call_target="tpu_custom_call" | custom-call | flops 100663296 | bytes 4194304 | tf_op jit(solution)/shard_map/blocks/pallas_call | solution.py:148
  36.6 0.7 collective-permute-done.7.refs_0_
  37.2 1.4 %blocks.9 = (bf16[1024,128]{1,0:T(8,128)(2,1)S(1)}, bf16[128,384]{1,0:T(8,128)(2,1)S(1)}, bf16[128,128]{1,0:T(8,128)(2,1)S(1)}, f32[1,2,128,128]{3,2,1,0:T(8,128...) custom-call(s32[3]{0:T(128)S(1)} %pad_add_fusion.place, bf16[1024,384]{1,0:T(8,128)(2,1)S(1)} %pad_maximum_fusion.w, ...), custom_call_target="tpu_custom_call" | custom-call | flops 100663296 | bytes 4194304 | tf_op jit(solution)/shard_map/blocks/pallas_call | solution.py:148
  38.7 0.6 totals.1
  39.3 3.3 %collective-permute-start.8 = (f32[2,128,128]{2,1,0:T(8,128)S(1)}, f32[2,128,128]{2,1,0:T(8,128)S(1)}, u32[]{:S(2)}, u32[]{:S(2)}) collective-permute-start(f32[2,128,128]{2,1,0:T(8,128)S(1)} %get-tuple-element.66), channel_id=1, source_target_pairs={{0,16},{1,17},{2,18},{3,19},{4,20},{5,21},{6,22},{7,23},{8,24},{9,... | collective-permute-start | bytes 393224 | tf_op jit(solution)/shard_map/ppermute | solution.py:38
  42.6 0.7 collective-permute-start.9
  43.3 2.6 %collective-permute-start.10 = (f32[2,128,128]{2,1,0:T(8,128)S(1)}, f32[2,128,128]{2,1,0:T(8,128)S(1)}, u32[]{:S(2)}, u32[]{:S(2)}) collective-permute-start(f32[2,128,128]{2,1,0:T(8,128)S(1)} %get-tuple-element.68), channel_id=1, source_target_pairs={{0,24},{1,25},{2,26},{3,27},{4,28},{5,29},{6,30},{7,31},{8,0},{9,1... | collective-permute-start | bytes 393224 | tf_op jit(solution)/shard_map/ppermute | solution.py:38
  45.8 1.4 %collective-permute-done.8.refs_0_ = f32[2,128,128]{2,1,0:T(8,128)S(1)} collective-permute-done((f32[2,128,128]{2,1,0:T(8,128)S(1)}, f32[2,128,128]{2,1,0:T(8,128)S(1)}, u32[]{:S(2)}, u32[]{:S(2)}) %collective-permute-start.8) | collective-permute-done | bytes 131104 | tf_op jit(solution)/shard_map/ppermute | solution.py:38
  47.2 2.3 %collective-permute-done.9.refs_1_ = f32[2,128,128]{2,1,0:T(8,128)S(1)} collective-permute-done((f32[2,128,128]{2,1,0:T(8,128)S(1)}, f32[2,128,128]{2,1,0:T(8,128)S(1)}, u32[]{:S(2)}, u32[]{:S(2)}) %collective-permute-start.9) | collective-permute-done | bytes 131104 | tf_op jit(solution)/shard_map/ppermute | solution.py:38
  49.6 0.0 collective-permute-done.10.refs_2_
  49.6 2.1 %gradients.1 = (bf16[1024,384]{1,0:T(8,128)(2,1)S(1)}, f32[512,384]{1,0:T(8,128)S(1)}, f32[8,32,384]{2,1,0:T(8,128)S(1)}) custom-call(s32[3]{0:T(128)S(1)} %pad_add_fusion.place, f32[2,128,128]{2,1,0:T(8,128)S(1)} %collective-permute-done.8.refs_0_, f32[2,128,128]{2,1,0:T(8,128)S(1)} %collective-permute-done.9.refs_1_, ...), custom_call_target="tpu_custom_call" | custom-call | flops 805306368 | bytes 10485760 | tf_op jit(solution)/shard_map/gradients/pallas_call | solution.py:295
  51.7 0.1 collective-permute-start.11
  51.8 2.2 %collective-permute-start.15 = (f32[8,32,384]{2,1,0:T(8,128)S(1)}, f32[8,32,384]{2,1,0:T(8,128)S(1)}, u32[]{:S(2)}, u32[]{:S(2)}) collective-permute-start(f32[8,32,384]{2,1,0:T(8,128)S(1)} %get-tuple-element.95), channel_id=1, source_target_pairs={{0,16},{1,17},{2,18},{3,19},{4,20},{5,21},{6,22},{7,23},{8,24},{9,... | collective-permute-start | bytes 1179656 | tf_op jit(solution)/shard_map/ppermute | solution.py:38
  54.0 1.6 %rest_of_rows.1 = (f32[8,32,384]{2,1,0:T(8,128)S(1)}, f32[8,32,384]{2,1,0:T(8,128)S(1)}, f32[8,32,384]{2,1,0:T(8,128)S(1)}) custom-call(s32[3]{0:T(128)S(1)} %pad_add_fusion.place, bf16[1024,256]{1,0:T(8,128)(2,1)S(1)} %get-tuple-element.69.refs_13_.refs_0_, bf16[1024,256]{1,0:T(8,128)(2,1)S(1)} %get-tuple-element.70.refs_14_.refs_1_, ...), custom_call_target="tpu_custom_call" | custom-call | flops 1048576 | bytes 4194304 | tf_op jit(solution)/shard_map/rest_of_rows/pallas_call | solution.py:277
  55.5 1.8 %collective-permute-start.16 = (f32[8,32,384]{2,1,0:T(8,128)S(1)}, f32[8,32,384]{2,1,0:T(8,128)S(1)}, u32[]{:S(2)}, u32[]{:S(2)}) collective-permute-start(f32[8,32,384]{2,1,0:T(8,128)S(1)} %get-tuple-element.96), channel_id=1, source_target_pairs={{0,8},{1,9},{2,10},{3,11},{4,12},{5,13},{6,14},{7,15},{8,16},{9,17... | collective-permute-start | bytes 1179656 | tf_op jit(solution)/shard_map/ppermute | solution.py:38
  57.3 1.5 %collective-permute-start.17 = (f32[8,32,384]{2,1,0:T(8,128)S(1)}, f32[8,32,384]{2,1,0:T(8,128)S(1)}, u32[]{:S(2)}, u32[]{:S(2)}) collective-permute-start(f32[8,32,384]{2,1,0:T(8,128)S(1)} %get-tuple-element.97), channel_id=1, source_target_pairs={{0,24},{1,25},{2,26},{3,27},{4,28},{5,29},{6,30},{7,31},{8,0},{9,1... | collective-permute-start | bytes 1179656 | tf_op jit(solution)/shard_map/ppermute | solution.py:38
  58.8 0.0 collective-permute-done.11.refs_1_
  58.8 0.8 relay.5
  59.7 2.8 %collective-permute-start.13 = (f32[256,384]{1,0:T(8,128)}, f32[256,384]{1,0:T(8,128)S(1)}, u32[]{:S(2)}, u32[]{:S(2)}) collective-permute-start(f32[256,384]{1,0:T(8,128)} %get-tuple-element.92), channel_id=1, source_target_pairs={{0,4},{1,5},{2,6},{3,7},{4,0},{5,1},{6,2},{7,3},{8,12},{9,13},{10,... | collective-permute-start | bytes 1179656 | tf_op jit(solution)/shard_map/ppermute | solution.py:38
  62.5 0.0 collective-permute-start.14
  62.5 2.8 %collective-permute-done.15.refs_0_ = f32[8,32,384]{2,1,0:T(8,128)S(1)} collective-permute-done((f32[8,32,384]{2,1,0:T(8,128)S(1)}, f32[8,32,384]{2,1,0:T(8,128)S(1)}, u32[]{:S(2)}, u32[]{:S(2)}) %collective-permute-start.15) | collective-permute-done | bytes 393248 | tf_op jit(solution)/shard_map/ppermute | solution.py:38
  65.3 0.9 collective-permute-start.12
  66.3 7.0 %collective-permute-done.16.refs_1_ = f32[8,32,384]{2,1,0:T(8,128)S(1)} collective-permute-done((f32[8,32,384]{2,1,0:T(8,128)S(1)}, f32[8,32,384]{2,1,0:T(8,128)S(1)}, u32[]{:S(2)}, u32[]{:S(2)}) %collective-permute-start.16) | collective-permute-done | bytes 393248 | tf_op jit(solution)/shard_map/ppermute | solution.py:38
  73.3 0.3 collective-permute-done.17.refs_2_
  73.6 1.4 %fold.1 = f32[8,32,384]{2,1,0:T(8,128)} custom-call(s32[3]{0:T(128)S(1)} %pad_add_fusion.place, f32[8,32,384]{2,1,0:T(8,128)S(1)} %collective-permute-done.15.refs_0_, f32[8,32,384]{2,1,0:T(8,128)S(1)} %collective-permute-done.16.refs_1_, f32[8,32,384]{2,1,0:T(8,128)S(1)} %collective-permute-done.17.refs_2_, f32[8,32,384]{2,1,0:T(8,128)S(1)} %get-tuple-element.98.refs_3_, ...), custom_call_target="tpu_custom_call" | custom-call | flops 1048576 | bytes 2097152 | tf_op jit(solution)/shard_map/fold/pallas_call | solution.py:374
  75.0 8.5 %all-to-all-start = ((f32[8,32,384]{2,1,0:T(8,128)}), f32[8,32,384]{2,1,0:T(8,128)S(1)}, u32[]{:S(2)}, u32[]{:S(2)}) async-start(f32[8,32,384]{2,1,0:T(8,128)} %fold.1), calls=%async_computation | async-start | bytes 786432 | tf_op jit(solution)/shard_map/all_to_all | solution.py:529
  83.4 0.0 collective-permute-done.13.refs_3_
  83.4 0.0 collective-permute-done.14.refs_4_
  83.5 0.0 collective-permute-done.12.refs_2_
  83.5 5.9 %input_gradient.1 = (bf16[128,1024]{1,0:T(8,128)(2,1)}, f32[8,128]{1,0:T(8,128)S(1)}) custom-call(s32[3]{0:T(128)S(1)} %pad_add_fusion.place, bf16[1024,384]{1,0:T(8,128)(2,1)S(1)} %get-tuple-element.89.refs_0_.refs_5_, f32[512,384]{1,0:T(8,128)S(1)} %collective-permute-done.11.refs_1_, f32[256,384]{1,0:T(8,128)} %collective-permute-done.12.refs_2_, ...), custom_call_target="tpu_custom_call" | custom-call | flops 6442450944 | bytes 83886080 | tf_op jit(solution)/shard_map/input_gradient/pallas_call | solution.py:341
  89.4 5.7 %all-to-all-done.got = f32[8,32,384]{2,1,0:T(8,128)S(1)} async-done(((f32[8,32,384]{2,1,0:T(8,128)}), f32[8,32,384]{2,1,0:T(8,128)S(1)}, u32[]{:S(2)}, u32[]{:S(2)}) %all-to-all-start) | async-done | bytes 393248 | tf_op jit(solution)/shard_map/all_to_all | solution.py:529
  95.1 0.1 square_sum.1
  95.2 9.3 %all_to_all.21.parts = f32[8,16,128]{2,1,0:T(8,128)S(1)} all-to-all(f32[8,16,128]{2,1,0:T(8,128)S(1)} %square_sum.1), channel_id=1, replica_groups={{0,1,2,3,4,5,6,7},{8,9,10,11,12,13,14,15},{16,17,18,19,20,21,22,23},{24..., dimensions={0} | all-to-all | bytes 131072 | tf_op jit(solution)/shard_map/all_to_all | solution.py:540
  104.5 18.0 %all_to_all.22 = f32[32,1,128]{2,1,0:T(1,128)S(1)} all-to-all(f32[32,1,128]{2,1,0:T(1,128)S(1)} %bitcast.8), channel_id=1, replica_groups={{0,8,16,24,32,40,48,56,64,72,80,88,96,104,112,120,128,136,144,152,160,1..., dimensions={0} | all-to-all | bytes 32768 | tf_op jit(solution)/shard_map/all_to_all | solution.py:543
  122.6 0.7 clip.1
  (6 shorter events, 0.1 us)
Async XLA Ops:
  0.7 1.0 copy-start
  1.7 0.9 copy-start.2
  4.4 18.1 %collective-permute-start.1 = (f32[22,64,128]{2,1,0:T(8,128)}, f32[22,64,128]{2,1,0:T(8,128)S(1)}, u32[]{:S(2)}, u32[]{:S(2)}) collective-permute-start(f32[22,64,128]{2,1,0:T(8,128)} %get-tuple-element.53), channel_id=1, source_target_pairs={{0,2},{1,3},{2,4},{3,5},{4,6},{5,7},{6,0},{7,1},{8,10},{9,11},{10,... | collective-permute-start | bytes 2162696 | tf_op jit(solution)/shard_map/ppermute | solution.py:38
  5.9 17.6 %collective-permute-start.2 = (f32[22,64,128]{2,1,0:T(8,128)S(1)}, f32[22,64,128]{2,1,0:T(8,128)S(1)}, u32[]{:S(2)}, u32[]{:S(2)}) collective-permute-start(f32[22,64,128]{2,1,0:T(8,128)S(1)} %get-tuple-element.54), channel_id=1, source_target_pairs={{0,6},{1,7},{2,0},{3,1},{4,2},{5,3},{6,4},{7,5},{8,14},{9,15},{10,... | collective-permute-start | bytes 2162696 | tf_op jit(solution)/shard_map/ppermute | solution.py:38
  6.7 2.2 %collective-permute-start = (f32[18,64,128]{2,1,0:T(8,128)}, f32[18,64,128]{2,1,0:T(8,128)S(1)}, u32[]{:S(2)}, u32[]{:S(2)}) collective-permute-start(f32[18,64,128]{2,1,0:T(8,128)} %get-tuple-element.51), channel_id=1, source_target_pairs={{0,1},{1,0},{2,3},{3,2},{4,5},{5,4},{6,7},{7,6},{8,9},{9,8},{10,11... | collective-permute-start | bytes 1769480 | tf_op jit(solution)/shard_map/ppermute | solution.py:38
  6.7 2.2 %copy-start.1 = (bf16[2,64,1024]{2,1,0:T(8,128)(2,1)S(1)}, bf16[2,64,1024]{2,1,0:T(8,128)(2,1)}, u32[]{:S(2)}) copy-start(bf16[2,64,1024]{2,1,0:T(8,128)(2,1)} %refs_0_.1) | copy-start | bytes 786436
  6.7 2.2 %copy-start.3 = (bf16[2,64,1024]{2,1,0:T(8,128)(2,1)S(1)}, bf16[2,64,1024]{2,1,0:T(8,128)(2,1)}, u32[]{:S(2)}) copy-start(bf16[2,64,1024]{2,1,0:T(8,128)(2,1)} %refs_1_.1) | copy-start | bytes 786436
  23.6 2.8 %collective-permute-start.3 = (f32[22,64,128]{2,1,0:T(8,128)S(1)}, f32[22,64,128]{2,1,0:T(8,128)S(1)}, u32[]{:S(2)}, u32[]{:S(2)}) collective-permute-start(f32[22,64,128]{2,1,0:T(8,128)S(1)} %get-tuple-element.55), channel_id=1, source_target_pairs={{0,1},{1,0},{2,3},{3,2},{4,5},{5,4},{6,7},{7,6},{8,9},{9,8},{10,11... | collective-permute-start | bytes 2162696 | tf_op jit(solution)/shard_map/ppermute | solution.py:38
  23.7 4.7 %collective-permute-start.6 = (f32[22,64,128]{2,1,0:T(8,128)S(1)}, f32[22,64,128]{2,1,0:T(8,128)S(1)}, u32[]{:S(2)}, u32[]{:S(2)}) collective-permute-start(f32[22,64,128]{2,1,0:T(8,128)S(1)} %get-tuple-element.57), channel_id=1, source_target_pairs={{0,1},{1,0},{2,3},{3,2},{4,5},{5,4},{6,7},{7,6},{8,9},{9,8},{10,11... | collective-permute-start | bytes 2162696 | tf_op jit(solution)/shard_map/ppermute | solution.py:38
  24.2 9.8 %collective-permute-start.4 = (f32[10,64,128]{2,1,0:T(8,128)S(1)}, f32[10,64,128]{2,1,0:T(8,128)S(1)}, u32[]{:S(2)}, u32[]{:S(2)}) collective-permute-start(f32[10,64,128]{2,1,0:T(8,128)S(1)} %slice.8), channel_id=1, source_target_pairs={{0,2},{1,3},{2,4},{3,5},{4,6},{5,7},{6,0},{7,1},{8,10},{9,11},{10,... | collective-permute-start | bytes 983048 | tf_op jit(solution)/shard_map/ppermute | solution.py:38
  25.5 9.5 %collective-permute-start.5 = (f32[10,64,128]{2,1,0:T(8,128)S(1)}, f32[10,64,128]{2,1,0:T(8,128)S(1)}, u32[]{:S(2)}, u32[]{:S(2)}) collective-permute-start(f32[10,64,128]{2,1,0:T(8,128)S(1)} %slice.9), channel_id=1, source_target_pairs={{0,6},{1,7},{2,0},{3,1},{4,2},{5,3},{6,4},{7,5},{8,14},{9,15},{10,... | collective-permute-start | bytes 983048 | tf_op jit(solution)/shard_map/ppermute | solution.py:38
  35.1 2.2 %collective-permute-start.7 = (f32[20,64,128]{2,1,0:T(8,128)S(1)}, f32[20,64,128]{2,1,0:T(8,128)S(1)}, u32[]{:S(2)}, u32[]{:S(2)}) collective-permute-start(f32[20,64,128]{2,1,0:T(8,128)S(1)} %relay.4.refs_0_), channel_id=1, source_target_pairs={{0,1},{1,0},{2,3},{3,2},{4,5},{5,4},{6,7},{7,6},{8,9},{9,8},{10,11... | collective-permute-start | bytes 1966088 | tf_op jit(solution)/shard_map/ppermute | solution.py:38
  39.3 7.9 %collective-permute-start.8 = (f32[2,128,128]{2,1,0:T(8,128)S(1)}, f32[2,128,128]{2,1,0:T(8,128)S(1)}, u32[]{:S(2)}, u32[]{:S(2)}) collective-permute-start(f32[2,128,128]{2,1,0:T(8,128)S(1)} %get-tuple-element.66), channel_id=1, source_target_pairs={{0,16},{1,17},{2,18},{3,19},{4,20},{5,21},{6,22},{7,23},{8,24},{9,... | collective-permute-start | bytes 393224 | tf_op jit(solution)/shard_map/ppermute | solution.py:38
  42.6 7.0 %collective-permute-start.9 = (f32[2,128,128]{2,1,0:T(8,128)S(1)}, f32[2,128,128]{2,1,0:T(8,128)S(1)}, u32[]{:S(2)}, u32[]{:S(2)}) collective-permute-start(f32[2,128,128]{2,1,0:T(8,128)S(1)} %get-tuple-element.67), channel_id=1, source_target_pairs={{0,8},{1,9},{2,10},{3,11},{4,12},{5,13},{6,14},{7,15},{8,16},{9,17... | collective-permute-start | bytes 393224 | tf_op jit(solution)/shard_map/ppermute | solution.py:38
  43.3 6.3 %collective-permute-start.10 = (f32[2,128,128]{2,1,0:T(8,128)S(1)}, f32[2,128,128]{2,1,0:T(8,128)S(1)}, u32[]{:S(2)}, u32[]{:S(2)}) collective-permute-start(f32[2,128,128]{2,1,0:T(8,128)S(1)} %get-tuple-element.68), channel_id=1, source_target_pairs={{0,24},{1,25},{2,26},{3,27},{4,28},{5,29},{6,30},{7,31},{8,0},{9,1... | collective-permute-start | bytes 393224 | tf_op jit(solution)/shard_map/ppermute | solution.py:38
  51.7 7.2 %collective-permute-start.11 = (f32[512,384]{1,0:T(8,128)S(1)}, f32[512,384]{1,0:T(8,128)S(1)}, u32[]{:S(2)}, u32[]{:S(2)}) collective-permute-start(f32[512,384]{1,0:T(8,128)S(1)} %get-tuple-element.90), channel_id=1, source_target_pairs={{0,1},{1,0},{2,3},{3,2},{4,5},{5,4},{6,7},{7,6},{8,9},{9,8},{10,11... | collective-permute-start | bytes 2359304 | tf_op jit(solution)/shard_map/ppermute | solution.py:38
  51.8 13.6 %collective-permute-start.15 = (f32[8,32,384]{2,1,0:T(8,128)S(1)}, f32[8,32,384]{2,1,0:T(8,128)S(1)}, u32[]{:S(2)}, u32[]{:S(2)}) collective-permute-start(f32[8,32,384]{2,1,0:T(8,128)S(1)} %get-tuple-element.95), channel_id=1, source_target_pairs={{0,16},{1,17},{2,18},{3,19},{4,20},{5,21},{6,22},{7,23},{8,24},{9,... | collective-permute-start | bytes 1179656 | tf_op jit(solution)/shard_map/ppermute | solution.py:38
  55.5 17.7 %collective-permute-start.16 = (f32[8,32,384]{2,1,0:T(8,128)S(1)}, f32[8,32,384]{2,1,0:T(8,128)S(1)}, u32[]{:S(2)}, u32[]{:S(2)}) collective-permute-start(f32[8,32,384]{2,1,0:T(8,128)S(1)} %get-tuple-element.96), channel_id=1, source_target_pairs={{0,8},{1,9},{2,10},{3,11},{4,12},{5,13},{6,14},{7,15},{8,16},{9,17... | collective-permute-start | bytes 1179656 | tf_op jit(solution)/shard_map/ppermute | solution.py:38
  57.3 16.2 %collective-permute-start.17 = (f32[8,32,384]{2,1,0:T(8,128)S(1)}, f32[8,32,384]{2,1,0:T(8,128)S(1)}, u32[]{:S(2)}, u32[]{:S(2)}) collective-permute-start(f32[8,32,384]{2,1,0:T(8,128)S(1)} %get-tuple-element.97), channel_id=1, source_target_pairs={{0,24},{1,25},{2,26},{3,27},{4,28},{5,29},{6,30},{7,31},{8,0},{9,1... | collective-permute-start | bytes 1179656 | tf_op jit(solution)/shard_map/ppermute | solution.py:38
  59.7 23.8 %collective-permute-start.13 = (f32[256,384]{1,0:T(8,128)}, f32[256,384]{1,0:T(8,128)S(1)}, u32[]{:S(2)}, u32[]{:S(2)}) collective-permute-start(f32[256,384]{1,0:T(8,128)} %get-tuple-element.92), channel_id=1, source_target_pairs={{0,4},{1,5},{2,6},{3,7},{4,0},{5,1},{6,2},{7,3},{8,12},{9,13},{10,... | collective-permute-start | bytes 1179656 | tf_op jit(solution)/shard_map/ppermute | solution.py:38
  62.5 20.9 %collective-permute-start.14 = (f32[256,384]{1,0:T(8,128)S(1)}, f32[256,384]{1,0:T(8,128)S(1)}, u32[]{:S(2)}, u32[]{:S(2)}) collective-permute-start(f32[256,384]{1,0:T(8,128)S(1)} %get-tuple-element.93), channel_id=1, source_target_pairs={{0,2},{1,3},{2,4},{3,5},{4,6},{5,7},{6,0},{7,1},{8,10},{9,11},{10,... | collective-permute-start | bytes 1179656 | tf_op jit(solution)/shard_map/ppermute | solution.py:38
  65.3 18.1 %collective-permute-start.12 = (f32[256,384]{1,0:T(8,128)S(1)}, f32[256,384]{1,0:T(8,128)}, u32[]{:S(2)}, u32[]{:S(2)}) collective-permute-start(f32[256,384]{1,0:T(8,128)S(1)} %get-tuple-element.91.refs_4_), channel_id=1, source_target_pairs={{0,6},{1,7},{2,0},{3,1},{4,2},{5,3},{6,4},{7,5},{8,14},{9,15},{10,... | collective-permute-start | bytes 1179656 | tf_op jit(solution)/shard_map/ppermute | solution.py:38
  75.0 20.1 %all-to-all-start = ((f32[8,32,384]{2,1,0:T(8,128)}), f32[8,32,384]{2,1,0:T(8,128)S(1)}, u32[]{:S(2)}, u32[]{:S(2)}) async-start(f32[8,32,384]{2,1,0:T(8,128)} %fold.1), calls=%async_computation | async-start | bytes 786432 | tf_op jit(solution)/shard_map/all_to_all | solution.py:529

commit v11 on v10

--- a/solution.py
+++ b/solution.py
@@ -535,7 +535,8 @@
         [first + t for t in range(GROUP)] for first in range(0, dp_count * seq_count, GROUP)
     ]
     half = len(groups) // 2
-    turned = (groups, groups[half:] + groups[:half])
+    spread = [groups[13 * i % len(groups)] for i in range(len(groups))]
+    turned = (spread, spread[half:] + spread[:half])
     across = [[t + first[0] for first in turned[t % 2]] for t in range(GROUP)]
     parts = lax.all_to_all(
         square_sum(got, done), ("dp", "seq"), 0, 0, axis_index_groups=groups

time: 124 us -> 124 us (level)
  no operation moved by 1% of the time
where the time goes in v11:
time: 124 us; the launch traced here: 123 us
  waiting for transfers between devices  38.4 us (31%)
  starting transfers between devices  29.5 us (24%)
  blocking collectives  27.4 us (22%)
  Pallas kernels  23.9 us (19%)
  local copies, waits for them, and re-layouts  3.19 us (3%)
    ppermute x18, waiting for transfers between devices, send(): return lax.ppermute(value, 'seq', seq_perm(dy, dx, dc))  32.7 us
    ppermute x18, starting transfers between devices, send(): return lax.ppermute(value, 'seq', seq_perm(dy, dx, dc))  21 us
    all_to_all x1, blocking collectives, body(): lax.all_to_all(group_square(parts, dp_count * NY), ('dp', 'seq'), 0, 0, a...  18.1 us
    all_to_all x1, blocking collectives, body(): lax.all_to_all(square_sum(got, done), ('dp', 'seq'), 0, 0, axis_index_gro...  9.29 us
    pallas_call x5, Pallas kernels, blocks(): pl.pallas_call(functools.partial(block_kernel, units), out_shape=(struct(...  8.76 us
    all_to_all x1, starting transfers between devices, body(): lax.all_to_all(folded, ('dp', 'seq'), 0, 0, axis_index_groups=columns_of)  8.47 us
    pallas_call x1, Pallas kernels, input_gradient(): pl.pallas_call(input_kernel, grid=(features // step,), out_shape=(struct(...  5.9 us
    all_to_all x1, waiting for transfers between devices, body(): lax.all_to_all(folded, ('dp', 'seq'), 0, 0, axis_index_groups=columns_of)  5.7 us
  transfers between devices with their start and end apart: 19, of which 12 were waited for; matrix products, arithmetic and copies ran while one was open for 1% of the time, Pallas kernels for 14%

profile of v11, /device:TPU:2, one launch (start us, length us, event | category | flops | bytes accessed | tf_op | source)
XLA Modules:
  0.0 123.3 jit_solution(16245831358579985461)
XLA Ops:
  0.7 0.1 pad_add_fusion.place
  0.7 0.0 copy-start
  0.7 0.9 copy-done
  1.7 0.9 copy-done.2
  2.6 1.7 %messages.1 = (f32[22,64,128]{2,1,0:T(8,128)}, f32[22,64,128]{2,1,0:T(8,128)S(1)}, f32[18,64,128]{2,1,0:T(8,128)}) custom-call(s32[3]{0:T(128)S(1)} %pad_add_fusion.place, bf16[2,64,1024]{2,1,0:T(8,128)(2,1)S(1)} %copy-done, bf16[2,64,1024]{2,1,0:T(8,128)(2,1)S(1)} %copy-done.2), custom_call_target="tpu_custom_call" | custom-call | flops 1048576 | bytes 3145728 | tf_op jit(solution)/shard_map/messages/pallas_call | solution.py:76
  4.4 1.5 %collective-permute-start.1 = (f32[22,64,128]{2,1,0:T(8,128)}, f32[22,64,128]{2,1,0:T(8,128)S(1)}, u32[]{:S(2)}, u32[]{:S(2)}) collective-permute-start(f32[22,64,128]{2,1,0:T(8,128)} %get-tuple-element.53), channel_id=1, source_target_pairs={{0,2},{1,3},{2,4},{3,5},{4,6},{5,7},{6,0},{7,1},{8,10},{9,11},{10,... | collective-permute-start | bytes 2162696 | tf_op jit(solution)/shard_map/ppermute | solution.py:38
  5.9 0.8 collective-permute-start.2
  6.7 0.0 collective-permute-start
  6.7 0.0 copy-start.1
  6.7 1.2 %constant_dynamic-slice_fusion.2 = (bf16[1024,128]{1,0:T(8,128)(2,1)S(1)}, bf16[1024,128]{1,0:T(8,128)(2,1)S(1)}, bf16[1024,128]{1,0:T(8,128)(2,1)S(1)}) fusion(bf16[1024,3072]{1,0:T(8,128)(2,1)} %refs_5_.1, s32[]{:T(128)S(6)} %select_n.31, s32[]{:T(128)S(6)} %select_n.32, s32[]{:T(128)S(6)} %select_n.33), kind=kLoop, calls=%fused_computation.3 | loop fusion | bytes 1572876 | tf_op jit(solution)/shard_map/dynamic_slice | solution.py:42
  7.9 0.1 pad_maximum_fusion.w
  8.0 0.9 collective-permute-done.refs_2_
  8.9 0.0 copy-done.1
  8.9 0.0 copy-done.3
  8.9 2.0 %blocks.5 = (bf16[1024,256]{1,0:T(8,128)(2,1)S(1)}, bf16[256,384]{1,0:T(8,128)(2,1)S(1)}, bf16[256,128]{1,0:T(8,128)(2,1)S(1)}, f32[2,2,128,128]{3,2,1,0:T(8,128...) custom-call(s32[3]{0:T(128)S(1)} %pad_add_fusion.place, bf16[1024,384]{1,0:T(8,128)(2,1)S(1)} %pad_maximum_fusion.w, ...), custom_call_target="tpu_custom_call" | custom-call | flops 201326592 | bytes 4194304 | tf_op jit(solution)/shard_map/blocks/pallas_call | solution.py:148
  10.9 11.6 %collective-permute-done.1.refs_0_ = f32[22,64,128]{2,1,0:T(8,128)S(1)} collective-permute-done((f32[22,64,128]{2,1,0:T(8,128)}, f32[22,64,128]{2,1,0:T(8,128)S(1)}, u32[]{:S(2)}, u32[]{:S(2)}) %collective-permute-start.1) | collective-permute-done | bytes 720928 | tf_op jit(solution)/shard_map/ppermute | solution.py:38
  22.5 1.0 collective-permute-done.2.refs_1_.refs_0_
  23.5 0.1 relay.3
  23.6 0.1 collective-permute-start.3
  23.7 0.5 collective-permute-start.6
  24.2 1.3 %collective-permute-start.4 = (f32[10,64,128]{2,1,0:T(8,128)S(1)}, f32[10,64,128]{2,1,0:T(8,128)S(1)}, u32[]{:S(2)}, u32[]{:S(2)}) collective-permute-start(f32[10,64,128]{2,1,0:T(8,128)S(1)} %slice.8), channel_id=1, source_target_pairs={{0,2},{1,3},{2,4},{3,5},{4,6},{5,7},{6,0},{7,1},{8,10},{9,11},{10,... | collective-permute-start | bytes 983048 | tf_op jit(solution)/shard_map/ppermute | solution.py:38
  25.5 0.9 collective-permute-start.5
  26.4 0.0 collective-permute-done.3.refs_1_
  26.4 2.0 %blocks.6 = (bf16[1024,256]{1,0:T(8,128)(2,1)S(1)}, bf16[256,384]{1,0:T(8,128)(2,1)S(1)}, bf16[256,128]{1,0:T(8,128)(2,1)S(1)}, f32[2,2,128,128]{3,2,1,0:T(8,128...) custom-call(s32[3]{0:T(128)S(1)} %pad_add_fusion.place, bf16[1024,384]{1,0:T(8,128)(2,1)S(1)} %pad_maximum_fusion.w, ...), custom_call_target="tpu_custom_call" | custom-call | flops 201326592 | bytes 4194304 | tf_op jit(solution)/shard_map/blocks/pallas_call | solution.py:148
  28.4 0.0 collective-permute-done.6.refs_1_
  28.4 2.0 %blocks.7 = (bf16[1024,256]{1,0:T(8,128)(2,1)S(1)}, bf16[256,384]{1,0:T(8,128)(2,1)S(1)}, bf16[256,128]{1,0:T(8,128)(2,1)S(1)}, f32[2,2,128,128]{3,2,1,0:T(8,128...) custom-call(s32[3]{0:T(128)S(1)} %pad_add_fusion.place, bf16[1024,384]{1,0:T(8,128)(2,1)S(1)} %pad_maximum_fusion.w, ...), custom_call_target="tpu_custom_call" | custom-call | flops 201326592 | bytes 4194304 | tf_op jit(solution)/shard_map/blocks/pallas_call | solution.py:148
  30.4 3.6 %collective-permute-done.4.refs_0_ = f32[10,64,128]{2,1,0:T(8,128)S(1)} collective-permute-done((f32[10,64,128]{2,1,0:T(8,128)S(1)}, f32[10,64,128]{2,1,0:T(8,128)S(1)}, u32[]{:S(2)}, u32[]{:S(2)}) %collective-permute-start.4) | collective-permute-done | bytes 327712 | tf_op jit(solution)/shard_map/ppermute | solution.py:38
  34.0 1.0 collective-permute-done.5.refs_1_
  35.1 0.1 collective-permute-start.7
  35.2 1.4 %blocks.8 = (bf16[1024,128]{1,0:T(8,128)(2,1)S(1)}, bf16[128,384]{1,0:T(8,128)(2,1)S(1)}, bf16[128,128]{1,0:T(8,128)(2,1)S(1)}, f32[1,2,128,128]{3,2,1,0:T(8,128...) custom-call(s32[3]{0:T(128)S(1)} %pad_add_fusion.place, bf16[1024,384]{1,0:T(8,128)(2,1)S(1)} %pad_maximum_fusion.w, ...), custom_call_target="tpu_custom_call" | custom-call | flops 100663296 | bytes 4194304 | tf_op jit(solution)/shard_map/blocks/pallas_call | solution.py:148
  36.6 0.7 collective-permute-done.7.refs_0_
  37.2 1.4 %blocks.9 = (bf16[1024,128]{1,0:T(8,128)(2,1)S(1)}, bf16[128,384]{1,0:T(8,128)(2,1)S(1)}, bf16[128,128]{1,0:T(8,128)(2,1)S(1)}, f32[1,2,128,128]{3,2,1,0:T(8,128...) custom-call(s32[3]{0:T(128)S(1)} %pad_add_fusion.place, bf16[1024,384]{1,0:T(8,128)(2,1)S(1)} %pad_maximum_fusion.w, ...), custom_call_target="tpu_custom_call" | custom-call | flops 100663296 | bytes 4194304 | tf_op jit(solution)/shard_map/blocks/pallas_call | solution.py:148
  38.7 0.6 totals.1
  39.3 3.3 %collective-permute-start.8 = (f32[2,128,128]{2,1,0:T(8,128)S(1)}, f32[2,128,128]{2,1,0:T(8,128)S(1)}, u32[]{:S(2)}, u32[]{:S(2)}) collective-permute-start(f32[2,128,128]{2,1,0:T(8,128)S(1)} %get-tuple-element.66), channel_id=1, source_target_pairs={{0,16},{1,17},{2,18},{3,19},{4,20},{5,21},{6,22},{7,23},{8,24},{9,... | collective-permute-start | bytes 393224 | tf_op jit(solution)/shard_map/ppermute | solution.py:38
  42.6 0.7 collective-permute-start.9
  43.3 2.6 %collective-permute-start.10 = (f32[2,128,128]{2,1,0:T(8,128)S(1)}, f32[2,128,128]{2,1,0:T(8,128)S(1)}, u32[]{:S(2)}, u32[]{:S(2)}) collective-permute-start(f32[2,128,128]{2,1,0:T(8,128)S(1)} %get-tuple-element.68), channel_id=1, source_target_pairs={{0,24},{1,25},{2,26},{3,27},{4,28},{5,29},{6,30},{7,31},{8,0},{9,1... | collective-permute-start | bytes 393224 | tf_op jit(solution)/shard_map/ppermute | solution.py:38
  45.8 1.4 %collective-permute-done.8.refs_0_ = f32[2,128,128]{2,1,0:T(8,128)S(1)} collective-permute-done((f32[2,128,128]{2,1,0:T(8,128)S(1)}, f32[2,128,128]{2,1,0:T(8,128)S(1)}, u32[]{:S(2)}, u32[]{:S(2)}) %collective-permute-start.8) | collective-permute-done | bytes 131104 | tf_op jit(solution)/shard_map/ppermute | solution.py:38
  47.2 2.3 %collective-permute-done.9.refs_1_ = f32[2,128,128]{2,1,0:T(8,128)S(1)} collective-permute-done((f32[2,128,128]{2,1,0:T(8,128)S(1)}, f32[2,128,128]{2,1,0:T(8,128)S(1)}, u32[]{:S(2)}, u32[]{:S(2)}) %collective-permute-start.9) | collective-permute-done | bytes 131104 | tf_op jit(solution)/shard_map/ppermute | solution.py:38
  49.6 0.0 collective-permute-done.10.refs_2_
  49.6 2.1 %gradients.1 = (bf16[1024,384]{1,0:T(8,128)(2,1)S(1)}, f32[512,384]{1,0:T(8,128)S(1)}, f32[8,32,384]{2,1,0:T(8,128)S(1)}) custom-call(s32[3]{0:T(128)S(1)} %pad_add_fusion.place, f32[2,128,128]{2,1,0:T(8,128)S(1)} %collective-permute-done.8.refs_0_, f32[2,128,128]{2,1,0:T(8,128)S(1)} %collective-permute-done.9.refs_1_, ...), custom_call_target="tpu_custom_call" | custom-call | flops 805306368 | bytes 10485760 | tf_op jit(solution)/shard_map/gradients/pallas_call | solution.py:295
  51.7 0.1 collective-permute-start.11
  51.8 2.2 %collective-permute-start.15 = (f32[8,32,384]{2,1,0:T(8,128)S(1)}, f32[8,32,384]{2,1,0:T(8,128)S(1)}, u32[]{:S(2)}, u32[]{:S(2)}) collective-permute-start(f32[8,32,384]{2,1,0:T(8,128)S(1)} %get-tuple-element.95), channel_id=1, source_target_pairs={{0,16},{1,17},{2,18},{3,19},{4,20},{5,21},{6,22},{7,23},{8,24},{9,... | collective-permute-start | bytes 1179656 | tf_op jit(solution)/shard_map/ppermute | solution.py:38
  54.0 1.6 %rest_of_rows.1 = (f32[8,32,384]{2,1,0:T(8,128)S(1)}, f32[8,32,384]{2,1,0:T(8,128)S(1)}, f32[8,32,384]{2,1,0:T(8,128)S(1)}) custom-call(s32[3]{0:T(128)S(1)} %pad_add_fusion.place, bf16[1024,256]{1,0:T(8,128)(2,1)S(1)} %get-tuple-element.69.refs_13_.refs_0_, bf16[1024,256]{1,0:T(8,128)(2,1)S(1)} %get-tuple-element.70.refs_14_.refs_1_, ...), custom_call_target="tpu_custom_call" | custom-call | flops 1048576 | bytes 4194304 | tf_op jit(solution)/shard_map/rest_of_rows/pallas_call | solution.py:277
  55.5 1.8 %collective-permute-start.16 = (f32[8,32,384]{2,1,0:T(8,128)S(1)}, f32[8,32,384]{2,1,0:T(8,128)S(1)}, u32[]{:S(2)}, u32[]{:S(2)}) collective-permute-start(f32[8,32,384]{2,1,0:T(8,128)S(1)} %get-tuple-element.96), channel_id=1, source_target_pairs={{0,8},{1,9},{2,10},{3,11},{4,12},{5,13},{6,14},{7,15},{8,16},{9,17... | collective-permute-start | bytes 1179656 | tf_op jit(solution)/shard_map/ppermute | solution.py:38
  57.3 1.5 %collective-permute-start.17 = (f32[8,32,384]{2,1,0:T(8,128)S(1)}, f32[8,32,384]{2,1,0:T(8,128)S(1)}, u32[]{:S(2)}, u32[]{:S(2)}) collective-permute-start(f32[8,32,384]{2,1,0:T(8,128)S(1)} %get-tuple-element.97), channel_id=1, source_target_pairs={{0,24},{1,25},{2,26},{3,27},{4,28},{5,29},{6,30},{7,31},{8,0},{9,1... | collective-permute-start | bytes 1179656 | tf_op jit(solution)/shard_map/ppermute | solution.py:38
  58.8 0.0 collective-permute-done.11.refs_1_
  58.8 0.8 relay.5
  59.7 2.8 %collective-permute-start.13 = (f32[256,384]{1,0:T(8,128)}, f32[256,384]{1,0:T(8,128)S(1)}, u32[]{:S(2)}, u32[]{:S(2)}) collective-permute-start(f32[256,384]{1,0:T(8,128)} %get-tuple-element.92), channel_id=1, source_target_pairs={{0,4},{1,5},{2,6},{3,7},{4,0},{5,1},{6,2},{7,3},{8,12},{9,13},{10,... | collective-permute-start | bytes 1179656 | tf_op jit(solution)/shard_map/ppermute | solution.py:38
  62.5 0.0 collective-permute-start.14
  62.5 2.8 %collective-permute-done.15.refs_0_ = f32[8,32,384]{2,1,0:T(8,128)S(1)} collective-permute-done((f32[8,32,384]{2,1,0:T(8,128)S(1)}, f32[8,32,384]{2,1,0:T(8,128)S(1)}, u32[]{:S(2)}, u32[]{:S(2)}) %collective-permute-start.15) | collective-permute-done | bytes 393248 | tf_op jit(solution)/shard_map/ppermute | solution.py:38
  65.3 0.9 collective-permute-start.12
  66.3 7.0 %collective-permute-done.16.refs_1_ = f32[8,32,384]{2,1,0:T(8,128)S(1)} collective-permute-done((f32[8,32,384]{2,1,0:T(8,128)S(1)}, f32[8,32,384]{2,1,0:T(8,128)S(1)}, u32[]{:S(2)}, u32[]{:S(2)}) %collective-permute-start.16) | collective-permute-done | bytes 393248 | tf_op jit(solution)/shard_map/ppermute | solution.py:38
  73.3 0.3 collective-permute-done.17.refs_2_
  73.6 1.4 %fold.1 = f32[8,32,384]{2,1,0:T(8,128)} custom-call(s32[3]{0:T(128)S(1)} %pad_add_fusion.place, f32[8,32,384]{2,1,0:T(8,128)S(1)} %collective-permute-done.15.refs_0_, f32[8,32,384]{2,1,0:T(8,128)S(1)} %collective-permute-done.16.refs_1_, f32[8,32,384]{2,1,0:T(8,128)S(1)} %collective-permute-done.17.refs_2_, f32[8,32,384]{2,1,0:T(8,128)S(1)} %get-tuple-element.98.refs_3_, ...), custom_call_target="tpu_custom_call" | custom-call | flops 1048576 | bytes 2097152 | tf_op jit(solution)/shard_map/fold/pallas_call | solution.py:374
  75.0 8.5 %all-to-all-start = ((f32[8,32,384]{2,1,0:T(8,128)}), f32[8,32,384]{2,1,0:T(8,128)S(1)}, u32[]{:S(2)}, u32[]{:S(2)}) async-start(f32[8,32,384]{2,1,0:T(8,128)} %fold.1), calls=%async_computation | async-start | bytes 786432 | tf_op jit(solution)/shard_map/all_to_all | solution.py:529
  83.4 0.0 collective-permute-done.13.refs_3_
  83.4 0.0 collective-permute-done.14.refs_4_
  83.5 0.0 collective-permute-done.12.refs_2_
  83.5 5.9 %input_gradient.1 = (bf16[128,1024]{1,0:T(8,128)(2,1)}, f32[8,128]{1,0:T(8,128)S(1)}) custom-call(s32[3]{0:T(128)S(1)} %pad_add_fusion.place, bf16[1024,384]{1,0:T(8,128)(2,1)S(1)} %get-tuple-element.89.refs_0_.refs_5_, f32[512,384]{1,0:T(8,128)S(1)} %collective-permute-done.11.refs_1_, f32[256,384]{1,0:T(8,128)} %collective-permute-done.12.refs_2_, ...), custom_call_target="tpu_custom_call" | custom-call | flops 6442450944 | bytes 83886080 | tf_op jit(solution)/shard_map/input_gradient/pallas_call | solution.py:341
  89.4 5.7 %all-to-all-done.got = f32[8,32,384]{2,1,0:T(8,128)S(1)} async-done(((f32[8,32,384]{2,1,0:T(8,128)}), f32[8,32,384]{2,1,0:T(8,128)S(1)}, u32[]{:S(2)}, u32[]{:S(2)}) %all-to-all-start) | async-done | bytes 393248 | tf_op jit(solution)/shard_map/all_to_all | solution.py:529
  95.1 0.1 square_sum.1
  95.2 9.3 %all_to_all.21.parts = f32[8,16,128]{2,1,0:T(8,128)S(1)} all-to-all(f32[8,16,128]{2,1,0:T(8,128)S(1)} %square_sum.1), channel_id=1, replica_groups={{0,1,2,3,4,5,6,7},{8,9,10,11,12,13,14,15},{16,17,18,19,20,21,22,23},{24..., dimensions={0} | all-to-all | bytes 131072 | tf_op jit(solution)/shard_map/all_to_all | solution.py:541
  104.5 18.1 %all_to_all.22 = f32[32,1,128]{2,1,0:T(1,128)S(1)} all-to-all(f32[32,1,128]{2,1,0:T(1,128)S(1)} %bitcast.8), channel_id=1, replica_groups={{0,104,208,56,160,8,112,216,64,168,16,120,224,72,176,24,128,232,80,184,..., dimensions={0} | all-to-all | bytes 32768 | tf_op jit(solution)/shard_map/all_to_all | solution.py:544
  122.6 0.7 clip.1
  (6 shorter events, 0.1 us)
Async XLA Ops:
  0.7 1.0 copy-start
  1.7 0.9 copy-start.2
  4.4 18.1 %collective-permute-start.1 = (f32[22,64,128]{2,1,0:T(8,128)}, f32[22,64,128]{2,1,0:T(8,128)S(1)}, u32[]{:S(2)}, u32[]{:S(2)}) collective-permute-start(f32[22,64,128]{2,1,0:T(8,128)} %get-tuple-element.53), channel_id=1, source_target_pairs={{0,2},{1,3},{2,4},{3,5},{4,6},{5,7},{6,0},{7,1},{8,10},{9,11},{10,... | collective-permute-start | bytes 2162696 | tf_op jit(solution)/shard_map/ppermute | solution.py:38
  5.9 17.6 %collective-permute-start.2 = (f32[22,64,128]{2,1,0:T(8,128)S(1)}, f32[22,64,128]{2,1,0:T(8,128)S(1)}, u32[]{:S(2)}, u32[]{:S(2)}) collective-permute-start(f32[22,64,128]{2,1,0:T(8,128)S(1)} %get-tuple-element.54), channel_id=1, source_target_pairs={{0,6},{1,7},{2,0},{3,1},{4,2},{5,3},{6,4},{7,5},{8,14},{9,15},{10,... | collective-permute-start | bytes 2162696 | tf_op jit(solution)/shard_map/ppermute | solution.py:38
  6.7 2.2 %collective-permute-start = (f32[18,64,128]{2,1,0:T(8,128)}, f32[18,64,128]{2,1,0:T(8,128)S(1)}, u32[]{:S(2)}, u32[]{:S(2)}) collective-permute-start(f32[18,64,128]{2,1,0:T(8,128)} %get-tuple-element.51), channel_id=1, source_target_pairs={{0,1},{1,0},{2,3},{3,2},{4,5},{5,4},{6,7},{7,6},{8,9},{9,8},{10,11... | collective-permute-start | bytes 1769480 | tf_op jit(solution)/shard_map/ppermute | solution.py:38
  6.7 2.2 %copy-start.1 = (bf16[2,64,1024]{2,1,0:T(8,128)(2,1)S(1)}, bf16[2,64,1024]{2,1,0:T(8,128)(2,1)}, u32[]{:S(2)}) copy-start(bf16[2,64,1024]{2,1,0:T(8,128)(2,1)} %refs_0_.1) | copy-start | bytes 786436
  6.7 2.2 %copy-start.3 = (bf16[2,64,1024]{2,1,0:T(8,128)(2,1)S(1)}, bf16[2,64,1024]{2,1,0:T(8,128)(2,1)}, u32[]{:S(2)}) copy-start(bf16[2,64,1024]{2,1,0:T(8,128)(2,1)} %refs_1_.1) | copy-start | bytes 786436
  23.6 2.8 %collective-permute-start.3 = (f32[22,64,128]{2,1,0:T(8,128)S(1)}, f32[22,64,128]{2,1,0:T(8,128)S(1)}, u32[]{:S(2)}, u32[]{:S(2)}) collective-permute-start(f32[22,64,128]{2,1,0:T(8,128)S(1)} %get-tuple-element.55), channel_id=1, source_target_pairs={{0,1},{1,0},{2,3},{3,2},{4,5},{5,4},{6,7},{7,6},{8,9},{9,8},{10,11... | collective-permute-start | bytes 2162696 | tf_op jit(solution)/shard_map/ppermute | solution.py:38
  23.7 4.7 %collective-permute-start.6 = (f32[22,64,128]{2,1,0:T(8,128)S(1)}, f32[22,64,128]{2,1,0:T(8,128)S(1)}, u32[]{:S(2)}, u32[]{:S(2)}) collective-permute-start(f32[22,64,128]{2,1,0:T(8,128)S(1)} %get-tuple-element.57), channel_id=1, source_target_pairs={{0,1},{1,0},{2,3},{3,2},{4,5},{5,4},{6,7},{7,6},{8,9},{9,8},{10,11... | collective-permute-start | bytes 2162696 | tf_op jit(solution)/shard_map/ppermute | solution.py:38
  24.2 9.8 %collective-permute-start.4 = (f32[10,64,128]{2,1,0:T(8,128)S(1)}, f32[10,64,128]{2,1,0:T(8,128)S(1)}, u32[]{:S(2)}, u32[]{:S(2)}) collective-permute-start(f32[10,64,128]{2,1,0:T(8,128)S(1)} %slice.8), channel_id=1, source_target_pairs={{0,2},{1,3},{2,4},{3,5},{4,6},{5,7},{6,0},{7,1},{8,10},{9,11},{10,... | collective-permute-start | bytes 983048 | tf_op jit(solution)/shard_map/ppermute | solution.py:38
  25.5 9.5 %collective-permute-start.5 = (f32[10,64,128]{2,1,0:T(8,128)S(1)}, f32[10,64,128]{2,1,0:T(8,128)S(1)}, u32[]{:S(2)}, u32[]{:S(2)}) collective-permute-start(f32[10,64,128]{2,1,0:T(8,128)S(1)} %slice.9), channel_id=1, source_target_pairs={{0,6},{1,7},{2,0},{3,1},{4,2},{5,3},{6,4},{7,5},{8,14},{9,15},{10,... | collective-permute-start | bytes 983048 | tf_op jit(solution)/shard_map/ppermute | solution.py:38
  35.1 2.2 %collective-permute-start.7 = (f32[20,64,128]{2,1,0:T(8,128)S(1)}, f32[20,64,128]{2,1,0:T(8,128)S(1)}, u32[]{:S(2)}, u32[]{:S(2)}) collective-permute-start(f32[20,64,128]{2,1,0:T(8,128)S(1)} %relay.4.refs_0_), channel_id=1, source_target_pairs={{0,1},{1,0},{2,3},{3,2},{4,5},{5,4},{6,7},{7,6},{8,9},{9,8},{10,11... | collective-permute-start | bytes 1966088 | tf_op jit(solution)/shard_map/ppermute | solution.py:38
  39.3 7.9 %collective-permute-start.8 = (f32[2,128,128]{2,1,0:T(8,128)S(1)}, f32[2,128,128]{2,1,0:T(8,128)S(1)}, u32[]{:S(2)}, u32[]{:S(2)}) collective-permute-start(f32[2,128,128]{2,1,0:T(8,128)S(1)} %get-tuple-element.66), channel_id=1, source_target_pairs={{0,16},{1,17},{2,18},{3,19},{4,20},{5,21},{6,22},{7,23},{8,24},{9,... | collective-permute-start | bytes 393224 | tf_op jit(solution)/shard_map/ppermute | solution.py:38
  42.6 7.0 %collective-permute-start.9 = (f32[2,128,128]{2,1,0:T(8,128)S(1)}, f32[2,128,128]{2,1,0:T(8,128)S(1)}, u32[]{:S(2)}, u32[]{:S(2)}) collective-permute-start(f32[2,128,128]{2,1,0:T(8,128)S(1)} %get-tuple-element.67), channel_id=1, source_target_pairs={{0,8},{1,9},{2,10},{3,11},{4,12},{5,13},{6,14},{7,15},{8,16},{9,17... | collective-permute-start | bytes 393224 | tf_op jit(solution)/shard_map/ppermute | solution.py:38
  43.3 6.3 %collective-permute-start.10 = (f32[2,128,128]{2,1,0:T(8,128)S(1)}, f32[2,128,128]{2,1,0:T(8,128)S(1)}, u32[]{:S(2)}, u32[]{:S(2)}) collective-permute-start(f32[2,128,128]{2,1,0:T(8,128)S(1)} %get-tuple-element.68), channel_id=1, source_target_pairs={{0,24},{1,25},{2,26},{3,27},{4,28},{5,29},{6,30},{7,31},{8,0},{9,1... | collective-permute-start | bytes 393224 | tf_op jit(solution)/shard_map/ppermute | solution.py:38
  51.7 7.2 %collective-permute-start.11 = (f32[512,384]{1,0:T(8,128)S(1)}, f32[512,384]{1,0:T(8,128)S(1)}, u32[]{:S(2)}, u32[]{:S(2)}) collective-permute-start(f32[512,384]{1,0:T(8,128)S(1)} %get-tuple-element.90), channel_id=1, source_target_pairs={{0,1},{1,0},{2,3},{3,2},{4,5},{5,4},{6,7},{7,6},{8,9},{9,8},{10,11... | collective-permute-start | bytes 2359304 | tf_op jit(solution)/shard_map/ppermute | solution.py:38
  51.8 13.6 %collective-permute-start.15 = (f32[8,32,384]{2,1,0:T(8,128)S(1)}, f32[8,32,384]{2,1,0:T(8,128)S(1)}, u32[]{:S(2)}, u32[]{:S(2)}) collective-permute-start(f32[8,32,384]{2,1,0:T(8,128)S(1)} %get-tuple-element.95), channel_id=1, source_target_pairs={{0,16},{1,17},{2,18},{3,19},{4,20},{5,21},{6,22},{7,23},{8,24},{9,... | collective-permute-start | bytes 1179656 | tf_op jit(solution)/shard_map/ppermute | solution.py:38
  55.5 17.7 %collective-permute-start.16 = (f32[8,32,384]{2,1,0:T(8,128)S(1)}, f32[8,32,384]{2,1,0:T(8,128)S(1)}, u32[]{:S(2)}, u32[]{:S(2)}) collective-permute-start(f32[8,32,384]{2,1,0:T(8,128)S(1)} %get-tuple-element.96), channel_id=1, source_target_pairs={{0,8},{1,9},{2,10},{3,11},{4,12},{5,13},{6,14},{7,15},{8,16},{9,17... | collective-permute-start | bytes 1179656 | tf_op jit(solution)/shard_map/ppermute | solution.py:38
  57.3 16.2 %collective-permute-start.17 = (f32[8,32,384]{2,1,0:T(8,128)S(1)}, f32[8,32,384]{2,1,0:T(8,128)S(1)}, u32[]{:S(2)}, u32[]{:S(2)}) collective-permute-start(f32[8,32,384]{2,1,0:T(8,128)S(1)} %get-tuple-element.97), channel_id=1, source_target_pairs={{0,24},{1,25},{2,26},{3,27},{4,28},{5,29},{6,30},{7,31},{8,0},{9,1... | collective-permute-start | bytes 1179656 | tf_op jit(solution)/shard_map/ppermute | solution.py:38
  59.7 23.8 %collective-permute-start.13 = (f32[256,384]{1,0:T(8,128)}, f32[256,384]{1,0:T(8,128)S(1)}, u32[]{:S(2)}, u32[]{:S(2)}) collective-permute-start(f32[256,384]{1,0:T(8,128)} %get-tuple-element.92), channel_id=1, source_target_pairs={{0,4},{1,5},{2,6},{3,7},{4,0},{5,1},{6,2},{7,3},{8,12},{9,13},{10,... | collective-permute-start | bytes 1179656 | tf_op jit(solution)/shard_map/ppermute | solution.py:38
  62.5 20.9 %collective-permute-start.14 = (f32[256,384]{1,0:T(8,128)S(1)}, f32[256,384]{1,0:T(8,128)S(1)}, u32[]{:S(2)}, u32[]{:S(2)}) collective-permute-start(f32[256,384]{1,0:T(8,128)S(1)} %get-tuple-element.93), channel_id=1, source_target_pairs={{0,2},{1,3},{2,4},{3,5},{4,6},{5,7},{6,0},{7,1},{8,10},{9,11},{10,... | collective-permute-start | bytes 1179656 | tf_op jit(solution)/shard_map/ppermute | solution.py:38
  65.3 18.1 %collective-permute-start.12 = (f32[256,384]{1,0:T(8,128)S(1)}, f32[256,384]{1,0:T(8,128)}, u32[]{:S(2)}, u32[]{:S(2)}) collective-permute-start(f32[256,384]{1,0:T(8,128)S(1)} %get-tuple-element.91.refs_4_), channel_id=1, source_target_pairs={{0,6},{1,7},{2,0},{3,1},{4,2},{5,3},{6,4},{7,5},{8,14},{9,15},{10,... | collective-permute-start | bytes 1179656 | tf_op jit(solution)/shard_map/ppermute | solution.py:38
  75.0 20.1 %all-to-all-start = ((f32[8,32,384]{2,1,0:T(8,128)}), f32[8,32,384]{2,1,0:T(8,128)S(1)}, u32[]{:S(2)}, u32[]{:S(2)}) async-start(f32[8,32,384]{2,1,0:T(8,128)} %fold.1), calls=%async_computation | async-start | bytes 786432 | tf_op jit(solution)/shard_map/all_to_all | solution.py:529
